TPU v7x, 32 devices: a whole 2x2x4 slice. The times are simulated.
32 devices in a mesh: group: 4 (over z), ctx: 2 (over x), tensor: 4 (over y, core).
Axes of the slice: x: 2, y: 2, z: 4, core: 2. Of those that a mesh axis runs over, the one named last changes fastest.
Arguments:
- tokens: bfloat16 [4, 3, 1024, 1280], P('group', None, 'ctx'), may hold values from -0.16992188 to 0.16992188
- cotangent: bfloat16 [4, 3, 1024, 1280], P('group', None, 'ctx'), may hold values from -6 to 6
- segments: int32 [4, 3, 1024], P('group'), may hold values from 0 to 7, never falling along the last dimension, each value on 1 to 512 neighbouring positions
- shard_order: int32 [2], replicated, may hold values from 0 to 1, each once
- attention_weights: float32 [4, 1280, 1280], P(None, ('tensor', 'ctx')), may hold values from -0.15625 to 0.15625
- feedforward_weights: float32 [3, 5120, 1280], P(None, ('tensor', 'ctx')), may hold values from -0.15625 to 0.15625
- head_scales: float32 [1280], P(('tensor', 'ctx')), may hold values from 0.8 to 1.6
- hidden_scales: float32 [2, 5120], P(None, ('tensor', 'ctx')), may hold values from 0.5 to 2
- residual_rates: float32 [2, 1280], P(None, 'ctx'), may hold values from 0.1 to 0.8
- attention_first: float32 [4, 4, 1280, 1280], P('group', None, ('tensor', 'ctx')), may hold values from -1.8 to 1.8
- feedforward_first: float32 [4, 3, 5120, 1280], P('group', None, ('tensor', 'ctx')), may hold values from -0.75 to 0.75
- heads_first: float32 [4, 1280], P('group', ('tensor', 'ctx')), may hold values from -24 to 24
- hidden_first: float32 [4, 2, 5120], P('group', None, ('tensor', 'ctx')), may hold values from -0.72 to 0.72
- rates_first: float32 [4, 2, 1280], P('group', None, 'ctx'), may hold values from -4.2 to 4.2
- attention_second: float32 [4, 4, 1280, 1280], P('group', None, ('tensor', 'ctx')), may hold values from 0.12 to 0.48
- feedforward_second: float32 [4, 3, 5120, 1280], P('group', None, ('tensor', 'ctx')), may hold values from 0.02 to 0.08
- heads_second: float32 [4, 1280], P('group', ('tensor', 'ctx')), may hold values from 3 to 12
- hidden_second: float32 [4, 2, 5120], P('group', None, ('tensor', 'ctx')), may hold values from 0.02 to 0.08
- rates_second: float32 [4, 2, 1280], P('group', None, 'ctx'), may hold values from 0.6 to 2.4
- attention_outer: float32 [4, 1280, 1280], P(None, ('tensor', 'ctx')), may hold values from -0.024 to 0.024
- feedforward_outer: float32 [3, 5120, 1280], P(None, ('tensor', 'ctx')), may hold values from -0.024 to 0.024
- heads_outer: float32 [1280], P(('tensor', 'ctx')), may hold values from -0.18 to 0.18
- hidden_outer: float32 [2, 5120], P(None, ('tensor', 'ctx')), may hold values from -0.18 to 0.18
- rates_outer: float32 [2, 1280], P(None, 'ctx'), may hold values from -0.18 to 0.18
Outputs:
- block_output: float32 [4, 3, 1024, 1280], P('group', None, 'ctx')
- input_gradient: float32 [4, 3, 1024, 1280], P('group', None, 'ctx')
- attention_gradient: float32 [4, 4, 1280, 1280], P('group', None, ('tensor', 'ctx'))
- feedforward_gradient: float32 [4, 3, 5120, 1280], P('group', None, ('tensor', 'ctx'))
- heads_gradient: float32 [4, 1280], P('group', ('tensor', 'ctx'))
- hidden_gradient: float32 [4, 2, 5120], P('group', None, ('tensor', 'ctx'))
- rates_gradient: float32 [4, 2, 1280], P('group', None, 'ctx')
- attention_moment: float32 [4, 4, 1280, 1280], P('group', None, ('tensor', 'ctx'))
- feedforward_moment: float32 [4, 3, 5120, 1280], P('group', None, ('tensor', 'ctx'))
- heads_moment: float32 [4, 1280], P('group', ('tensor', 'ctx'))
- hidden_moment: float32 [4, 2, 5120], P('group', None, ('tensor', 'ctx'))
- rates_moment: float32 [4, 2, 1280], P('group', None, 'ctx')
- attention_variance: float32 [4, 4, 1280, 1280], P('group', None, ('tensor', 'ctx'))
- feedforward_variance: float32 [4, 3, 5120, 1280], P('group', None, ('tensor', 'ctx'))
- heads_variance: float32 [4, 1280], P('group', ('tensor', 'ctx'))
- hidden_variance: float32 [4, 2, 5120], P('group', None, ('tensor', 'ctx'))
- rates_variance: float32 [4, 2, 1280], P('group', None, 'ctx')
- attention_momentum: float32 [4, 1280, 1280], P(None, ('tensor', 'ctx'))
- feedforward_momentum: float32 [3, 5120, 1280], P(None, ('tensor', 'ctx'))
- heads_momentum: float32 [1280], P(('tensor', 'ctx'))
- hidden_momentum: float32 [2, 5120], P(None, ('tensor', 'ctx'))
- rates_momentum: float32 [2, 1280], P(None, 'ctx')
- attention_master: float32 [4, 1280, 1280], P(None, ('tensor', 'ctx'))
- feedforward_master: float32 [3, 5120, 1280], P(None, ('tensor', 'ctx'))
- heads_master: float32 [1280], P(('tensor', 'ctx'))
- hidden_master: float32 [2, 5120], P(None, ('tensor', 'ctx'))
- rates_master: float32 [2, 1280], P(None, 'ctx')
Inputs may be any that keep to these rules, and one draw needn't show every extreme that they name: `segments`: along each sequence the document number never falls; each document covers 1 to 512 positions and one covers exactly 512. `shard_order`: A permutation: every ctx index appears once.
All inputs are finite; a program needn't handle non-finite values.
Results may differ from a plain program's by a relative error of at most 0.015.
The roundings to bfloat16 on the way count: a program that leaves them out, or rounds other values in their place, can miss the bound.
Values may be sent and summed in bfloat16 or wider, within the bound.
A program may use at most 384 MiB of HBM per device.

v0:
```python
from functools import partial
import math

import jax
import jax.numpy as jnp
from jax import lax
from jax.sharding import PartitionSpec as P

HEAD_DIM = 64


EPSILON = 1e-06
BETA_ONE = 0.9
BETA_TWO = 0.95
CORR_ONE = 1.0 - 0.9**4
CORR_TWO = 1.0 - 0.95**4
ADAM_EPS = 1e-08
DECAY = 0.1
MATRIX_RATE = 0.02
SCALE_RATE = 0.3
OUTER_RATE = 0.7
OUTER_MOMENTUM = 0.9


def unit_rows(values):
    scale = lax.rsqrt(jnp.sum(values * values, axis=-1, keepdims=True) + EPSILON)
    return (values * scale, scale)


def unit_only(values):
    return values * lax.rsqrt(jnp.sum(values * values, axis=-1, keepdims=True) + EPSILON)


def unit_back(unit, scale, upstream):
    return scale * (upstream - unit * jnp.sum(upstream * unit, axis=-1, keepdims=True))


def lookup_order(block_ids, shard_order):
    table = jnp.arange(shard_order.shape[0], dtype=jnp.int32)
    return jnp.sum(jnp.where(block_ids[:, None] == table[None, :], shard_order[None, :], 0), axis=1)


def key_positions(row_start, key_count, rows_local, shard_order):
    index_row = row_start + jnp.arange(key_count, dtype=jnp.int32)
    return lookup_order(index_row // rows_local, shard_order) * rows_local + index_row % rows_local


def piece_weights(
    query_block, query_place, query_segment, piece, row_start, segment_row, rows_local, shard_order
):
    key_count = piece.shape[0]
    head_count = query_block.shape[1]
    half_width = piece.shape[1] // 2
    key_part = piece[:, :half_width].reshape(key_count, head_count, -1)
    value_part = piece[:, half_width:].reshape(key_count, head_count, -1)
    places = key_positions(row_start, key_count, rows_local, shard_order)
    key_segment = jnp.take(segment_row, places)
    allowed = (query_segment[:, None] == key_segment[None, :]) & (
        places[None, :] <= query_place[:, None]
    )
    scores = jnp.einsum("qhd,khd->hqk", query_block, key_part, preferred_element_type=jnp.float32)
    raised = jnp.where(allowed[None], jnp.exp(scores), 0.0)
    return (raised, key_part, value_part)


def accumulate(
    running,
    piece,
    row_start,
    query_block,
    query_place,
    query_segment,
    segment_row,
    rows_local,
    shard_order,
):
    raised, key_part, value_part = piece_weights(
        query_block,
        query_place,
        query_segment,
        piece,
        row_start,
        segment_row,
        rows_local,
        shard_order,
    )
    row_total = jnp.sum(raised, axis=-1)
    summed = jnp.einsum(
        "hqk,khd->hqd", raised.astype(jnp.bfloat16), value_part, preferred_element_type=jnp.float32
    )
    return (row_total, summed)


def adam_step(master, gradient, first_state, second_state, step_rate, is_matrix):
    moment = BETA_ONE * first_state + (1.0 - BETA_ONE) * gradient
    variance = BETA_TWO * second_state + (1.0 - BETA_TWO) * gradient * gradient
    update = moment / CORR_ONE / (jnp.sqrt(variance / CORR_TWO) + ADAM_EPS)
    updated = master - step_rate * (update + DECAY * master)
    if is_matrix:
        updated = unit_only(updated)
    return (moment, variance, updated)


def outer_step(master, shift, outer_state, is_matrix):
    momentum = OUTER_MOMENTUM * outer_state + shift
    result = master - OUTER_RATE * (shift + OUTER_MOMENTUM * momentum)
    if is_matrix:
        result = unit_only(result)
    return (momentum, result)


def on_device(
    tokens,
    cotangent,
    segments,
    shard_order,
    attention_weights,
    feedforward_weights,
    head_scales,
    hidden_scales,
    residual_rates,
    attention_first,
    feedforward_first,
    heads_first,
    hidden_first,
    rates_first,
    attention_second,
    feedforward_second,
    heads_second,
    hidden_second,
    rates_second,
    attention_outer,
    feedforward_outer,
    heads_outer,
    hidden_outer,
    rates_outer,
):
    attention_full, feed_full, heads_full, hidden_full, rates_full = (
        lax.all_gather(attention_weights.astype(jnp.bfloat16), "ctx", axis=1, tiled=True),
        lax.all_gather(feedforward_weights.astype(jnp.bfloat16), "ctx", axis=1, tiled=True),
        lax.all_gather(head_scales.astype(jnp.bfloat16), "ctx", axis=0, tiled=True),
        lax.all_gather(hidden_scales.astype(jnp.bfloat16), "ctx", axis=1, tiled=True),
        lax.all_gather(residual_rates.astype(jnp.bfloat16), "ctx", axis=1, tiled=True),
    )
    micro_count = tokens.shape[1]
    rows_local = tokens.shape[2]
    model_width = tokens.shape[3]
    all_rows = micro_count * rows_local
    head_width = attention_full.shape[1]
    head_count = head_width // HEAD_DIM
    seq_length = rows_local * lax.axis_size("ctx")
    root_head = math.sqrt(HEAD_DIM)
    root_width = math.sqrt(model_width)
    token_rows = tokens[0].reshape(all_rows, model_width)
    token_float = token_rows.astype(jnp.float32)
    cotangent_rows = cotangent[0].reshape(all_rows, model_width).astype(jnp.float32)
    projected = jnp.einsum(
        "rd,khd->krh", token_rows, attention_full[:3], preferred_element_type=jnp.float32
    )
    query_unit, query_norm = unit_rows(projected[0].reshape(all_rows, head_count, HEAD_DIM))
    key_unit, key_norm = unit_rows(projected[1].reshape(all_rows, head_count, HEAD_DIM))
    scale_heads = heads_full.astype(jnp.float32).reshape(head_count, HEAD_DIM)
    query_low = (query_unit * scale_heads * root_head).astype(jnp.bfloat16)
    key_low = (key_unit * scale_heads).astype(jnp.bfloat16).reshape(all_rows, head_width)
    key_value = jnp.concatenate([key_low, projected[2].astype(jnp.bfloat16)], axis=1).reshape(
        micro_count, rows_local, 2 * head_width
    )
    own_places = key_positions(
        lax.axis_index("ctx") * rows_local, rows_local, rows_local, shard_order
    )
    totals = []
    summeds = []
    head_outputs = []
    for micro_index in range(micro_count):
        segment_row = segments[0, micro_index]
        query_block = query_low[micro_index * rows_local : (micro_index + 1) * rows_local]
        query_segment = jnp.take(segment_row, own_places)
        fold_keys = partial(
            accumulate,
            query_block=query_block,
            query_place=own_places,
            query_segment=query_segment,
            segment_row=segment_row,
            rows_local=rows_local,
            shard_order=shard_order,
        )
        empty_carry = (
            jnp.zeros((head_count, rows_local), jnp.float32),
            jnp.zeros((head_count, rows_local, HEAD_DIM), jnp.float32),
        )
        row_total, summed = fold_keys(
            empty_carry,
            lax.all_gather(key_value[micro_index], "ctx", axis=0, tiled=True),
            jnp.int32(0),
        )
        totals.append(row_total)
        summeds.append(summed)
        head_outputs.append(
            jnp.transpose(summed / row_total[:, :, None], (1, 0, 2)).reshape(rows_local, head_width)
        )
    heads_low = jnp.concatenate(head_outputs, axis=0).astype(jnp.bfloat16)
    attention_part = jnp.dot(heads_low, attention_full[3], preferred_element_type=jnp.float32)
    attention_total = lax.psum(attention_part, "tensor")
    attention_unit, attention_norm = unit_rows(attention_total)
    rates_float = rates_full.astype(jnp.float32)
    rate_attention = rates_float[0]
    rate_feed = rates_float[1]
    after_attention, after_norm = unit_rows(
        token_float + rate_attention * (attention_unit - token_float)
    )
    normed_low = after_attention.astype(jnp.bfloat16)
    gate_up = jnp.einsum(
        "rd,khd->krh", normed_low, feed_full[:2], preferred_element_type=jnp.float32
    )
    hidden_float = hidden_full.astype(jnp.float32)
    up_scaled = gate_up[0] * hidden_float[0]
    gate_scaled = gate_up[1] * hidden_float[1] * root_width
    sigmoid_gate = jax.nn.sigmoid(gate_scaled)
    silu_gate = gate_scaled * sigmoid_gate
    hidden_low = (silu_gate * up_scaled).astype(jnp.bfloat16)
    feed_part = jnp.dot(hidden_low, feed_full[2], preferred_element_type=jnp.float32)
    feed_total = lax.psum(feed_part, "tensor")
    feed_unit, feed_norm = unit_rows(feed_total)
    output_rows, output_norm = unit_rows(
        after_attention + rate_feed * (feed_unit - after_attention)
    )
    second_back = unit_back(output_rows, output_norm, cotangent_rows)
    feed_rate_term = jnp.sum(second_back * (feed_unit - after_attention), axis=0)
    feed_back = unit_back(feed_unit, feed_norm, second_back * rate_feed).astype(jnp.bfloat16)
    down_grad = jnp.einsum("rf,rd->fd", hidden_low, feed_back, preferred_element_type=jnp.float32)
    hidden_back = jnp.einsum(
        "rd,fd->rf", feed_back, feed_full[2], preferred_element_type=jnp.float32
    )
    up_back = hidden_back * silu_gate
    gate_back = hidden_back * up_scaled * sigmoid_gate * (1.0 + gate_scaled * (1.0 - sigmoid_gate))
    gate_up_back = jnp.stack(
        [up_back * hidden_float[0], gate_back * hidden_float[1] * root_width]
    ).astype(jnp.bfloat16)
    hidden_terms = jnp.stack(
        [
            jnp.sum(up_back * gate_up[0], axis=0),
            jnp.sum(gate_back * gate_up[1] * root_width, axis=0),
        ]
    )
    gate_up_grad = jnp.einsum(
        "krf,rd->kfd", gate_up_back, normed_low, preferred_element_type=jnp.float32
    )
    feed_terms = jnp.concatenate([gate_up_grad, down_grad[None]], axis=0)
    normed_part = jnp.einsum(
        "krf,kfd->rd", gate_up_back, feed_full[:2], preferred_element_type=jnp.float32
    )
    normed_sum = lax.psum(normed_part, "tensor")
    after_grad = second_back * (1.0 - rate_feed) + normed_sum
    first_back = unit_back(after_attention, after_norm, after_grad)
    attention_rate_term = jnp.sum(first_back * (attention_unit - token_float), axis=0)
    attention_back = unit_back(attention_unit, attention_norm, first_back * rate_attention).astype(
        jnp.bfloat16
    )
    output_weight_grad = jnp.einsum(
        "rh,rd->hd", heads_low, attention_back, preferred_element_type=jnp.float32
    )
    heads_back = jnp.einsum(
        "rd,hd->rh", attention_back, attention_full[3], preferred_element_type=jnp.float32
    ).astype(jnp.bfloat16)
    query_grads = []
    reduced_list = []
    for micro_index in range(micro_count):
        segment_row = segments[0, micro_index]
        query_block = query_low[micro_index * rows_local : (micro_index + 1) * rows_local]
        query_segment = jnp.take(segment_row, own_places)
        whole_keys = lax.all_gather(key_value[micro_index], "ctx", axis=0, tiled=True)
        raised, key_part, value_part = piece_weights(
            query_block,
            own_places,
            query_segment,
            whole_keys,
            0,
            segment_row,
            rows_local,
            shard_order,
        )
        row_total = totals[micro_index]
        summed = summeds[micro_index]
        output_back = jnp.transpose(
            heads_back[micro_index * rows_local : (micro_index + 1) * rows_local].reshape(
                rows_local, head_count, HEAD_DIM
            ),
            (1, 0, 2),
        ).astype(jnp.float32)
        summed_back = (output_back / row_total[:, :, None]).astype(jnp.bfloat16)
        raised_back = jnp.einsum(
            "hqd,khd->hqk", summed_back, value_part, preferred_element_type=jnp.float32
        )
        total_back = -jnp.sum(output_back * summed, axis=-1) / (row_total * row_total)
        score_back = (raised * (raised_back + total_back[:, :, None])).astype(jnp.bfloat16)
        query_grads.append(
            jnp.einsum("hqk,khd->qhd", score_back, key_part, preferred_element_type=jnp.float32)
        )
        key_grad = jnp.einsum(
            "hqk,qhd->khd", score_back, query_block, preferred_element_type=jnp.float32
        )
        value_grad = jnp.einsum(
            "hqk,hqd->khd",
            raised.astype(jnp.bfloat16),
            summed_back,
            preferred_element_type=jnp.float32,
        )
        key_sides = jnp.concatenate(
            [key_grad.reshape(seq_length, head_width), value_grad.reshape(seq_length, head_width)],
            axis=1,
        )
        reduced_list.append(lax.psum_scatter(key_sides, "ctx", scatter_dimension=0, tiled=True))
    query_scaled_grad = jnp.concatenate(query_grads, axis=0)
    reduced_all = jnp.concatenate(reduced_list, axis=0)
    key_scaled_grad = reduced_all[:, :head_width].reshape(all_rows, head_count, HEAD_DIM)
    value_sum = reduced_all[:, head_width:]
    head_terms = (
        jnp.sum(query_scaled_grad * query_unit * root_head, axis=0)
        + jnp.sum(key_scaled_grad * key_unit, axis=0)
    ).reshape(head_width)
    query_back = (
        unit_back(query_unit, query_norm, query_scaled_grad * scale_heads * root_head)
        .astype(jnp.bfloat16)
        .reshape(all_rows, head_width)
    )
    key_back = (
        unit_back(key_unit, key_norm, key_scaled_grad * scale_heads)
        .astype(jnp.bfloat16)
        .reshape(all_rows, head_width)
    )
    triple_back = jnp.stack([query_back, key_back, value_sum.astype(jnp.bfloat16)])
    triple_grad = jnp.einsum(
        "krh,rd->khd", triple_back, token_rows, preferred_element_type=jnp.float32
    )
    attention_terms = jnp.concatenate([triple_grad, output_weight_grad[None]], axis=0)
    input_part = jnp.einsum(
        "krh,khd->rd", triple_back, attention_full[:3], preferred_element_type=jnp.float32
    )
    input_sum = lax.psum(input_part, "tensor")
    input_rows = first_back * (1.0 - rate_attention) + input_sum
    rate_terms = jnp.stack([attention_rate_term, feed_rate_term])
    owned_grads = (
        lax.psum_scatter(attention_terms, "ctx", scatter_dimension=1, tiled=True),
        lax.psum_scatter(feed_terms, "ctx", scatter_dimension=1, tiled=True),
        lax.psum_scatter(head_terms, "ctx", scatter_dimension=0, tiled=True),
        lax.psum_scatter(hidden_terms, "ctx", scatter_dimension=1, tiled=True),
        lax.psum_scatter(rate_terms, "ctx", scatter_dimension=1, tiled=True),
    )
    masters = (attention_weights, feedforward_weights, head_scales, hidden_scales, residual_rates)
    firsts = (
        attention_first[0],
        feedforward_first[0],
        heads_first[0],
        hidden_first[0],
        rates_first[0],
    )
    seconds = (
        attention_second[0],
        feedforward_second[0],
        heads_second[0],
        hidden_second[0],
        rates_second[0],
    )
    outers = (attention_outer, feedforward_outer, heads_outer, hidden_outer, rates_outer)
    matrix_flags = (True, True, False, False, False)
    step_rates = (MATRIX_RATE, MATRIX_RATE, SCALE_RATE, SCALE_RATE, SCALE_RATE)
    moments = []
    variances = []
    shifts = []
    for which in range(5):
        moment, variance, updated = adam_step(
            masters[which],
            owned_grads[which],
            firsts[which],
            seconds[which],
            step_rates[which],
            matrix_flags[which],
        )
        moments.append(moment)
        variances.append(variance)
        shifts.append(masters[which] - updated)
    shift_sums = lax.psum((shifts[0], shifts[1], shifts[2], shifts[3], shifts[4]), "group")
    group_count = lax.axis_size("group")
    mean_shifts = [entry / group_count for entry in shift_sums]
    momenta = []
    results = []
    for which in range(5):
        momentum, result = outer_step(
            masters[which], mean_shifts[which], outers[which], matrix_flags[which]
        )
        momenta.append(momentum)
        results.append(result)
    block_output = output_rows.reshape(1, micro_count, rows_local, model_width)
    input_gradient = input_rows.reshape(1, micro_count, rows_local, model_width)
    return (
        block_output,
        input_gradient,
        owned_grads[0][None],
        owned_grads[1][None],
        owned_grads[2][None],
        owned_grads[3][None],
        owned_grads[4][None],
        moments[0][None],
        moments[1][None],
        moments[2][None],
        moments[3][None],
        moments[4][None],
        variances[0][None],
        variances[1][None],
        variances[2][None],
        variances[3][None],
        variances[4][None],
        momenta[0],
        momenta[1],
        momenta[2],
        momenta[3],
        momenta[4],
        results[0],
        results[1],
        results[2],
        results[3],
        results[4],
    )


def solution(mesh):
    placed = (
        P("group", None, "ctx", None),
        P("group", None, "ctx", None),
        P("group", None, None),
        P(),
        P(None, ("tensor", "ctx"), None),
        P(None, ("tensor", "ctx"), None),
        P(("tensor", "ctx")),
        P(None, ("tensor", "ctx")),
        P(None, "ctx"),
        P("group", None, ("tensor", "ctx"), None),
        P("group", None, ("tensor", "ctx"), None),
        P("group", ("tensor", "ctx")),
        P("group", None, ("tensor", "ctx")),
        P("group", None, "ctx"),
        P("group", None, ("tensor", "ctx"), None),
        P("group", None, ("tensor", "ctx"), None),
        P("group", ("tensor", "ctx")),
        P("group", None, ("tensor", "ctx")),
        P("group", None, "ctx"),
        P(None, ("tensor", "ctx"), None),
        P(None, ("tensor", "ctx"), None),
        P(("tensor", "ctx")),
        P(None, ("tensor", "ctx")),
        P(None, "ctx"),
    )
    return jax.shard_map(
        on_device,
        mesh=mesh,
        in_specs=placed,
        out_specs=(
            P("group", None, "ctx", None),
            P("group", None, "ctx", None),
            P("group", None, ("tensor", "ctx"), None),
            P("group", None, ("tensor", "ctx"), None),
            P("group", ("tensor", "ctx")),
            P("group", None, ("tensor", "ctx")),
            P("group", None, "ctx"),
            P("group", None, ("tensor", "ctx"), None),
            P("group", None, ("tensor", "ctx"), None),
            P("group", ("tensor", "ctx")),
            P("group", None, ("tensor", "ctx")),
            P("group", None, "ctx"),
            P("group", None, ("tensor", "ctx"), None),
            P("group", None, ("tensor", "ctx"), None),
            P("group", ("tensor", "ctx")),
            P("group", None, ("tensor", "ctx")),
            P("group", None, "ctx"),
            P(None, ("tensor", "ctx"), None),
            P(None, ("tensor", "ctx"), None),
            P(("tensor", "ctx")),
            P(None, ("tensor", "ctx")),
            P(None, "ctx"),
            P(None, ("tensor", "ctx"), None),
            P(None, ("tensor", "ctx"), None),
            P(("tensor", "ctx")),
            P(None, ("tensor", "ctx")),
            P(None, "ctx"),
        ),
        check_vma=False,
    )
```

profile of v0, /device:TPU:0, one launch (start us, length us, event | category | flops | bytes accessed | tf_op | source)
XLA Modules:
  0.0 1997.0 jit_solution(13774541494419864222)
XLA Ops:
  7.3 3.3 convert_element_type.135
  12.2 5.8 all-reduce
  18.2 41.6 %all-gather.6.cloned.1.call-done = bf16[4,320,1280]{2,1,0:T(8,128)(2,1)} async-done(((bf16[4,160,1280]{2,1,0:T(8,128)(2,1)}), bf16[4,320,1280]{2,1,0:T(8,128)(2,1)}) %all-gather.6.cloned.1.call-update) | async-done | bytes 3276816 | tf_op jit(solution)/shard_map/all_gather | solution.py:139
  59.8 6.9 convolution_bitcast_fusion.4
  72.5 4.5 gather_fusion.1
  79.4 4.5 gather_fusion.3
  86.2 4.5 gather_fusion.5
  99.1 24.2 %all-gather.10.cloned.1.call-done = bf16[1024,640]{0,1:T(8,128)(2,1)} async-done(((bf16[512,640]{0,1:T(8,128)(2,1)}), bf16[1024,640]{0,1:T(8,128)(2,1)}) %all-gather.10.cloned.1.call-update) | async-done | bytes 1310736 | tf_op jit(solution)/shard_map/all_gather | solution.py:193
  125.5 6.6 fusion.7
  132.1 6.5 fusion.5
  138.6 10.9 all-gather.8.cloned.1.call-done
  151.8 6.8 fusion.3
  158.6 4.0 fusion.74
  162.7 6.8 fusion.75
  173.3 6.6 fusion.59
  180.0 7.3 convert_element_type.145
  187.4 4.3 all_gather.27
  191.8 4.3 all_gather.34
  196.8 128.4 %all-reduce.10.cloned.1.call-done = f32[1536,1280]{1,0:T(8,128)} async-done(((f32[1536,1280]{1,0:T(8,128)}), f32[1536,1280]{1,0:T(8,128)}) %all-reduce.10.cloned.1.call-update) | async-done | bytes 7864336 | tf_op jit(solution)/shard_map/psum | solution.py:203
  325.3 4.0 multiply_reduce_fusion.10
  330.7 7.4 multiply_reduce_fusion.9
  338.1 110.7 %all-gather.14.cloned.1.call-done = bf16[3,1280,1280]{2,1,0:T(8,128)(2,1)} async-done(((bf16[3,640,1280]{2,1,0:T(8,128)(2,1)}), bf16[3,1280,1280]{2,1,0:T(8,128)(2,1)}) %all-gather.14.cloned.1.call-update) | async-done | bytes 9830416 | tf_op jit(solution)/shard_map/all_gather | solution.py:140
  448.8 17.9 convolution_bitcast_fusion
  466.7 13.4 fusion.22
  480.6 144.9 %all-reduce.12.cloned.1.call-done = f32[1536,1280]{1,0:T(8,128)} async-done(((f32[1536,1280]{1,0:T(8,128)}), f32[1536,1280]{1,0:T(8,128)}) %all-reduce.12.cloned.1.call-update) | async-done | bytes 7864336 | tf_op jit(solution)/shard_map/psum | solution.py:222
  625.4 4.0 multiply_reduce_fusion.8
  629.5 7.4 multiply_reduce_fusion.7
  639.1 5.2 fusion.9
  644.2 7.7 multiply_reduce_fusion.2
  655.2 18.0 fusion.11
  673.2 4.2 fusion.21
  679.3 16.6 convolution_bitcast_fusion.1
  696.0 145.5 %all-reduce.14.cloned.1.call-done = f32[1536,1280]{1,0:T(8,128)} async-done(((f32[1536,1280]{1,0:T(8,128)}), f32[1536,1280]{1,0:T(8,128)}) %all-reduce.14.cloned.1.call-update) | async-done | bytes 7864336 | tf_op jit(solution)/shard_map/psum | solution.py:252
  841.6 9.1 multiply_reduce_fusion.5
  851.6 11.5 multiply_reduce_fusion.3
  867.1 4.8 convolution_convert_fusion
  883.8 6.1 multiply_convert_fusion.1
  898.3 5.9 multiply_convert_fusion
  912.8 4.3 fusion.148
  917.1 4.5 fusion.147
  921.6 4.5 fusion.146
  933.2 28.7 %reduce-scatter.14.cloned.1.call-done = f32[512,640]{0,1:T(8,128)} async-done(((f32[1024,640]{0,1:T(8,128)}), f32[512,640]{0,1:T(8,128)}) %reduce-scatter.14.cloned.1.call-update) | async-done | bytes 1310736 | tf_op jit(solution)/shard_map/reduce_scatter | solution.py:312
  964.3 38.0 %reduce-scatter.16.cloned.1.call-done = f32[512,640]{0,1:T(8,128)} async-done(((f32[1024,640]{0,1:T(8,128)}), f32[512,640]{0,1:T(8,128)}) %reduce-scatter.16.cloned.1.call-update) | async-done | bytes 1310736 | tf_op jit(solution)/shard_map/reduce_scatter | solution.py:312
  1012.0 4.0 bitcast_multiply_fusion.7
  1016.1 4.0 fusion.40
  1020.1 3.3 pad_maximum_fusion.2
  1023.7 16.3 fusion.18
  1040.0 10.7 convolution_bitcast_fusion.2
  1050.7 6.9 pad_maximum_fusion
  1060.8 8.2 convolution_bitcast_fusion.3
  1069.3 34.2 %reduce-scatter.18.cloned.1.call-done = f32[4,160,1280]{2,1,0:T(8,128)} async-done(((f32[4,320,1280]{2,1,0:T(8,128)}), f32[4,160,1280]{2,1,0:T(8,128)}) %reduce-scatter.18.cloned.1.call-update) | async-done | bytes 3276816 | tf_op jit(solution)/shard_map/reduce_scatter | solution.py:343
  1103.5 8.2 multiply_reduce_fusion.12
  1114.0 212.5 %reduce-scatter.20.cloned.1.call-done = f32[3,640,1280]{2,1,0:T(8,128)} async-done(((f32[3,1280,1280]{2,1,0:T(8,128)}), f32[3,640,1280]{2,1,0:T(8,128)}) %reduce-scatter.20.cloned.1.call-update) | async-done | bytes 9830416 | tf_op jit(solution)/shard_map/reduce_scatter | solution.py:344
  1326.6 27.8 %multiply_reduce_fusion.1 = (f32[3,640]{1,0:T(4,128)S(1)}, f32[3,640,1280]{2,1,0:T(8,128)}, f32[1,3,640,1280]{3,2,1,0:T(8,128)}, f32[1,3,640,1280]{3,2,1,0:T(8,128)}) fusion(f32[3,640,1280]{2,1,0:T(8,128)} %param.33, f32[3,640,1280]{2,1,0:T(8,128)} %reduce-scatter.20.cloned.1.call-done, f32[1,3,640,1280]{3,2,1,0:T(8,128)} %param.43, ...), kind=kLoop, calls=%fused_computation.24 | loop fusion | flops 41777280 | bytes 68820480 | tf_op jit(solution)/shard_map/reduce_sum | solution.py:31
  1354.4 11.5 multiply_subtract_fusion.1
  1370.4 3.5 multiply_reduce_fusion.14
  1373.9 4.9 all-reduce.1
  1379.5 18.9 all-reduce.2
  1400.1 110.8 %all-reduce.16.cloned.1.call-done = f32[1536,1280]{1,0:T(8,128)} async-done(((f32[1536,1280]{1,0:T(8,128)}), f32[1536,1280]{1,0:T(8,128)}) %all-reduce.16.cloned.1.call-update) | async-done | bytes 7864336 | tf_op jit(solution)/shard_map/psum | solution.py:339
  1511.0 10.2 multiply_add_fusion.1
  1521.2 436.9 %all-reduce.18.cloned.1.call-done = (f32[4,160,1280]{2,1,0:T(8,128)}, f32[3,640,1280]{2,1,0:T(8,128)}) async-done(((f32[4,160,1280]{2,1,0:T(8,128)}, f32[3,640,1280]{2,1,0:T(8,128)}), (f32[4,160,1280]{2,1,0:T(8,128)}, f32[3,640,1280]{2,1,0:T(8,128)})) %all-reduce.18.cloned.1.call-update) | async-done | bytes 13107216 | tf_op jit(solution)/shard_map/psum | solution.py:382
  1958.2 4.1 multiply_reduce_fusion.11
  1965.1 13.1 multiply_reduce_fusion
  1980.7 9.5 broadcast_multiply_fusion
  (413 shorter events, 107.7 us)
Async XLA Ops:
  7.2 10.8 copy-start.106
  7.2 11.0 copy-start.93
  7.2 52.6 %all-gather.6.cloned.1.call-start = ((), (), s32[]{:S(2)}) async-start(), calls=%async_computation.7 | async-start | bytes 4915200 | tf_op jit(solution)/shard_map/all_gather | solution.py:139
  10.6 86.3 %all-gather.12.cloned.1.call-start = ((), (), s32[]{:S(2)}) async-start(), calls=%async_computation.10 | async-start | bytes 1966080 | tf_op jit(solution)/shard_map/all_gather | solution.py:193
  18.0 49.4 %copy-start.87 = (f32[320]{0:T(512)}, f32[320]{0:T(512)S(1)}, u32[]{:S(2)}) copy-start(f32[320]{0:T(512)S(1)} %convert_element_type.137) | copy-start | bytes 3844
  67.0 28.7 %copy-start.10 = (f32[1,1536,320]{1,2,0:T(8,128)}, f32[1,1536,320]{1,2,0:T(8,128)S(1)}, u32[]{:S(2)}) copy-start(f32[1,1536,320]{1,2,0:T(8,128)S(1)} %get-tuple-element.87) | copy-start | bytes 5898244
  72.5 50.8 %all-gather.10.cloned.1.call-start = ((), (), s32[]{:S(2)}) async-start(), calls=%async_computation.9 | async-start | bytes 1966080 | tf_op jit(solution)/shard_map/all_gather | solution.py:193
  93.1 56.4 %all-gather.8.cloned.1.call-start = ((), (), s32[]{:S(2)}) async-start(), calls=%async_computation.8 | async-start | bytes 1966080 | tf_op jit(solution)/shard_map/all_gather | solution.py:193
  95.3 63.3 %copy-start.34 = (pred[512,1024]{1,0:T(8,128)(4,1)}, pred[512,1024]{1,0:T(8,128)(4,1)S(1)}, u32[]{:S(2)}) copy-start(pred[512,1024]{1,0:T(8,128)(4,1)S(1)} %get-tuple-element.114) | copy-start | bytes 1572868
  96.3 55.5 %copy-start.19 = (bf16[1536,5,64]{0,2,1:T(8,128)(2,1)}, bf16[1536,5,64]{0,2,1:T(8,128)(2,1)S(1)}, u32[]{:S(2)}) copy-start(bf16[1536,5,64]{0,2,1:T(8,128)(2,1)S(1)} %multiply_convert_fusion.13) | copy-start | bytes 2949124
  96.3 228.9 %all-reduce.10.cloned.1.call-start = ((), (), s32[]{:S(2)}) async-start(), calls=%async_computation.11 | async-start | bytes 15728640 | tf_op jit(solution)/shard_map/psum | solution.py:203
  99.1 33.0 %copy-start.28 = (bf16[1024,320]{0,1:T(8,128)(2,1)}, bf16[1024,320]{0,1:T(8,128)(2,1)S(1)}, u32[]{:S(2)}) copy-start(bf16[1024,320]{0,1:T(8,128)(2,1)S(1)} %get-tuple-element.98) | copy-start | bytes 1966084
  132.1 26.5 %copy-start.74 = (f32[5,512]{1,0:T(8,128)}, f32[5,512]{1,0:T(8,128)S(1)}, u32[]{:S(2)}) copy-start(f32[5,512]{1,0:T(8,128)S(1)} %get-tuple-element.123) | copy-start | bytes 30724
  132.1 19.7 copy-start.38
  138.6 24.1 %copy-start.76 = (f32[5,512]{1,0:T(8,128)}, f32[5,512]{1,0:T(8,128)S(1)}, u32[]{:S(2)}) copy-start(f32[5,512]{1,0:T(8,128)S(1)} %get-tuple-element.127) | copy-start | bytes 30724
  158.6 10.9 copy-start.78
  158.6 10.9 slice-start.15
  158.6 10.9 slice-start.16
  162.7 9.9 copy-start.68
  179.9 11.8 copy-start.83
  180.0 268.8 %all-gather.14.cloned.1.call-start = ((), (), s32[]{:S(2)}) async-start(), calls=%async_computation.12 | async-start | bytes 14745600 | tf_op jit(solution)/shard_map/all_gather | solution.py:140
  187.4 438.1 %all-reduce.12.cloned.1.call-start = ((), (), s32[]{:S(2)}) async-start(), calls=%async_computation.13 | async-start | bytes 15728640 | tf_op jit(solution)/shard_map/psum | solution.py:222
  196.2 457.5 %copy-start.94 = (f32[1280]{0:T(1024)}, f32[1280]{0:T(1024)S(1)}, u32[]{:S(2)}) copy-start(f32[1280]{0:T(1024)S(1)} %get-tuple-element.40) | copy-start | bytes 15364
  480.1 361.5 %all-reduce.14.cloned.1.call-start = ((), (), s32[]{:S(2)}) async-start(), calls=%async_computation.14 | async-start | bytes 15728640 | tf_op jit(solution)/shard_map/psum | solution.py:252
  625.4 11.5 slice-start
  625.4 11.5 slice-start.5
  629.4 9.6 copy-start.16
  655.2 18.0 copy-start.42
  696.0 145.6 %copy-start.80 = (f32[1280]{0:T(1024)S(1)}, f32[1280]{0:T(1024)}, u32[]{:S(2)}) copy-start(f32[1280]{0:T(1024)} %get-tuple-element.36) | copy-start | bytes 15364
  696.0 234.5 %reduce-scatter.12.cloned.1.call-start = ((), (), s32[]{:S(2)}) async-start(), calls=%async_computation.15 | async-start | bytes 3932160 | tf_op jit(solution)/shard_map/reduce_scatter | solution.py:312
  841.6 10.0 copy-start.9
  841.6 21.5 %slice-start.7 = ((s8[7864320]{0:T(1024)(128)(4,1)}), s8[4194304]{0:T(1024)(128)(4,1)S(1)}, s32[]{:S(2)}) async-start(s8[7864320]{0:T(1024)(128)(4,1)} %bitcast.335), calls=%async_computation.31 | async-start | bytes 8388608
  851.6 11.5 slice-start.8
  863.1 9.7 slice-start.18
  863.1 9.7 slice-start.19
  883.5 78.4 %reduce-scatter.14.cloned.1.call-start = ((), (), s32[]{:S(2)}) async-start(), calls=%async_computation.16 | async-start | bytes 3932160 | tf_op jit(solution)/shard_map/reduce_scatter | solution.py:312
  897.9 104.4 %reduce-scatter.16.cloned.1.call-start = ((), (), s32[]{:S(2)}) async-start(), calls=%async_computation.17 | async-start | bytes 3932160 | tf_op jit(solution)/shard_map/reduce_scatter | solution.py:312
  912.2 9.3 copy-start.33
  912.2 191.3 %reduce-scatter.18.cloned.1.call-start = ((), (), s32[]{:S(2)}) async-start(), calls=%async_computation.19 | async-start | bytes 9830400 | tf_op jit(solution)/shard_map/reduce_scatter | solution.py:343
  917.1 93.9 %copy-start.21 = (f32[5,64,512]{2,1,0:T(8,128)}, f32[5,64,512]{2,1,0:T(8,128)S(1)}, u32[]{:S(2)}) copy-start(f32[5,64,512]{2,1,0:T(8,128)S(1)} %fusion.148) | copy-start | bytes 1966084
  921.6 89.4 %copy-start.22 = (f32[5,64,512]{2,1,0:T(8,128)}, f32[5,64,512]{2,1,0:T(8,128)S(1)}, u32[]{:S(2)}) copy-start(f32[5,64,512]{2,1,0:T(8,128)S(1)} %fusion.147) | copy-start | bytes 1966084
  964.3 44.9 %copy-start.14 = (f32[1,1536,320]{1,2,0:T(8,128)S(1)}, f32[1,1536,320]{1,2,0:T(8,128)}, u32[]{:S(2)}) copy-start(f32[1,1536,320]{1,2,0:T(8,128)} %copy-done.13) | copy-start | bytes 5898244
  964.3 44.9 %copy-start.57 = (f32[1536,5]{0,1:T(8,128)S(1)}, f32[1536,5]{0,1:T(8,128)}, u32[]{:S(2)}) copy-start(f32[1536,5]{0,1:T(8,128)} %copy-done.56) | copy-start | bytes 92164
  1006.7 9.3 copy-start.50
  1023.4 16.5 copy-start.95
  1023.4 303.1 %reduce-scatter.20.cloned.1.call-start = ((), (), s32[]{:S(2)}) async-start(), calls=%async_computation.20 | async-start | bytes 29491200 | tf_op jit(solution)/shard_map/reduce_scatter | solution.py:344
  1023.7 16.3 copy-start.43
  1057.7 309.2 %reduce-scatter.22.cloned.1.call-start = ((), (), s32[]{:S(2)}) async-start(), calls=%async_computation.21 | async-start | bytes 983040
  1059.5 309.1 %reduce-scatter.24.cloned.1.call-start = ((), (), s32[]{:S(2)}) async-start(), calls=%async_computation.22 | async-start | bytes 983040
  1060.7 450.2 %all-reduce.16.cloned.1.call-start = ((), (), s32[]{:S(2)}) async-start(), calls=%async_computation.18 | async-start | bytes 15728640 | tf_op jit(solution)/shard_map/psum | solution.py:339
  1069.0 34.5 %copy-start.2 = (f32[4,160,1280]{2,1,0:T(8,128)S(1)}, f32[4,160,1280]{2,1,0:T(8,128)}, u32[]{:S(2)}) copy-start(f32[4,160,1280]{2,1,0:T(8,128)} %param.32) | copy-start | bytes 9830404
  1069.0 889.2 %all-reduce.18.cloned.1.call-start = ((), (), s32[]{:S(2)}) async-start(), calls=%async_computation.23 | async-start | bytes 26214400 | tf_op jit(solution)/shard_map/psum | solution.py:382
  1366.0 12.9 copy-start.105
  1366.0 32.4 %copy-start.108 = (f32[160]{0:T(256)S(1)}, f32[160]{0:T(256)}, u32[]{:S(2)}) copy-start(f32[160]{0:T(256)} %param.49) | copy-start | bytes 1924
  1366.0 32.9 %copy-start.102 = (f32[2,640]{1,0:T(2,128)S(1)}, f32[2,640]{1,0:T(2,128)}, u32[]{:S(2)}) copy-start(f32[2,640]{1,0:T(2,128)} %param.50) | copy-start | bytes 15364
  1366.0 33.5 %copy-start.103 = (f32[2,640]{1,0:T(2,128)S(1)}, f32[2,640]{1,0:T(2,128)}, u32[]{:S(2)}) copy-start(f32[2,640]{1,0:T(2,128)} %param.51) | copy-start | bytes 15364
  1366.0 145.0 %copy-start.89 = (f32[1280]{0:T(1024)S(1)}, f32[1280]{0:T(1024)}, u32[]{:S(2)}) copy-start(f32[1280]{0:T(1024)} %get-tuple-element.35) | copy-start | bytes 15364
  1368.0 153.3 %copy-start.91 = (f32[2,640]{1,0:T(2,128)}, f32[2,640]{1,0:T(2,128)S(1)}, u32[]{:S(2)}) copy-start(f32[2,640]{1,0:T(2,128)S(1)} %copy.57) | copy-start | bytes 15364
  1369.7 151.5 %copy-start.92 = (f32[2,640]{1,0:T(2,128)}, f32[2,640]{1,0:T(2,128)S(1)}, u32[]{:S(2)}) copy-start(f32[2,640]{1,0:T(2,128)S(1)} %copy.59) | copy-start | bytes 15364
  1958.2 22.5 %slice-start.2 = ((s8[9830400]{0:T(1024)(128)(4,1)}), s8[4194304]{0:T(1024)(128)(4,1)S(1)}, s32[]{:S(2)}) async-start(s8[9830400]{0:T(1024)(128)(4,1)} %bitcast.331), calls=%async_computation.26 | async-start | bytes 8388608
  1962.3 15.9 copy-start.18
  1965.1 13.1 copy-start.17
  1965.1 15.6 slice-start.3
  1965.1 15.6 slice-start.4
  (88 other events, 377.3 us)
Sparse Core Ops, SparseCore 0:
  10.7 49.1 all-gather.5
  72.6 24.2 all-gather.11
  99.0 24.2 all-gather.9
  125.3 24.2 all-gather.7
  180.1 145.1 all-reduce.9
  327.2 121.4 all-gather.13
  480.2 145.1 all-reduce.11
  696.1 145.4 all-reduce.13
  883.6 37.8 reduce-scatter.11
  924.2 37.5 reduce-scatter.13
  964.7 37.5 reduce-scatter.15
  1023.6 79.8 reduce-scatter.17
  1106.4 220.1 reduce-scatter.19
  1328.7 15.9 reduce-scatter.21
  1346.9 15.9 reduce-scatter.23
  1365.8 145.1 all-reduce.15
  1514.2 443.9 all-reduce.17
where the time goes:
time: 2000 us
  waiting for transfers between devices  1470 us (74%)
  other arithmetic  204 us (10%)
  matrix products  197 us (10%)
  local copies, waits for them, and re-layouts  70 us (4%)
  blocking collectives  38.3 us (2%)
    psum x1, waiting for transfers between devices, on_device(): lax.psum((shifts[0], shifts[1], shifts[2], shifts[3], shifts[4]), 'group')  437 us
    reduce_scatter x1, waiting for transfers between devices, on_device(): lax.psum_scatter(feed_terms, 'ctx', scatter_dimension=1, tiled=True)  213 us
    psum x1, waiting for transfers between devices, on_device(): normed_sum = lax.psum(normed_part, 'tensor')  146 us
    psum x1, waiting for transfers between devices, on_device(): feed_total = lax.psum(feed_part, 'tensor')  145 us
    psum x1, waiting for transfers between devices, on_device(): attention_total = lax.psum(attention_part, 'tensor')  128 us
    psum x1, waiting for transfers between devices, on_device(): input_sum = lax.psum(input_part, 'tensor')  111 us
    all_gather x1, waiting for transfers between devices, on_device(): lax.all_gather(feedforward_weights.astype(jnp.bfloat16), 'ctx', axis=1, t...  111 us
    reduce_scatter x3, waiting for transfers between devices, on_device(): lax.psum_scatter(key_sides, 'ctx', scatter_dimension=0, tiled=True)  66.6 us
  transfers between devices with their start and end apart: 17, of which 14 were waited for; matrix products, arithmetic and copies ran while one was open for 11% of the time, Pallas kernels for 0%

commit v1 on v0

v1 whole, which is shorter than its diff:
```python
from functools import partial
import math

import jax
import jax.numpy as jnp
from jax import lax
from jax.experimental import pallas as pl
from jax.experimental.pallas import tpu as pltpu
from jax.sharding import PartitionSpec as P

HEAD_DIM = 64


EPSILON = 1e-06
BETA_ONE = 0.9
BETA_TWO = 0.95
CORR_ONE = 1.0 - 0.9**4
CORR_TWO = 1.0 - 0.95**4
ADAM_EPS = 1e-08
DECAY = 0.1
MATRIX_RATE = 0.02
SCALE_RATE = 0.3
OUTER_RATE = 0.7
OUTER_MOMENTUM = 0.9
MASKED = -1e30
VMEM_BYTES = 40 * 1024 * 1024
F32 = jnp.float32
LOW = jnp.bfloat16


def unit_rows(values, axis=-1):
    scale = lax.rsqrt(jnp.sum(values * values, axis=axis, keepdims=True) + EPSILON)
    return (values * scale, scale)


def unit_only(values):
    return values * lax.rsqrt(jnp.sum(values * values, axis=-1, keepdims=True) + EPSILON)


def unit_back(unit, scale, upstream, axis=-1):
    return scale * (upstream - unit * jnp.sum(upstream * unit, axis=axis, keepdims=True))


def dot(left, right, contract, out=F32):
    return lax.dot_general(
        left, right, (((contract[0],), (contract[1],)), ((), ())), preferred_element_type=F32
    ).astype(out)


def trade(values, axis, bit):
    count = lax.axis_size(axis)
    return lax.ppermute(values, axis, [(i, i ^ bit) for i in range(count)])


def ordered(first, own, other, axis):
    return jnp.where(
        first,
        jnp.concatenate([own, other], axis=axis),
        jnp.concatenate([other, own], axis=axis),
    )


def split_low(values):
    return lax.optimization_barrier(values.astype(LOW))


def add_low(left, right):
    return left.astype(F32) + right.astype(F32)


def tensor_sum(own_part, other_part):
    from_core = trade(other_part, "tensor", 1)
    pair = split_low(own_part + from_core.astype(F32))
    return add_low(pair, trade(pair, "tensor", 2))


def group_sum(values):
    dtype = values.dtype
    here = lax.axis_index("group")
    last = lax.axis_size("group") - 1
    pair = lax.optimization_barrier(
        add_low(values, lax.ppermute(values, "group", [(0, 1), (3, 2)])).astype(dtype)
    )
    whole = lax.optimization_barrier(
        add_low(pair, lax.ppermute(pair, "group", [(1, 2), (2, 1)])).astype(dtype)
    )
    back = lax.ppermute(whole, "group", [(1, 0), (2, 3)])
    return jnp.where((here == 0) | (here == last), back, whole).astype(F32)


def mask_bias(seg_q, place_q, seg_k, place_k):
    allowed = (seg_k == seg_q) & (place_k <= place_q)
    return jnp.where(allowed, 0.0, MASKED).astype(F32)


def attend_kernel(
    head_count, seg_q, place_q, seg_k, place_k, query, key_value, summed, total, heads, bias
):
    blocks, _, rows = key_value.shape
    width = head_count * HEAD_DIM
    for j in range(blocks):
        part = pl.ds(j * rows, rows)
        bias[part, :] = mask_bias(seg_q[...], place_q[...], seg_k[part, :], place_k[part, :])
    for head in range(head_count):
        cols = pl.ds(head * HEAD_DIM, HEAD_DIM)
        value_cols = pl.ds(width + head * HEAD_DIM, HEAD_DIM)
        block_query = query[cols, :]
        row_total = jnp.zeros((1, query.shape[1]), F32)
        acc = jnp.zeros((HEAD_DIM, query.shape[1]), F32)
        for j in range(blocks):
            scores = dot(key_value[j, cols, :], block_query, (0, 0))
            raised = jnp.exp(scores + bias[pl.ds(j * rows, rows), :])
            row_total = row_total + jnp.sum(raised, axis=0, keepdims=True)
            acc = acc + dot(key_value[j, value_cols, :], raised.astype(LOW), (1, 0))
        summed[cols, :] = acc
        total[pl.ds(head, 1), :] = row_total
        heads[cols, :] = (acc / row_total).astype(LOW)


def attend(head_count, places, query, key_value):
    blocks, _, rows = key_value.shape
    width, count = query.shape
    work = head_count * blocks * rows * count * HEAD_DIM * 4
    return pl.pallas_call(
        partial(attend_kernel, head_count),
        out_shape=(
            jax.ShapeDtypeStruct((width, count), F32),
            jax.ShapeDtypeStruct((head_count, count), F32),
            jax.ShapeDtypeStruct((width, count), LOW),
        ),
        scratch_shapes=[pltpu.VMEM((blocks * rows, count), F32)],
        compiler_params=pltpu.CompilerParams(vmem_limit_bytes=VMEM_BYTES),
        cost_estimate=pl.CostEstimate(
            flops=4 * work, bytes_accessed=6 * width * count, transcendentals=work // 256
        ),
    )(*places, query, key_value)


def attend_back_kernel(
    head_count,
    seg_q,
    place_q,
    seg_k,
    place_k,
    query,
    key_value,
    heads_back,
    summed,
    total,
    query_grad,
    own_grad,
    other_grad,
    bias,
):
    blocks, _, rows = key_value.shape
    width = head_count * HEAD_DIM
    for j in range(blocks):
        part = pl.ds(j * rows, rows)
        bias[part, :] = mask_bias(seg_q[...], place_q[...], seg_k[part, :], place_k[part, :])
    for head in range(head_count):
        cols = pl.ds(head * HEAD_DIM, HEAD_DIM)
        value_cols = pl.ds(width + head * HEAD_DIM, HEAD_DIM)
        block_query = query[cols, :]
        output_back = heads_back[cols, :].astype(F32)
        row_total = total[pl.ds(head, 1), :]
        summed_back = (output_back / row_total).astype(LOW)
        total_back = -jnp.sum(output_back * summed[cols, :], axis=0, keepdims=True) / (
            row_total * row_total
        )
        acc = jnp.zeros((HEAD_DIM, query.shape[1]), F32)
        for j in range(blocks):
            key_part = key_value[j, cols, :]
            scores = dot(key_part, block_query, (0, 0))
            raised = jnp.exp(scores + bias[pl.ds(j * rows, rows), :])
            raised_back = dot(key_value[j, value_cols, :], summed_back, (0, 0))
            score_back = (raised * (raised_back + total_back)).astype(LOW)
            acc = acc + dot(key_part, score_back, (1, 0))
            key_grad = dot(block_query, score_back, (1, 1))
            value_grad = dot(summed_back, raised.astype(LOW), (1, 1))
            if j == 0:
                own_grad[cols, :] = key_grad
                own_grad[value_cols, :] = value_grad
            else:
                other_grad[j - 1, cols, :] = key_grad.astype(other_grad.dtype)
                other_grad[j - 1, value_cols, :] = value_grad.astype(other_grad.dtype)
        query_grad[cols, :] = acc


def attend_back(head_count, places, query, key_value, heads_back, summed, total):
    blocks, both, rows = key_value.shape
    width, count = query.shape
    work = head_count * blocks * rows * count * HEAD_DIM * 2
    return pl.pallas_call(
        partial(attend_back_kernel, head_count),
        out_shape=(
            jax.ShapeDtypeStruct((width, count), F32),
            jax.ShapeDtypeStruct((both, rows), F32),
            jax.ShapeDtypeStruct((blocks - 1, both, rows), LOW if blocks == 2 else F32),
        ),
        scratch_shapes=[pltpu.VMEM((blocks * rows, count), F32)],
        compiler_params=pltpu.CompilerParams(vmem_limit_bytes=VMEM_BYTES),
        cost_estimate=pl.CostEstimate(
            flops=5 * 4 * work, bytes_accessed=16 * width * count, transcendentals=work // 128
        ),
    )(*places, query, key_value, heads_back, summed, total)


def adam_step(master, gradient, first_state, second_state, step_rate, is_matrix):
    moment = BETA_ONE * first_state + (1.0 - BETA_ONE) * gradient
    variance = BETA_TWO * second_state + (1.0 - BETA_TWO) * gradient * gradient
    update = moment / CORR_ONE / (jnp.sqrt(variance / CORR_TWO) + ADAM_EPS)
    updated = master - step_rate * (update + DECAY * master)
    if is_matrix:
        updated = unit_only(updated)
    return (moment, variance, updated)


def outer_step(master, shift, outer_state, is_matrix):
    momentum = OUTER_MOMENTUM * outer_state + shift
    result = master - OUTER_RATE * (shift + OUTER_MOMENTUM * momentum)
    if is_matrix:
        result = unit_only(result)
    return (momentum, result)


def on_device(
    tokens,
    cotangent,
    segments,
    shard_order,
    attention_weights,
    feedforward_weights,
    head_scales,
    hidden_scales,
    residual_rates,
    attention_first,
    feedforward_first,
    heads_first,
    hidden_first,
    rates_first,
    attention_second,
    feedforward_second,
    heads_second,
    hidden_second,
    rates_second,
    attention_outer,
    feedforward_outer,
    heads_outer,
    hidden_outer,
    rates_outer,
):
    micro_count, rows, model_width = tokens.shape[1:]
    half = rows // 2
    ctx_count = lax.axis_size("ctx")
    pair = ctx_count == 2
    group_count = lax.axis_size("group")
    own_rows = attention_weights.shape[1]
    own_units = feedforward_weights.shape[1]
    head_width = own_rows * ctx_count
    head_count = head_width // HEAD_DIM
    units = own_units * ctx_count
    root_head = math.sqrt(HEAD_DIM)
    root_width = math.sqrt(model_width)
    me = lax.axis_index("ctx")
    ctx_first = me == 0
    core_first = lax.rem(lax.axis_index("tensor"), 2) == 0
    even_group = lax.rem(lax.axis_index("group"), 2) == 0
    micros = range(micro_count)

    attention_low = attention_weights.astype(LOW)
    feed_low = feedforward_weights.astype(LOW)
    small_low = jnp.concatenate(
        [head_scales, hidden_scales[0], hidden_scales[1], residual_rates[0], residual_rates[1]]
    ).astype(LOW)
    own_cols = residual_rates.shape[1]
    if pair:
        triple_other = trade(attention_low[:3], "ctx", 1)
        triple_weights = ordered(ctx_first, attention_low[:3], triple_other, 1)
        small_other = trade(small_low, "ctx", 1)
        cuts = [own_rows, own_units, own_units, own_cols, own_cols]
        small_pieces = []
        start = 0
        for which, size in enumerate(cuts):
            mine = small_low[start : start + size].astype(F32)
            theirs = small_other[start : start + size].astype(F32)
            start += size
            if which in (1, 2):
                small_pieces.append(jnp.concatenate([mine, theirs]))
            else:
                small_pieces.append(ordered(ctx_first, mine, theirs, 0))
        scale_heads, scale_up, scale_gate, rate_attention, rate_feed = small_pieces
    else:
        triple_weights = lax.all_gather(attention_low[:3], "ctx", axis=1, tiled=True)
        scale_heads = lax.all_gather(head_scales.astype(LOW), "ctx", axis=0, tiled=True).astype(F32)
        scale_up, scale_gate = lax.all_gather(
            hidden_scales.astype(LOW), "ctx", axis=1, tiled=True
        ).astype(F32)
        rate_attention, rate_feed = lax.all_gather(
            residual_rates.astype(LOW), "ctx", axis=1, tiled=True
        ).astype(F32)
    triple_weights = triple_weights.reshape(3 * head_width, model_width)
    scale_column = scale_heads.reshape(head_count, HEAD_DIM, 1)

    token_halves = tokens[0].reshape(micro_count, 2, half, model_width)
    token_own = jnp.where(core_first, token_halves[:, 0], token_halves[:, 1])
    token_other = jnp.where(core_first, token_halves[:, 1], token_halves[:, 0])
    token_rows = jnp.concatenate([token_own, token_other], axis=1)
    cotangent_halves = cotangent[0].reshape(micro_count, 2, half, model_width)
    cotangent_own = jnp.where(core_first, cotangent_halves[:, 0], cotangent_halves[:, 1])

    if pair:
        block_ids = jnp.stack([me, 1 - me])
    else:
        block_ids = lax.rem(me + jnp.arange(ctx_count, dtype=jnp.int32), ctx_count)
    table = jnp.arange(ctx_count, dtype=jnp.int32)
    order_of = jnp.sum(
        jnp.where(block_ids[:, None] == table[None, :], shard_order[None, :], 0), axis=1
    )
    local = jnp.arange(rows, dtype=jnp.int32)
    local = jnp.where(core_first, local, lax.rem(local + half, rows))
    place_blocks = order_of[:, None] * rows + local[None, :]
    segment_blocks = segments[0].reshape(micro_count, ctx_count, rows)
    segment_blocks = jnp.sum(
        jnp.where(
            (order_of[:, None] == table[None, :])[None, :, :, None], segment_blocks[:, None], 0
        ),
        axis=2,
    )
    segment_blocks = jnp.where(
        core_first,
        segment_blocks,
        jnp.concatenate([segment_blocks[:, :, half:], segment_blocks[:, :, :half]], axis=2),
    )
    places = [
        (
            segment_blocks[b, 0][None, :],
            place_blocks[0][None, :],
            segment_blocks[b].reshape(ctx_count * rows, 1),
            place_blocks.reshape(ctx_count * rows, 1),
        )
        for b in micros
    ]

    queries, key_values = [], []
    query_low = []
    query_units, query_norms, key_units, key_norms = [], [], [], []
    for b in micros:
        projected = dot(triple_weights, token_rows[b], (1, 1)).reshape(
            3, head_count, HEAD_DIM, rows
        )
        query_unit, query_norm = unit_rows(projected[0], axis=1)
        key_unit, key_norm = unit_rows(projected[1], axis=1)
        query_units.append(query_unit)
        query_norms.append(query_norm)
        key_units.append(key_unit)
        key_norms.append(key_norm)
        query_low.append(
            (query_unit * scale_column * root_head).astype(LOW).reshape(head_width, rows)
        )
        key_value = jnp.concatenate(
            [
                (key_unit * scale_column).astype(LOW).reshape(head_width, rows),
                projected[2].astype(LOW).reshape(head_width, rows),
            ],
            axis=0,
        )
        if pair:
            key_values.append(jnp.stack([key_value, trade(key_value, "ctx", 1)]))
        else:
            gathered = lax.all_gather(key_value, "ctx", axis=0)
            key_values.append(jnp.take(gathered, block_ids, axis=0))

    if pair:
        output_source, feed_source, _ = lax.optimization_barrier(
            (attention_low[3], feed_low, key_values[-1])
        )
        output_weights = ordered(ctx_first, output_source, trade(output_source, "ctx", 1), 0)
        part = own_units // 2
        feed_full = []
        for which in (0, 1, 2):
            source = feed_source[which]
            piece = jnp.where(even_group, source[:part], source[part:])
            across = trade(piece, "ctx", 1)
            along = trade(across, "group", 1)
            feed_full.append(
                jnp.concatenate([source, ordered(even_group, across, along, 0)], axis=0)
            )
    else:
        output_weights = lax.all_gather(attention_low[3], "ctx", axis=0, tiled=True)
        feed_full = list(lax.all_gather(feed_low, "ctx", axis=1, tiled=True))
    up_weights, gate_weights, down_weights = feed_full

    summeds, totals, heads_lows = [], [], []
    attention_units, attention_norms, afters, after_norms, normed_rows = [], [], [], [], []
    for b in micros:
        summed, total, heads_low = attend(head_count, places[b], query_low[b], key_values[b])
        summeds.append(summed)
        totals.append(total)
        heads_lows.append(heads_low)
        other_part = dot(heads_low[:, half:], output_weights, (0, 0), LOW)
        own_part = dot(heads_low[:, :half], output_weights, (0, 0))
        attention_unit, attention_norm = unit_rows(tensor_sum(own_part, other_part))
        token_float = token_own[b].astype(F32)
        after, after_norm = unit_rows(
            token_float + rate_attention * (attention_unit - token_float)
        )
        attention_units.append(attention_unit)
        attention_norms.append(attention_norm)
        afters.append(after)
        after_norms.append(after_norm)
        normed_low = split_low(after)
        normed_rows.append(
            jnp.concatenate([normed_low, trade(normed_low, "tensor", 1)], axis=0)
        )

    ups, gates, hidden_rows = [], [], []
    output_pieces, second_backs, feed_back_rows = [], [], []
    feed_rate_term = jnp.zeros((model_width,), F32)
    for b in micros:
        up = dot(normed_rows[b], up_weights, (1, 1))
        gate = dot(normed_rows[b], gate_weights, (1, 1))
        ups.append(up)
        gates.append(gate)
        gate_scaled = gate * scale_gate * root_width
        hidden = (gate_scaled * jax.nn.sigmoid(gate_scaled) * (up * scale_up)).astype(LOW)
        hidden_rows.append(hidden)
        other_part = dot(hidden[half:], down_weights, (1, 0), LOW)
        own_part = dot(hidden[:half], down_weights, (1, 0))
        feed_unit, feed_norm = unit_rows(tensor_sum(own_part, other_part))
        output, output_norm = unit_rows(afters[b] + rate_feed * (feed_unit - afters[b]))
        second_back = unit_back(output, output_norm, cotangent_own[b].astype(F32))
        feed_rate_term = feed_rate_term + jnp.sum(second_back * (feed_unit - afters[b]), axis=0)
        feed_back = split_low(unit_back(feed_unit, feed_norm, second_back * rate_feed))
        second_backs.append(second_back)
        feed_back_rows.append(jnp.concatenate([feed_back, trade(feed_back, "tensor", 1)], axis=0))
        output_pieces.append(ordered(core_first, output, trade(output, "tensor", 1), 0))

    up_back_rows, gate_back_rows = [], []
    first_backs, attention_back_rows = [], []
    up_terms = jnp.zeros((units,), F32)
    gate_terms = jnp.zeros((units,), F32)
    attention_rate_term = jnp.zeros((model_width,), F32)
    for b in micros:
        hidden_back = dot(feed_back_rows[b], down_weights, (1, 1))
        gate_scaled = gates[b] * scale_gate * root_width
        sigmoid_gate = jax.nn.sigmoid(gate_scaled)
        up_back = hidden_back * gate_scaled * sigmoid_gate
        gate_back = (
            hidden_back
            * (ups[b] * scale_up)
            * sigmoid_gate
            * (1.0 + gate_scaled * (1.0 - sigmoid_gate))
        )
        up_terms = up_terms + jnp.sum(up_back * ups[b], axis=0)
        gate_terms = gate_terms + jnp.sum(gate_back * gates[b] * root_width, axis=0)
        up_low = (up_back * scale_up).astype(LOW)
        gate_low = (gate_back * scale_gate * root_width).astype(LOW)
        up_back_rows.append(up_low)
        gate_back_rows.append(gate_low)
        other_part = (
            dot(up_low[half:], up_weights, (1, 0)) + dot(gate_low[half:], gate_weights, (1, 0))
        ).astype(LOW)
        own_part = dot(up_low[:half], up_weights, (1, 0)) + dot(
            gate_low[:half], gate_weights, (1, 0)
        )
        after_grad = second_backs[b] * (1.0 - rate_feed) + tensor_sum(own_part, other_part)
        first_back = unit_back(afters[b], after_norms[b], after_grad)
        first_backs.append(first_back)
        attention_rate_term = attention_rate_term + jnp.sum(
            first_back * (attention_units[b] - token_own[b].astype(F32)), axis=0
        )
        attention_back = split_low(
            unit_back(attention_units[b], attention_norms[b], first_back * rate_attention)
        )
        attention_back_rows.append(
            jnp.concatenate([attention_back, trade(attention_back, "tensor", 1)], axis=0)
        )

    def to_owner(gradient):
        if not pair:
            return lax.psum_scatter(gradient, "ctx", scatter_dimension=0, tiled=True)
        size = gradient.shape[0] // 2
        return gradient[:size] + trade(gradient[size:].astype(LOW), "ctx", 1).astype(F32)

    def to_owner_ordered(gradient):
        if not pair:
            return lax.psum_scatter(gradient, "ctx", scatter_dimension=0, tiled=True)
        size = gradient.shape[0] // 2
        own = jnp.where(ctx_first, gradient[:size], gradient[size:])
        other = jnp.where(ctx_first, gradient[size:], gradient[:size])
        return own + trade(other.astype(LOW), "ctx", 1).astype(F32)

    normed_all = jnp.concatenate(normed_rows, axis=0)
    down_grad = to_owner(
        dot(
            jnp.concatenate(hidden_rows, axis=0), jnp.concatenate(feed_back_rows, axis=0), (0, 0)
        )
    )
    up_grad = to_owner(dot(jnp.concatenate(up_back_rows, axis=0), normed_all, (0, 0)))
    gate_grad = to_owner(dot(jnp.concatenate(gate_back_rows, axis=0), normed_all, (0, 0)))
    output_grad = to_owner_ordered(
        dot(
            jnp.concatenate(heads_lows, axis=1), jnp.concatenate(attention_back_rows, axis=0), (1, 0)
        )
    )

    input_pieces, triples = [], []
    head_terms = jnp.zeros((head_count, HEAD_DIM), F32)
    for b in micros:
        heads_back = dot(output_weights, attention_back_rows[b], (1, 1), LOW)
        query_grad, own_grad, other_grad = attend_back(
            head_count, places[b], query_low[b], key_values[b], heads_back, summeds[b], totals[b]
        )
        if pair:
            side_grad = own_grad + trade(other_grad[0], "ctx", 1).astype(F32)
        else:
            sides = jnp.concatenate([own_grad[None], other_grad], axis=0)
            sides = jnp.take(sides, lax.rem(table - me + ctx_count, ctx_count), axis=0)
            side_grad = lax.psum_scatter(sides, "ctx", scatter_dimension=0)
        query_grad = query_grad.reshape(head_count, HEAD_DIM, rows)
        key_grad = side_grad[:head_width].reshape(head_count, HEAD_DIM, rows)
        head_terms = head_terms + jnp.sum(
            query_grad * query_units[b] * root_head + key_grad * key_units[b], axis=2
        )
        triple = jnp.concatenate(
            [
                unit_back(
                    query_units[b], query_norms[b], query_grad * scale_column * root_head, axis=1
                ).reshape(head_width, rows),
                unit_back(key_units[b], key_norms[b], key_grad * scale_column, axis=1).reshape(
                    head_width, rows
                ),
                side_grad[head_width:],
            ],
            axis=0,
        ).astype(LOW)
        triples.append(triple)
        other_part = dot(triple[:, half:], triple_weights, (0, 0), LOW)
        own_part = dot(triple[:, :half], triple_weights, (0, 0))
        input_own = first_backs[b] * (1.0 - rate_attention) + tensor_sum(own_part, other_part)
        input_pieces.append(ordered(core_first, input_own, trade(input_own, "tensor", 1), 0))

    triple_grad = dot(
        jnp.concatenate(triples, axis=1),
        token_rows.reshape(micro_count * rows, model_width),
        (1, 0),
    ).reshape(3, head_width, model_width)
    attention_grads = [to_owner_ordered(triple_grad[which]) for which in range(3)] + [output_grad]
    feed_grads = [up_grad, gate_grad, down_grad]

    rate_terms = jnp.concatenate([attention_rate_term, feed_rate_term])
    rate_terms = rate_terms + trade(rate_terms, "tensor", 1)
    rate_terms = rate_terms.reshape(2, model_width)
    head_terms = head_terms.reshape(head_width)
    hidden_terms = jnp.stack([up_terms, gate_terms])
    if pair:
        heads_own = jnp.where(ctx_first, head_terms[:own_rows], head_terms[own_rows:])
        heads_other = jnp.where(ctx_first, head_terms[own_rows:], head_terms[:own_rows])
        rates_own = jnp.where(ctx_first, rate_terms[:, :own_cols], rate_terms[:, own_cols:])
        rates_other = jnp.where(ctx_first, rate_terms[:, own_cols:], rate_terms[:, :own_cols])
        flat = jnp.concatenate(
            [heads_other, hidden_terms[:, own_units:].reshape(-1), rates_other.reshape(-1)]
        )
        flat = trade(flat, "ctx", 1)
        heads_grad = heads_own + flat[:own_rows]
        hidden_grad = hidden_terms[:, :own_units] + flat[
            own_rows : own_rows + 2 * own_units
        ].reshape(2, own_units)
        rates_grad = rates_own + flat[own_rows + 2 * own_units :].reshape(2, own_cols)
    else:
        heads_grad = lax.psum_scatter(head_terms, "ctx", scatter_dimension=0, tiled=True)
        hidden_grad = lax.psum_scatter(hidden_terms, "ctx", scatter_dimension=1, tiled=True)
        rates_grad = lax.psum_scatter(rate_terms, "ctx", scatter_dimension=1, tiled=True)

    def matrix_steps(gradients, masters, firsts, seconds, outers):
        moments, variances, momenta, results = [], [], [], []
        for which, gradient in enumerate(gradients):
            master = masters[which]
            moment, variance, updated = adam_step(
                master, gradient, firsts[0, which], seconds[0, which], MATRIX_RATE, True
            )
            shift = group_sum(split_low(master - updated)) / group_count
            momentum, result = outer_step(master, shift, outers[which], True)
            moments.append(moment)
            variances.append(variance)
            momenta.append(momentum)
            results.append(result)
        return (
            jnp.stack(gradients)[None],
            jnp.stack(moments)[None],
            jnp.stack(variances)[None],
            jnp.stack(momenta),
            jnp.stack(results),
        )

    feed_outs = matrix_steps(
        feed_grads, feedforward_weights, feedforward_first, feedforward_second, feedforward_outer
    )
    attention_outs = matrix_steps(
        attention_grads, attention_weights, attention_first, attention_second, attention_outer
    )

    masters = (head_scales, hidden_scales, residual_rates)
    firsts = (heads_first[0], hidden_first[0], rates_first[0])
    seconds = (heads_second[0], hidden_second[0], rates_second[0])
    outers = (heads_outer, hidden_outer, rates_outer)
    small_grads = (heads_grad, hidden_grad, rates_grad)
    small_moments, small_variances, small_shifts = [], [], []
    for which in range(3):
        moment, variance, updated = adam_step(
            masters[which],
            small_grads[which],
            firsts[which],
            seconds[which],
            SCALE_RATE,
            False,
        )
        small_moments.append(moment)
        small_variances.append(variance)
        small_shifts.append((masters[which] - updated).reshape(-1))
    shift_flat = group_sum(jnp.concatenate(small_shifts)) / group_count
    small_momenta, small_results = [], []
    start = 0
    for which in range(3):
        size = masters[which].size
        shift = shift_flat[start : start + size].reshape(masters[which].shape)
        start += size
        momentum, result = outer_step(masters[which], shift, outers[which], False)
        small_momenta.append(momentum)
        small_results.append(result)

    return (
        jnp.stack(output_pieces)[None],
        jnp.stack(input_pieces)[None],
        attention_outs[0],
        feed_outs[0],
        *[entry[None] for entry in small_grads],
        attention_outs[1],
        feed_outs[1],
        *[entry[None] for entry in small_moments],
        attention_outs[2],
        feed_outs[2],
        *[entry[None] for entry in small_variances],
        attention_outs[3],
        feed_outs[3],
        *small_momenta,
        attention_outs[4],
        feed_outs[4],
        *small_results,
    )


def solution(mesh):
    placed = (
        P("group", None, "ctx", None),
        P("group", None, "ctx", None),
        P("group", None, None),
        P(),
        P(None, ("tensor", "ctx"), None),
        P(None, ("tensor", "ctx"), None),
        P(("tensor", "ctx")),
        P(None, ("tensor", "ctx")),
        P(None, "ctx"),
        P("group", None, ("tensor", "ctx"), None),
        P("group", None, ("tensor", "ctx"), None),
        P("group", ("tensor", "ctx")),
        P("group", None, ("tensor", "ctx")),
        P("group", None, "ctx"),
        P("group", None, ("tensor", "ctx"), None),
        P("group", None, ("tensor", "ctx"), None),
        P("group", ("tensor", "ctx")),
        P("group", None, ("tensor", "ctx")),
        P("group", None, "ctx"),
        P(None, ("tensor", "ctx"), None),
        P(None, ("tensor", "ctx"), None),
        P(("tensor", "ctx")),
        P(None, ("tensor", "ctx")),
        P(None, "ctx"),
    )
    return jax.shard_map(
        on_device,
        mesh=mesh,
        in_specs=placed,
        out_specs=(
            P("group", None, "ctx", None),
            P("group", None, "ctx", None),
            P("group", None, ("tensor", "ctx"), None),
            P("group", None, ("tensor", "ctx"), None),
            P("group", ("tensor", "ctx")),
            P("group", None, ("tensor", "ctx")),
            P("group", None, "ctx"),
            P("group", None, ("tensor", "ctx"), None),
            P("group", None, ("tensor", "ctx"), None),
            P("group", ("tensor", "ctx")),
            P("group", None, ("tensor", "ctx")),
            P("group", None, "ctx"),
            P("group", None, ("tensor", "ctx"), None),
            P("group", None, ("tensor", "ctx"), None),
            P("group", ("tensor", "ctx")),
            P("group", None, ("tensor", "ctx")),
            P("group", None, "ctx"),
            P(None, ("tensor", "ctx"), None),
            P(None, ("tensor", "ctx"), None),
            P(("tensor", "ctx")),
            P(None, ("tensor", "ctx")),
            P(None, "ctx"),
            P(None, ("tensor", "ctx"), None),
            P(None, ("tensor", "ctx"), None),
            P(("tensor", "ctx")),
            P(None, ("tensor", "ctx")),
            P(None, "ctx"),
        ),
        check_vma=False,
    )
```

time: 2000 us -> 1070 us (0.54)
  waiting for transfers between devices: 1470 us -> 422 us
  local copies, waits for them, and re-layouts: 70 us -> 185 us
  starting transfers between devices: 2.13 us -> 84.7 us
  matrix products: 197 us -> 129 us
  blocking collectives: 38.3 us -> 0 us
  Pallas kernels: 0 us -> 33.1 us
    psum x5 -> x0, waiting for transfers between devices: 967 us -> none  [the longest x1 437 us: on_device(): lax.psum((shifts[0], shifts[1], shifts[2], shifts[3], shifts[4]), 'group')]
    ppermute x0 -> x87, waiting for transfers between devices: none -> 422 us  [the longest x63 249 us: trade(): return lax.ppermute(values, axis, [(i, i ^ bit) for i in range(count)])]
    reduce_scatter x5 -> x0, waiting for transfers between devices: 313 us -> none  [the longest x1 213 us: on_device(): lax.psum_scatter(feed_terms, 'ctx', scatter_dimension=1, tiled=True)]
    all_gather x5 -> x0, waiting for transfers between devices: 188 us -> none  [the longest x1 111 us: on_device(): lax.all_gather(feedforward_weights.astype(jnp.bfloat16), 'ctx', axis=1, t...]
    unnamed x279 -> x473, local copies, waits for them, and re-layouts: 37.1 us -> 146 us
    ppermute x0 -> x87, starting transfers between devices: none -> 84.7 us  [the longest x63 50.6 us: trade(): return lax.ppermute(values, axis, [(i, i ^ bit) for i in range(count)])]
    dot_general x30 -> x50, matrix products: 197 us -> 129 us  [dot(): lax.dot_general(left, right, (((contract[0],), (contract[1],)), ((), ()))...]
    reduce_sum x17 -> x24, other arithmetic: 63.1 us -> 20.5 us  [the longest x2 6.97 us: on_device(): jnp.sum(second_back * (feed_unit - afters[b]), axis=0)]
  transfers between devices with their start and end apart: 17 -> 87, of which waited for: 14 -> 37; matrix products, arithmetic and copies ran while one was open for 11% -> 39% of each run, Pallas kernels for 0% -> 3%
where the time goes in v1:
time: 1070 us; the launch traced here: 1060 us
  waiting for transfers between devices  422 us (39%)
  other arithmetic  198 us (19%)
  local copies, waits for them, and re-layouts  185 us (17%)
  matrix products  129 us (12%)
  starting transfers between devices  84.7 us (8%)
  Pallas kernels  33.1 us (3%)
    ppermute x63, waiting for transfers between devices, trade(): return lax.ppermute(values, axis, [(i, i ^ bit) for i in range(count)])  249 us
    ppermute x8, waiting for transfers between devices, group_sum(): back = lax.ppermute(whole, 'group', [(1, 0), (2, 3)])  154 us
    unnamed x473, local copies, waits for them, and re-layouts  146 us
    dot_general x50, matrix products, dot(): lax.dot_general(left, right, (((contract[0],), (contract[1],)), ((), ()))...  129 us
    ppermute x63, starting transfers between devices, trade(): return lax.ppermute(values, axis, [(i, i ^ bit) for i in range(count)])  50.6 us
    reduce_sum x9, other arithmetic, unit_only(): jnp.sum(values * values, axis=-1, keepdims=True) + EPSILON  44.5 us
    pallas_call x3, Pallas kernels, attend_back(): pl.pallas_call(partial(attend_back_kernel, head_count), out_shape=(jax.Sh...  22.9 us
  transfers between devices with their start and end apart: 87, of which 37 were waited for; matrix products, arithmetic and copies ran while one was open for 39% of the time, Pallas kernels for 3%

profile of v1, /device:TPU:0, one launch (start us, length us, event | category | flops | bytes accessed | tf_op | source)
XLA Modules:
  0.0 1057.3 jit_solution(552202976408167721)
XLA Ops:
  16.2 8.7 fusion.315
  24.9 8.0 fusion.316
  37.6 7.8 fusion.314
  49.0 6.5 convert_element_type.572
  56.5 4.6 copy.146
  65.7 4.6 copy.152
  70.2 4.6 copy.145
  79.3 4.6 copy.150
  88.5 4.6 copy.141
  93.0 4.6 copy.148
  97.6 4.6 copy.151
  102.2 4.6 copy.149
  106.8 4.6 copy.147
  128.4 12.4 %collective-permute-done.3 = bf16[640,512]{1,0:T(8,128)(2,1)S(1)} collective-permute-done((bf16[640,512]{1,0:T(8,128)(2,1)S(1)}, bf16[640,512]{1,0:T(8,128)(2,1)S(1)}, u32[]{:S(2)}, u32[]{:S(2)}) %collective-permute-start.3) | collective-permute-done | bytes 655392 | tf_op jit(solution)/shard_map/ppermute | solution.py:52
  145.0 9.9 collective-permute-done.17
  163.2 5.8 collective-permute-done.2
  172.8 4.9 collective-permute-done.4
  180.0 15.2 %collective-permute-done.8 = bf16[320,1280]{1,0:T(8,128)(2,1)S(1)} collective-permute-done((bf16[320,1280]{1,0:T(8,128)(2,1)S(1)}, bf16[320,1280]{1,0:T(8,128)(2,1)S(1)}, u32[]{:S(2)}, u32[]{:S(2)}) %collective-permute-start.8) | collective-permute-done | bytes 819232 | tf_op jit(solution)/shard_map/ppermute | solution.py:52
  195.3 17.6 %collective-permute-done.10 = bf16[320,1280]{1,0:T(8,128)(2,1)S(1)} collective-permute-done((bf16[320,1280]{1,0:T(8,128)(2,1)S(1)}, bf16[320,1280]{1,0:T(8,128)(2,1)S(1)}, u32[]{:S(2)}, u32[]{:S(2)}) %collective-permute-start.10) | collective-permute-done | bytes 819232 | tf_op jit(solution)/shard_map/ppermute | solution.py:52
  214.8 14.1 %collective-permute-done.12 = bf16[320,1280]{1,0:T(8,128)(2,1)S(1)} collective-permute-done((bf16[320,1280]{1,0:T(8,128)(2,1)S(1)}, bf16[320,1280]{1,0:T(8,128)(2,1)S(1)}, u32[]{:S(2)}, u32[]{:S(2)}) %collective-permute-start.12) | collective-permute-done | bytes 819232 | tf_op jit(solution)/shard_map/ppermute | solution.py:52
  237.0 13.0 %collective-permute-done.11 = bf16[320,1280]{1,0:T(8,128)(2,1)S(1)} collective-permute-done((bf16[320,1280]{1,0:T(8,128)(2,1)S(1)}, bf16[320,1280]{1,0:T(8,128)(2,1)S(1)}, u32[]{:S(2)}, u32[]{:S(2)}) %collective-permute-start.11) | collective-permute-done | bytes 819232 | tf_op jit(solution)/shard_map/ppermute | solution.py:52
  250.7 14.5 %collective-permute-done.13 = bf16[320,1280]{1,0:T(8,128)(2,1)S(1)} collective-permute-done((bf16[320,1280]{1,0:T(8,128)(2,1)S(1)}, bf16[320,1280]{1,0:T(8,128)(2,1)S(1)}, u32[]{:S(2)}, u32[]{:S(2)}) %collective-permute-start.13) | collective-permute-done | bytes 819232 | tf_op jit(solution)/shard_map/ppermute | solution.py:52
  266.6 7.8 collective-permute-done.6
  295.8 9.6 multiply_convert_fusion.6
  318.4 11.8 %collective-permute-done.15 = bf16[256,1280]{1,0:T(8,128)(2,1)S(1)} collective-permute-done((bf16[256,1280]{1,0:T(8,128)(2,1)S(1)}, bf16[256,1280]{1,0:T(8,128)(2,1)S(1)}, u32[]{:S(2)}, u32[]{:S(2)}) %collective-permute-start.15) | collective-permute-done | bytes 655392 | tf_op jit(solution)/shard_map/ppermute | solution.py:52
  330.5 13.8 %collective-permute-done.22 = bf16[256,1280]{1,0:T(8,128)(2,1)S(1)} collective-permute-done((bf16[256,1280]{1,0:T(8,128)(2,1)S(1)}, bf16[256,1280]{1,0:T(8,128)(2,1)S(1)}, u32[]{:S(2)}, u32[]{:S(2)}) %collective-permute-start.22) | collective-permute-done | bytes 655392 | tf_op jit(solution)/shard_map/ppermute | solution.py:52
  344.6 13.0 %collective-permute-done.28 = bf16[256,1280]{1,0:T(8,128)(2,1)S(1)} collective-permute-done((bf16[256,1280]{1,0:T(8,128)(2,1)S(1)}, bf16[256,1280]{1,0:T(8,128)(2,1)S(1)}, u32[]{:S(2)}, u32[]{:S(2)}) %collective-permute-start.28) | collective-permute-done | bytes 655392 | tf_op jit(solution)/shard_map/ppermute | solution.py:52
  381.4 13.9 %multiply_reduce_fusion.6 = (f32[1280]{0:T(1024)S(1)}, f32[1280]{0:T(1024)S(1)}, f32[512,1280]{1,0:T(8,128)S(1)}, bf16[512,1280]{1,0:T(8,128)(2,1)}, bf16[512,12...) fusion(f32[512,1280]{1,0:T(8,128)} %fusion.145, ...), kind=kOutput, calls=%fused_computation.146 | convolution fusion | flops 1728176640 | bytes 37396480 | tf_op jit(solution)/shard_map/dot_general | solution.py:45
  412.6 6.1 fusion.12
  418.8 8.3 fusion.6
  433.5 8.9 fusion.18
  480.3 13.1 %collective-permute-done.40 = bf16[256,1280]{1,0:T(8,128)(2,1)S(1)} collective-permute-done((bf16[256,1280]{1,0:T(8,128)(2,1)S(1)}, bf16[256,1280]{1,0:T(8,128)(2,1)S(1)}, u32[]{:S(2)}, u32[]{:S(2)}) %collective-permute-start.40) | collective-permute-done | bytes 655392 | tf_op jit(solution)/shard_map/ppermute | solution.py:52
  493.3 12.8 %collective-permute-done.48 = bf16[256,1280]{1,0:T(8,128)(2,1)S(1)} collective-permute-done((bf16[256,1280]{1,0:T(8,128)(2,1)S(1)}, bf16[256,1280]{1,0:T(8,128)(2,1)S(1)}, u32[]{:S(2)}, u32[]{:S(2)}) %collective-permute-start.48) | collective-permute-done | bytes 655392 | tf_op jit(solution)/shard_map/ppermute | solution.py:52
  518.0 9.8 multiply_reduce_fusion.3
  530.4 7.4 multiply_reduce_fusion.4
  537.8 27.1 %collective-permute-done.58 = bf16[640,1280]{0,1:T(8,128)(2,1)} collective-permute-done((bf16[640,1280]{0,1:T(8,128)(2,1)}, bf16[640,1280]{0,1:T(8,128)(2,1)}, u32[]{:S(2)}, u32[]{:S(2)}) %collective-permute-start.58) | collective-permute-done | bytes 1638432 | tf_op jit(solution)/shard_map/ppermute | solution.py:52
  564.8 6.7 multiply_reduce_fusion.5
  576.1 11.0 %copy.134 = f32[1,3,640,1280]{3,2,1,0:T(8,128)} copy(f32[1,3,640,1280]{2,3,1,0:T(8,128)} %maximum_bitcast_fusion) | data formatting | bytes 19660800
  587.0 8.4 maximum_bitcast_fusion.1
  595.4 11.0 %copy.135 = f32[1,3,640,1280]{3,2,1,0:T(8,128)} copy(f32[1,3,640,1280]{2,3,1,0:T(8,128)} %maximum_bitcast_fusion.1) | data formatting | bytes 19660800
  606.4 8.4 maximum_bitcast_fusion.2
  614.7 11.0 %copy.136 = f32[1,3,640,1280]{3,2,1,0:T(8,128)} copy(f32[1,3,640,1280]{2,3,1,0:T(8,128)} %maximum_bitcast_fusion.2) | data formatting | bytes 19660800
  625.7 4.7 fusion.29
  630.4 4.6 collective-permute-start.81
  643.5 7.5 shard_map.442
  654.0 7.9 shard_map.443
  664.8 7.5 shard_map.444
  683.8 11.2 %collective-permute-done.50 = bf16[640,512]{1,0:T(8,128)(2,1)S(1)} collective-permute-done((bf16[640,512]{1,0:T(8,128)(2,1)S(1)}, bf16[640,512]{1,0:T(8,128)(2,1)S(1)}, u32[]{:S(2)}, u32[]{:S(2)}) %collective-permute-start.50) | collective-permute-done | bytes 655392 | tf_op jit(solution)/shard_map/ppermute | solution.py:52
  742.3 4.9 collective-permute-done.55
  748.2 7.8 collective-permute-done.56
  755.9 6.7 multiply_reduce_fusion.46
  788.8 5.3 collective-permute-done.72
  795.8 7.2 collective-permute-done.69
  804.6 6.9 collective-permute-done.66
  820.1 12.3 %collective-permute-done.52 = bf16[256,1280]{1,0:T(8,128)(2,1)S(1)} collective-permute-done((bf16[256,1280]{1,0:T(8,128)(2,1)S(1)}, bf16[256,1280]{1,0:T(8,128)(2,1)S(1)}, u32[]{:S(2)}, u32[]{:S(2)}) %collective-permute-start.52) | collective-permute-done | bytes 655392 | tf_op jit(solution)/shard_map/ppermute | solution.py:52
  834.5 42.0 %collective-permute-done.65 = bf16[160,1280]{1,0:T(8,128)(2,1)S(1)} collective-permute-done((bf16[160,1280]{1,0:T(8,128)(2,1)S(1)}, bf16[160,1280]{1,0:T(8,128)(2,1)S(1)}, u32[]{:S(2)}, u32[]{:S(2)}) %collective-permute-start.65) | collective-permute-done | bytes 409632 | tf_op jit(solution)/shard_map/ppermute | solution.py:87
  877.3 8.0 collective-permute-done.74
  886.3 7.7 collective-permute-done.71
  923.1 31.5 %collective-permute-done.83 = bf16[640,1280]{0,1:T(8,128)(2,1)S(1)} collective-permute-done((bf16[640,1280]{0,1:T(8,128)(2,1)S(1)}, bf16[640,1280]{0,1:T(8,128)(2,1)S(1)}, u32[]{:S(2)}, u32[]{:S(2)}) %collective-permute-start.83) | collective-permute-done | bytes 1638432 | tf_op jit(solution)/shard_map/ppermute | solution.py:87
  956.0 33.9 %collective-permute-done.80 = bf16[640,1280]{0,1:T(8,128)(2,1)} collective-permute-done((bf16[640,1280]{0,1:T(8,128)(2,1)}, bf16[640,1280]{0,1:T(8,128)(2,1)}, u32[]{:S(2)}, u32[]{:S(2)}) %collective-permute-start.80) | collective-permute-done | bytes 1638432 | tf_op jit(solution)/shard_map/ppermute | solution.py:87
  994.4 23.0 %collective-permute-done.77 = bf16[640,1280]{0,1:T(8,128)(2,1)} collective-permute-done((bf16[640,1280]{0,1:T(8,128)(2,1)}, bf16[640,1280]{0,1:T(8,128)(2,1)}, u32[]{:S(2)}, u32[]{:S(2)}) %collective-permute-start.77) | collective-permute-done | bytes 1638432 | tf_op jit(solution)/shard_map/ppermute | solution.py:87
  1017.4 4.6 multiply_reduce_fusion.2
  1026.5 11.0 %copy.137 = f32[3,640,1280]{2,1,0:T(8,128)} copy(f32[3,640,1280]{1,2,0:T(8,128)} %pad_maximum_fusion) | data formatting | bytes 19660800
  1045.9 11.0 %copy.138 = f32[3,640,1280]{2,1,0:T(8,128)} copy(f32[3,640,1280]{1,2,0:T(8,128)} %pad_maximum_fusion.1) | data formatting | bytes 19660800
  (883 shorter events, 385.9 us)
Async XLA Ops:
  2.9 109.3 %collective-permute-start.1 = (bf16[3,160,1280]{2,1,0:T(8,128)(2,1)S(1)}, bf16[3,160,1280]{2,1,0:T(8,128)(2,1)}, u32[]{:S(2)}, u32[]{:S(2)}) collective-permute-start(bf16[3,160,1280]{2,1,0:T(8,128)(2,1)S(1)} %slice.660), channel_id=1, source_target_pairs={{0,4},{4,0},{1,5},{5,1},{2,6},{6,2},{3,7},{7,3},{8,12},{12,8},{9,1... | collective-permute-start | bytes 3686408 | tf_op jit(solution)/shard_map/ppermute | solution.py:52
  6.1 105.3 %collective-permute-start = (bf16[2720]{0:T(1024)(128)(2,1)S(1)}, bf16[2720]{0:T(1024)(128)(2,1)S(1)}, u32[]{:S(2)}, u32[]{:S(2)}) collective-permute-start(bf16[2720]{0:T(1024)(128)(2,1)S(1)} %concatenate.335), channel_id=1, source_target_pairs={{0,4},{4,0},{1,5},{5,1},{2,6},{6,2},{3,7},{7,3},{8,12},{12,8},{9,1... | collective-permute-start | bytes 16328 | tf_op jit(solution)/shard_map/ppermute | solution.py:52
  123.1 17.7 %collective-permute-start.3 = (bf16[640,512]{1,0:T(8,128)(2,1)S(1)}, bf16[640,512]{1,0:T(8,128)(2,1)S(1)}, u32[]{:S(2)}, u32[]{:S(2)}) collective-permute-start(bf16[640,512]{1,0:T(8,128)(2,1)S(1)} %get-tuple-element.357), channel_id=1, source_target_pairs={{0,4},{4,0},{1,5},{5,1},{2,6},{6,2},{3,7},{7,3},{8,12},{12,8},{9,1... | collective-permute-start | bytes 1966088 | tf_op jit(solution)/shard_map/ppermute | solution.py:52
  126.2 28.7 %collective-permute-start.17 = (bf16[640,512]{1,0:T(8,128)(2,1)S(1)}, bf16[640,512]{1,0:T(8,128)(2,1)S(1)}, u32[]{:S(2)}, u32[]{:S(2)}) collective-permute-start(bf16[640,512]{1,0:T(8,128)(2,1)S(1)} %get-tuple-element.355), channel_id=1, source_target_pairs={{0,4},{4,0},{1,5},{5,1},{2,6},{6,2},{3,7},{7,3},{8,12},{12,8},{9,1... | collective-permute-start | bytes 1966088 | tf_op jit(solution)/shard_map/ppermute | solution.py:52
  126.8 42.1 %collective-permute-start.2 = (bf16[640,512]{1,0:T(8,128)(2,1)S(1)}, bf16[640,512]{1,0:T(8,128)(2,1)S(1)}, u32[]{:S(2)}, u32[]{:S(2)}) collective-permute-start(bf16[640,512]{1,0:T(8,128)(2,1)S(1)} %get-tuple-element.359), channel_id=1, source_target_pairs={{0,4},{4,0},{1,5},{5,1},{2,6},{6,2},{3,7},{7,3},{8,12},{12,8},{9,1... | collective-permute-start | bytes 1966088 | tf_op jit(solution)/shard_map/ppermute | solution.py:52
  141.0 36.7 %collective-permute-start.4 = (bf16[160,1280]{1,0:T(8,128)(2,1)S(1)}, bf16[160,1280]{1,0:T(8,128)(2,1)S(1)}, u32[]{:S(2)}, u32[]{:S(2)}) collective-permute-start(bf16[160,1280]{1,0:T(8,128)(2,1)S(1)} %copy-done.147), channel_id=1, source_target_pairs={{0,4},{4,0},{1,5},{5,1},{2,6},{6,2},{3,7},{7,3},{8,12},{12,8},{9,1... | collective-permute-start | bytes 1228808 | tf_op jit(solution)/shard_map/ppermute | solution.py:52
  142.9 52.4 %collective-permute-start.8 = (bf16[320,1280]{1,0:T(8,128)(2,1)S(1)}, bf16[320,1280]{1,0:T(8,128)(2,1)S(1)}, u32[]{:S(2)}, u32[]{:S(2)}) collective-permute-start(bf16[320,1280]{1,0:T(8,128)(2,1)S(1)} %get-tuple-element.300), channel_id=1, source_target_pairs={{0,4},{4,0},{1,5},{5,1},{2,6},{6,2},{3,7},{7,3},{8,12},{12,8},{9,1... | collective-permute-start | bytes 2457608 | tf_op jit(solution)/shard_map/ppermute | solution.py:52
  143.4 69.4 %collective-permute-start.10 = (bf16[320,1280]{1,0:T(8,128)(2,1)S(1)}, bf16[320,1280]{1,0:T(8,128)(2,1)S(1)}, u32[]{:S(2)}, u32[]{:S(2)}) collective-permute-start(bf16[320,1280]{1,0:T(8,128)(2,1)S(1)} %get-tuple-element.299), channel_id=1, source_target_pairs={{0,4},{4,0},{1,5},{5,1},{2,6},{6,2},{3,7},{7,3},{8,12},{12,8},{9,1... | collective-permute-start | bytes 2457608 | tf_op jit(solution)/shard_map/ppermute | solution.py:52
  154.9 74.0 %collective-permute-start.12 = (bf16[320,1280]{1,0:T(8,128)(2,1)S(1)}, bf16[320,1280]{1,0:T(8,128)(2,1)S(1)}, u32[]{:S(2)}, u32[]{:S(2)}) collective-permute-start(bf16[320,1280]{1,0:T(8,128)(2,1)S(1)} %get-tuple-element.298), channel_id=1, source_target_pairs={{0,4},{4,0},{1,5},{5,1},{2,6},{6,2},{3,7},{7,3},{8,12},{12,8},{9,1... | collective-permute-start | bytes 2457608 | tf_op jit(solution)/shard_map/ppermute | solution.py:52
  178.3 52.2 %collective-permute-start.24 = (bf16[256,1280]{1,0:T(8,128)(2,1)S(1)}, bf16[256,1280]{1,0:T(8,128)(2,1)S(1)}, u32[]{:S(2)}, u32[]{:S(2)}) collective-permute-start(bf16[256,1280]{1,0:T(8,128)(2,1)S(1)} %convolution_convert_fusion.6), channel_id=1, source_target_pairs={{0,1},{1,0},{2,3},{3,2},{4,5},{5,4},{6,7},{7,6},{8,9},{9,8},{10,11... | collective-permute-start | bytes 1966088 | tf_op jit(solution)/shard_map/ppermute | solution.py:52
  178.9 52.6 %collective-permute-start.18 = (bf16[256,1280]{1,0:T(8,128)(2,1)S(1)}, bf16[256,1280]{1,0:T(8,128)(2,1)S(1)}, u32[]{:S(2)}, u32[]{:S(2)}) collective-permute-start(bf16[256,1280]{1,0:T(8,128)(2,1)S(1)} %convolution_convert_fusion.7), channel_id=1, source_target_pairs={{0,1},{1,0},{2,3},{3,2},{4,5},{5,4},{6,7},{7,6},{8,9},{9,8},{10,11... | collective-permute-start | bytes 1966088 | tf_op jit(solution)/shard_map/ppermute | solution.py:52
  195.3 38.4 %collective-permute-start.5 = (bf16[256,1280]{1,0:T(8,128)(2,1)S(1)}, bf16[256,1280]{1,0:T(8,128)(2,1)S(1)}, u32[]{:S(2)}, u32[]{:S(2)}) collective-permute-start(bf16[256,1280]{1,0:T(8,128)(2,1)S(1)} %convolution_convert_fusion.8), channel_id=1, source_target_pairs={{0,1},{1,0},{2,3},{3,2},{4,5},{5,4},{6,7},{7,6},{8,9},{9,8},{10,11... | collective-permute-start | bytes 1966088 | tf_op jit(solution)/shard_map/ppermute | solution.py:52
  212.8 22.0 %collective-permute-start.9 = (bf16[320,1280]{1,0:T(8,128)(2,1)S(1)}, bf16[320,1280]{1,0:T(8,128)(2,1)S(1)}, u32[]{:S(2)}, u32[]{:S(2)}) collective-permute-start(bf16[320,1280]{1,0:T(8,128)(2,1)S(1)} %collective-permute-done.8), channel_id=1, source_target_pairs={{0,8},{8,0},{16,24},{24,16},{1,9},{9,1},{17,25},{25,17},{2,10},{10... | collective-permute-start | bytes 2457608 | tf_op jit(solution)/shard_map/ppermute | solution.py:52
  228.9 21.2 %collective-permute-start.11 = (bf16[320,1280]{1,0:T(8,128)(2,1)S(1)}, bf16[320,1280]{1,0:T(8,128)(2,1)S(1)}, u32[]{:S(2)}, u32[]{:S(2)}) collective-permute-start(bf16[320,1280]{1,0:T(8,128)(2,1)S(1)} %collective-permute-done.10), channel_id=1, source_target_pairs={{0,8},{8,0},{16,24},{24,16},{1,9},{9,1},{17,25},{25,17},{2,10},{10... | collective-permute-start | bytes 2457608 | tf_op jit(solution)/shard_map/ppermute | solution.py:52
  230.5 34.8 %collective-permute-start.13 = (bf16[320,1280]{1,0:T(8,128)(2,1)S(1)}, bf16[320,1280]{1,0:T(8,128)(2,1)S(1)}, u32[]{:S(2)}, u32[]{:S(2)}) collective-permute-start(bf16[320,1280]{1,0:T(8,128)(2,1)S(1)} %collective-permute-done.12), channel_id=1, source_target_pairs={{0,8},{8,0},{16,24},{24,16},{1,9},{9,1},{17,25},{25,17},{2,10},{10... | collective-permute-start | bytes 2457608 | tf_op jit(solution)/shard_map/ppermute | solution.py:52
  231.5 34.4 %collective-permute-start.25 = (bf16[256,1280]{1,0:T(8,128)(2,1)S(1)}, bf16[256,1280]{1,0:T(8,128)(2,1)S(1)}, u32[]{:S(2)}, u32[]{:S(2)}) collective-permute-start(bf16[256,1280]{1,0:T(8,128)(2,1)S(1)} %fusion.71), channel_id=1, source_target_pairs={{0,2},{1,3},{2,0},{3,1},{4,6},{5,7},{6,4},{7,5},{8,10},{9,11},{10,... | collective-permute-start | bytes 1966088 | tf_op jit(solution)/shard_map/ppermute | solution.py:52
  233.7 32.5 %collective-permute-start.19 = (bf16[256,1280]{1,0:T(8,128)(2,1)S(1)}, bf16[256,1280]{1,0:T(8,128)(2,1)S(1)}, u32[]{:S(2)}, u32[]{:S(2)}) collective-permute-start(bf16[256,1280]{1,0:T(8,128)(2,1)S(1)} %fusion.70), channel_id=1, source_target_pairs={{0,2},{1,3},{2,0},{3,1},{4,6},{5,7},{6,4},{7,5},{8,10},{9,11},{10,... | collective-permute-start | bytes 1966088 | tf_op jit(solution)/shard_map/ppermute | solution.py:52
  234.8 39.6 %collective-permute-start.6 = (bf16[256,1280]{1,0:T(8,128)(2,1)S(1)}, bf16[256,1280]{1,0:T(8,128)(2,1)S(1)}, u32[]{:S(2)}, u32[]{:S(2)}) collective-permute-start(bf16[256,1280]{1,0:T(8,128)(2,1)S(1)} %fusion.69), channel_id=1, source_target_pairs={{0,2},{1,3},{2,0},{3,1},{4,6},{5,7},{6,4},{7,5},{8,10},{9,11},{10,... | collective-permute-start | bytes 1966088 | tf_op jit(solution)/shard_map/ppermute | solution.py:52
  312.6 17.6 %collective-permute-start.15 = (bf16[256,1280]{1,0:T(8,128)(2,1)S(1)}, bf16[256,1280]{1,0:T(8,128)(2,1)S(1)}, u32[]{:S(2)}, u32[]{:S(2)}) collective-permute-start(bf16[256,1280]{1,0:T(8,128)(2,1)S(1)} %add_convert_fusion.8), channel_id=1, source_target_pairs={{0,2},{1,3},{2,0},{3,1},{4,6},{5,7},{6,4},{7,5},{8,10},{9,11},{10,... | collective-permute-start | bytes 1966088 | tf_op jit(solution)/shard_map/ppermute | solution.py:52
  315.2 29.1 %collective-permute-start.22 = (bf16[256,1280]{1,0:T(8,128)(2,1)S(1)}, bf16[256,1280]{1,0:T(8,128)(2,1)S(1)}, u32[]{:S(2)}, u32[]{:S(2)}) collective-permute-start(bf16[256,1280]{1,0:T(8,128)(2,1)S(1)} %add_convert_fusion.7), channel_id=1, source_target_pairs={{0,2},{1,3},{2,0},{3,1},{4,6},{5,7},{6,4},{7,5},{8,10},{9,11},{10,... | collective-permute-start | bytes 1966088 | tf_op jit(solution)/shard_map/ppermute | solution.py:52
  316.9 40.7 %collective-permute-start.28 = (bf16[256,1280]{1,0:T(8,128)(2,1)S(1)}, bf16[256,1280]{1,0:T(8,128)(2,1)S(1)}, u32[]{:S(2)}, u32[]{:S(2)}) collective-permute-start(bf16[256,1280]{1,0:T(8,128)(2,1)S(1)} %add_convert_fusion.6), channel_id=1, source_target_pairs={{0,2},{1,3},{2,0},{3,1},{4,6},{5,7},{6,4},{7,5},{8,10},{9,11},{10,... | collective-permute-start | bytes 1966088 | tf_op jit(solution)/shard_map/ppermute | solution.py:52
  370.8 90.8 %collective-permute-start.29 = (f32[256,1280]{1,0:T(8,128)}, f32[256,1280]{1,0:T(8,128)}, u32[]{:S(2)}, u32[]{:S(2)}) collective-permute-start(f32[256,1280]{1,0:T(8,128)} %get-tuple-element.244), channel_id=1, source_target_pairs={{0,1},{1,0},{2,3},{3,2},{4,5},{5,4},{6,7},{7,6},{8,9},{9,8},{10,11... | collective-permute-start | bytes 3932168 | tf_op jit(solution)/shard_map/ppermute | solution.py:52
  371.4 94.8 %collective-permute-start.23 = (f32[256,1280]{1,0:T(8,128)}, f32[256,1280]{1,0:T(8,128)}, u32[]{:S(2)}, u32[]{:S(2)}) collective-permute-start(f32[256,1280]{1,0:T(8,128)} %get-tuple-element.243), channel_id=1, source_target_pairs={{0,1},{1,0},{2,3},{3,2},{4,5},{5,4},{6,7},{7,6},{8,9},{9,8},{10,11... | collective-permute-start | bytes 3932168 | tf_op jit(solution)/shard_map/ppermute | solution.py:52
  373.3 96.3 %collective-permute-start.16 = (f32[256,1280]{1,0:T(8,128)}, f32[256,1280]{1,0:T(8,128)}, u32[]{:S(2)}, u32[]{:S(2)}) collective-permute-start(f32[256,1280]{1,0:T(8,128)} %get-tuple-element.242), channel_id=1, source_target_pairs={{0,1},{1,0},{2,3},{3,2},{4,5},{5,4},{6,7},{7,6},{8,9},{9,8},{10,11... | collective-permute-start | bytes 3932168 | tf_op jit(solution)/shard_map/ppermute | solution.py:52
  407.6 44.4 %collective-permute-start.31 = (bf16[256,1280]{1,0:T(8,128)(2,1)}, bf16[256,1280]{1,0:T(8,128)(2,1)}, u32[]{:S(2)}, u32[]{:S(2)}) collective-permute-start(bf16[256,1280]{1,0:T(8,128)(2,1)} %fusion.60), channel_id=1, source_target_pairs={{0,1},{1,0},{2,3},{3,2},{4,5},{5,4},{6,7},{7,6},{8,9},{9,8},{10,11... | collective-permute-start | bytes 1966088 | tf_op jit(solution)/shard_map/ppermute | solution.py:52
  409.9 46.4 %collective-permute-start.39 = (bf16[256,1280]{1,0:T(8,128)(2,1)}, bf16[256,1280]{1,0:T(8,128)(2,1)}, u32[]{:S(2)}, u32[]{:S(2)}) collective-permute-start(bf16[256,1280]{1,0:T(8,128)(2,1)} %fusion.61), channel_id=1, source_target_pairs={{0,1},{1,0},{2,3},{3,2},{4,5},{5,4},{6,7},{7,6},{8,9},{9,8},{10,11... | collective-permute-start | bytes 1966088 | tf_op jit(solution)/shard_map/ppermute | solution.py:52
  456.2 61.2 %collective-permute-start.60 = (bf16[640,1280]{0,1:T(8,128)(2,1)}, bf16[640,1280]{0,1:T(8,128)(2,1)}, u32[]{:S(2)}, u32[]{:S(2)}) collective-permute-start(bf16[640,1280]{0,1:T(8,128)(2,1)} %slice.1066), channel_id=1, source_target_pairs={{0,4},{4,0},{1,5},{5,1},{2,6},{6,2},{3,7},{7,3},{8,12},{12,8},{9,1... | collective-permute-start | bytes 4915208 | tf_op jit(solution)/shard_map/ppermute | solution.py:52
  459.4 70.9 %collective-permute-start.59 = (bf16[640,1280]{0,1:T(8,128)(2,1)}, bf16[640,1280]{0,1:T(8,128)(2,1)}, u32[]{:S(2)}, u32[]{:S(2)}) collective-permute-start(bf16[640,1280]{0,1:T(8,128)(2,1)} %slice.1067), channel_id=1, source_target_pairs={{0,4},{4,0},{1,5},{5,1},{2,6},{6,2},{3,7},{7,3},{8,12},{12,8},{9,1... | collective-permute-start | bytes 4915208 | tf_op jit(solution)/shard_map/ppermute | solution.py:52
  461.6 17.7 %collective-permute-start.32 = (bf16[256,1280]{1,0:T(8,128)(2,1)S(1)}, bf16[256,1280]{1,0:T(8,128)(2,1)S(1)}, u32[]{:S(2)}, u32[]{:S(2)}) collective-permute-start(bf16[256,1280]{1,0:T(8,128)(2,1)S(1)} %fusion.68), channel_id=1, source_target_pairs={{0,2},{1,3},{2,0},{3,1},{4,6},{5,7},{6,4},{7,5},{8,10},{9,11},{10,... | collective-permute-start | bytes 1966088 | tf_op jit(solution)/shard_map/ppermute | solution.py:52
  466.2 27.1 %collective-permute-start.40 = (bf16[256,1280]{1,0:T(8,128)(2,1)S(1)}, bf16[256,1280]{1,0:T(8,128)(2,1)S(1)}, u32[]{:S(2)}, u32[]{:S(2)}) collective-permute-start(bf16[256,1280]{1,0:T(8,128)(2,1)S(1)} %fusion.67), channel_id=1, source_target_pairs={{0,2},{1,3},{2,0},{3,1},{4,6},{5,7},{6,4},{7,5},{8,10},{9,11},{10,... | collective-permute-start | bytes 1966088 | tf_op jit(solution)/shard_map/ppermute | solution.py:52
  469.7 36.4 %collective-permute-start.48 = (bf16[256,1280]{1,0:T(8,128)(2,1)S(1)}, bf16[256,1280]{1,0:T(8,128)(2,1)S(1)}, u32[]{:S(2)}, u32[]{:S(2)}) collective-permute-start(bf16[256,1280]{1,0:T(8,128)(2,1)S(1)} %fusion.66), channel_id=1, source_target_pairs={{0,2},{1,3},{2,0},{3,1},{4,6},{5,7},{6,4},{7,5},{8,10},{9,11},{10,... | collective-permute-start | bytes 1966088 | tf_op jit(solution)/shard_map/ppermute | solution.py:52
  479.3 85.5 %collective-permute-start.58 = (bf16[640,1280]{0,1:T(8,128)(2,1)}, bf16[640,1280]{0,1:T(8,128)(2,1)}, u32[]{:S(2)}, u32[]{:S(2)}) collective-permute-start(bf16[640,1280]{0,1:T(8,128)(2,1)} %slice.1068), channel_id=1, source_target_pairs={{0,4},{4,0},{1,5},{5,1},{2,6},{6,2},{3,7},{7,3},{8,12},{12,8},{9,1... | collective-permute-start | bytes 4915208 | tf_op jit(solution)/shard_map/ppermute | solution.py:52
  514.7 126.7 %collective-permute-start.33 = (bf16[256,1280]{1,0:T(8,128)(2,1)}, bf16[256,1280]{1,0:T(8,128)(2,1)}, u32[]{:S(2)}, u32[]{:S(2)}) collective-permute-start(bf16[256,1280]{1,0:T(8,128)(2,1)} %get-tuple-element.386), channel_id=1, source_target_pairs={{0,1},{1,0},{2,3},{3,2},{4,5},{5,4},{6,7},{7,6},{8,9},{9,8},{10,11... | collective-permute-start | bytes 1966088 | tf_op jit(solution)/shard_map/ppermute | solution.py:52
  517.3 134.8 %collective-permute-start.41 = (bf16[256,1280]{1,0:T(8,128)(2,1)}, bf16[256,1280]{1,0:T(8,128)(2,1)}, u32[]{:S(2)}, u32[]{:S(2)}) collective-permute-start(bf16[256,1280]{1,0:T(8,128)(2,1)} %get-tuple-element.388), channel_id=1, source_target_pairs={{0,1},{1,0},{2,3},{3,2},{4,5},{5,4},{6,7},{7,6},{8,9},{9,8},{10,11... | collective-permute-start | bytes 1966088 | tf_op jit(solution)/shard_map/ppermute | solution.py:52
  517.4 145.7 %collective-permute-start.49 = (bf16[256,1280]{1,0:T(8,128)(2,1)}, bf16[256,1280]{1,0:T(8,128)(2,1)}, u32[]{:S(2)}, u32[]{:S(2)}) collective-permute-start(bf16[256,1280]{1,0:T(8,128)(2,1)} %get-tuple-element.387), channel_id=1, source_target_pairs={{0,1},{1,0},{2,3},{3,2},{4,5},{5,4},{6,7},{7,6},{8,9},{9,8},{10,11... | collective-permute-start | bytes 1966088 | tf_op jit(solution)/shard_map/ppermute | solution.py:52
  630.4 141.4 %collective-permute-start.81 = (bf16[640,1280]{0,1:T(8,128)(2,1)}, bf16[640,1280]{0,1:T(8,128)(2,1)}, u32[]{:S(2)}, u32[]{:S(2)}) collective-permute-start(bf16[640,1280]{0,1:T(8,128)(2,1)} %fusion.29), channel_id=1, source_target_pairs={{0,8},{24,16},{1,9},{25,17},{2,10},{26,18},{3,11},{27,19},{4,12},{... | collective-permute-start | bytes 4915208 | tf_op jit(solution)/shard_map/ppermute | solution.py:82
  636.7 137.4 %collective-permute-start.78 = (bf16[640,1280]{0,1:T(8,128)(2,1)}, bf16[640,1280]{0,1:T(8,128)(2,1)}, u32[]{:S(2)}, u32[]{:S(2)}) collective-permute-start(bf16[640,1280]{0,1:T(8,128)(2,1)} %fusion.32), channel_id=1, source_target_pairs={{0,8},{24,16},{1,9},{25,17},{2,10},{26,18},{3,11},{27,19},{4,12},{... | collective-permute-start | bytes 4915208 | tf_op jit(solution)/shard_map/ppermute | solution.py:82
  651.0 31.4 %collective-permute-start.34 = (bf16[640,512]{1,0:T(8,128)(2,1)S(1)}, bf16[640,512]{1,0:T(8,128)(2,1)S(1)}, u32[]{:S(2)}, u32[]{:S(2)}) collective-permute-start(bf16[640,512]{1,0:T(8,128)(2,1)S(1)} %bitcast.648), channel_id=1, source_target_pairs={{0,4},{4,0},{1,5},{5,1},{2,6},{6,2},{3,7},{7,3},{8,12},{12,8},{9,1... | collective-permute-start | bytes 1966088 | tf_op jit(solution)/shard_map/ppermute | solution.py:52
  662.0 20.8 %collective-permute-start.42 = (bf16[640,512]{1,0:T(8,128)(2,1)S(1)}, bf16[640,512]{1,0:T(8,128)(2,1)S(1)}, u32[]{:S(2)}, u32[]{:S(2)}) collective-permute-start(bf16[640,512]{1,0:T(8,128)(2,1)S(1)} %bitcast.649), channel_id=1, source_target_pairs={{0,4},{4,0},{1,5},{5,1},{2,6},{6,2},{3,7},{7,3},{8,12},{12,8},{9,1... | collective-permute-start | bytes 1966088 | tf_op jit(solution)/shard_map/ppermute | solution.py:52
  672.3 22.7 %collective-permute-start.50 = (bf16[640,512]{1,0:T(8,128)(2,1)S(1)}, bf16[640,512]{1,0:T(8,128)(2,1)S(1)}, u32[]{:S(2)}, u32[]{:S(2)}) collective-permute-start(bf16[640,512]{1,0:T(8,128)(2,1)S(1)} %bitcast.650), channel_id=1, source_target_pairs={{0,4},{4,0},{1,5},{5,1},{2,6},{6,2},{3,7},{7,3},{8,12},{12,8},{9,1... | collective-permute-start | bytes 1966088 | tf_op jit(solution)/shard_map/ppermute | solution.py:52
  726.7 20.5 %collective-permute-start.55 = (bf16[160,1280]{1,0:T(8,128)(2,1)}, bf16[160,1280]{1,0:T(8,128)(2,1)}, u32[]{:S(2)}, u32[]{:S(2)}) collective-permute-start(bf16[160,1280]{1,0:T(8,128)(2,1)} %get-tuple-element.294), channel_id=1, source_target_pairs={{0,4},{4,0},{1,5},{5,1},{2,6},{6,2},{3,7},{7,3},{8,12},{12,8},{9,1... | collective-permute-start | bytes 1228808 | tf_op jit(solution)/shard_map/ppermute | solution.py:52
  735.1 20.8 %collective-permute-start.56 = (bf16[160,1280]{1,0:T(8,128)(2,1)}, bf16[160,1280]{1,0:T(8,128)(2,1)}, u32[]{:S(2)}, u32[]{:S(2)}) collective-permute-start(bf16[160,1280]{1,0:T(8,128)(2,1)} %get-tuple-element.293), channel_id=1, source_target_pairs={{0,4},{4,0},{1,5},{5,1},{2,6},{6,2},{3,7},{7,3},{8,12},{12,8},{9,1... | collective-permute-start | bytes 1228808 | tf_op jit(solution)/shard_map/ppermute | solution.py:52
  740.1 37.8 %collective-permute-start.75 = (bf16[640,1280]{0,1:T(8,128)(2,1)}, bf16[640,1280]{0,1:T(8,128)(2,1)S(1)}, u32[]{:S(2)}, u32[]{:S(2)}) collective-permute-start(bf16[640,1280]{0,1:T(8,128)(2,1)} %fusion.35), channel_id=1, source_target_pairs={{0,8},{24,16},{1,9},{25,17},{2,10},{26,18},{3,11},{27,19},{4,12},{... | collective-permute-start | bytes 4915208 | tf_op jit(solution)/shard_map/ppermute | solution.py:82
  747.2 15.5 %collective-permute-start.57 = (bf16[160,1280]{1,0:T(8,128)(2,1)}, bf16[160,1280]{1,0:T(8,128)(2,1)S(1)}, u32[]{:S(2)}, u32[]{:S(2)}) collective-permute-start(bf16[160,1280]{1,0:T(8,128)(2,1)} %select_convert_fusion), channel_id=1, source_target_pairs={{0,4},{4,0},{1,5},{5,1},{2,6},{6,2},{3,7},{7,3},{8,12},{12,8},{9,1... | collective-permute-start | bytes 1228808 | tf_op jit(solution)/shard_map/ppermute | solution.py:52
  755.9 23.8 %collective-permute-start.35 = (bf16[256,1280]{1,0:T(8,128)(2,1)}, bf16[256,1280]{1,0:T(8,128)(2,1)S(1)}, u32[]{:S(2)}, u32[]{:S(2)}) collective-permute-start(bf16[256,1280]{1,0:T(8,128)(2,1)} %convolution_convert_fusion.2), channel_id=1, source_target_pairs={{0,1},{1,0},{2,3},{3,2},{4,5},{5,4},{6,7},{7,6},{8,9},{9,8},{10,11... | collective-permute-start | bytes 1966088 | tf_op jit(solution)/shard_map/ppermute | solution.py:52
  762.7 19.4 %collective-permute-start.43 = (bf16[256,1280]{1,0:T(8,128)(2,1)S(1)}, bf16[256,1280]{1,0:T(8,128)(2,1)S(1)}, u32[]{:S(2)}, u32[]{:S(2)}) collective-permute-start(bf16[256,1280]{1,0:T(8,128)(2,1)S(1)} %copy-done.139), channel_id=1, source_target_pairs={{0,1},{1,0},{2,3},{3,2},{4,5},{5,4},{6,7},{7,6},{8,9},{9,8},{10,11... | collective-permute-start | bytes 1966088 | tf_op jit(solution)/shard_map/ppermute | solution.py:52
  777.9 16.2 %collective-permute-start.72 = (bf16[160,1280]{1,0:T(8,128)(2,1)S(1)}, bf16[160,1280]{1,0:T(8,128)(2,1)S(1)}, u32[]{:S(2)}, u32[]{:S(2)}) collective-permute-start(bf16[160,1280]{1,0:T(8,128)(2,1)S(1)} %get-tuple-element.308), channel_id=1, source_target_pairs={{0,8},{24,16},{1,9},{25,17},{2,10},{26,18},{3,11},{27,19},{4,12},{... | collective-permute-start | bytes 1228808 | tf_op jit(solution)/shard_map/ppermute | solution.py:82
  779.7 23.2 %collective-permute-start.69 = (bf16[160,1280]{1,0:T(8,128)(2,1)S(1)}, bf16[160,1280]{1,0:T(8,128)(2,1)S(1)}, u32[]{:S(2)}, u32[]{:S(2)}) collective-permute-start(bf16[160,1280]{1,0:T(8,128)(2,1)S(1)} %get-tuple-element.307), channel_id=1, source_target_pairs={{0,8},{24,16},{1,9},{25,17},{2,10},{26,18},{3,11},{27,19},{4,12},{... | collective-permute-start | bytes 1228808 | tf_op jit(solution)/shard_map/ppermute | solution.py:82
  782.1 29.4 %collective-permute-start.66 = (bf16[160,1280]{1,0:T(8,128)(2,1)S(1)}, bf16[160,1280]{1,0:T(8,128)(2,1)S(1)}, u32[]{:S(2)}, u32[]{:S(2)}) collective-permute-start(bf16[160,1280]{1,0:T(8,128)(2,1)S(1)} %get-tuple-element.306), channel_id=1, source_target_pairs={{0,8},{24,16},{1,9},{25,17},{2,10},{26,18},{3,11},{27,19},{4,12},{... | collective-permute-start | bytes 1228808 | tf_op jit(solution)/shard_map/ppermute | solution.py:82
  784.4 120.7 %collective-permute-start.82 = (bf16[640,1280]{0,1:T(8,128)(2,1)S(1)}, bf16[640,1280]{0,1:T(8,128)(2,1)}, u32[]{:S(2)}, u32[]{:S(2)}) collective-permute-start(bf16[640,1280]{0,1:T(8,128)(2,1)S(1)} %add_convert_fusion.1), channel_id=1, source_target_pairs={{8,16},{16,8},{9,17},{17,9},{10,18},{18,10},{11,19},{19,11},{12,20... | collective-permute-start | bytes 4915208 | tf_op jit(solution)/shard_map/ppermute | solution.py:85
  787.2 29.3 %collective-permute-start.36 = (bf16[256,1280]{1,0:T(8,128)(2,1)S(1)}, bf16[256,1280]{1,0:T(8,128)(2,1)S(1)}, u32[]{:S(2)}, u32[]{:S(2)}) collective-permute-start(bf16[256,1280]{1,0:T(8,128)(2,1)S(1)} %fusion.63), channel_id=1, source_target_pairs={{0,2},{1,3},{2,0},{3,1},{4,6},{5,7},{6,4},{7,5},{8,10},{9,11},{10,... | collective-permute-start | bytes 1966088 | tf_op jit(solution)/shard_map/ppermute | solution.py:52
  794.2 24.6 %collective-permute-start.44 = (bf16[256,1280]{1,0:T(8,128)(2,1)S(1)}, bf16[256,1280]{1,0:T(8,128)(2,1)S(1)}, u32[]{:S(2)}, u32[]{:S(2)}) collective-permute-start(bf16[256,1280]{1,0:T(8,128)(2,1)S(1)} %fusion.64), channel_id=1, source_target_pairs={{0,2},{1,3},{2,0},{3,1},{4,6},{5,7},{6,4},{7,5},{8,10},{9,11},{10,... | collective-permute-start | bytes 1966088 | tf_op jit(solution)/shard_map/ppermute | solution.py:52
  803.0 29.5 %collective-permute-start.52 = (bf16[256,1280]{1,0:T(8,128)(2,1)S(1)}, bf16[256,1280]{1,0:T(8,128)(2,1)S(1)}, u32[]{:S(2)}, u32[]{:S(2)}) collective-permute-start(bf16[256,1280]{1,0:T(8,128)(2,1)S(1)} %fusion.65), channel_id=1, source_target_pairs={{0,2},{1,3},{2,0},{3,1},{4,6},{5,7},{6,4},{7,5},{8,10},{9,11},{10,... | collective-permute-start | bytes 1966088 | tf_op jit(solution)/shard_map/ppermute | solution.py:52
  815.1 61.4 %collective-permute-start.65 = (bf16[160,1280]{1,0:T(8,128)(2,1)S(1)}, bf16[160,1280]{1,0:T(8,128)(2,1)S(1)}, u32[]{:S(2)}, u32[]{:S(2)}) collective-permute-start(bf16[160,1280]{1,0:T(8,128)(2,1)S(1)} %add_convert_fusion.15), channel_id=1, source_target_pairs={{8,0},{16,24},{9,1},{17,25},{10,2},{18,26},{11,3},{19,27},{12,4},{... | collective-permute-start | bytes 1228808 | tf_op jit(solution)/shard_map/ppermute | solution.py:87
  816.5 68.8 %collective-permute-start.74 = (bf16[160,1280]{1,0:T(8,128)(2,1)S(1)}, bf16[160,1280]{1,0:T(8,128)(2,1)S(1)}, u32[]{:S(2)}, u32[]{:S(2)}) collective-permute-start(bf16[160,1280]{1,0:T(8,128)(2,1)S(1)} %add_convert_fusion.9), channel_id=1, source_target_pairs={{8,0},{16,24},{9,1},{17,25},{10,2},{18,26},{11,3},{19,27},{12,4},{... | collective-permute-start | bytes 1228808 | tf_op jit(solution)/shard_map/ppermute | solution.py:87
  818.8 75.2 %collective-permute-start.71 = (bf16[160,1280]{1,0:T(8,128)(2,1)S(1)}, bf16[160,1280]{1,0:T(8,128)(2,1)S(1)}, u32[]{:S(2)}, u32[]{:S(2)}) collective-permute-start(bf16[160,1280]{1,0:T(8,128)(2,1)S(1)} %add_convert_fusion.11), channel_id=1, source_target_pairs={{8,0},{16,24},{9,1},{17,25},{10,2},{18,26},{11,3},{19,27},{12,4},{... | collective-permute-start | bytes 1228808 | tf_op jit(solution)/shard_map/ppermute | solution.py:87
  832.4 66.0 %collective-permute-start.68 = (bf16[160,1280]{1,0:T(8,128)(2,1)S(1)}, bf16[160,1280]{1,0:T(8,128)(2,1)S(1)}, u32[]{:S(2)}, u32[]{:S(2)}) collective-permute-start(bf16[160,1280]{1,0:T(8,128)(2,1)S(1)} %add_convert_fusion.13), channel_id=1, source_target_pairs={{8,0},{16,24},{9,1},{17,25},{10,2},{18,26},{11,3},{19,27},{12,4},{... | collective-permute-start | bytes 1228808 | tf_op jit(solution)/shard_map/ppermute | solution.py:87
  876.5 31.0 %collective-permute-start.79 = (bf16[640,1280]{0,1:T(8,128)(2,1)S(1)}, bf16[640,1280]{0,1:T(8,128)(2,1)S(1)}, u32[]{:S(2)}, u32[]{:S(2)}) collective-permute-start(bf16[640,1280]{0,1:T(8,128)(2,1)S(1)} %add_convert_fusion.3), channel_id=1, source_target_pairs={{8,16},{16,8},{9,17},{17,9},{10,18},{18,10},{11,19},{19,11},{12,20... | collective-permute-start | bytes 4915208 | tf_op jit(solution)/shard_map/ppermute | solution.py:85
  885.3 25.1 %collective-permute-start.76 = (bf16[640,1280]{0,1:T(8,128)(2,1)S(1)}, bf16[640,1280]{0,1:T(8,128)(2,1)S(1)}, u32[]{:S(2)}, u32[]{:S(2)}) collective-permute-start(bf16[640,1280]{0,1:T(8,128)(2,1)S(1)} %add_convert_fusion.5), channel_id=1, source_target_pairs={{8,16},{16,8},{9,17},{17,9},{10,18},{18,10},{11,19},{19,11},{12,20... | collective-permute-start | bytes 4915208 | tf_op jit(solution)/shard_map/ppermute | solution.py:85
  894.0 19.3 %collective-permute-start.53 = (f32[256,1280]{1,0:T(8,128)S(1)}, f32[256,1280]{1,0:T(8,128)}, u32[]{:S(2)}, u32[]{:S(2)}) collective-permute-start(f32[256,1280]{1,0:T(8,128)S(1)} %get-tuple-element.385), channel_id=1, source_target_pairs={{0,1},{1,0},{2,3},{3,2},{4,5},{5,4},{6,7},{7,6},{8,9},{9,8},{10,11... | collective-permute-start | bytes 3932168 | tf_op jit(solution)/shard_map/ppermute | solution.py:52
  898.4 18.2 %collective-permute-start.45 = (f32[256,1280]{1,0:T(8,128)S(1)}, f32[256,1280]{1,0:T(8,128)}, u32[]{:S(2)}, u32[]{:S(2)}) collective-permute-start(f32[256,1280]{1,0:T(8,128)S(1)} %get-tuple-element.384), channel_id=1, source_target_pairs={{0,1},{1,0},{2,3},{3,2},{4,5},{5,4},{6,7},{7,6},{8,9},{9,8},{10,11... | collective-permute-start | bytes 3932168 | tf_op jit(solution)/shard_map/ppermute | solution.py:52
  907.5 47.2 %collective-permute-start.83 = (bf16[640,1280]{0,1:T(8,128)(2,1)S(1)}, bf16[640,1280]{0,1:T(8,128)(2,1)S(1)}, u32[]{:S(2)}, u32[]{:S(2)}) collective-permute-start(bf16[640,1280]{0,1:T(8,128)(2,1)S(1)} %add_convert_fusion), channel_id=1, source_target_pairs={{8,0},{16,24},{9,1},{17,25},{10,2},{18,26},{11,3},{19,27},{12,4},{... | collective-permute-start | bytes 4915208 | tf_op jit(solution)/shard_map/ppermute | solution.py:87
  910.4 79.5 %collective-permute-start.80 = (bf16[640,1280]{0,1:T(8,128)(2,1)}, bf16[640,1280]{0,1:T(8,128)(2,1)}, u32[]{:S(2)}, u32[]{:S(2)}) collective-permute-start(bf16[640,1280]{0,1:T(8,128)(2,1)} %add_convert_fusion.2), channel_id=1, source_target_pairs={{8,0},{16,24},{9,1},{17,25},{10,2},{18,26},{11,3},{19,27},{12,4},{... | collective-permute-start | bytes 4915208 | tf_op jit(solution)/shard_map/ppermute | solution.py:87
  913.3 104.1 %collective-permute-start.77 = (bf16[640,1280]{0,1:T(8,128)(2,1)}, bf16[640,1280]{0,1:T(8,128)(2,1)}, u32[]{:S(2)}, u32[]{:S(2)}) collective-permute-start(bf16[640,1280]{0,1:T(8,128)(2,1)} %add_convert_fusion.4), channel_id=1, source_target_pairs={{8,0},{16,24},{9,1},{17,25},{10,2},{18,26},{11,3},{19,27},{12,4},{... | collective-permute-start | bytes 4915208 | tf_op jit(solution)/shard_map/ppermute | solution.py:87
  (242 other events, 3402.6 us)

commit v2 on v1

--- a/solution.py
+++ b/solution.py
@@ -76,8 +76,6 @@
 
 def group_sum(values):
     dtype = values.dtype
-    here = lax.axis_index("group")
-    last = lax.axis_size("group") - 1
     pair = lax.optimization_barrier(
         add_low(values, lax.ppermute(values, "group", [(0, 1), (3, 2)])).astype(dtype)
     )
@@ -85,7 +83,7 @@
         add_low(pair, lax.ppermute(pair, "group", [(1, 2), (2, 1)])).astype(dtype)
     )
     back = lax.ppermute(whole, "group", [(1, 0), (2, 3)])
-    return jnp.where((here == 0) | (here == last), back, whole).astype(F32)
+    return (whole, back)
 
 
 def mask_bias(seg_q, place_q, seg_k, place_k):
@@ -221,6 +219,128 @@
     if is_matrix:
         result = unit_only(result)
     return (momentum, result)
+
+
+def row_tile(rows):
+    for size in (160, 128):
+        if rows % size == 0:
+            return size
+    return rows
+
+
+def adam_kernel(has_partner, offset, own, partner, master, first, second, *rest):
+    del offset
+    gradient_out, moment_out, variance_out, shift_out = rest[-4:]
+    gradient = own[...]
+    if has_partner:
+        gradient = gradient + partner[...].astype(F32)
+    moment, variance, updated = adam_step(
+        master[0], gradient, first[0, 0], second[0, 0], MATRIX_RATE, True
+    )
+    gradient_out[0, 0] = gradient
+    moment_out[0, 0] = moment
+    variance_out[0, 0] = variance
+    shift_out[...] = (master[0] - updated).astype(LOW)
+
+
+def adam_slab(which, own_block, gradient, partner, master, first, second, earlier):
+    slabs, rows, width = master.shape
+    tile = row_tile(rows)
+    steps = rows // tile
+    has_partner = partner is not None
+    if not has_partner:
+        partner = jnp.zeros((tile, width), LOW)
+    flat = pl.BlockSpec((tile, width), lambda i, at: (i, 0))
+    held = pl.BlockSpec((tile, width), lambda i, at: (at[0] * steps + i, 0))
+    once = pl.BlockSpec((tile, width), lambda i, at: (0, 0))
+    slab = pl.BlockSpec((1, tile, width), lambda i, at: (which, i, 0))
+    grouped = pl.BlockSpec((1, 1, tile, width), lambda i, at: (0, which, i, 0))
+    whole = jax.ShapeDtypeStruct((1, slabs, rows, width), F32)
+    earlier = () if earlier is None else earlier
+    return pl.pallas_call(
+        partial(adam_kernel, has_partner),
+        grid_spec=pltpu.PrefetchScalarGridSpec(
+            num_scalar_prefetch=1,
+            grid=(steps,),
+            in_specs=[held, flat if has_partner else once, slab, grouped, grouped]
+            + [pl.BlockSpec(memory_space=pl.ANY)] * len(earlier),
+            out_specs=[grouped, grouped, grouped, flat],
+        ),
+        out_shape=[whole, whole, whole, jax.ShapeDtypeStruct((rows, width), LOW)],
+        input_output_aliases={6 + n: n for n in range(len(earlier))},
+        compiler_params=pltpu.CompilerParams(vmem_limit_bytes=VMEM_BYTES),
+        cost_estimate=pl.CostEstimate(
+            flops=30 * rows * width, bytes_accessed=32 * rows * width, transcendentals=rows * width
+        ),
+    )(own_block, gradient, partner, master, first, second, *earlier)
+
+
+def outer_kernel(group_count, at_end, whole, back, master, outer, *rest):
+    momentum_out, result_out = rest[-2:]
+    shift = jnp.where(at_end[0] == 1, back[...].astype(F32), whole[...].astype(F32)) / group_count
+    momentum, result = outer_step(master[0], shift, outer[0], True)
+    momentum_out[0] = momentum
+    result_out[0] = result
+
+
+def outer_slab(which, group_count, at_end, whole, back, master, outer, earlier):
+    slabs, rows, width = master.shape
+    tile = row_tile(rows)
+    flat = pl.BlockSpec((tile, width), lambda i, at: (i, 0))
+    slab = pl.BlockSpec((1, tile, width), lambda i, at: (which, i, 0))
+    result = jax.ShapeDtypeStruct((slabs, rows, width), F32)
+    earlier = () if earlier is None else earlier
+    return pl.pallas_call(
+        partial(outer_kernel, group_count),
+        grid_spec=pltpu.PrefetchScalarGridSpec(
+            num_scalar_prefetch=1,
+            grid=(rows // tile,),
+            in_specs=[flat, flat, slab, slab]
+            + [pl.BlockSpec(memory_space=pl.ANY)] * len(earlier),
+            out_specs=[slab, slab],
+        ),
+        out_shape=[result, result],
+        input_output_aliases={5 + n: n for n in range(len(earlier))},
+        compiler_params=pltpu.CompilerParams(vmem_limit_bytes=VMEM_BYTES),
+        cost_estimate=pl.CostEstimate(
+            flops=20 * rows * width, bytes_accessed=20 * rows * width, transcendentals=rows
+        ),
+    )(at_end, whole, back, master, outer, *earlier)
+
+
+def place_kernel(core, own, other, *rest):
+    out = rest[-1]
+
+    @pl.when(pl.program_id(0) == 0)
+    def _():
+        out[0, 0] = own[...]
+
+    @pl.when(pl.program_id(0) == 1)
+    def _():
+        out[0, 0] = other[...]
+
+
+def place_rows(which, count, core, own, other, earlier):
+    half, width = own.shape
+    held = pl.BlockSpec((half, width), lambda i, at: (0, 0))
+    earlier = () if earlier is None else (earlier,)
+    return pl.pallas_call(
+        place_kernel,
+        grid_spec=pltpu.PrefetchScalarGridSpec(
+            num_scalar_prefetch=1,
+            grid=(2,),
+            in_specs=[held, held] + [pl.BlockSpec(memory_space=pl.ANY)] * len(earlier),
+            out_specs=pl.BlockSpec(
+                (1, 1, half, width), lambda i, at: (0, which, lax.rem(at[0] + i, 2), 0)
+            ),
+        ),
+        out_shape=jax.ShapeDtypeStruct((1, count, 2 * half, width), F32),
+        input_output_aliases={3: 0} if earlier else {},
+        compiler_params=pltpu.CompilerParams(vmem_limit_bytes=VMEM_BYTES),
+        cost_estimate=pl.CostEstimate(
+            flops=0, bytes_accessed=16 * half * width, transcendentals=0
+        ),
+    )(core, own, other, *earlier)
 
 
 def on_device(
@@ -263,7 +383,8 @@
     root_width = math.sqrt(model_width)
     me = lax.axis_index("ctx")
     ctx_first = me == 0
-    core_first = lax.rem(lax.axis_index("tensor"), 2) == 0
+    core_index = lax.rem(lax.axis_index("tensor"), 2).reshape(1)
+    core_first = core_index[0] == 0
     even_group = lax.rem(lax.axis_index("group"), 2) == 0
     micros = range(micro_count)
 
@@ -414,7 +535,8 @@
         )
 
     ups, gates, hidden_rows = [], [], []
-    output_pieces, second_backs, feed_back_rows = [], [], []
+    second_backs, feed_back_rows = [], []
+    block_output = None
     feed_rate_term = jnp.zeros((model_width,), F32)
     for b in micros:
         up = dot(normed_rows[b], up_weights, (1, 1))
@@ -433,7 +555,9 @@
         feed_back = split_low(unit_back(feed_unit, feed_norm, second_back * rate_feed))
         second_backs.append(second_back)
         feed_back_rows.append(jnp.concatenate([feed_back, trade(feed_back, "tensor", 1)], axis=0))
-        output_pieces.append(ordered(core_first, output, trade(output, "tensor", 1), 0))
+        block_output = place_rows(
+            b, micro_count, core_index, output, trade(output, "tensor", 1), block_output
+        )
 
     up_back_rows, gate_back_rows = [], []
     first_backs, attention_back_rows = [], []
@@ -476,35 +600,36 @@
             jnp.concatenate([attention_back, trade(attention_back, "tensor", 1)], axis=0)
         )
 
-    def to_owner(gradient):
+    def to_owner(gradient, in_order):
         if not pair:
-            return lax.psum_scatter(gradient, "ctx", scatter_dimension=0, tiled=True)
+            summed_rows = lax.psum_scatter(gradient, "ctx", scatter_dimension=0, tiled=True)
+            return (summed_rows, None, jnp.zeros((1,), jnp.int32))
         size = gradient.shape[0] // 2
-        return gradient[:size] + trade(gradient[size:].astype(LOW), "ctx", 1).astype(F32)
-
-    def to_owner_ordered(gradient):
-        if not pair:
-            return lax.psum_scatter(gradient, "ctx", scatter_dimension=0, tiled=True)
-        size = gradient.shape[0] // 2
-        own = jnp.where(ctx_first, gradient[:size], gradient[size:])
-        other = jnp.where(ctx_first, gradient[size:], gradient[:size])
-        return own + trade(other.astype(LOW), "ctx", 1).astype(F32)
+        other = gradient[size:]
+        block = jnp.zeros((1,), jnp.int32)
+        if in_order:
+            other = jnp.where(ctx_first, gradient[size:], gradient[:size])
+            block = me.reshape(1)
+        return (gradient, trade(other.astype(LOW), "ctx", 1), block)
 
     normed_all = jnp.concatenate(normed_rows, axis=0)
     down_grad = to_owner(
         dot(
             jnp.concatenate(hidden_rows, axis=0), jnp.concatenate(feed_back_rows, axis=0), (0, 0)
-        )
-    )
-    up_grad = to_owner(dot(jnp.concatenate(up_back_rows, axis=0), normed_all, (0, 0)))
-    gate_grad = to_owner(dot(jnp.concatenate(gate_back_rows, axis=0), normed_all, (0, 0)))
-    output_grad = to_owner_ordered(
+        ),
+        False,
+    )
+    up_grad = to_owner(dot(jnp.concatenate(up_back_rows, axis=0), normed_all, (0, 0)), False)
+    gate_grad = to_owner(dot(jnp.concatenate(gate_back_rows, axis=0), normed_all, (0, 0)), False)
+    output_grad = to_owner(
         dot(
             jnp.concatenate(heads_lows, axis=1), jnp.concatenate(attention_back_rows, axis=0), (1, 0)
-        )
-    )
-
-    input_pieces, triples = [], []
+        ),
+        True,
+    )
+
+    triples = []
+    input_gradient = None
     head_terms = jnp.zeros((head_count, HEAD_DIM), F32)
     for b in micros:
         heads_back = dot(output_weights, attention_back_rows[b], (1, 1), LOW)
@@ -538,14 +663,16 @@
         other_part = dot(triple[:, half:], triple_weights, (0, 0), LOW)
         own_part = dot(triple[:, :half], triple_weights, (0, 0))
         input_own = first_backs[b] * (1.0 - rate_attention) + tensor_sum(own_part, other_part)
-        input_pieces.append(ordered(core_first, input_own, trade(input_own, "tensor", 1), 0))
+        input_gradient = place_rows(
+            b, micro_count, core_index, input_own, trade(input_own, "tensor", 1), input_gradient
+        )
 
     triple_grad = dot(
         jnp.concatenate(triples, axis=1),
         token_rows.reshape(micro_count * rows, model_width),
         (1, 0),
     ).reshape(3, head_width, model_width)
-    attention_grads = [to_owner_ordered(triple_grad[which]) for which in range(3)] + [output_grad]
+    attention_grads = [to_owner(triple_grad[which], True) for which in range(3)] + [output_grad]
     feed_grads = [up_grad, gate_grad, down_grad]
 
     rate_terms = jnp.concatenate([attention_rate_term, feed_rate_term])
@@ -572,32 +699,27 @@
         hidden_grad = lax.psum_scatter(hidden_terms, "ctx", scatter_dimension=1, tiled=True)
         rates_grad = lax.psum_scatter(rate_terms, "ctx", scatter_dimension=1, tiled=True)
 
-    def matrix_steps(gradients, masters, firsts, seconds, outers):
-        moments, variances, momenta, results = [], [], [], []
-        for which, gradient in enumerate(gradients):
-            master = masters[which]
-            moment, variance, updated = adam_step(
-                master, gradient, firsts[0, which], seconds[0, which], MATRIX_RATE, True
+    at_end = lax.axis_index("group")
+    at_end = ((at_end == 0) | (at_end == group_count - 1)).astype(jnp.int32)
+
+    def matrix_steps(order, gradients, masters, firsts, seconds, outers):
+        adam_outs, outer_outs = None, None
+        for which in order:
+            gradient, partner, block = gradients[which]
+            *adam_outs, shift = adam_slab(
+                which, block, gradient, partner, masters, firsts, seconds, adam_outs
             )
-            shift = group_sum(split_low(master - updated)) / group_count
-            momentum, result = outer_step(master, shift, outers[which], True)
-            moments.append(moment)
-            variances.append(variance)
-            momenta.append(momentum)
-            results.append(result)
-        return (
-            jnp.stack(gradients)[None],
-            jnp.stack(moments)[None],
-            jnp.stack(variances)[None],
-            jnp.stack(momenta),
-            jnp.stack(results),
-        )
+            whole, back = group_sum(shift)
+            outer_outs = outer_slab(
+                which, group_count, at_end.reshape(1), whole, back, masters, outers, outer_outs
+            )
+        return (*adam_outs, *outer_outs)
 
     feed_outs = matrix_steps(
-        feed_grads, feedforward_weights, feedforward_first, feedforward_second, feedforward_outer
+        (2, 0, 1), feed_grads, feedforward_weights, feedforward_first, feedforward_second, feedforward_outer
     )
     attention_outs = matrix_steps(
-        attention_grads, attention_weights, attention_first, attention_second, attention_outer
+        (3, 0, 1, 2), attention_grads, attention_weights, attention_first, attention_second, attention_outer
     )
 
     masters = (head_scales, hidden_scales, residual_rates)
@@ -618,7 +740,8 @@
         small_moments.append(moment)
         small_variances.append(variance)
         small_shifts.append((masters[which] - updated).reshape(-1))
-    shift_flat = group_sum(jnp.concatenate(small_shifts)) / group_count
+    whole, back = group_sum(jnp.concatenate(small_shifts))
+    shift_flat = jnp.where(at_end == 1, back, whole) / group_count
     small_momenta, small_results = [], []
     start = 0
     for which in range(3):
@@ -630,8 +753,8 @@
         small_results.append(result)
 
     return (
-        jnp.stack(output_pieces)[None],
-        jnp.stack(input_pieces)[None],
+        block_output,
+        input_gradient,
         attention_outs[0],
         feed_outs[0],
         *[entry[None] for entry in small_grads],

time: 1070 us -> 863 us (0.81)
  local copies, waits for them, and re-layouts: 185 us -> 67.6 us
  other arithmetic: 198 us -> 81.9 us
  Pallas kernels: 33.1 us -> 116 us
  waiting for transfers between devices: 422 us -> 391 us
  matrix products: 129 us -> 115 us
    unnamed x473 -> x556, local copies, waits for them, and re-layouts: 146 us -> 54.7 us
    pallas_call x0 -> x20, Pallas kernels: none -> 83 us  [the longest x7 40.6 us: adam_slab(): pl.pallas_call(partial(adam_kernel, has_partner), grid_spec=pltpu.Prefetc...]
    reduce_sum x9 -> x0, other arithmetic: 44.5 us -> none  [unit_only(): jnp.sum(values * values, axis=-1, keepdims=True) + EPSILON]
    broadcast_in_dim x8 -> x0, other arithmetic: 35.9 us -> none  [the longest x2 10.4 us: matrix_steps(): jnp.stack(variances)[None]]
    slice x7 -> x5, local copies, waits for them, and re-layouts: 32.7 us -> 6.36 us  [the longest x3 3.98 us: to_owner(): other = gradient[size:]]
    ppermute x8, waiting for transfers between devices: 154 us -> 130 us  [group_sum(): back = lax.ppermute(whole, 'group', [(1, 0), (2, 3)])]
    ppermute x63, waiting for transfers between devices: 249 us -> 233 us  [trade(): return lax.ppermute(values, axis, [(i, i ^ bit) for i in range(count)])]
    dot_general x50, matrix products: 129 us -> 115 us  [dot(): lax.dot_general(left, right, (((contract[0],), (contract[1],)), ((), ()))...]
  transfers between devices with their start and end apart: 87 -> 87, of which waited for: 37 -> 36; matrix products, arithmetic and copies ran while one was open for 39% -> 17% of each run, Pallas kernels for 3% -> 13%
where the time goes in v2:
time: 863 us; the launch traced here: 858 us
  waiting for transfers between devices  391 us (45%)
  Pallas kernels  116 us (13%)
  matrix products  115 us (13%)
  other arithmetic  81.9 us (9%)
  starting transfers between devices  81.2 us (9%)
  local copies, waits for them, and re-layouts  67.6 us (8%)
    ppermute x63, waiting for transfers between devices, trade(): return lax.ppermute(values, axis, [(i, i ^ bit) for i in range(count)])  233 us
    ppermute x8, waiting for transfers between devices, group_sum(): back = lax.ppermute(whole, 'group', [(1, 0), (2, 3)])  130 us
    dot_general x50, matrix products, dot(): lax.dot_general(left, right, (((contract[0],), (contract[1],)), ((), ()))...  115 us
    unnamed x556, local copies, waits for them, and re-layouts  54.7 us
    ppermute x63, starting transfers between devices, trade(): return lax.ppermute(values, axis, [(i, i ^ bit) for i in range(count)])  44.1 us
    pallas_call x7, Pallas kernels, adam_slab(): pl.pallas_call(partial(adam_kernel, has_partner), grid_spec=pltpu.Prefetc...  40.6 us
    ppermute x8, waiting for transfers between devices, group_sum(): lax.ppermute(values, 'group', [(0, 1), (3, 2)])  28.5 us
    pallas_call x7, Pallas kernels, outer_slab(): pl.pallas_call(partial(outer_kernel, group_count), grid_spec=pltpu.Prefet...  26.9 us
  transfers between devices with their start and end apart: 87, of which 36 were waited for; matrix products, arithmetic and copies ran while one was open for 17% of the time, Pallas kernels for 13%

profile of v2, /device:TPU:0, one launch (start us, length us, event | category | flops | bytes accessed | tf_op | source)
XLA Modules:
  0.0 857.9 jit_solution(10248953348885100647)
XLA Ops:
  2.9 2.9 collective-permute-start
  22.4 6.7 convert_element_type.512
  29.9 6.8 collective-permute-done.1
  51.5 13.6 %collective-permute-done.2 = bf16[640,512]{1,0:T(8,128)(2,1)S(1)} collective-permute-done((bf16[640,512]{1,0:T(8,128)(2,1)S(1)}, bf16[640,512]{1,0:T(8,128)(2,1)S(1)}, u32[]{:S(2)}, u32[]{:S(2)}) %collective-permute-start.2) | collective-permute-done | bytes 655392 | tf_op jit(solution)/shard_map/ppermute | solution.py:52
  67.9 25.2 %collective-permute-done.16 = bf16[640,512]{1,0:T(8,128)(2,1)S(1)} collective-permute-done((bf16[640,512]{1,0:T(8,128)(2,1)S(1)}, bf16[640,512]{1,0:T(8,128)(2,1)S(1)}, u32[]{:S(2)}, u32[]{:S(2)}) %collective-permute-start.16) | collective-permute-done | bytes 655392 | tf_op jit(solution)/shard_map/ppermute | solution.py:52
  93.6 3.3 shard_map.439
  97.8 3.3 shard_map.440
  102.1 3.8 shard_map.441
  108.4 11.1 %collective-permute-done.11 = bf16[320,1280]{1,0:T(8,128)(2,1)S(1)} collective-permute-done((bf16[320,1280]{1,0:T(8,128)(2,1)S(1)}, bf16[320,1280]{1,0:T(8,128)(2,1)S(1)}, u32[]{:S(2)}, u32[]{:S(2)}) %collective-permute-start.11) | collective-permute-done | bytes 819232 | tf_op jit(solution)/shard_map/ppermute | solution.py:52
  119.5 17.6 %collective-permute-done.9 = bf16[320,1280]{1,0:T(8,128)(2,1)S(1)} collective-permute-done((bf16[320,1280]{1,0:T(8,128)(2,1)S(1)}, bf16[320,1280]{1,0:T(8,128)(2,1)S(1)}, u32[]{:S(2)}, u32[]{:S(2)}) %collective-permute-start.9) | collective-permute-done | bytes 819232 | tf_op jit(solution)/shard_map/ppermute | solution.py:52
  139.0 13.2 %collective-permute-done.7 = bf16[320,1280]{1,0:T(8,128)(2,1)S(1)} collective-permute-done((bf16[320,1280]{1,0:T(8,128)(2,1)S(1)}, bf16[320,1280]{1,0:T(8,128)(2,1)S(1)}, u32[]{:S(2)}, u32[]{:S(2)}) %collective-permute-start.7) | collective-permute-done | bytes 819232 | tf_op jit(solution)/shard_map/ppermute | solution.py:52
  160.4 13.0 %collective-permute-done.10 = bf16[320,1280]{1,0:T(8,128)(2,1)S(1)} collective-permute-done((bf16[320,1280]{1,0:T(8,128)(2,1)S(1)}, bf16[320,1280]{1,0:T(8,128)(2,1)S(1)}, u32[]{:S(2)}, u32[]{:S(2)}) %collective-permute-start.10) | collective-permute-done | bytes 819232 | tf_op jit(solution)/shard_map/ppermute | solution.py:52
  174.1 13.6 %collective-permute-done.8 = bf16[320,1280]{1,0:T(8,128)(2,1)S(1)} collective-permute-done((bf16[320,1280]{1,0:T(8,128)(2,1)S(1)}, bf16[320,1280]{1,0:T(8,128)(2,1)S(1)}, u32[]{:S(2)}, u32[]{:S(2)}) %collective-permute-start.8) | collective-permute-done | bytes 819232 | tf_op jit(solution)/shard_map/ppermute | solution.py:52
  189.0 7.8 collective-permute-done.5
  204.0 3.6 fusion.125
  207.6 3.4 fusion.124
  211.0 3.4 fusion.126
  214.4 3.4 fusion.128
  217.8 9.1 %multiply_convert_fusion.8 = (bf16[512,1280]{1,0:T(8,128)(2,1)S(1)}, bf16[512,1280]{1,0:T(8,128)(2,1)}, bf16[512,1280]{1,0:T(8,128)(2,1)}, f32[512,1280]{1,0:T(8,128)}) fusion(f32[512,1280]{1,0:T(8,128)} %fusion.128, f32[1280]{0:T(1024)S(1)} %get-tuple-element.333, f32[1280]{0:T(1024)S(1)} %get-tuple-element.332, f32[512,1280]{1,0:T(8,128)} %fusion.125, ...), kind=kOutput, calls=%fused_computation.101 | convolution fusion | flops 1704591360 | bytes 24258560 | tf_op jit(solution)/shard_map/dot_general | solution.py:45
  240.2 11.7 %collective-permute-done.28 = bf16[256,1280]{1,0:T(8,128)(2,1)S(1)} collective-permute-done((bf16[256,1280]{1,0:T(8,128)(2,1)S(1)}, bf16[256,1280]{1,0:T(8,128)(2,1)S(1)}, u32[]{:S(2)}, u32[]{:S(2)}) %collective-permute-start.28) | collective-permute-done | bytes 655392 | tf_op jit(solution)/shard_map/ppermute | solution.py:52
  252.2 13.8 %collective-permute-done.21 = bf16[256,1280]{1,0:T(8,128)(2,1)S(1)} collective-permute-done((bf16[256,1280]{1,0:T(8,128)(2,1)S(1)}, bf16[256,1280]{1,0:T(8,128)(2,1)S(1)}, u32[]{:S(2)}, u32[]{:S(2)}) %collective-permute-start.21) | collective-permute-done | bytes 655392 | tf_op jit(solution)/shard_map/ppermute | solution.py:52
  266.3 12.9 %collective-permute-done.14 = bf16[256,1280]{1,0:T(8,128)(2,1)S(1)} collective-permute-done((bf16[256,1280]{1,0:T(8,128)(2,1)S(1)}, bf16[256,1280]{1,0:T(8,128)(2,1)S(1)}, u32[]{:S(2)}, u32[]{:S(2)}) %collective-permute-start.14) | collective-permute-done | bytes 655392 | tf_op jit(solution)/shard_map/ppermute | solution.py:52
  290.0 3.4 fusion.83
  293.4 3.4 fusion.91
  296.8 14.3 %multiply_reduce_fusion = (f32[1280]{0:T(1024)S(1)}, f32[1280]{0:T(1024)S(1)}, f32[512,1280]{1,0:T(8,128)S(1)}, bf16[512,1280]{1,0:T(8,128)(2,1)}, bf16[512,1280...) fusion(f32[512,1280]{1,0:T(8,128)} %fusion.128, ...), kind=kOutput, calls=%fused_computation.77 | convolution fusion | flops 1728176640 | bytes 37396480 | tf_op jit(solution)/shard_map/dot_general | solution.py:45
  311.1 4.2 multiply_convert_fusion.4
  327.1 7.8 fusion.18.own
  348.8 5.5 fusion.6.own
  367.3 5.7 fusion.12.own
  380.5 13.0 %collective-permute-done.40 = bf16[256,1280]{1,0:T(8,128)(2,1)S(1)} collective-permute-done((bf16[256,1280]{1,0:T(8,128)(2,1)S(1)}, bf16[256,1280]{1,0:T(8,128)(2,1)S(1)}, u32[]{:S(2)}, u32[]{:S(2)}) %collective-permute-start.40) | collective-permute-done | bytes 655392 | tf_op jit(solution)/shard_map/ppermute | solution.py:52
  393.5 13.4 %collective-permute-done.48 = bf16[256,1280]{1,0:T(8,128)(2,1)S(1)} collective-permute-done((bf16[256,1280]{1,0:T(8,128)(2,1)S(1)}, bf16[256,1280]{1,0:T(8,128)(2,1)S(1)}, u32[]{:S(2)}, u32[]{:S(2)}) %collective-permute-start.48) | collective-permute-done | bytes 655392 | tf_op jit(solution)/shard_map/ppermute | solution.py:52
  409.6 3.3 multiply_reduce_fusion.9
  418.4 2.9 copy-done.16
  421.2 10.2 %shard_map.455 = (f32[1,3,640,1280]{3,2,1,0:T(8,128)}, f32[1,3,640,1280]{3,2,1,0:T(8,128)}, f32[1,3,640,1280]{3,2,1,0:T(8,128)}, bf16[640,1280]{1,0:T(8,128)(2,1)S(1)}) custom-call(s32[1]{0:T(128)} %constant.18.clone.1.offset, f32[1280,1280]{1,0:T(8,128)S(1)} %copy-done.16, bf16[640,1280]{1,0:T(8,128)(2,1)S(1)} %collective-permute-done.60.partner, ...), custom_call_target="tpu_custom_call" | custom-call | flops 24576000 | bytes 26214400 | tf_op jit(solution)/shard_map/pallas_call | solution.py:260
  432.6 11.0 %shard_map.456 = (f32[1,3,640,1280]{3,2,1,0:T(8,128)}, f32[1,3,640,1280]{3,2,1,0:T(8,128)}, f32[1,3,640,1280]{3,2,1,0:T(8,128)}, bf16[640,1280]{1,0:T(8,128)(2,1)}) custom-call(s32[1]{0:T(128)} %constant.18.clone.1.offset, f32[1280,1280]{1,0:T(8,128)S(1)} %copy-done.19, ...), custom_call_target="tpu_custom_call", output_to_operand_aliasing={{0}: (6, {}), {1}: (7, {}), {2}: (8, {})} | custom-call | flops 24576000 | bytes 26214400 | tf_op jit(solution)/shard_map/pallas_call | solution.py:260
  443.7 6.1 collective-permute-done.58.partner
  449.8 10.1 %shard_map.457 = (f32[1,3,640,1280]{3,2,1,0:T(8,128)}, f32[1,3,640,1280]{3,2,1,0:T(8,128)}, f32[1,3,640,1280]{3,2,1,0:T(8,128)}, bf16[640,1280]{1,0:T(8,128)(2,1)}) custom-call(s32[1]{0:T(128)} %constant.18.clone.1.offset, f32[1280,1280]{1,0:T(8,128)S(1)} %bitcast.292, ...), custom_call_target="tpu_custom_call", output_to_operand_aliasing={{0}: (6, {}), {1}: (7, {}), {2}: (8, {})} | custom-call | flops 24576000 | bytes 26214400 | tf_op jit(solution)/shard_map/pallas_call | solution.py:260
  459.9 5.3 collective-permute-start.75
  467.1 7.5 shard_map.446
  478.2 7.7 shard_map.447
  493.6 7.6 shard_map.445
  504.5 10.7 %collective-permute-done.57.partner = bf16[160,1280]{1,0:T(8,128)(2,1)S(1)} collective-permute-done((bf16[160,1280]{1,0:T(8,128)(2,1)}, bf16[160,1280]{1,0:T(8,128)(2,1)S(1)}, u32[]{:S(2)}, u32[]{:S(2)}) %collective-permute-start.57) | collective-permute-done | bytes 409632 | tf_op jit(solution)/shard_map/ppermute | solution.py:52
  538.1 4.0 fusion.24
  548.3 3.6 convolution_convert_fusion.2
  555.6 2.8 convolution_convert_fusion.1
  563.2 7.7 collective-permute-done.56.partner
  576.7 2.9 collective-permute-done.55.partner
  593.4 23.7 %collective-permute-done.81 = bf16[640,1280]{1,0:T(8,128)(2,1)S(1)} collective-permute-done((bf16[640,1280]{1,0:T(8,128)(2,1)S(1)}, bf16[640,1280]{1,0:T(8,128)(2,1)S(1)}, u32[]{:S(2)}, u32[]{:S(2)}) %collective-permute-start.81) | collective-permute-done | bytes 1638432 | tf_op jit(solution)/shard_map/ppermute | solution.py:80
  617.2 4.5 collective-permute-start.66
  631.1 3.8 collective-permute-done.69
  639.7 7.0 collective-permute-done.44
  646.7 7.0 collective-permute-done.36
  664.4 35.0 %collective-permute-done.86 = f32[2720]{0:T(1024)S(1)} collective-permute-done((f32[2720]{0:T(1024)S(1)}, f32[2720]{0:T(1024)S(1)}, u32[]{:S(2)}, u32[]{:S(2)}) %collective-permute-start.86) | collective-permute-done | bytes 10912 | tf_op jit(solution)/shard_map/ppermute | solution.py:85
  700.7 8.6 %collective-permute-done.74.back = bf16[160,1280]{1,0:T(8,128)(2,1)S(1)} collective-permute-done((bf16[160,1280]{1,0:T(8,128)(2,1)S(1)}, bf16[160,1280]{1,0:T(8,128)(2,1)S(1)}, u32[]{:S(2)}, u32[]{:S(2)}) %collective-permute-start.74) | collective-permute-done | bytes 409632 | tf_op jit(solution)/shard_map/ppermute | solution.py:85
  710.6 7.0 collective-permute-done.65.back
  721.8 15.3 %collective-permute-done.68.back = bf16[160,1280]{1,0:T(8,128)(2,1)S(1)} collective-permute-done((bf16[160,1280]{1,0:T(8,128)(2,1)S(1)}, bf16[160,1280]{1,0:T(8,128)(2,1)S(1)}, u32[]{:S(2)}, u32[]{:S(2)}) %collective-permute-start.68) | collective-permute-done | bytes 409632 | tf_op jit(solution)/shard_map/ppermute | solution.py:85
  763.7 3.3 shard_map.448.rest_0_
  767.0 3.5 shard_map.449.rest_0_
  770.5 4.0 shard_map.450
  774.6 41.7 %collective-permute-done.83.back = bf16[640,1280]{1,0:T(8,128)(2,1)} collective-permute-done((bf16[640,1280]{1,0:T(8,128)(2,1)}, bf16[640,1280]{1,0:T(8,128)(2,1)}, u32[]{:S(2)}, u32[]{:S(2)}) %collective-permute-start.83) | collective-permute-done | bytes 1638432 | tf_op jit(solution)/shard_map/ppermute | solution.py:85
  816.3 6.5 shard_map.462
  822.8 6.5 shard_map.463
  829.4 21.8 %collective-permute-done.77.back = bf16[640,1280]{1,0:T(8,128)(2,1)} collective-permute-done((bf16[640,1280]{1,0:T(8,128)(2,1)}, bf16[640,1280]{1,0:T(8,128)(2,1)}, u32[]{:S(2)}, u32[]{:S(2)}) %collective-permute-start.77) | collective-permute-done | bytes 1638432 | tf_op jit(solution)/shard_map/ppermute | solution.py:85
  851.2 6.5 shard_map.464
  (932 shorter events, 269.6 us)
Async XLA Ops:
  2.9 26.2 %collective-permute-start = (bf16[2720]{0:T(1024)(128)(2,1)S(1)}, bf16[2720]{0:T(1024)(128)(2,1)S(1)}, u32[]{:S(2)}, u32[]{:S(2)}) collective-permute-start(bf16[2720]{0:T(1024)(128)(2,1)S(1)} %concatenate.191), channel_id=1, source_target_pairs={{0,4},{4,0},{1,5},{5,1},{2,6},{6,2},{3,7},{7,3},{8,12},{12,8},{9,1... | collective-permute-start | bytes 16328 | tf_op jit(solution)/shard_map/ppermute | solution.py:52
  8.0 28.7 %collective-permute-start.1 = (bf16[3,160,1280]{2,1,0:T(8,128)(2,1)S(1)}, bf16[3,160,1280]{2,1,0:T(8,128)(2,1)}, u32[]{:S(2)}, u32[]{:S(2)}) collective-permute-start(bf16[3,160,1280]{2,1,0:T(8,128)(2,1)S(1)} %slice.534), channel_id=1, source_target_pairs={{0,4},{4,0},{1,5},{5,1},{2,6},{6,2},{3,7},{7,3},{8,12},{12,8},{9,1... | collective-permute-start | bytes 3686408 | tf_op jit(solution)/shard_map/ppermute | solution.py:52
  47.4 17.7 %collective-permute-start.2 = (bf16[640,512]{1,0:T(8,128)(2,1)S(1)}, bf16[640,512]{1,0:T(8,128)(2,1)S(1)}, u32[]{:S(2)}, u32[]{:S(2)}) collective-permute-start(bf16[640,512]{1,0:T(8,128)(2,1)S(1)} %get-tuple-element.279), channel_id=1, source_target_pairs={{0,4},{4,0},{1,5},{5,1},{2,6},{6,2},{3,7},{7,3},{8,12},{12,8},{9,1... | collective-permute-start | bytes 1966088 | tf_op jit(solution)/shard_map/ppermute | solution.py:52
  49.4 52.6 %collective-permute-start.23 = (bf16[640,512]{1,0:T(8,128)(2,1)S(1)}, bf16[640,512]{1,0:T(8,128)(2,1)S(1)}, u32[]{:S(2)}, u32[]{:S(2)}) collective-permute-start(bf16[640,512]{1,0:T(8,128)(2,1)S(1)} %get-tuple-element.281), channel_id=1, source_target_pairs={{0,4},{4,0},{1,5},{5,1},{2,6},{6,2},{3,7},{7,3},{8,12},{12,8},{9,1... | collective-permute-start | bytes 1966088 | tf_op jit(solution)/shard_map/ppermute | solution.py:52
  51.2 42.0 %collective-permute-start.16 = (bf16[640,512]{1,0:T(8,128)(2,1)S(1)}, bf16[640,512]{1,0:T(8,128)(2,1)S(1)}, u32[]{:S(2)}, u32[]{:S(2)}) collective-permute-start(bf16[640,512]{1,0:T(8,128)(2,1)S(1)} %get-tuple-element.334), channel_id=1, source_target_pairs={{0,4},{4,0},{1,5},{5,1},{2,6},{6,2},{3,7},{7,3},{8,12},{12,8},{9,1... | collective-permute-start | bytes 1966088 | tf_op jit(solution)/shard_map/ppermute | solution.py:52
  65.2 40.7 %collective-permute-start.3 = (bf16[160,1280]{1,0:T(8,128)(2,1)S(1)}, bf16[160,1280]{1,0:T(8,128)(2,1)S(1)}, u32[]{:S(2)}, u32[]{:S(2)}) collective-permute-start(bf16[160,1280]{1,0:T(8,128)(2,1)S(1)} %copy-done.186), channel_id=1, source_target_pairs={{0,4},{4,0},{1,5},{5,1},{2,6},{6,2},{3,7},{7,3},{8,12},{12,8},{9,1... | collective-permute-start | bytes 1228808 | tf_op jit(solution)/shard_map/ppermute | solution.py:52
  65.9 53.7 %collective-permute-start.11 = (bf16[320,1280]{1,0:T(8,128)(2,1)S(1)}, bf16[320,1280]{1,0:T(8,128)(2,1)S(1)}, u32[]{:S(2)}, u32[]{:S(2)}) collective-permute-start(bf16[320,1280]{1,0:T(8,128)(2,1)S(1)} %get-tuple-element.236), channel_id=1, source_target_pairs={{0,4},{4,0},{1,5},{5,1},{2,6},{6,2},{3,7},{7,3},{8,12},{12,8},{9,1... | collective-permute-start | bytes 2457608 | tf_op jit(solution)/shard_map/ppermute | solution.py:52
  67.6 69.4 %collective-permute-start.9 = (bf16[320,1280]{1,0:T(8,128)(2,1)S(1)}, bf16[320,1280]{1,0:T(8,128)(2,1)S(1)}, u32[]{:S(2)}, u32[]{:S(2)}) collective-permute-start(bf16[320,1280]{1,0:T(8,128)(2,1)S(1)} %get-tuple-element.237), channel_id=1, source_target_pairs={{0,4},{4,0},{1,5},{5,1},{2,6},{6,2},{3,7},{7,3},{8,12},{12,8},{9,1... | collective-permute-start | bytes 2457608 | tf_op jit(solution)/shard_map/ppermute | solution.py:52
  93.2 59.1 %collective-permute-start.7 = (bf16[320,1280]{1,0:T(8,128)(2,1)S(1)}, bf16[320,1280]{1,0:T(8,128)(2,1)S(1)}, u32[]{:S(2)}, u32[]{:S(2)}) collective-permute-start(bf16[320,1280]{1,0:T(8,128)(2,1)S(1)} %get-tuple-element.238), channel_id=1, source_target_pairs={{0,4},{4,0},{1,5},{5,1},{2,6},{6,2},{3,7},{7,3},{8,12},{12,8},{9,1... | collective-permute-start | bytes 2457608 | tf_op jit(solution)/shard_map/ppermute | solution.py:52
  106.7 47.1 %collective-permute-start.24 = (bf16[256,1280]{1,0:T(8,128)(2,1)S(1)}, bf16[256,1280]{1,0:T(8,128)(2,1)S(1)}, u32[]{:S(2)}, u32[]{:S(2)}) collective-permute-start(bf16[256,1280]{1,0:T(8,128)(2,1)S(1)} %convolution_convert_fusion.6), channel_id=1, source_target_pairs={{0,1},{1,0},{2,3},{3,2},{4,5},{5,4},{6,7},{7,6},{8,9},{9,8},{10,11... | collective-permute-start | bytes 1966088 | tf_op jit(solution)/shard_map/ppermute | solution.py:52
  107.3 47.5 %collective-permute-start.17 = (bf16[256,1280]{1,0:T(8,128)(2,1)S(1)}, bf16[256,1280]{1,0:T(8,128)(2,1)S(1)}, u32[]{:S(2)}, u32[]{:S(2)}) collective-permute-start(bf16[256,1280]{1,0:T(8,128)(2,1)S(1)} %convolution_convert_fusion.7), channel_id=1, source_target_pairs={{0,1},{1,0},{2,3},{3,2},{4,5},{5,4},{6,7},{7,6},{8,9},{9,8},{10,11... | collective-permute-start | bytes 1966088 | tf_op jit(solution)/shard_map/ppermute | solution.py:52
  119.5 37.5 %collective-permute-start.4 = (bf16[256,1280]{1,0:T(8,128)(2,1)S(1)}, bf16[256,1280]{1,0:T(8,128)(2,1)S(1)}, u32[]{:S(2)}, u32[]{:S(2)}) collective-permute-start(bf16[256,1280]{1,0:T(8,128)(2,1)S(1)} %convolution_convert_fusion.8), channel_id=1, source_target_pairs={{0,1},{1,0},{2,3},{3,2},{4,5},{5,4},{6,7},{7,6},{8,9},{9,8},{10,11... | collective-permute-start | bytes 1966088 | tf_op jit(solution)/shard_map/ppermute | solution.py:52
  137.1 21.1 %collective-permute-start.12 = (bf16[320,1280]{1,0:T(8,128)(2,1)S(1)}, bf16[320,1280]{1,0:T(8,128)(2,1)S(1)}, u32[]{:S(2)}, u32[]{:S(2)}) collective-permute-start(bf16[320,1280]{1,0:T(8,128)(2,1)S(1)} %collective-permute-done.11), channel_id=1, source_target_pairs={{0,8},{8,0},{16,24},{24,16},{1,9},{9,1},{17,25},{25,17},{2,10},{10... | collective-permute-start | bytes 2457608 | tf_op jit(solution)/shard_map/ppermute | solution.py:52
  152.2 21.2 %collective-permute-start.10 = (bf16[320,1280]{1,0:T(8,128)(2,1)S(1)}, bf16[320,1280]{1,0:T(8,128)(2,1)S(1)}, u32[]{:S(2)}, u32[]{:S(2)}) collective-permute-start(bf16[320,1280]{1,0:T(8,128)(2,1)S(1)} %collective-permute-done.9), channel_id=1, source_target_pairs={{0,8},{8,0},{16,24},{24,16},{1,9},{9,1},{17,25},{25,17},{2,10},{10... | collective-permute-start | bytes 2457608 | tf_op jit(solution)/shard_map/ppermute | solution.py:52
  153.8 33.8 %collective-permute-start.8 = (bf16[320,1280]{1,0:T(8,128)(2,1)S(1)}, bf16[320,1280]{1,0:T(8,128)(2,1)S(1)}, u32[]{:S(2)}, u32[]{:S(2)}) collective-permute-start(bf16[320,1280]{1,0:T(8,128)(2,1)S(1)} %collective-permute-done.7), channel_id=1, source_target_pairs={{0,8},{8,0},{16,24},{24,16},{1,9},{9,1},{17,25},{25,17},{2,10},{10... | collective-permute-start | bytes 2457608 | tf_op jit(solution)/shard_map/ppermute | solution.py:52
  154.9 33.4 %collective-permute-start.25 = (bf16[256,1280]{1,0:T(8,128)(2,1)S(1)}, bf16[256,1280]{1,0:T(8,128)(2,1)S(1)}, u32[]{:S(2)}, u32[]{:S(2)}) collective-permute-start(bf16[256,1280]{1,0:T(8,128)(2,1)S(1)} %fusion.56), channel_id=1, source_target_pairs={{0,2},{1,3},{2,0},{3,1},{4,6},{5,7},{6,4},{7,5},{8,10},{9,11},{10,... | collective-permute-start | bytes 1966088 | tf_op jit(solution)/shard_map/ppermute | solution.py:52
  157.0 31.6 %collective-permute-start.18 = (bf16[256,1280]{1,0:T(8,128)(2,1)S(1)}, bf16[256,1280]{1,0:T(8,128)(2,1)S(1)}, u32[]{:S(2)}, u32[]{:S(2)}) collective-permute-start(bf16[256,1280]{1,0:T(8,128)(2,1)S(1)} %fusion.55), channel_id=1, source_target_pairs={{0,2},{1,3},{2,0},{3,1},{4,6},{5,7},{6,4},{7,5},{8,10},{9,11},{10,... | collective-permute-start | bytes 1966088 | tf_op jit(solution)/shard_map/ppermute | solution.py:52
  158.2 38.6 %collective-permute-start.5 = (bf16[256,1280]{1,0:T(8,128)(2,1)S(1)}, bf16[256,1280]{1,0:T(8,128)(2,1)S(1)}, u32[]{:S(2)}, u32[]{:S(2)}) collective-permute-start(bf16[256,1280]{1,0:T(8,128)(2,1)S(1)} %fusion.54), channel_id=1, source_target_pairs={{0,2},{1,3},{2,0},{3,1},{4,6},{5,7},{6,4},{7,5},{8,10},{9,11},{10,... | collective-permute-start | bytes 1966088 | tf_op jit(solution)/shard_map/ppermute | solution.py:52
  234.3 17.6 %collective-permute-start.28 = (bf16[256,1280]{1,0:T(8,128)(2,1)S(1)}, bf16[256,1280]{1,0:T(8,128)(2,1)S(1)}, u32[]{:S(2)}, u32[]{:S(2)}) collective-permute-start(bf16[256,1280]{1,0:T(8,128)(2,1)S(1)} %add_convert_fusion.6), channel_id=1, source_target_pairs={{0,2},{1,3},{2,0},{3,1},{4,6},{5,7},{6,4},{7,5},{8,10},{9,11},{10,... | collective-permute-start | bytes 1966088 | tf_op jit(solution)/shard_map/ppermute | solution.py:52
  236.9 29.1 %collective-permute-start.21 = (bf16[256,1280]{1,0:T(8,128)(2,1)S(1)}, bf16[256,1280]{1,0:T(8,128)(2,1)S(1)}, u32[]{:S(2)}, u32[]{:S(2)}) collective-permute-start(bf16[256,1280]{1,0:T(8,128)(2,1)S(1)} %add_convert_fusion.7), channel_id=1, source_target_pairs={{0,2},{1,3},{2,0},{3,1},{4,6},{5,7},{6,4},{7,5},{8,10},{9,11},{10,... | collective-permute-start | bytes 1966088 | tf_op jit(solution)/shard_map/ppermute | solution.py:52
  238.6 40.6 %collective-permute-start.14 = (bf16[256,1280]{1,0:T(8,128)(2,1)S(1)}, bf16[256,1280]{1,0:T(8,128)(2,1)S(1)}, u32[]{:S(2)}, u32[]{:S(2)}) collective-permute-start(bf16[256,1280]{1,0:T(8,128)(2,1)S(1)} %add_convert_fusion.8), channel_id=1, source_target_pairs={{0,2},{1,3},{2,0},{3,1},{4,6},{5,7},{6,4},{7,5},{8,10},{9,11},{10,... | collective-permute-start | bytes 1966088 | tf_op jit(solution)/shard_map/ppermute | solution.py:52
  339.0 78.8 %collective-permute-start.60 = (bf16[640,1280]{1,0:T(8,128)(2,1)}, bf16[640,1280]{1,0:T(8,128)(2,1)S(1)}, u32[]{:S(2)}, u32[]{:S(2)}) collective-permute-start(bf16[640,1280]{1,0:T(8,128)(2,1)} %slice.841), channel_id=1, source_target_pairs={{0,4},{4,0},{1,5},{5,1},{2,6},{6,2},{3,7},{7,3},{8,12},{12,8},{9,1... | collective-permute-start | bytes 4915208 | tf_op jit(solution)/shard_map/ppermute | solution.py:52
  341.0 19.5 %collective-permute-start.31 = (bf16[256,1280]{1,0:T(8,128)(2,1)S(1)}, bf16[256,1280]{1,0:T(8,128)(2,1)S(1)}, u32[]{:S(2)}, u32[]{:S(2)}) collective-permute-start(bf16[256,1280]{1,0:T(8,128)(2,1)S(1)} %fusion.45), channel_id=1, source_target_pairs={{0,1},{1,0},{2,3},{3,2},{4,5},{5,4},{6,7},{7,6},{8,9},{9,8},{10,11... | collective-permute-start | bytes 1966088 | tf_op jit(solution)/shard_map/ppermute | solution.py:52
  344.6 18.4 %collective-permute-start.39 = (bf16[256,1280]{1,0:T(8,128)(2,1)S(1)}, bf16[256,1280]{1,0:T(8,128)(2,1)S(1)}, u32[]{:S(2)}, u32[]{:S(2)}) collective-permute-start(bf16[256,1280]{1,0:T(8,128)(2,1)S(1)} %fusion.46), channel_id=1, source_target_pairs={{0,1},{1,0},{2,3},{3,2},{4,5},{5,4},{6,7},{7,6},{8,9},{9,8},{10,11... | collective-permute-start | bytes 1966088 | tf_op jit(solution)/shard_map/ppermute | solution.py:52
  347.4 17.7 %collective-permute-start.47 = (bf16[256,1280]{1,0:T(8,128)(2,1)S(1)}, bf16[256,1280]{1,0:T(8,128)(2,1)S(1)}, u32[]{:S(2)}, u32[]{:S(2)}) collective-permute-start(bf16[256,1280]{1,0:T(8,128)(2,1)S(1)} %fusion.47), channel_id=1, source_target_pairs={{0,1},{1,0},{2,3},{3,2},{4,5},{5,4},{6,7},{7,6},{8,9},{9,8},{10,11... | collective-permute-start | bytes 1966088 | tf_op jit(solution)/shard_map/ppermute | solution.py:52
  361.8 17.6 %collective-permute-start.32 = (bf16[256,1280]{1,0:T(8,128)(2,1)S(1)}, bf16[256,1280]{1,0:T(8,128)(2,1)S(1)}, u32[]{:S(2)}, u32[]{:S(2)}) collective-permute-start(bf16[256,1280]{1,0:T(8,128)(2,1)S(1)} %fusion.53), channel_id=1, source_target_pairs={{0,2},{1,3},{2,0},{3,1},{4,6},{5,7},{6,4},{7,5},{8,10},{9,11},{10,... | collective-permute-start | bytes 1966088 | tf_op jit(solution)/shard_map/ppermute | solution.py:52
  364.1 29.4 %collective-permute-start.40 = (bf16[256,1280]{1,0:T(8,128)(2,1)S(1)}, bf16[256,1280]{1,0:T(8,128)(2,1)S(1)}, u32[]{:S(2)}, u32[]{:S(2)}) collective-permute-start(bf16[256,1280]{1,0:T(8,128)(2,1)S(1)} %fusion.52), channel_id=1, source_target_pairs={{0,2},{1,3},{2,0},{3,1},{4,6},{5,7},{6,4},{7,5},{8,10},{9,11},{10,... | collective-permute-start | bytes 1966088 | tf_op jit(solution)/shard_map/ppermute | solution.py:52
  366.1 40.8 %collective-permute-start.48 = (bf16[256,1280]{1,0:T(8,128)(2,1)S(1)}, bf16[256,1280]{1,0:T(8,128)(2,1)S(1)}, u32[]{:S(2)}, u32[]{:S(2)}) collective-permute-start(bf16[256,1280]{1,0:T(8,128)(2,1)S(1)} %fusion.51), channel_id=1, source_target_pairs={{0,2},{1,3},{2,0},{3,1},{4,6},{5,7},{6,4},{7,5},{8,10},{9,11},{10,... | collective-permute-start | bytes 1966088 | tf_op jit(solution)/shard_map/ppermute | solution.py:52
  377.2 55.5 %collective-permute-start.59 = (bf16[640,1280]{1,0:T(8,128)(2,1)}, bf16[640,1280]{1,0:T(8,128)(2,1)}, u32[]{:S(2)}, u32[]{:S(2)}) collective-permute-start(bf16[640,1280]{1,0:T(8,128)(2,1)} %slice.842), channel_id=1, source_target_pairs={{0,4},{4,0},{1,5},{5,1},{2,6},{6,2},{3,7},{7,3},{8,12},{12,8},{9,1... | collective-permute-start | bytes 4915208 | tf_op jit(solution)/shard_map/ppermute | solution.py:52
  379.4 70.3 %collective-permute-start.58 = (bf16[640,1280]{1,0:T(8,128)(2,1)}, bf16[640,1280]{1,0:T(8,128)(2,1)}, u32[]{:S(2)}, u32[]{:S(2)}) collective-permute-start(bf16[640,1280]{1,0:T(8,128)(2,1)} %slice.843), channel_id=1, source_target_pairs={{0,4},{4,0},{1,5},{5,1},{2,6},{6,2},{3,7},{7,3},{8,12},{12,8},{9,1... | collective-permute-start | bytes 4915208 | tf_op jit(solution)/shard_map/ppermute | solution.py:52
  415.1 50.1 %collective-permute-start.41 = (bf16[256,1280]{1,0:T(8,128)(2,1)S(1)}, bf16[256,1280]{1,0:T(8,128)(2,1)}, u32[]{:S(2)}, u32[]{:S(2)}) collective-permute-start(bf16[256,1280]{1,0:T(8,128)(2,1)S(1)} %get-tuple-element.309), channel_id=1, source_target_pairs={{0,1},{1,0},{2,3},{3,2},{4,5},{5,4},{6,7},{7,6},{8,9},{9,8},{10,11... | collective-permute-start | bytes 1966088 | tf_op jit(solution)/shard_map/ppermute | solution.py:52
  417.7 58.4 %collective-permute-start.49 = (bf16[256,1280]{1,0:T(8,128)(2,1)}, bf16[256,1280]{1,0:T(8,128)(2,1)}, u32[]{:S(2)}, u32[]{:S(2)}) collective-permute-start(bf16[256,1280]{1,0:T(8,128)(2,1)} %get-tuple-element.308), channel_id=1, source_target_pairs={{0,1},{1,0},{2,3},{3,2},{4,5},{5,4},{6,7},{7,6},{8,9},{9,8},{10,11... | collective-permute-start | bytes 1966088 | tf_op jit(solution)/shard_map/ppermute | solution.py:52
  417.8 71.3 %collective-permute-start.33 = (bf16[256,1280]{1,0:T(8,128)(2,1)S(1)}, bf16[256,1280]{1,0:T(8,128)(2,1)S(1)}, u32[]{:S(2)}, u32[]{:S(2)}) collective-permute-start(bf16[256,1280]{1,0:T(8,128)(2,1)S(1)} %get-tuple-element.310), channel_id=1, source_target_pairs={{0,1},{1,0},{2,3},{3,2},{4,5},{5,4},{6,7},{7,6},{8,9},{9,8},{10,11... | collective-permute-start | bytes 1966088 | tf_op jit(solution)/shard_map/ppermute | solution.py:52
  459.9 127.4 %collective-permute-start.75 = (bf16[640,1280]{1,0:T(8,128)(2,1)}, bf16[640,1280]{1,0:T(8,128)(2,1)}, u32[]{:S(2)}, u32[]{:S(2)}) collective-permute-start(bf16[640,1280]{1,0:T(8,128)(2,1)} %get-tuple-element.141), channel_id=1, source_target_pairs={{0,8},{24,16},{1,9},{25,17},{2,10},{26,18},{3,11},{27,19},{4,12},{... | collective-permute-start | bytes 4915208 | tf_op jit(solution)/shard_map/ppermute | solution.py:80
  474.6 45.5 %collective-permute-start.42 = (bf16[640,512]{1,0:T(8,128)(2,1)S(1)}, bf16[640,512]{1,0:T(8,128)(2,1)}, u32[]{:S(2)}, u32[]{:S(2)}) collective-permute-start(bf16[640,512]{1,0:T(8,128)(2,1)S(1)} %bitcast.308), channel_id=1, source_target_pairs={{0,4},{4,0},{1,5},{5,1},{2,6},{6,2},{3,7},{7,3},{8,12},{12,8},{9,1... | collective-permute-start | bytes 1966088 | tf_op jit(solution)/shard_map/ppermute | solution.py:52
  485.9 37.8 %collective-permute-start.50 = (bf16[640,512]{1,0:T(8,128)(2,1)S(1)}, bf16[640,512]{1,0:T(8,128)(2,1)}, u32[]{:S(2)}, u32[]{:S(2)}) collective-permute-start(bf16[640,512]{1,0:T(8,128)(2,1)S(1)} %bitcast.309), channel_id=1, source_target_pairs={{0,4},{4,0},{1,5},{5,1},{2,6},{6,2},{3,7},{7,3},{8,12},{12,8},{9,1... | collective-permute-start | bytes 1966088 | tf_op jit(solution)/shard_map/ppermute | solution.py:52
  491.5 23.7 %collective-permute-start.57 = (bf16[160,1280]{1,0:T(8,128)(2,1)}, bf16[160,1280]{1,0:T(8,128)(2,1)S(1)}, u32[]{:S(2)}, u32[]{:S(2)}) collective-permute-start(bf16[160,1280]{1,0:T(8,128)(2,1)} %fusion.129), channel_id=1, source_target_pairs={{0,4},{4,0},{1,5},{5,1},{2,6},{6,2},{3,7},{7,3},{8,12},{12,8},{9,1... | collective-permute-start | bytes 1228808 | tf_op jit(solution)/shard_map/ppermute | solution.py:52
  502.9 23.6 %collective-permute-start.34 = (bf16[640,512]{1,0:T(8,128)(2,1)S(1)}, bf16[640,512]{1,0:T(8,128)(2,1)S(1)}, u32[]{:S(2)}, u32[]{:S(2)}) collective-permute-start(bf16[640,512]{1,0:T(8,128)(2,1)S(1)} %bitcast.310), channel_id=1, source_target_pairs={{0,4},{4,0},{1,5},{5,1},{2,6},{6,2},{3,7},{7,3},{8,12},{12,8},{9,1... | collective-permute-start | bytes 1966088 | tf_op jit(solution)/shard_map/ppermute | solution.py:52
  515.2 74.6 %collective-permute-start.78 = (bf16[640,1280]{1,0:T(8,128)(2,1)}, bf16[640,1280]{1,0:T(8,128)(2,1)}, u32[]{:S(2)}, u32[]{:S(2)}) collective-permute-start(bf16[640,1280]{1,0:T(8,128)(2,1)} %get-tuple-element.142), channel_id=1, source_target_pairs={{0,8},{24,16},{1,9},{25,17},{2,10},{26,18},{3,11},{27,19},{4,12},{... | collective-permute-start | bytes 4915208 | tf_op jit(solution)/shard_map/ppermute | solution.py:80
  520.1 40.4 %collective-permute-start.72 = (bf16[160,1280]{1,0:T(8,128)(2,1)}, bf16[160,1280]{1,0:T(8,128)(2,1)}, u32[]{:S(2)}, u32[]{:S(2)}) collective-permute-start(bf16[160,1280]{1,0:T(8,128)(2,1)} %get-tuple-element.133), channel_id=1, source_target_pairs={{0,8},{24,16},{1,9},{25,17},{2,10},{26,18},{3,11},{27,19},{4,12},{... | collective-permute-start | bytes 1228808 | tf_op jit(solution)/shard_map/ppermute | solution.py:80
  559.0 20.6 %collective-permute-start.55 = (bf16[160,1280]{1,0:T(8,128)(2,1)S(1)}, bf16[160,1280]{1,0:T(8,128)(2,1)S(1)}, u32[]{:S(2)}, u32[]{:S(2)}) collective-permute-start(bf16[160,1280]{1,0:T(8,128)(2,1)S(1)} %copy-done.189), channel_id=1, source_target_pairs={{0,4},{4,0},{1,5},{5,1},{2,6},{6,2},{3,7},{7,3},{8,12},{12,8},{9,1... | collective-permute-start | bytes 1228808 | tf_op jit(solution)/shard_map/ppermute | solution.py:52
  562.6 21.9 %collective-permute-start.54 = (bf16[160,1280]{1,0:T(8,128)(2,1)S(1)}, bf16[160,1280]{1,0:T(8,128)(2,1)S(1)}, u32[]{:S(2)}, u32[]{:S(2)}) collective-permute-start(bf16[160,1280]{1,0:T(8,128)(2,1)S(1)} %copy-done.188), channel_id=1, source_target_pairs={{0,4},{4,0},{1,5},{5,1},{2,6},{6,2},{3,7},{7,3},{8,12},{12,8},{9,1... | collective-permute-start | bytes 1228808 | tf_op jit(solution)/shard_map/ppermute | solution.py:52
  579.7 37.5 %collective-permute-start.81 = (bf16[640,1280]{1,0:T(8,128)(2,1)S(1)}, bf16[640,1280]{1,0:T(8,128)(2,1)S(1)}, u32[]{:S(2)}, u32[]{:S(2)}) collective-permute-start(bf16[640,1280]{1,0:T(8,128)(2,1)S(1)} %copy-done.24), channel_id=1, source_target_pairs={{0,8},{24,16},{1,9},{25,17},{2,10},{26,18},{3,11},{27,19},{4,12},{... | collective-permute-start | bytes 4915208 | tf_op jit(solution)/shard_map/ppermute | solution.py:80
  584.4 37.7 %collective-permute-start.51 = (bf16[256,1280]{1,0:T(8,128)(2,1)S(1)}, bf16[256,1280]{1,0:T(8,128)(2,1)S(1)}, u32[]{:S(2)}, u32[]{:S(2)}) collective-permute-start(bf16[256,1280]{1,0:T(8,128)(2,1)S(1)} %convolution_convert_fusion), channel_id=1, source_target_pairs={{0,1},{1,0},{2,3},{3,2},{4,5},{5,4},{6,7},{7,6},{8,9},{9,8},{10,11... | collective-permute-start | bytes 1966088 | tf_op jit(solution)/shard_map/ppermute | solution.py:52
  586.7 37.8 %collective-permute-start.43 = (bf16[256,1280]{1,0:T(8,128)(2,1)S(1)}, bf16[256,1280]{1,0:T(8,128)(2,1)S(1)}, u32[]{:S(2)}, u32[]{:S(2)}) collective-permute-start(bf16[256,1280]{1,0:T(8,128)(2,1)S(1)} %convolution_convert_fusion.1), channel_id=1, source_target_pairs={{0,1},{1,0},{2,3},{3,2},{4,5},{5,4},{6,7},{7,6},{8,9},{9,8},{10,11... | collective-permute-start | bytes 1966088 | tf_op jit(solution)/shard_map/ppermute | solution.py:52
  587.3 39.0 %collective-permute-start.35 = (bf16[256,1280]{1,0:T(8,128)(2,1)S(1)}, bf16[256,1280]{1,0:T(8,128)(2,1)S(1)}, u32[]{:S(2)}, u32[]{:S(2)}) collective-permute-start(bf16[256,1280]{1,0:T(8,128)(2,1)S(1)} %copy-done.181), channel_id=1, source_target_pairs={{0,1},{1,0},{2,3},{3,2},{4,5},{5,4},{6,7},{7,6},{8,9},{9,8},{10,11... | collective-permute-start | bytes 1966088 | tf_op jit(solution)/shard_map/ppermute | solution.py:52
  589.8 38.0 %collective-permute-start.63 = (bf16[160,1280]{1,0:T(8,128)(2,1)S(1)}, bf16[160,1280]{1,0:T(8,128)(2,1)S(1)}, u32[]{:S(2)}, u32[]{:S(2)}) collective-permute-start(bf16[160,1280]{1,0:T(8,128)(2,1)S(1)} %get-tuple-element.130), channel_id=1, source_target_pairs={{0,8},{24,16},{1,9},{25,17},{2,10},{26,18},{3,11},{27,19},{4,12},{... | collective-permute-start | bytes 1228808 | tf_op jit(solution)/shard_map/ppermute | solution.py:80
  624.6 29.2 %collective-permute-start.79 = (bf16[640,1280]{1,0:T(8,128)(2,1)S(1)}, bf16[640,1280]{1,0:T(8,128)(2,1)S(1)}, u32[]{:S(2)}, u32[]{:S(2)}) collective-permute-start(bf16[640,1280]{1,0:T(8,128)(2,1)S(1)} %add_convert_fusion.3), channel_id=1, source_target_pairs={{8,16},{16,8},{9,17},{17,9},{10,18},{18,10},{11,19},{19,11},{12,20... | collective-permute-start | bytes 4915208 | tf_op jit(solution)/shard_map/ppermute | solution.py:83
  627.8 18.9 %collective-permute-start.44 = (bf16[256,1280]{1,0:T(8,128)(2,1)S(1)}, bf16[256,1280]{1,0:T(8,128)(2,1)S(1)}, u32[]{:S(2)}, u32[]{:S(2)}) collective-permute-start(bf16[256,1280]{1,0:T(8,128)(2,1)S(1)} %fusion.49), channel_id=1, source_target_pairs={{0,2},{1,3},{2,0},{3,1},{4,6},{5,7},{6,4},{7,5},{8,10},{9,11},{10,... | collective-permute-start | bytes 1966088 | tf_op jit(solution)/shard_map/ppermute | solution.py:52
  630.5 23.2 %collective-permute-start.36 = (bf16[256,1280]{1,0:T(8,128)(2,1)S(1)}, bf16[256,1280]{1,0:T(8,128)(2,1)S(1)}, u32[]{:S(2)}, u32[]{:S(2)}) collective-permute-start(bf16[256,1280]{1,0:T(8,128)(2,1)S(1)} %fusion.48), channel_id=1, source_target_pairs={{0,2},{1,3},{2,0},{3,1},{4,6},{5,7},{6,4},{7,5},{8,10},{9,11},{10,... | collective-permute-start | bytes 1966088 | tf_op jit(solution)/shard_map/ppermute | solution.py:52
  637.6 24.6 %collective-permute-start.82 = (bf16[640,1280]{1,0:T(8,128)(2,1)S(1)}, bf16[640,1280]{1,0:T(8,128)(2,1)S(1)}, u32[]{:S(2)}, u32[]{:S(2)}) collective-permute-start(bf16[640,1280]{1,0:T(8,128)(2,1)S(1)} %add_convert_fusion.1), channel_id=1, source_target_pairs={{8,16},{16,8},{9,17},{17,9},{10,18},{18,10},{11,19},{19,11},{12,20... | collective-permute-start | bytes 4915208 | tf_op jit(solution)/shard_map/ppermute | solution.py:83
  639.7 18.6 %collective-permute-start.29 = (f32[256,1280]{1,0:T(8,128)S(1)}, f32[256,1280]{1,0:T(8,128)S(1)}, u32[]{:S(2)}, u32[]{:S(2)}) collective-permute-start(f32[256,1280]{1,0:T(8,128)S(1)} %copy-done.13), channel_id=1, source_target_pairs={{0,1},{1,0},{2,3},{3,2},{4,5},{5,4},{6,7},{7,6},{8,9},{9,8},{10,11... | collective-permute-start | bytes 3932168 | tf_op jit(solution)/shard_map/ppermute | solution.py:52
  653.8 65.2 %collective-permute-start.76 = (bf16[640,1280]{1,0:T(8,128)(2,1)S(1)}, bf16[640,1280]{1,0:T(8,128)(2,1)S(1)}, u32[]{:S(2)}, u32[]{:S(2)}) collective-permute-start(bf16[640,1280]{1,0:T(8,128)(2,1)S(1)} %add_convert_fusion.5), channel_id=1, source_target_pairs={{8,16},{16,8},{9,17},{17,9},{10,18},{18,10},{11,19},{19,11},{12,20... | collective-permute-start | bytes 4915208 | tf_op jit(solution)/shard_map/ppermute | solution.py:83
  658.3 41.1 %collective-permute-start.86 = (f32[2720]{0:T(1024)S(1)}, f32[2720]{0:T(1024)S(1)}, u32[]{:S(2)}, u32[]{:S(2)}) collective-permute-start(f32[2720]{0:T(1024)S(1)} %add.652), channel_id=1, source_target_pairs={{8,0},{16,24},{9,1},{17,25},{10,2},{18,26},{11,3},{19,27},{12,4},{... | collective-permute-start | bytes 32648 | tf_op jit(solution)/shard_map/ppermute | solution.py:85
  659.6 49.7 %collective-permute-start.74 = (bf16[160,1280]{1,0:T(8,128)(2,1)S(1)}, bf16[160,1280]{1,0:T(8,128)(2,1)S(1)}, u32[]{:S(2)}, u32[]{:S(2)}) collective-permute-start(bf16[160,1280]{1,0:T(8,128)(2,1)S(1)} %add_convert_fusion.9.whole), channel_id=1, source_target_pairs={{8,0},{16,24},{9,1},{17,25},{10,2},{18,26},{11,3},{19,27},{12,4},{... | collective-permute-start | bytes 1228808 | tf_op jit(solution)/shard_map/ppermute | solution.py:85
  660.9 56.7 %collective-permute-start.65 = (bf16[160,1280]{1,0:T(8,128)(2,1)S(1)}, bf16[160,1280]{1,0:T(8,128)(2,1)S(1)}, u32[]{:S(2)}, u32[]{:S(2)}) collective-permute-start(bf16[160,1280]{1,0:T(8,128)(2,1)S(1)} %add_convert_fusion.15.whole), channel_id=1, source_target_pairs={{8,0},{16,24},{9,1},{17,25},{10,2},{18,26},{11,3},{19,27},{12,4},{... | collective-permute-start | bytes 1228808 | tf_op jit(solution)/shard_map/ppermute | solution.py:85
  662.3 87.3 %collective-permute-start.53 = (f32[256,1280]{1,0:T(8,128)}, f32[256,1280]{1,0:T(8,128)}, u32[]{:S(2)}, u32[]{:S(2)}) collective-permute-start(f32[256,1280]{1,0:T(8,128)} %get-tuple-element.305.own), channel_id=1, source_target_pairs={{0,1},{1,0},{2,3},{3,2},{4,5},{5,4},{6,7},{7,6},{8,9},{9,8},{10,11... | collective-permute-start | bytes 3932168 | tf_op jit(solution)/shard_map/ppermute | solution.py:52
  699.4 37.7 %collective-permute-start.68 = (bf16[160,1280]{1,0:T(8,128)(2,1)S(1)}, bf16[160,1280]{1,0:T(8,128)(2,1)S(1)}, u32[]{:S(2)}, u32[]{:S(2)}) collective-permute-start(bf16[160,1280]{1,0:T(8,128)(2,1)S(1)} %add_convert_fusion.13.whole), channel_id=1, source_target_pairs={{8,0},{16,24},{9,1},{17,25},{10,2},{18,26},{11,3},{19,27},{12,4},{... | collective-permute-start | bytes 1228808 | tf_op jit(solution)/shard_map/ppermute | solution.py:85
  709.3 40.2 %collective-permute-start.71 = (bf16[160,1280]{1,0:T(8,128)(2,1)}, bf16[160,1280]{1,0:T(8,128)(2,1)}, u32[]{:S(2)}, u32[]{:S(2)}) collective-permute-start(bf16[160,1280]{1,0:T(8,128)(2,1)} %add_convert_fusion.11.whole), channel_id=1, source_target_pairs={{8,0},{16,24},{9,1},{17,25},{10,2},{18,26},{11,3},{19,27},{12,4},{... | collective-permute-start | bytes 1228808 | tf_op jit(solution)/shard_map/ppermute | solution.py:85
  717.7 105.2 %collective-permute-start.80 = (bf16[640,1280]{1,0:T(8,128)(2,1)}, bf16[640,1280]{1,0:T(8,128)(2,1)}, u32[]{:S(2)}, u32[]{:S(2)}) collective-permute-start(bf16[640,1280]{1,0:T(8,128)(2,1)} %add_convert_fusion.2.whole), channel_id=1, source_target_pairs={{8,0},{16,24},{9,1},{17,25},{10,2},{18,26},{11,3},{19,27},{12,4},{... | collective-permute-start | bytes 4915208 | tf_op jit(solution)/shard_map/ppermute | solution.py:85
  719.0 97.3 %collective-permute-start.83 = (bf16[640,1280]{1,0:T(8,128)(2,1)}, bf16[640,1280]{1,0:T(8,128)(2,1)}, u32[]{:S(2)}, u32[]{:S(2)}) collective-permute-start(bf16[640,1280]{1,0:T(8,128)(2,1)} %add_convert_fusion.whole), channel_id=1, source_target_pairs={{8,0},{16,24},{9,1},{17,25},{10,2},{18,26},{11,3},{19,27},{12,4},{... | collective-permute-start | bytes 4915208 | tf_op jit(solution)/shard_map/ppermute | solution.py:85
  737.9 113.3 %collective-permute-start.77 = (bf16[640,1280]{1,0:T(8,128)(2,1)}, bf16[640,1280]{1,0:T(8,128)(2,1)}, u32[]{:S(2)}, u32[]{:S(2)}) collective-permute-start(bf16[640,1280]{1,0:T(8,128)(2,1)} %add_convert_fusion.4.whole), channel_id=1, source_target_pairs={{8,0},{16,24},{9,1},{17,25},{10,2},{18,26},{11,3},{19,27},{12,4},{... | collective-permute-start | bytes 4915208 | tf_op jit(solution)/shard_map/ppermute | solution.py:85
  749.5 17.5 %collective-permute-start.45 = (f32[256,1280]{1,0:T(8,128)}, f32[256,1280]{1,0:T(8,128)}, u32[]{:S(2)}, u32[]{:S(2)}) collective-permute-start(f32[256,1280]{1,0:T(8,128)} %get-tuple-element.306.own), channel_id=1, source_target_pairs={{0,1},{1,0},{2,3},{3,2},{4,5},{5,4},{6,7},{7,6},{8,9},{9,8},{10,11... | collective-permute-start | bytes 3932168 | tf_op jit(solution)/shard_map/ppermute | solution.py:52
  749.5 21.0 %collective-permute-start.37 = (f32[256,1280]{1,0:T(8,128)}, f32[256,1280]{1,0:T(8,128)}, u32[]{:S(2)}, u32[]{:S(2)}) collective-permute-start(f32[256,1280]{1,0:T(8,128)} %get-tuple-element.307.own), channel_id=1, source_target_pairs={{0,1},{1,0},{2,3},{3,2},{4,5},{5,4},{6,7},{7,6},{8,9},{9,8},{10,11... | collective-permute-start | bytes 3932168 | tf_op jit(solution)/shard_map/ppermute | solution.py:52
  (292 other events, 4205.1 us)

commit v3 on v2

--- a/solution.py
+++ b/solution.py
@@ -24,6 +24,7 @@
 OUTER_MOMENTUM = 0.9
 MASKED = -1e30
 VMEM_BYTES = 40 * 1024 * 1024
+LARGE_VMEM_BYTES = 56 * 1024 * 1024
 F32 = jnp.float32
 LOW = jnp.bfloat16
 
@@ -68,10 +69,35 @@
     return left.astype(F32) + right.astype(F32)
 
 
+def ordered_after(body, count, deps):
+    def wrapped(*refs):
+        return body(*refs[:count], *refs[count + len(deps) :])
+
+    return wrapped
+
+
+UNREAD = pl.BlockSpec(memory_space=pl.ANY)
+IN_VMEM = pl.BlockSpec(memory_space=pltpu.VMEM)
+
+
+def tie_kernel(*refs):
+    del refs
+
+
+def tie(values, *deps):
+    return pl.pallas_call(
+        tie_kernel,
+        in_specs=[UNREAD] * (1 + len(deps)),
+        out_specs=UNREAD,
+        out_shape=jax.ShapeDtypeStruct(values.shape, values.dtype),
+        input_output_aliases={0: 0},
+    )(values, *deps)
+
+
 def tensor_sum(own_part, other_part):
     from_core = trade(other_part, "tensor", 1)
     pair = split_low(own_part + from_core.astype(F32))
-    return add_low(pair, trade(pair, "tensor", 2))
+    return (pair, trade(pair, "tensor", 2))
 
 
 def group_sum(values):
@@ -83,12 +109,147 @@
         add_low(pair, lax.ppermute(pair, "group", [(1, 2), (2, 1)])).astype(dtype)
     )
     back = lax.ppermute(whole, "group", [(1, 0), (2, 3)])
-    return (whole, back)
+    return (pair, whole, back)
 
 
 def mask_bias(seg_q, place_q, seg_k, place_k):
     allowed = (seg_k == seg_q) & (place_k <= place_q)
     return jnp.where(allowed, 0.0, MASKED).astype(F32)
+
+
+def project_kernel(head_count, weights, own, other, scale, projected, query_low, key_value):
+    width = head_count * HEAD_DIM
+    rows = jnp.concatenate([own[...], other[...]], axis=0)
+    projected[...] = dot(weights[...], rows, (1, 1))
+    for head in range(head_count):
+        cols = pl.ds(head * HEAD_DIM, HEAD_DIM)
+        key_cols = pl.ds(width + head * HEAD_DIM, HEAD_DIM)
+        head_scale = scale[cols, :]
+        query_unit, _ = unit_rows(projected[cols, :], axis=0)
+        key_unit, _ = unit_rows(projected[key_cols, :], axis=0)
+        query_low[cols, :] = (query_unit * head_scale * math.sqrt(HEAD_DIM)).astype(LOW)
+        key_value[cols, :] = (key_unit * head_scale).astype(LOW)
+    key_value[width : 2 * width, :] = projected[2 * width : 3 * width, :].astype(LOW)
+
+
+def project(head_count, weights, own, other, scale, deps=()):
+    total, model_width = weights.shape
+    width = head_count * HEAD_DIM
+    rows = own.shape[0] + other.shape[0]
+    return pl.pallas_call(
+        ordered_after(partial(project_kernel, head_count), 4, deps),
+        in_specs=[IN_VMEM] * 4 + [UNREAD] * len(deps),
+        out_shape=[
+            jax.ShapeDtypeStruct((total, rows), F32),
+            jax.ShapeDtypeStruct((width, rows), LOW),
+            jax.ShapeDtypeStruct((2 * width, rows), LOW),
+        ],
+        compiler_params=pltpu.CompilerParams(vmem_limit_bytes=VMEM_BYTES),
+        cost_estimate=pl.CostEstimate(
+            flops=2 * total * rows * model_width,
+            bytes_accessed=2 * total * model_width + 6 * total * rows,
+            transcendentals=0,
+        ),
+    )(weights, own, other, scale, *deps)
+
+
+def sides_kernel(head_count, has_partner, own, arrived, query_grad, projected, scale, triple, terms):
+    width = head_count * HEAD_DIM
+    root_head = math.sqrt(HEAD_DIM)
+
+    def side(cols):
+        gradient = own[cols, :]
+        if has_partner:
+            gradient = gradient + arrived[cols, :].astype(F32)
+        return gradient
+
+    for head in range(head_count):
+        cols = pl.ds(head * HEAD_DIM, HEAD_DIM)
+        key_cols = pl.ds(width + head * HEAD_DIM, HEAD_DIM)
+        head_scale = scale[cols, :]
+        query_unit, query_norm = unit_rows(projected[cols, :], axis=0)
+        key_unit, key_norm = unit_rows(projected[key_cols, :], axis=0)
+        query_scaled = query_grad[cols, :] * root_head
+        key_scaled = side(cols)
+        terms[cols, :] = jnp.sum(
+            query_scaled * query_unit + key_scaled * key_unit, axis=1, keepdims=True
+        )
+        triple[cols, :] = unit_back(
+            query_unit, query_norm, query_scaled * head_scale, axis=0
+        ).astype(LOW)
+        triple[key_cols, :] = unit_back(
+            key_unit, key_norm, key_scaled * head_scale, axis=0
+        ).astype(LOW)
+    triple[2 * width : 3 * width, :] = side(pl.ds(width, width)).astype(LOW)
+
+
+def sides_back(head_count, own, arrived, query_grad, projected, scale, deps=()):
+    total, rows = projected.shape
+    width = head_count * HEAD_DIM
+    has_partner = arrived is not None
+    if not has_partner:
+        arrived = jnp.zeros((16, rows), LOW)
+    return pl.pallas_call(
+        ordered_after(partial(sides_kernel, head_count, has_partner), 5, deps),
+        in_specs=[IN_VMEM] * 5 + [UNREAD] * len(deps),
+        out_shape=[
+            jax.ShapeDtypeStruct((total, rows), LOW),
+            jax.ShapeDtypeStruct((width, 1), F32),
+        ],
+        compiler_params=pltpu.CompilerParams(vmem_limit_bytes=VMEM_BYTES),
+        cost_estimate=pl.CostEstimate(
+            flops=40 * total * rows, bytes_accessed=14 * total * rows, transcendentals=rows
+        ),
+    )(own, arrived, query_grad, projected, scale, *deps)
+
+
+def triple_grad_kernel(count, parts, own_part, me, *refs):
+    lefts, rights = refs[:count], refs[count : 3 * count]
+    own_out, other_outs = refs[3 * count], refs[3 * count + 1 :]
+    right = jnp.concatenate([ref[...] for ref in rights], axis=0)
+    rows = lefts[0].shape[0] // parts
+    for side in range(2):
+        place = me[0] if side == 0 else 1 - me[0]
+        left = jnp.concatenate(
+            [
+                jnp.concatenate(
+                    [
+                        ref[pl.ds(pl.multiple_of(n * rows + place * own_part, 16), own_part), :]
+                        for n in range(parts)
+                    ],
+                    axis=0,
+                )
+                for ref in lefts
+            ],
+            axis=1,
+        )
+        total = dot(left, right, (1, 0))
+        if side == 0:
+            own_out[...] = total
+        else:
+            for n in range(parts):
+                other_outs[n][...] = total[n * own_part : (n + 1) * own_part, :].astype(LOW)
+
+
+def triple_grad(me, parts, lefts, rights, deps=()):
+    count = len(lefts)
+    total, rows = lefts[0].shape
+    own_part = total // parts // 2
+    width = rights[0][0].shape[1]
+    return pl.pallas_call(
+        ordered_after(partial(triple_grad_kernel, count, parts, own_part), 1 + 3 * count, deps),
+        in_specs=[pl.BlockSpec(memory_space=pltpu.SMEM)]
+        + [IN_VMEM] * (3 * count)
+        + [UNREAD] * len(deps),
+        out_shape=[jax.ShapeDtypeStruct((parts * own_part, width), F32)]
+        + [jax.ShapeDtypeStruct((own_part, width), LOW)] * parts,
+        compiler_params=pltpu.CompilerParams(vmem_limit_bytes=VMEM_BYTES),
+        cost_estimate=pl.CostEstimate(
+            flops=2 * count * rows * total * width,
+            bytes_accessed=2 * count * rows * (total + width) + 3 * total * width,
+            transcendentals=0,
+        ),
+    )(me, *lefts, *[side for right in rights for side in right], *deps)
 
 
 def attend_kernel(
@@ -115,12 +276,13 @@
         heads[cols, :] = (acc / row_total).astype(LOW)
 
 
-def attend(head_count, places, query, key_value):
+def attend(head_count, places, query, key_value, deps=()):
     blocks, _, rows = key_value.shape
     width, count = query.shape
     work = head_count * blocks * rows * count * HEAD_DIM * 4
     return pl.pallas_call(
-        partial(attend_kernel, head_count),
+        ordered_after(partial(attend_kernel, head_count), 6, deps),
+        in_specs=[IN_VMEM] * 6 + [UNREAD] * len(deps),
         out_shape=(
             jax.ShapeDtypeStruct((width, count), F32),
             jax.ShapeDtypeStruct((head_count, count), F32),
@@ -131,7 +293,7 @@
         cost_estimate=pl.CostEstimate(
             flops=4 * work, bytes_accessed=6 * width * count, transcendentals=work // 256
         ),
-    )(*places, query, key_value)
+    )(*places, query, key_value, *deps)
 
 
 def attend_back_kernel(
@@ -184,12 +346,13 @@
         query_grad[cols, :] = acc
 
 
-def attend_back(head_count, places, query, key_value, heads_back, summed, total):
+def attend_back(head_count, places, query, key_value, heads_back, summed, total, deps=()):
     blocks, both, rows = key_value.shape
     width, count = query.shape
     work = head_count * blocks * rows * count * HEAD_DIM * 2
     return pl.pallas_call(
-        partial(attend_back_kernel, head_count),
+        ordered_after(partial(attend_back_kernel, head_count), 9, deps),
+        in_specs=[IN_VMEM] * 9 + [UNREAD] * len(deps),
         out_shape=(
             jax.ShapeDtypeStruct((width, count), F32),
             jax.ShapeDtypeStruct((both, rows), F32),
@@ -200,7 +363,287 @@
         cost_estimate=pl.CostEstimate(
             flops=5 * 4 * work, bytes_accessed=16 * width * count, transcendentals=work // 128
         ),
-    )(*places, query, key_value, heads_back, summed, total)
+    )(*places, query, key_value, heads_back, summed, total, *deps)
+
+
+def sigmoid(values):
+    return 1.0 / (1.0 + jnp.exp(-values))
+
+
+def feed_kernel(
+    root_width,
+    own,
+    other,
+    up_weights,
+    gate_weights,
+    down_weights,
+    scale_up,
+    scale_gate,
+    up_out,
+    gate_out,
+    hidden_out,
+    own_out,
+    other_out,
+    total,
+):
+    half = own.shape[0]
+    rows = jnp.concatenate([own[...], other[...]], axis=0)
+    up = dot(rows, up_weights[...], (1, 1))
+    gate = dot(rows, gate_weights[...], (1, 1))
+    up_out[...] = up
+    gate_out[...] = gate
+    gate_scaled = gate * scale_gate[...] * root_width
+    hidden = (gate_scaled * sigmoid(gate_scaled) * (up * scale_up[...])).astype(LOW)
+    hidden_out[...] = hidden
+    part = dot(hidden, down_weights[...], (1, 0))
+    step = pl.program_id(0)
+
+    @pl.when(step == 0)
+    def _():
+        total[...] = part
+
+    @pl.when(step > 0)
+    def _():
+        total[...] += part
+
+    @pl.when(step == pl.num_programs(0) - 1)
+    def _():
+        own_out[...] = total[:half, :]
+        other_out[...] = total[half:, :].astype(LOW)
+
+
+def feed_forward(own, other, feed_full, scale_up, scale_gate, deps=()):
+    half, width = own.shape
+    units = feed_full[0].shape[0]
+    tile = units
+    held = pl.BlockSpec((half, width), lambda i: (0, 0))
+    weight = pl.BlockSpec((tile, width), lambda i: (i, 0))
+    scale = pl.BlockSpec((1, tile), lambda i: (0, i))
+    piece = pl.BlockSpec((2 * half, tile), lambda i: (0, i))
+    kept = jax.ShapeDtypeStruct((2 * half, units), F32)
+    return pl.pallas_call(
+        ordered_after(partial(feed_kernel, math.sqrt(width)), 7, deps),
+        grid=(units // tile,),
+        in_specs=[held, held, weight, weight, weight, scale, scale] + [UNREAD] * len(deps),
+        out_specs=[piece, piece, piece, held, held],
+        out_shape=[
+            kept,
+            kept,
+            jax.ShapeDtypeStruct((2 * half, units), LOW),
+            jax.ShapeDtypeStruct((half, width), F32),
+            jax.ShapeDtypeStruct((half, width), LOW),
+        ],
+        scratch_shapes=[pltpu.VMEM((2 * half, width), F32)],
+        compiler_params=pltpu.CompilerParams(vmem_limit_bytes=LARGE_VMEM_BYTES),
+        cost_estimate=pl.CostEstimate(
+            flops=12 * half * width * units,
+            bytes_accessed=6 * width * units + 20 * half * units + 10 * half * width,
+            transcendentals=2 * half * units,
+        ),
+    )(own, other, *feed_full, scale_up, scale_gate, *deps)
+
+
+def feed_back_kernel(
+    root_width,
+    own,
+    other,
+    up_ref,
+    gate_ref,
+    up_weights,
+    gate_weights,
+    down_weights,
+    scale_up,
+    scale_gate,
+    up_out,
+    gate_out,
+    terms_out,
+    own_out,
+    other_out,
+    total,
+):
+    half = own.shape[0]
+    rows = jnp.concatenate([own[...], other[...]], axis=0)
+    hidden_back = dot(rows, down_weights[...], (1, 1))
+    up = up_ref[...]
+    gate = gate_ref[...]
+    gate_scaled = gate * scale_gate[...] * root_width
+    sigmoid_gate = sigmoid(gate_scaled)
+    up_back = hidden_back * (gate_scaled * sigmoid_gate)
+    gate_back = (
+        hidden_back
+        * (up * scale_up[...])
+        * (sigmoid_gate * (1.0 + gate_scaled * (1.0 - sigmoid_gate)))
+    )
+    terms_out[...] = jnp.concatenate(
+        [
+            jnp.sum(up_back * up, axis=0, keepdims=True),
+            jnp.sum(gate_back * gate, axis=0, keepdims=True) * root_width,
+        ],
+        axis=0,
+    )
+    up_low = (up_back * scale_up[...]).astype(LOW)
+    gate_low = (gate_back * scale_gate[...] * root_width).astype(LOW)
+    up_out[...] = up_low
+    gate_out[...] = gate_low
+    part = dot(up_low, up_weights[...], (1, 0)) + dot(gate_low, gate_weights[...], (1, 0))
+    step = pl.program_id(0)
+
+    @pl.when(step == 0)
+    def _():
+        total[...] = part
+
+    @pl.when(step > 0)
+    def _():
+        total[...] += part
+
+    @pl.when(step == pl.num_programs(0) - 1)
+    def _():
+        own_out[...] = total[:half, :]
+        other_out[...] = total[half:, :].astype(LOW)
+
+
+def feed_backward(own, other, up, gate, feed_full, scale_up, scale_gate, deps=()):
+    half, width = own.shape
+    units = feed_full[0].shape[0]
+    tile = units
+    held = pl.BlockSpec((half, width), lambda i: (0, 0))
+    weight = pl.BlockSpec((tile, width), lambda i: (i, 0))
+    scale = pl.BlockSpec((1, tile), lambda i: (0, i))
+    piece = pl.BlockSpec((2 * half, tile), lambda i: (0, i))
+    return pl.pallas_call(
+        ordered_after(partial(feed_back_kernel, math.sqrt(width)), 9, deps),
+        grid=(units // tile,),
+        in_specs=[held, held, piece, piece, weight, weight, weight, scale, scale]
+        + [UNREAD] * len(deps),
+        out_specs=[piece, piece, pl.BlockSpec((2, tile), lambda i: (0, i)), held, held],
+        out_shape=[
+            jax.ShapeDtypeStruct((2 * half, units), LOW),
+            jax.ShapeDtypeStruct((2 * half, units), LOW),
+            jax.ShapeDtypeStruct((2, units), F32),
+            jax.ShapeDtypeStruct((half, width), F32),
+            jax.ShapeDtypeStruct((half, width), LOW),
+        ],
+        scratch_shapes=[pltpu.VMEM((2 * half, width), F32)],
+        compiler_params=pltpu.CompilerParams(vmem_limit_bytes=LARGE_VMEM_BYTES),
+        cost_estimate=pl.CostEstimate(
+            flops=12 * half * width * units,
+            bytes_accessed=6 * width * units + 24 * half * units + 10 * half * width,
+            transcendentals=2 * half * units,
+        ),
+    )(own, other, up, gate, *feed_full, scale_up, scale_gate, *deps)
+
+
+def weight_grad_kernel(count, *refs):
+    lefts, rights = refs[:count], refs[count : 3 * count]
+    own_out, other_out = refs[3 * count :]
+    part = own_out.shape[0]
+    right = jnp.concatenate([ref[...] for ref in rights], axis=0)
+    for side in range(2):
+        left = jnp.concatenate([ref[:, side * part : (side + 1) * part] for ref in lefts], axis=0)
+        total = dot(left, right, (0, 0))
+        if side == 0:
+            own_out[...] = total
+        else:
+            other_out[...] = total.astype(LOW)
+
+
+def weight_grad(lefts, rights, deps=()):
+    count = len(lefts)
+    rows, units = lefts[0].shape
+    half, width = rights[0][0].shape
+    part = units // 2
+    return pl.pallas_call(
+        ordered_after(partial(weight_grad_kernel, count), 3 * count, deps),
+        in_specs=[IN_VMEM] * (3 * count) + [UNREAD] * len(deps),
+        out_shape=[
+            jax.ShapeDtypeStruct((part, width), F32),
+            jax.ShapeDtypeStruct((part, width), LOW),
+        ],
+        compiler_params=pltpu.CompilerParams(vmem_limit_bytes=LARGE_VMEM_BYTES),
+        cost_estimate=pl.CostEstimate(
+            flops=2 * count * rows * units * width,
+            bytes_accessed=2 * count * rows * (units + width) + 3 * units * width,
+            transcendentals=0,
+        ),
+    )(*lefts, *[side for right in rights for side in right], *deps)
+
+
+def first_part(pair, partner, token, rate):
+    attention_unit, attention_norm = unit_rows(add_low(pair[...], partner[...]))
+    token_float = token[...].astype(F32)
+    after, after_norm = unit_rows(token_float + rate * (attention_unit - token_float))
+    return (attention_unit, attention_norm, token_float, after, after_norm)
+
+
+def normed_kernel(pair, partner, token, rates, normed_out):
+    normed_out[...] = first_part(pair, partner, token, rates[0:1, :])[3].astype(LOW)
+
+
+def output_kernel(
+    pair, partner, token, feed_pair, feed_partner, cotangent, rates, output_out, second_out, back_out, term_out
+):
+    after = first_part(pair, partner, token, rates[0:1, :])[3]
+    rate = rates[1:2, :]
+    feed_unit, feed_norm = unit_rows(add_low(feed_pair[...], feed_partner[...]))
+    output, output_norm = unit_rows(after + rate * (feed_unit - after))
+    output_out[...] = output
+    second_back = unit_back(output, output_norm, cotangent[...].astype(F32))
+    second_out[...] = second_back
+    back_out[...] = unit_back(feed_unit, feed_norm, second_back * rate).astype(LOW)
+    term = jnp.sum(second_back * (feed_unit - after), axis=0, keepdims=True)
+
+    @pl.when(pl.program_id(0) == 0)
+    def _():
+        term_out[...] = term
+
+    @pl.when(pl.program_id(0) > 0)
+    def _():
+        term_out[...] += term
+
+
+def first_back_kernel(
+    pair, partner, token, second, grad_pair, grad_partner, rates, skip_out, back_out, term_out
+):
+    rate = rates[0:1, :]
+    attention_unit, attention_norm, token_float, after, after_norm = first_part(
+        pair, partner, token, rate
+    )
+    after_grad = second[...] * (1.0 - rates[1:2, :]) + add_low(grad_pair[...], grad_partner[...])
+    first_back = unit_back(after, after_norm, after_grad)
+    skip_out[...] = first_back * (1.0 - rate)
+    back_out[...] = unit_back(attention_unit, attention_norm, first_back * rate).astype(LOW)
+    term = jnp.sum(first_back * (attention_unit - token_float), axis=0, keepdims=True)
+
+    @pl.when(pl.program_id(0) == 0)
+    def _():
+        term_out[...] = term
+
+    @pl.when(pl.program_id(0) > 0)
+    def _():
+        term_out[...] += term
+
+
+def rowwise(body, arrays, rates, outs, has_term, deps=()):
+    half, width = arrays[0].shape
+    tile = 128 if half % 128 == 0 else half
+    flat = pl.BlockSpec((tile, width), lambda i: (i, 0))
+    term = [pl.BlockSpec((1, width), lambda i: (0, 0))] if has_term else []
+    term_shape = [jax.ShapeDtypeStruct((1, width), F32)] if has_term else []
+    return pl.pallas_call(
+        ordered_after(body, len(arrays) + 1, deps),
+        grid=(half // tile,),
+        in_specs=[flat] * len(arrays)
+        + [pl.BlockSpec((2, width), lambda i: (0, 0))]
+        + [UNREAD] * len(deps),
+        out_specs=[flat] * len(outs) + term,
+        out_shape=[jax.ShapeDtypeStruct((half, width), kind) for kind in outs] + term_shape,
+        compiler_params=pltpu.CompilerParams(vmem_limit_bytes=VMEM_BYTES),
+        cost_estimate=pl.CostEstimate(
+            flops=40 * half * width,
+            bytes_accessed=(2 * len(arrays) + 4 * len(outs)) * half * width,
+            transcendentals=4 * half,
+        ),
+    )(*arrays, rates, *deps)
 
 
 def adam_step(master, gradient, first_state, second_state, step_rate, is_matrix):
@@ -228,9 +671,9 @@
     return rows
 
 
-def adam_kernel(has_partner, offset, own, partner, master, first, second, *rest):
+def adam_kernel(has_partner, chunks, offset, own, partner, master, first, second, *rest):
     del offset
-    gradient_out, moment_out, variance_out, shift_out = rest[-4:]
+    gradient_out, moment_out, variance_out = rest[-3 - chunks : -chunks]
     gradient = own[...]
     if has_partner:
         gradient = gradient + partner[...].astype(F32)
@@ -240,13 +683,20 @@
     gradient_out[0, 0] = gradient
     moment_out[0, 0] = moment
     variance_out[0, 0] = variance
-    shift_out[...] = (master[0] - updated).astype(LOW)
-
-
-def adam_slab(which, own_block, gradient, partner, master, first, second, earlier):
+    shift = (master[0] - updated).astype(LOW)
+    each = pl.num_programs(0) // chunks
+    for n in range(chunks):
+
+        @pl.when(pl.program_id(0) // each == n)
+        def _(n=n):
+            rest[n - chunks][...] = shift
+
+
+def adam_slab(which, chunks, own_block, gradient, partner, master, first, second, earlier, deps=()):
     slabs, rows, width = master.shape
     tile = row_tile(rows)
     steps = rows // tile
+    each = steps // chunks
     has_partner = partner is not None
     if not has_partner:
         partner = jnp.zeros((tile, width), LOW)
@@ -257,22 +707,27 @@
     grouped = pl.BlockSpec((1, 1, tile, width), lambda i, at: (0, which, i, 0))
     whole = jax.ShapeDtypeStruct((1, slabs, rows, width), F32)
     earlier = () if earlier is None else earlier
+    pieces = [
+        pl.BlockSpec((tile, width), lambda i, at, n=n: (jnp.clip(i - n * each, 0, each - 1), 0))
+        for n in range(chunks)
+    ]
     return pl.pallas_call(
-        partial(adam_kernel, has_partner),
+        partial(adam_kernel, has_partner, chunks),
         grid_spec=pltpu.PrefetchScalarGridSpec(
             num_scalar_prefetch=1,
             grid=(steps,),
             in_specs=[held, flat if has_partner else once, slab, grouped, grouped]
-            + [pl.BlockSpec(memory_space=pl.ANY)] * len(earlier),
-            out_specs=[grouped, grouped, grouped, flat],
-        ),
-        out_shape=[whole, whole, whole, jax.ShapeDtypeStruct((rows, width), LOW)],
+            + [UNREAD] * (len(earlier) + len(deps)),
+            out_specs=[grouped, grouped, grouped] + pieces,
+        ),
+        out_shape=[whole, whole, whole]
+        + [jax.ShapeDtypeStruct((rows // chunks, width), LOW)] * chunks,
         input_output_aliases={6 + n: n for n in range(len(earlier))},
         compiler_params=pltpu.CompilerParams(vmem_limit_bytes=VMEM_BYTES),
         cost_estimate=pl.CostEstimate(
             flops=30 * rows * width, bytes_accessed=32 * rows * width, transcendentals=rows * width
         ),
-    )(own_block, gradient, partner, master, first, second, *earlier)
+    )(own_block, gradient, partner, master, first, second, *earlier, *deps)
 
 
 def outer_kernel(group_count, at_end, whole, back, master, outer, *rest):
@@ -283,29 +738,72 @@
     result_out[0] = result
 
 
-def outer_slab(which, group_count, at_end, whole, back, master, outer, earlier):
+def outer_slab(which, chunk, group_count, at_end, whole, back, master, outer, earlier, deps=()):
     slabs, rows, width = master.shape
-    tile = row_tile(rows)
+    part = whole.shape[0]
+    tile = row_tile(part)
+    steps = part // tile
     flat = pl.BlockSpec((tile, width), lambda i, at: (i, 0))
-    slab = pl.BlockSpec((1, tile, width), lambda i, at: (which, i, 0))
+    slab = pl.BlockSpec((1, tile, width), lambda i, at: (which, chunk * steps + i, 0))
     result = jax.ShapeDtypeStruct((slabs, rows, width), F32)
     earlier = () if earlier is None else earlier
     return pl.pallas_call(
         partial(outer_kernel, group_count),
         grid_spec=pltpu.PrefetchScalarGridSpec(
             num_scalar_prefetch=1,
-            grid=(rows // tile,),
-            in_specs=[flat, flat, slab, slab]
-            + [pl.BlockSpec(memory_space=pl.ANY)] * len(earlier),
+            grid=(steps,),
+            in_specs=[flat, flat, slab, slab] + [UNREAD] * (len(earlier) + len(deps)),
             out_specs=[slab, slab],
         ),
         out_shape=[result, result],
         input_output_aliases={5 + n: n for n in range(len(earlier))},
         compiler_params=pltpu.CompilerParams(vmem_limit_bytes=VMEM_BYTES),
         cost_estimate=pl.CostEstimate(
-            flops=20 * rows * width, bytes_accessed=20 * rows * width, transcendentals=rows
-        ),
-    )(at_end, whole, back, master, outer, *earlier)
+            flops=20 * part * width, bytes_accessed=20 * part * width, transcendentals=part
+        ),
+    )(at_end, whole, back, master, outer, *earlier, *deps)
+
+
+class MatrixSteps:
+    def __init__(self, chunks, at_end, master, first, second, outer):
+        self.chunks = chunks
+        self.at_end = at_end.reshape(1)
+        self.arrays = (master, first, second)
+        self.outer_state = outer
+        self.inner_outs = None
+        self.sums = {}
+
+    def inner(self, which, gradient, deps):
+        own, partner, block = gradient
+        outs = adam_slab(
+            which, self.chunks, block, own, partner, *self.arrays, self.inner_outs, deps
+        )
+        self.inner_outs = outs[:3]
+        self.sums[which] = [group_sum(shift) for shift in outs[3:]]
+        return outs[3]
+
+    def pairs(self, which):
+        return [step[0] for step in self.sums[which]]
+
+    def wholes(self, which):
+        return [step[1] for step in self.sums[which]]
+
+    def outer(self):
+        outs = None
+        for which, chunk_sums in self.sums.items():
+            for chunk, (_, whole, back) in enumerate(chunk_sums):
+                outs = outer_slab(
+                    which,
+                    chunk,
+                    lax.axis_size("group"),
+                    self.at_end,
+                    whole,
+                    back,
+                    self.arrays[0],
+                    self.outer_state,
+                    outs,
+                )
+        return (*self.inner_outs, *outs)
 
 
 def place_kernel(core, own, other, *rest):
@@ -320,7 +818,7 @@
         out[0, 0] = other[...]
 
 
-def place_rows(which, count, core, own, other, earlier):
+def place_rows(which, count, core, own, other, earlier, deps=()):
     half, width = own.shape
     held = pl.BlockSpec((half, width), lambda i, at: (0, 0))
     earlier = () if earlier is None else (earlier,)
@@ -329,7 +827,7 @@
         grid_spec=pltpu.PrefetchScalarGridSpec(
             num_scalar_prefetch=1,
             grid=(2,),
-            in_specs=[held, held] + [pl.BlockSpec(memory_space=pl.ANY)] * len(earlier),
+            in_specs=[held, held] + [UNREAD] * (len(earlier) + len(deps)),
             out_specs=pl.BlockSpec(
                 (1, 1, half, width), lambda i, at: (0, which, lax.rem(at[0] + i, 2), 0)
             ),
@@ -340,7 +838,7 @@
         cost_estimate=pl.CostEstimate(
             flops=0, bytes_accessed=16 * half * width, transcendentals=0
         ),
-    )(core, own, other, *earlier)
+    )(core, own, other, *earlier, *deps)
 
 
 def on_device(
@@ -387,6 +885,8 @@
     core_first = core_index[0] == 0
     even_group = lax.rem(lax.axis_index("group"), 2) == 0
     micros = range(micro_count)
+    at_end = lax.axis_index("group")
+    at_end = ((at_end == 0) | (at_end == group_count - 1)).astype(jnp.int32)
 
     attention_low = attention_weights.astype(LOW)
     feed_low = feedforward_weights.astype(LOW)
@@ -395,7 +895,10 @@
     ).astype(LOW)
     own_cols = residual_rates.shape[1]
     if pair:
-        triple_other = trade(attention_low[:3], "ctx", 1)
+        part = own_rows // 2
+        piece = jnp.where(even_group, attention_low[:3, :part], attention_low[:3, part:])
+        triple_across = trade(piece, "ctx", 1)
+        triple_other = ordered(even_group, triple_across, trade(triple_across, "group", 1), 1)
         triple_weights = ordered(ctx_first, attention_low[:3], triple_other, 1)
         small_other = trade(small_low, "ctx", 1)
         cuts = [own_rows, own_units, own_units, own_cols, own_cols]
@@ -420,12 +923,11 @@
             residual_rates.astype(LOW), "ctx", axis=1, tiled=True
         ).astype(F32)
     triple_weights = triple_weights.reshape(3 * head_width, model_width)
-    scale_column = scale_heads.reshape(head_count, HEAD_DIM, 1)
+    scale_column = scale_heads.reshape(head_width, 1)
 
     token_halves = tokens[0].reshape(micro_count, 2, half, model_width)
     token_own = jnp.where(core_first, token_halves[:, 0], token_halves[:, 1])
     token_other = jnp.where(core_first, token_halves[:, 1], token_halves[:, 0])
-    token_rows = jnp.concatenate([token_own, token_other], axis=1)
     cotangent_halves = cotangent[0].reshape(micro_count, 2, half, model_width)
     cotangent_own = jnp.where(core_first, cotangent_halves[:, 0], cotangent_halves[:, 1])
 
@@ -462,142 +964,152 @@
         for b in micros
     ]
 
-    queries, key_values = [], []
-    query_low = []
-    query_units, query_norms, key_units, key_norms = [], [], [], []
-    for b in micros:
-        projected = dot(triple_weights, token_rows[b], (1, 1)).reshape(
-            3, head_count, HEAD_DIM, rows
-        )
-        query_unit, query_norm = unit_rows(projected[0], axis=1)
-        key_unit, key_norm = unit_rows(projected[1], axis=1)
-        query_units.append(query_unit)
-        query_norms.append(query_norm)
-        key_units.append(key_unit)
-        key_norms.append(key_norm)
-        query_low.append(
-            (query_unit * scale_column * root_head).astype(LOW).reshape(head_width, rows)
-        )
-        key_value = jnp.concatenate(
-            [
-                (key_unit * scale_column).astype(LOW).reshape(head_width, rows),
-                projected[2].astype(LOW).reshape(head_width, rows),
-            ],
-            axis=0,
-        )
-        if pair:
-            key_values.append(jnp.stack([key_value, trade(key_value, "ctx", 1)]))
-        else:
-            gathered = lax.all_gather(key_value, "ctx", axis=0)
-            key_values.append(jnp.take(gathered, block_ids, axis=0))
-
     if pair:
-        output_source, feed_source, _ = lax.optimization_barrier(
-            (attention_low[3], feed_low, key_values[-1])
-        )
-        output_weights = ordered(ctx_first, output_source, trade(output_source, "ctx", 1), 0)
-        part = own_units // 2
+        arrivals = []
+        before = triple_across
         feed_full = []
-        for which in (0, 1, 2):
-            source = feed_source[which]
-            piece = jnp.where(even_group, source[:part], source[part:])
+        for which in range(3):
+            source = feed_low[which]
+            part = own_units // 2
+            piece = tie(jnp.where(even_group, source[:part], source[part:]), before)
             across = trade(piece, "ctx", 1)
+            before = across
+            arrivals.append(across)
             along = trade(across, "group", 1)
             feed_full.append(
                 jnp.concatenate([source, ordered(even_group, across, along, 0)], axis=0)
             )
+        part = own_rows // 2
+        piece = tie(
+            jnp.where(even_group, attention_low[3, :part], attention_low[3, part:]), triple_across
+        )
+        across = trade(piece, "ctx", 1)
+        output_other = ordered(even_group, across, trade(across, "group", 1), 0)
+        output_weights = ordered(ctx_first, attention_low[3], output_other, 0)
     else:
         output_weights = lax.all_gather(attention_low[3], "ctx", axis=0, tiled=True)
         feed_full = list(lax.all_gather(feed_low, "ctx", axis=1, tiled=True))
+        arrivals = []
     up_weights, gate_weights, down_weights = feed_full
 
-    summeds, totals, heads_lows = [], [], []
-    attention_units, attention_norms, afters, after_norms, normed_rows = [], [], [], [], []
+    projections, query_low, key_values = [], [], []
     for b in micros:
-        summed, total, heads_low = attend(head_count, places[b], query_low[b], key_values[b])
+        projected, query, key_value = project(
+            head_count,
+            triple_weights,
+            token_own[b],
+            token_other[b],
+            scale_column,
+            projections[-1:],
+        )
+        projections.append(projected)
+        query_low.append(query)
+        if pair:
+            sent = tie(key_value, arrivals[0]) if b == 0 else key_value
+            key_values.append(jnp.stack([key_value, trade(sent, "ctx", 1)]))
+        else:
+            gathered = lax.all_gather(key_value, "ctx", axis=0)
+            key_values.append(jnp.take(gathered, block_ids, axis=0))
+
+    rates_both = jnp.stack([rate_attention, rate_feed])
+    scale_up = scale_up.reshape(1, units)
+    scale_gate = scale_gate.reshape(1, units)
+    summeds, totals, heads_lows, attention_sums, normed_rows = [], [], [], [], []
+
+    def normed_part(b, deps):
+        (normed_low,) = rowwise(
+            normed_kernel, attention_sums[b], rates_both, [LOW], False, deps
+        )
+        normed_rows.append((normed_low, trade(normed_low, "tensor", 1)))
+
+    for b in micros:
+        deps = totals[-1:] + arrivals[1:2] * (b == 0)
+        if b == micro_count - 1 and b > 1:
+            normed_part(0, totals[-1:])
+            deps = [normed_rows[0][0]] + arrivals[2:]
+        summed, total, heads_low = attend(
+            head_count, places[b], query_low[b], key_values[b], deps
+        )
         summeds.append(summed)
         totals.append(total)
         heads_lows.append(heads_low)
         other_part = dot(heads_low[:, half:], output_weights, (0, 0), LOW)
         own_part = dot(heads_low[:, :half], output_weights, (0, 0))
-        attention_unit, attention_norm = unit_rows(tensor_sum(own_part, other_part))
-        token_float = token_own[b].astype(F32)
-        after, after_norm = unit_rows(
-            token_float + rate_attention * (attention_unit - token_float)
-        )
-        attention_units.append(attention_unit)
-        attention_norms.append(attention_norm)
-        afters.append(after)
-        after_norms.append(after_norm)
-        normed_low = split_low(after)
-        normed_rows.append(
-            jnp.concatenate([normed_low, trade(normed_low, "tensor", 1)], axis=0)
-        )
-
-    ups, gates, hidden_rows = [], [], []
-    second_backs, feed_back_rows = [], []
-    block_output = None
-    feed_rate_term = jnp.zeros((model_width,), F32)
+        attention_sums.append((*tensor_sum(own_part, other_part), token_own[b]))
+    for b in micros[len(normed_rows) :]:
+        normed_part(b, [rows_of[0] for rows_of in normed_rows[-1:]] + totals[-1:])
+
+    ups, gates, hidden_rows, feed_parts = [], [], [], []
     for b in micros:
-        up = dot(normed_rows[b], up_weights, (1, 1))
-        gate = dot(normed_rows[b], gate_weights, (1, 1))
+        up, gate, hidden, own_part, other_part = feed_forward(
+            *normed_rows[b],
+            feed_full,
+            scale_up,
+            scale_gate,
+            [normed_rows[-1][0] if b == 0 else feed_parts[-1][1]],
+        )
         ups.append(up)
         gates.append(gate)
-        gate_scaled = gate * scale_gate * root_width
-        hidden = (gate_scaled * jax.nn.sigmoid(gate_scaled) * (up * scale_up)).astype(LOW)
         hidden_rows.append(hidden)
-        other_part = dot(hidden[half:], down_weights, (1, 0), LOW)
-        own_part = dot(hidden[:half], down_weights, (1, 0))
-        feed_unit, feed_norm = unit_rows(tensor_sum(own_part, other_part))
-        output, output_norm = unit_rows(afters[b] + rate_feed * (feed_unit - afters[b]))
-        second_back = unit_back(output, output_norm, cotangent_own[b].astype(F32))
-        feed_rate_term = feed_rate_term + jnp.sum(second_back * (feed_unit - afters[b]), axis=0)
-        feed_back = split_low(unit_back(feed_unit, feed_norm, second_back * rate_feed))
+        feed_parts.append((own_part, other_part))
+
+    outputs, second_backs, feed_back_rows, feed_rate_terms = [], [], [], []
+    up_back_rows, gate_back_rows, hidden_terms, grad_sums = [], [], [], []
+    skips, attention_back_rows, attention_rate_terms = [], [], []
+    attention_grads = []
+    down_grad = None
+
+    def output_part(b, deps):
+        output, second_back, feed_back, term = rowwise(
+            output_kernel,
+            (*attention_sums[b], *tensor_sum(*feed_parts[b]), cotangent_own[b]),
+            rates_both,
+            [F32, F32, LOW],
+            True,
+            deps,
+        )
+        outputs.append(output)
         second_backs.append(second_back)
-        feed_back_rows.append(jnp.concatenate([feed_back, trade(feed_back, "tensor", 1)], axis=0))
-        block_output = place_rows(
-            b, micro_count, core_index, output, trade(output, "tensor", 1), block_output
-        )
-
-    up_back_rows, gate_back_rows = [], []
-    first_backs, attention_back_rows = [], []
-    up_terms = jnp.zeros((units,), F32)
-    gate_terms = jnp.zeros((units,), F32)
-    attention_rate_term = jnp.zeros((model_width,), F32)
-    for b in micros:
-        hidden_back = dot(feed_back_rows[b], down_weights, (1, 1))
-        gate_scaled = gates[b] * scale_gate * root_width
-        sigmoid_gate = jax.nn.sigmoid(gate_scaled)
-        up_back = hidden_back * gate_scaled * sigmoid_gate
-        gate_back = (
-            hidden_back
-            * (ups[b] * scale_up)
-            * sigmoid_gate
-            * (1.0 + gate_scaled * (1.0 - sigmoid_gate))
-        )
-        up_terms = up_terms + jnp.sum(up_back * ups[b], axis=0)
-        gate_terms = gate_terms + jnp.sum(gate_back * gates[b] * root_width, axis=0)
-        up_low = (up_back * scale_up).astype(LOW)
-        gate_low = (gate_back * scale_gate * root_width).astype(LOW)
+        feed_rate_terms.append(term)
+        feed_back_rows.append((feed_back, trade(feed_back, "tensor", 1)))
+
+    def feed_part_back(b, deps):
+        up_low, gate_low, terms, own_part, other_part = feed_backward(
+            *feed_back_rows[b], ups[b], gates[b], feed_full, scale_up, scale_gate, deps
+        )
         up_back_rows.append(up_low)
         gate_back_rows.append(gate_low)
-        other_part = (
-            dot(up_low[half:], up_weights, (1, 0)) + dot(gate_low[half:], gate_weights, (1, 0))
-        ).astype(LOW)
-        own_part = dot(up_low[:half], up_weights, (1, 0)) + dot(
-            gate_low[:half], gate_weights, (1, 0)
-        )
-        after_grad = second_backs[b] * (1.0 - rate_feed) + tensor_sum(own_part, other_part)
-        first_back = unit_back(afters[b], after_norms[b], after_grad)
-        first_backs.append(first_back)
-        attention_rate_term = attention_rate_term + jnp.sum(
-            first_back * (attention_units[b] - token_own[b].astype(F32)), axis=0
-        )
-        attention_back = split_low(
-            unit_back(attention_units[b], attention_norms[b], first_back * rate_attention)
-        )
+        hidden_terms.append(terms)
+        grad_sums.append(tensor_sum(own_part, other_part))
+
+    def first_part_back(b, deps):
+        skip, attention_back, term = rowwise(
+            first_back_kernel,
+            (*attention_sums[b], second_backs[b], *grad_sums[b]),
+            rates_both,
+            [F32, LOW],
+            True,
+            deps,
+        )
+        skips.append(skip)
+        attention_rate_terms.append(term)
         attention_back_rows.append(
             jnp.concatenate([attention_back, trade(attention_back, "tensor", 1)], axis=0)
+        )
+
+    def attention_part_back(b, deps):
+        heads_back = dot(output_weights, attention_back_rows[b], (1, 1), LOW)
+        attention_grads.append(
+            attend_back(
+                head_count,
+                places[b],
+                query_low[b],
+                key_values[b],
+                heads_back,
+                summeds[b],
+                totals[b],
+                deps,
+            )
         )
 
     def to_owner(gradient, in_order):
@@ -612,74 +1124,121 @@
             block = me.reshape(1)
         return (gradient, trade(other.astype(LOW), "ctx", 1), block)
 
-    normed_all = jnp.concatenate(normed_rows, axis=0)
-    down_grad = to_owner(
-        dot(
-            jnp.concatenate(hidden_rows, axis=0), jnp.concatenate(feed_back_rows, axis=0), (0, 0)
-        ),
-        False,
-    )
-    up_grad = to_owner(dot(jnp.concatenate(up_back_rows, axis=0), normed_all, (0, 0)), False)
-    gate_grad = to_owner(dot(jnp.concatenate(gate_back_rows, axis=0), normed_all, (0, 0)), False)
+    def feed_gradient(lefts, rights, deps, hold=()):
+        if not pair:
+            right = jnp.concatenate([side for entry in rights for side in entry], axis=0)
+            grad = to_owner(dot(jnp.concatenate(lefts, axis=0), right, (0, 0)), False)
+            return (grad, grad[0])
+        own, other = weight_grad(lefts, rights, deps)
+        sent = tie(other, *hold) if hold else other
+        return ((own, trade(sent, "ctx", 1), jnp.zeros((1,), jnp.int32)), own)
+
+    triples, head_terms, input_sums = [], [], []
+
+    def sides_part_back(b, deps):
+        query_grad, own_grad, other_grad = attention_grads[b]
+        arrived = None
+        if pair:
+            arrived = side_arrivals[b]
+        else:
+            sides = jnp.concatenate([own_grad[None], other_grad], axis=0)
+            sides = jnp.take(sides, lax.rem(table - me + ctx_count, ctx_count), axis=0)
+            own_grad = lax.psum_scatter(sides, "ctx", scatter_dimension=0)
+        triple, terms = sides_back(
+            head_count, own_grad, arrived, query_grad, projections[b], scale_column, deps
+        )
+        triples.append(triple)
+        head_terms.append(terms)
+        other_part = dot(triple[:, half:], triple_weights, (0, 0), LOW)
+        own_part = dot(triple[:, :half], triple_weights, (0, 0))
+        input_sums.append(tensor_sum(own_part, other_part))
+
+    last = micro_count - 1
+    tag = feed_parts[-1][1]
+    for b in micros:
+        output_part(b, [tag])
+        if b == last:
+            down_grad, tag = feed_gradient(hidden_rows, feed_back_rows, [])
+            first_part_back(0, [tag])
+            tag = attention_rate_terms[0]
+        feed_part_back(b, [tag])
+        tag = hidden_terms[b]
+    up_grad, tag = feed_gradient(up_back_rows, normed_rows, [tag])
+    feed_steps = MatrixSteps(
+        2 if own_units % 320 == 0 else 1,
+        at_end,
+        feedforward_weights,
+        feedforward_first,
+        feedforward_second,
+        feedforward_outer,
+    )
+    side_arrivals = []
+
+    def send_sides(b):
+        if pair:
+            side_arrivals.append(trade(attention_grads[b][2][0], "ctx", 1))
+
+    token_halves_of = [(token_own[b], token_other[b]) for b in micros]
+    arrived_down = [down_grad[1]] if pair else []
+    attention_part_back(0, [tag] + arrived_down)
+    send_sides(0)
+    first_part_back(1, [attention_grads[0][0]])
+    attention_part_back(1, [attention_rate_terms[1]])
+    send_sides(1)
+    tag = feed_steps.inner(2, down_grad, [attention_grads[1][0]])
+    sides_part_back(0, [tag])
+    for b in micros[2:]:
+        first_part_back(b, [head_terms[-1]])
+        attention_part_back(b, [attention_rate_terms[b]])
+        send_sides(b)
+        sides_part_back(b - 1, [attention_grads[b][0]])
     output_grad = to_owner(
         dot(
             jnp.concatenate(heads_lows, axis=1), jnp.concatenate(attention_back_rows, axis=0), (1, 0)
         ),
         True,
     )
-
-    triples = []
-    input_gradient = None
-    head_terms = jnp.zeros((head_count, HEAD_DIM), F32)
+    gate_grad, gate_tag = feed_gradient(
+        gate_back_rows,
+        normed_rows,
+        [head_terms[-1]] + feed_steps.pairs(2)[:1],
+        side_arrivals[-1:],
+    )
+    tag = feed_steps.inner(0, up_grad, [gate_tag] + feed_steps.pairs(2))
+    sides_part_back(last, [tag])
+    if pair:
+        own, *others = triple_grad(
+            me.reshape(1), 3, triples, token_halves_of, feed_steps.wholes(2)[:1]
+        )
+        tag = own
+        projection_grads = [
+            (own, trade(others[which], "ctx", 1), jnp.full((1,), which, jnp.int32))
+            for which in range(3)
+        ]
+    else:
+        triple_all = dot(
+            jnp.concatenate(triples, axis=1),
+            jnp.concatenate([side for sides in token_halves_of for side in sides], axis=0),
+            (1, 0),
+        ).reshape(3, head_width, model_width)
+        projection_grads = [to_owner(triple_all[which], True) for which in range(3)]
+
+    block_output = None
     for b in micros:
-        heads_back = dot(output_weights, attention_back_rows[b], (1, 1), LOW)
-        query_grad, own_grad, other_grad = attend_back(
-            head_count, places[b], query_low[b], key_values[b], heads_back, summeds[b], totals[b]
-        )
-        if pair:
-            side_grad = own_grad + trade(other_grad[0], "ctx", 1).astype(F32)
-        else:
-            sides = jnp.concatenate([own_grad[None], other_grad], axis=0)
-            sides = jnp.take(sides, lax.rem(table - me + ctx_count, ctx_count), axis=0)
-            side_grad = lax.psum_scatter(sides, "ctx", scatter_dimension=0)
-        query_grad = query_grad.reshape(head_count, HEAD_DIM, rows)
-        key_grad = side_grad[:head_width].reshape(head_count, HEAD_DIM, rows)
-        head_terms = head_terms + jnp.sum(
-            query_grad * query_units[b] * root_head + key_grad * key_units[b], axis=2
-        )
-        triple = jnp.concatenate(
-            [
-                unit_back(
-                    query_units[b], query_norms[b], query_grad * scale_column * root_head, axis=1
-                ).reshape(head_width, rows),
-                unit_back(key_units[b], key_norms[b], key_grad * scale_column, axis=1).reshape(
-                    head_width, rows
-                ),
-                side_grad[head_width:],
-            ],
-            axis=0,
-        ).astype(LOW)
-        triples.append(triple)
-        other_part = dot(triple[:, half:], triple_weights, (0, 0), LOW)
-        own_part = dot(triple[:, :half], triple_weights, (0, 0))
-        input_own = first_backs[b] * (1.0 - rate_attention) + tensor_sum(own_part, other_part)
-        input_gradient = place_rows(
-            b, micro_count, core_index, input_own, trade(input_own, "tensor", 1), input_gradient
-        )
-
-    triple_grad = dot(
-        jnp.concatenate(triples, axis=1),
-        token_rows.reshape(micro_count * rows, model_width),
-        (1, 0),
-    ).reshape(3, head_width, model_width)
-    attention_grads = [to_owner(triple_grad[which], True) for which in range(3)] + [output_grad]
-    feed_grads = [up_grad, gate_grad, down_grad]
-
-    rate_terms = jnp.concatenate([attention_rate_term, feed_rate_term])
+        block_output = place_rows(
+            b,
+            micro_count,
+            core_index,
+            outputs[b],
+            trade(outputs[b], "tensor", 1),
+            block_output,
+            [tag],
+        )
+
+    rate_terms = jnp.concatenate([sum(attention_rate_terms), sum(feed_rate_terms)], axis=0)
     rate_terms = rate_terms + trade(rate_terms, "tensor", 1)
-    rate_terms = rate_terms.reshape(2, model_width)
-    head_terms = head_terms.reshape(head_width)
-    hidden_terms = jnp.stack([up_terms, gate_terms])
+    head_terms = sum(head_terms).reshape(head_width)
+    hidden_terms = sum(hidden_terms)
     if pair:
         heads_own = jnp.where(ctx_first, head_terms[:own_rows], head_terms[own_rows:])
         heads_other = jnp.where(ctx_first, head_terms[own_rows:], head_terms[:own_rows])
@@ -699,28 +1258,31 @@
         hidden_grad = lax.psum_scatter(hidden_terms, "ctx", scatter_dimension=1, tiled=True)
         rates_grad = lax.psum_scatter(rate_terms, "ctx", scatter_dimension=1, tiled=True)
 
-    at_end = lax.axis_index("group")
-    at_end = ((at_end == 0) | (at_end == group_count - 1)).astype(jnp.int32)
-
-    def matrix_steps(order, gradients, masters, firsts, seconds, outers):
-        adam_outs, outer_outs = None, None
-        for which in order:
-            gradient, partner, block = gradients[which]
-            *adam_outs, shift = adam_slab(
-                which, block, gradient, partner, masters, firsts, seconds, adam_outs
-            )
-            whole, back = group_sum(shift)
-            outer_outs = outer_slab(
-                which, group_count, at_end.reshape(1), whole, back, masters, outers, outer_outs
-            )
-        return (*adam_outs, *outer_outs)
-
-    feed_outs = matrix_steps(
-        (2, 0, 1), feed_grads, feedforward_weights, feedforward_first, feedforward_second, feedforward_outer
-    )
-    attention_outs = matrix_steps(
-        (3, 0, 1, 2), attention_grads, attention_weights, attention_first, attention_second, attention_outer
-    )
+    attention_steps = MatrixSteps(
+        1,
+        at_end,
+        attention_weights,
+        attention_first,
+        attention_second,
+        attention_outer,
+    )
+    attention_steps.inner(3, output_grad, [tag])
+    input_gradient = None
+    arrived_inputs = [sums[1] for sums in input_sums]
+    feed_steps.inner(1, gate_grad, feed_steps.pairs(0) + arrived_inputs[:2])
+    for which in range(3):
+        attention_steps.inner(
+            which,
+            projection_grads[which],
+            feed_steps.wholes(0) + arrived_inputs[2:] if which == 0 else [],
+        )
+    for b in micros:
+        input_own = skips[b] + add_low(*input_sums[b])
+        input_gradient = place_rows(
+            b, micro_count, core_index, input_own, trade(input_own, "tensor", 1), input_gradient
+        )
+    feed_outs = feed_steps.outer()
+    attention_outs = attention_steps.outer()
 
     masters = (head_scales, hidden_scales, residual_rates)
     firsts = (heads_first[0], hidden_first[0], rates_first[0])
@@ -740,7 +1302,7 @@
         small_moments.append(moment)
         small_variances.append(variance)
         small_shifts.append((masters[which] - updated).reshape(-1))
-    whole, back = group_sum(jnp.concatenate(small_shifts))
+    _, whole, back = group_sum(jnp.concatenate(small_shifts))
     shift_flat = jnp.where(at_end == 1, back, whole) / group_count
     small_momenta, small_results = [], []
     start = 0

time: 863 us -> 815 us (0.944)
  Pallas kernels: 116 us -> 266 us
  waiting for transfers between devices: 391 us -> 250 us
  matrix products: 115 us -> 27.4 us
  starting transfers between devices: 81.2 us -> 130 us
  other arithmetic: 81.9 us -> 69.3 us
    pallas_call x13 -> x44, Pallas kernels: 73.7 us -> 220 us  [the longest x7 43.3 us: adam_slab(): pl.pallas_call(partial(adam_kernel, has_partner, chunks), grid_spec=pltpu...]
    ppermute x63 -> x65, waiting for transfers between devices: 233 us -> 131 us  [trade(): return lax.ppermute(values, axis, [(i, i ^ bit) for i in range(count)])]
    dot_general x50 -> x16, matrix products: 115 us -> 27.4 us  [dot(): lax.dot_general(left, right, (((contract[0],), (contract[1],)), ((), ()))...]
    ppermute x8 -> x11, waiting for transfers between devices: 130 us -> 82.3 us  [group_sum(): back = lax.ppermute(whole, 'group', [(1, 0), (2, 3)])]
    ppermute x8 -> x11, starting transfers between devices: 20.5 us -> 58.3 us  [group_sum(): lax.ppermute(values, 'group', [(0, 1), (3, 2)])]
    reduce_sum x22 -> x0, other arithmetic: 15.8 us -> none  [the longest x14 5.12 us: unit_rows(): jnp.sum(values * values, axis=axis, keepdims=True) + EPSILON]
    slice x20 -> x1, local copies, waits for them, and re-layouts: 8.88 us -> 0.01 us  [on_device(): hidden_terms[:, own_units:].reshape(-1)]
    ppermute x8 -> x11, waiting for transfers between devices: 28.5 us -> 36.4 us  [group_sum(): lax.ppermute(values, 'group', [(0, 1), (3, 2)])]
  transfers between devices with their start and end apart: 87 -> 98, of which waited for: 36 -> 32; matrix products, arithmetic and copies ran while one was open for 17% -> 15% of each run, Pallas kernels for 13% -> 33%
where the time goes in v3:
time: 815 us; the launch traced here: 808 us
  Pallas kernels  266 us (33%)
  waiting for transfers between devices  250 us (31%)
  starting transfers between devices  130 us (16%)
  other arithmetic  69.3 us (9%)
  local copies, waits for them, and re-layouts  61.5 us (8%)
  matrix products  27.4 us (3%)
    ppermute x65, waiting for transfers between devices, trade(): return lax.ppermute(values, axis, [(i, i ^ bit) for i in range(count)])  131 us
    ppermute x11, waiting for transfers between devices, group_sum(): back = lax.ppermute(whole, 'group', [(1, 0), (2, 3)])  82.3 us
    ppermute x11, starting transfers between devices, group_sum(): lax.ppermute(values, 'group', [(0, 1), (3, 2)])  58.3 us
    unnamed x461, local copies, waits for them, and re-layouts  49.1 us
    ppermute x65, starting transfers between devices, trade(): return lax.ppermute(values, axis, [(i, i ^ bit) for i in range(count)])  48.1 us
    pallas_call x7, Pallas kernels, adam_slab(): pl.pallas_call(partial(adam_kernel, has_partner, chunks), grid_spec=pltpu...  43.3 us
    pallas_call x3, Pallas kernels, feed_backward(): pl.pallas_call(ordered_after(partial(feed_back_kernel, math.sqrt(width)),...  41.2 us
    ppermute x11, waiting for transfers between devices, group_sum(): lax.ppermute(values, 'group', [(0, 1), (3, 2)])  36.4 us
  transfers between devices with their start and end apart: 98, of which 32 were waited for; matrix products, arithmetic and copies ran while one was open for 15% of the time, Pallas kernels for 33%

profile of v3, /device:TPU:0, one launch (start us, length us, event | category | flops | bytes accessed | tf_op | source)
XLA Modules:
  0.0 808.2 jit_solution(4842527729200656255)
XLA Ops:
  8.3 4.3 convert_element_type.321
  31.6 10.7 %collective-permute-done.1 = bf16[3,80,1280]{2,1,0:T(8,128)(2,1)S(1)} collective-permute-done((bf16[3,80,1280]{2,1,0:T(8,128)(2,1)S(1)}, bf16[3,80,1280]{2,1,0:T(8,128)(2,1)S(1)}, u32[]{:S(2)}, u32[]{:S(2)}) %collective-permute-start.1) | collective-permute-done | bytes 614432 | tf_op jit(solution)/shard_map/ppermute | solution.py:53
  66.4 5.4 collective-permute-done.3
  74.3 11.6 %collective-permute-done.11 = bf16[640,512]{1,0:T(8,128)(2,1)} collective-permute-done((bf16[640,512]{1,0:T(8,128)(2,1)}, bf16[640,512]{1,0:T(8,128)(2,1)}, u32[]{:S(2)}, u32[]{:S(2)}) %collective-permute-start.11) | collective-permute-done | bytes 655392 | tf_op jit(solution)/shard_map/ppermute | solution.py:53
  88.4 11.6 %collective-permute-done.5 = bf16[640,512]{1,0:T(8,128)(2,1)} collective-permute-done((bf16[640,512]{1,0:T(8,128)(2,1)}, bf16[640,512]{1,0:T(8,128)(2,1)}, u32[]{:S(2)}, u32[]{:S(2)}) %collective-permute-start.5) | collective-permute-done | bytes 655392 | tf_op jit(solution)/shard_map/ppermute | solution.py:53
  101.2 13.9 %collective-permute-done.6.refs_6_.refs_1_ = bf16[320,1280]{1,0:T(8,128)(2,1)S(1)} collective-permute-done((bf16[320,1280]{1,0:T(8,128)(2,1)}, bf16[320,1280]{1,0:T(8,128)(2,1)S(1)}, u32[]{:S(2)}, u32[]{:S(2)}) %collective-permute-start.6) | collective-permute-done | bytes 819232 | tf_op jit(solution)/shard_map/ppermute | solution.py:53
  142.2 9.4 %collective-permute-done.19 = bf16[320,1280]{1,0:T(8,128)(2,1)S(1)} collective-permute-done((bf16[320,1280]{1,0:T(8,128)(2,1)S(1)}, bf16[320,1280]{1,0:T(8,128)(2,1)S(1)}, u32[]{:S(2)}, u32[]{:S(2)}) %collective-permute-start.19) | collective-permute-done | bytes 819232 | tf_op jit(solution)/shard_map/ppermute | solution.py:53
  161.8 5.0 collective-permute-done.16.refs_1_
  173.1 13.1 %collective-permute-done.14.refs_1_ = bf16[256,1280]{1,0:T(8,128)(2,1)S(1)} collective-permute-done((bf16[256,1280]{1,0:T(8,128)(2,1)S(1)}, bf16[256,1280]{1,0:T(8,128)(2,1)S(1)}, u32[]{:S(2)}, u32[]{:S(2)}) %collective-permute-start.14) | collective-permute-done | bytes 655392 | tf_op jit(solution)/shard_map/ppermute | solution.py:53
  188.1 11.2 %shard_map.453 = (f32[512,1280]{1,0:T(8,128)}, f32[512,1280]{1,0:T(8,128)}, bf16[512,1280]{1,0:T(8,128)(2,1)}, f32[256,1280]{1,0:T(8,128)}, bf16[256,1280]{1,0:T(8,128)(2,1)}) custom-call(bf16[256,1280]{1,0:T(8,128)(2,1)} %copy-done.65, bf16[256,1280]{1,0:T(8,128)(2,1)} %collective-permute-done.22.refs_1_.refs_4_, ...), custom_call_target="tpu_custom_call" | custom-call | flops 5033164800 | bytes 19660800 | tf_op jit(solution)/shard_map/pallas_call | solution.py:424
  202.2 11.2 %shard_map.454 = (f32[512,1280]{1,0:T(8,128)}, f32[512,1280]{1,0:T(8,128)}, bf16[512,1280]{1,0:T(8,128)(2,1)}, f32[256,1280]{1,0:T(8,128)}, bf16[256,1280]{1,0:T(8,128)(2,1)}) custom-call(bf16[256,1280]{1,0:T(8,128)(2,1)} %copy-done.66, bf16[256,1280]{1,0:T(8,128)(2,1)} %collective-permute-done.21.refs_1_.refs_6_, ...), custom_call_target="tpu_custom_call" | custom-call | flops 5033164800 | bytes 19660800 | tf_op jit(solution)/shard_map/pallas_call | solution.py:424
  217.4 11.5 %shard_map.455 = (f32[512,1280]{1,0:T(8,128)}, f32[512,1280]{1,0:T(8,128)}, bf16[512,1280]{1,0:T(8,128)(2,1)}, f32[256,1280]{1,0:T(8,128)}, bf16[256,1280]{1,0:T(8,128)(2,1)}) custom-call(bf16[256,1280]{1,0:T(8,128)(2,1)} %shard_map.452.refs_7_.refs_0_, bf16[256,1280]{1,0:T(8,128)(2,1)} %collective-permute-done.17.refs_1_.refs_8_, ...), custom_call_target="tpu_custom_call" | custom-call | flops 5033164800 | bytes 19660800 | tf_op jit(solution)/shard_map/pallas_call | solution.py:424
  233.0 4.0 shard_map.456
  241.2 13.8 %shard_map.457 = (bf16[512,1280]{1,0:T(8,128)(2,1)}, bf16[512,1280]{1,0:T(8,128)(2,1)}, f32[2,1280]{1,0:T(2,128)}, f32[256,1280]{1,0:T(8,128)}, bf16[256,1280]{1,0:T(8,128)(2,1)}) custom-call(bf16[256,1280]{1,0:T(8,128)(2,1)} %copy-done.154, bf16[256,1280]{1,0:T(8,128)(2,1)} %copy-done.216, f32[512,1280]{1,0:T(8,128)} %get-tuple-element.193.refs_2_, ...), custom_call_target="tpu_custom_call" | custom-call | flops 5033164800 | bytes 20971520 | tf_op jit(solution)/shard_map/pallas_call | solution.py:513
  256.3 4.0 shard_map.458
  264.7 13.8 %shard_map.459 = (bf16[512,1280]{1,0:T(8,128)(2,1)}, bf16[512,1280]{1,0:T(8,128)(2,1)}, f32[2,1280]{1,0:T(2,128)}, f32[256,1280]{1,0:T(8,128)}, bf16[256,1280]{1,0:T(8,128)(2,1)}) custom-call(bf16[256,1280]{1,0:T(8,128)(2,1)} %copy-done.156, bf16[256,1280]{1,0:T(8,128)(2,1)} %copy-done.218, f32[512,1280]{1,0:T(8,128)} %get-tuple-element.197.refs_2_, ...), custom_call_target="tpu_custom_call" | custom-call | flops 5033164800 | bytes 20971520 | tf_op jit(solution)/shard_map/pallas_call | solution.py:513
  280.8 3.8 shard_map.460
  288.9 9.8 %shard_map.461 = (f32[640,1280]{1,0:T(8,128)}, bf16[640,1280]{1,0:T(8,128)(2,1)}) custom-call(bf16[512,1280]{1,0:T(8,128)(2,1)} %get-tuple-element.206.refs_0_, bf16[512,1280]{1,0:T(8,128)(2,1)} %get-tuple-element.207.refs_1_, bf16[512,1280]{1,0:T(8,128)(2,1)} %get-tuple-element.208.refs_2_, bf16[256,1280]{1,0:T(8,128)(2,1)} %copy-done.154, ...), custom_call_target="tpu_custom_call" | custom-call | flops 5033164800 | bytes 12779520 | tf_op jit(solution)/shard_map/pallas_call | solution.py:555
  298.6 4.6 collective-permute-done.35.refs_5_
  312.9 13.7 %shard_map.463 = (bf16[512,1280]{1,0:T(8,128)(2,1)}, bf16[512,1280]{1,0:T(8,128)(2,1)}, f32[2,1280]{1,0:T(2,128)}, f32[256,1280]{1,0:T(8,128)}, bf16[256,1280]{1,0:T(8,128)(2,1)}) custom-call(bf16[256,1280]{1,0:T(8,128)(2,1)} %copy-done.155, bf16[256,1280]{1,0:T(8,128)(2,1)} %copy-done.217, f32[512,1280]{1,0:T(8,128)} %get-tuple-element.215.refs_2_, ...), custom_call_target="tpu_custom_call" | custom-call | flops 5033164800 | bytes 20971520 | tf_op jit(solution)/shard_map/pallas_call | solution.py:513
  326.6 9.7 %shard_map.464 = (f32[640,1280]{1,0:T(8,128)}, bf16[640,1280]{1,0:T(8,128)(2,1)}) custom-call(bf16[512,1280]{1,0:T(8,128)(2,1)} %get-tuple-element.213.refs_0_, bf16[512,1280]{1,0:T(8,128)(2,1)} %get-tuple-element.214.refs_1_, bf16[512,1280]{1,0:T(8,128)(2,1)} %get-tuple-element.218.refs_2_, bf16[256,1280]{1,0:T(8,128)(2,1)} %copy-done.65, ...), custom_call_target="tpu_custom_call" | custom-call | flops 5033164800 | bytes 12779520 | tf_op jit(solution)/shard_map/pallas_call | solution.py:555
  342.4 5.5 collective-permute-done.38.refs_10_.partner
  347.9 7.7 shard_map.465
  366.8 8.4 %shard_map.467 = (f32[320,512]{1,0:T(8,128)S(1)}, f32[640,512]{1,0:T(8,128)S(1)}, bf16[1,640,512]{2,1,0:T(8,128)(2,1)}) custom-call(s32[1,512]{1,0:T(1,128)S(1)} %get-tuple-element.363.refs_0_, s32[1,512]{1,0:T(1,128)S(1)} %slice.343.refs_1_, s32[1024,1]{1,0:T(8,128)S(1)} %bitcast.142, s32[1024,1]{1,0:T(8,128)S(1)} %bitcast.139, ...), custom_call_target="tpu_custom_call" | custom-call | flops 6710886400 | bytes 2621440 | tf_op jit(solution)/shard_map/pallas_call | solution.py:353
  376.7 10.8 %shard_map.468 = (f32[1,3,640,1280]{3,2,1,0:T(8,128)}, f32[1,3,640,1280]{3,2,1,0:T(8,128)}, f32[1,3,640,1280]{3,2,1,0:T(8,128)}, bf16[320,1280]{1,0:T(8,128)(2,1)}, bf16[320,1280]{1,0:T(8,128)(2,1)}) custom-call(s32[1]{0:T(128)} %constant.30.clone.1.offset, f32[640,1280]{1,0:T(8,128)S(1)} %copy-done.17, ...), custom_call_target="tpu_custom_call" | custom-call | flops 24576000 | bytes 26214400 | tf_op jit(solution)/shard_map/pallas_call | solution.py:714
  387.5 3.9 collective-permute-start.49
  391.3 5.6 collective-permute-done.39.refs_1_
  406.7 4.0 collective-permute-start.50
  412.8 3.7 fusion.26.own
  419.5 8.4 %shard_map.471 = (f32[320,512]{1,0:T(8,128)S(1)}, f32[640,512]{1,0:T(8,128)S(1)}, bf16[1,640,512]{2,1,0:T(8,128)(2,1)}) custom-call(s32[1,512]{1,0:T(1,128)S(1)} %get-tuple-element.365.refs_0_, s32[1,512]{1,0:T(1,128)S(1)} %slice.343.refs_1_, s32[1024,1]{1,0:T(8,128)S(1)} %bitcast.134, s32[1024,1]{1,0:T(8,128)S(1)} %bitcast.140, ...), custom_call_target="tpu_custom_call" | custom-call | flops 6710886400 | bytes 2621440 | tf_op jit(solution)/shard_map/pallas_call | solution.py:353
  443.8 10.2 %shard_map.473 = (f32[640,1280]{1,0:T(8,128)}, bf16[640,1280]{1,0:T(8,128)(2,1)}) custom-call(bf16[512,1280]{1,0:T(8,128)(2,1)} %get-tuple-element.252.refs_0_, bf16[512,1280]{1,0:T(8,128)(2,1)} %get-tuple-element.253.refs_1_, bf16[512,1280]{1,0:T(8,128)(2,1)} %get-tuple-element.254.refs_2_, bf16[256,1280]{1,0:T(8,128)(2,1)} %copy-done.65, ...), custom_call_target="tpu_custom_call" | custom-call | flops 5033164800 | bytes 12779520 | tf_op jit(solution)/shard_map/pallas_call | solution.py:555
  457.5 10.6 %shard_map.474 = (f32[1,3,640,1280]{3,2,1,0:T(8,128)}, f32[1,3,640,1280]{3,2,1,0:T(8,128)}, f32[1,3,640,1280]{3,2,1,0:T(8,128)}, bf16[320,1280]{1,0:T(8,128)(2,1)}, bf16[320,1280]{1,0:T(8,128)(2,1)S(1)}) custom-call(s32[1]{0:T(128)} %constant.30.clone.1.offset, ...), custom_call_target="tpu_custom_call", output_to_operand_aliasing={{0}: (6, {}), {1}: (7, {}), {2}: (8, {})} | custom-call | flops 24576000 | bytes 26214400 | tf_op jit(solution)/shard_map/pallas_call | solution.py:714
  469.0 3.7 collective-permute-start.65
  492.7 7.8 collective-permute-done.97
  507.1 9.9 %collective-permute-done.67 = bf16[320,1280]{1,0:T(8,128)(2,1)S(1)} collective-permute-done((bf16[320,1280]{1,0:T(8,128)(2,1)S(1)}, bf16[320,1280]{1,0:T(8,128)(2,1)S(1)}, u32[]{:S(2)}, u32[]{:S(2)}) %collective-permute-start.67) | collective-permute-done | bytes 819232 | tf_op jit(solution)/shard_map/ppermute | solution.py:106
  517.8 5.0 shard_map.476
  528.2 3.7 shard_map.483
  534.7 7.0 collective-permute-start.81
  543.1 4.1 collective-permute-done.81
  550.7 26.8 %collective-permute-done.63.partner = bf16[160,1280]{1,0:T(8,128)(2,1)S(1)} collective-permute-done((bf16[160,1280]{1,0:T(8,128)(2,1)}, bf16[160,1280]{1,0:T(8,128)(2,1)S(1)}, u32[]{:S(2)}, u32[]{:S(2)}) %collective-permute-start.63) | collective-permute-done | bytes 409632 | tf_op jit(solution)/shard_map/ppermute | solution.py:53
  578.0 3.5 shard_map.484
  587.9 12.7 %collective-permute-start.72 = (bf16[160,1280]{1,0:T(8,128)(2,1)S(1)}, bf16[160,1280]{1,0:T(8,128)(2,1)S(1)}, u32[]{:S(2)}, u32[]{:S(2)}) collective-permute-start(bf16[160,1280]{1,0:T(8,128)(2,1)S(1)} %get-tuple-element.291), channel_id=1, source_target_pairs={{0,8},{24,16},{1,9},{25,17},{2,10},{26,18},{3,11},{27,19},{4,12},{... | collective-permute-start | bytes 1228808 | tf_op jit(solution)/shard_map/ppermute | solution.py:106
  603.5 10.2 %shard_map.488 = (f32[1,3,640,1280]{3,2,1,0:T(8,128)}, f32[1,3,640,1280]{3,2,1,0:T(8,128)}, f32[1,3,640,1280]{3,2,1,0:T(8,128)}, bf16[320,1280]{1,0:T(8,128)(2,1)S(1)}, bf16[320,1280]{1,0:T(8,128)(2,1)S(1)}) custom-call(s32[1]{0:T(128)} %constant.30.clone.1.offset, ...), custom_call_target="tpu_custom_call", output_to_operand_aliasing={{0}: (6, {}), {1}: (7, {}), {2}: (8, {})} | custom-call | flops 24576000 | bytes 26214400 | tf_op jit(solution)/shard_map/pallas_call | solution.py:714
  615.2 3.9 collective-permute-done.75
  619.1 4.6 collective-permute-start.84
  623.8 4.1 collective-permute-done.78
  628.7 16.3 %collective-permute-start.87 = (bf16[320,1280]{1,0:T(8,128)(2,1)S(1)}, bf16[320,1280]{1,0:T(8,128)(2,1)S(1)}, u32[]{:S(2)}, u32[]{:S(2)}) collective-permute-start(bf16[320,1280]{1,0:T(8,128)(2,1)S(1)} %get-tuple-element.303), channel_id=1, source_target_pairs={{0,8},{24,16},{1,9},{25,17},{2,10},{26,18},{3,11},{27,19},{4,12},{... | collective-permute-start | bytes 2457608 | tf_op jit(solution)/shard_map/ppermute | solution.py:106
  649.5 13.1 %collective-permute-done.87 = bf16[320,1280]{1,0:T(8,128)(2,1)S(1)} collective-permute-done((bf16[320,1280]{1,0:T(8,128)(2,1)S(1)}, bf16[320,1280]{1,0:T(8,128)(2,1)S(1)}, u32[]{:S(2)}, u32[]{:S(2)}) %collective-permute-start.87) | collective-permute-done | bytes 819232 | tf_op jit(solution)/shard_map/ppermute | solution.py:106
  663.5 5.4 collective-permute-done.93.back
  670.7 13.8 %collective-permute-done.94.back = bf16[320,1280]{1,0:T(8,128)(2,1)S(1)} collective-permute-done((bf16[320,1280]{1,0:T(8,128)(2,1)S(1)}, bf16[320,1280]{1,0:T(8,128)(2,1)S(1)}, u32[]{:S(2)}, u32[]{:S(2)}) %collective-permute-start.94) | collective-permute-done | bytes 819232 | tf_op jit(solution)/shard_map/ppermute | solution.py:111
  689.5 26.8 %collective-permute-done.83.back = bf16[160,1280]{1,0:T(8,128)(2,1)S(1)} collective-permute-done((bf16[160,1280]{1,0:T(8,128)(2,1)S(1)}, bf16[160,1280]{1,0:T(8,128)(2,1)S(1)}, u32[]{:S(2)}, u32[]{:S(2)}) %collective-permute-start.83) | collective-permute-done | bytes 409632 | tf_op jit(solution)/shard_map/ppermute | solution.py:111
  723.3 10.6 %collective-permute-done.91.back = bf16[320,1280]{1,0:T(8,128)(2,1)S(1)} collective-permute-done((bf16[320,1280]{1,0:T(8,128)(2,1)S(1)}, bf16[320,1280]{1,0:T(8,128)(2,1)S(1)}, u32[]{:S(2)}, u32[]{:S(2)}) %collective-permute-start.91) | collective-permute-done | bytes 819232 | tf_op jit(solution)/shard_map/ppermute | solution.py:111
  736.1 6.6 collective-permute-done.80.back
  745.9 3.3 shard_map.477.rest_0_
  750.9 3.4 shard_map.478.rest_0_
  754.4 4.1 shard_map.479
  758.5 3.3 shard_map.493
  761.8 3.4 shard_map.494
  772.8 3.4 shard_map.495
  776.2 3.4 shard_map.496
  781.2 11.3 %collective-permute-done.77.back = bf16[160,1280]{1,0:T(8,128)(2,1)} collective-permute-done((bf16[160,1280]{1,0:T(8,128)(2,1)S(1)}, bf16[160,1280]{1,0:T(8,128)(2,1)}, u32[]{:S(2)}, u32[]{:S(2)}) %collective-permute-start.77) | collective-permute-done | bytes 409632 | tf_op jit(solution)/shard_map/ppermute | solution.py:111
  797.6 3.3 shard_map.482
  800.9 3.5 shard_map.497
  804.5 3.5 shard_map.498
  (792 shorter events, 284.2 us)
Async XLA Ops:
  3.7 23.2 %collective-permute-start = (bf16[3,80,1280]{2,1,0:T(8,128)(2,1)}, bf16[3,80,1280]{2,1,0:T(8,128)(2,1)S(1)}, u32[]{:S(2)}, u32[]{:S(2)}) collective-permute-start(bf16[3,80,1280]{2,1,0:T(8,128)(2,1)} %slice_select_fusion.5), channel_id=1, source_target_pairs={{0,4},{4,0},{1,5},{5,1},{2,6},{6,2},{3,7},{7,3},{8,12},{12,8},{9,1... | collective-permute-start | bytes 1843208 | tf_op jit(solution)/shard_map/ppermute | solution.py:53
  6.9 22.1 %collective-permute-start.2 = (bf16[2720]{0:T(1024)(128)(2,1)S(1)}, bf16[2720]{0:T(1024)(128)(2,1)S(1)}, u32[]{:S(2)}, u32[]{:S(2)}) collective-permute-start(bf16[2720]{0:T(1024)(128)(2,1)S(1)} %concatenate.178), channel_id=1, source_target_pairs={{0,4},{4,0},{1,5},{5,1},{2,6},{6,2},{3,7},{7,3},{8,12},{12,8},{9,1... | collective-permute-start | bytes 16328 | tf_op jit(solution)/shard_map/ppermute | solution.py:53
  29.5 30.3 %collective-permute-start.4 = (bf16[320,1280]{1,0:T(8,128)(2,1)}, bf16[320,1280]{1,0:T(8,128)(2,1)}, u32[]{:S(2)}, u32[]{:S(2)}) collective-permute-start(bf16[320,1280]{1,0:T(8,128)(2,1)} %shard_map.442), channel_id=1, source_target_pairs={{0,4},{4,0},{1,5},{5,1},{2,6},{6,2},{3,7},{7,3},{8,12},{12,8},{9,1... | collective-permute-start | bytes 2457608 | tf_op jit(solution)/shard_map/ppermute | solution.py:53
  31.1 26.1 %collective-permute-start.7 = (bf16[80,1280]{1,0:T(8,128)(2,1)}, bf16[80,1280]{1,0:T(8,128)(2,1)}, u32[]{:S(2)}, u32[]{:S(2)}) collective-permute-start(bf16[80,1280]{1,0:T(8,128)(2,1)} %shard_map.446), channel_id=1, source_target_pairs={{0,4},{4,0},{1,5},{5,1},{2,6},{6,2},{3,7},{7,3},{8,12},{12,8},{9,1... | collective-permute-start | bytes 614408 | tf_op jit(solution)/shard_map/ppermute | solution.py:53
  55.5 30.4 %collective-permute-start.11 = (bf16[640,512]{1,0:T(8,128)(2,1)}, bf16[640,512]{1,0:T(8,128)(2,1)}, u32[]{:S(2)}, u32[]{:S(2)}) collective-permute-start(bf16[640,512]{1,0:T(8,128)(2,1)} %get-tuple-element.180), channel_id=1, source_target_pairs={{0,4},{4,0},{1,5},{5,1},{2,6},{6,2},{3,7},{7,3},{8,12},{12,8},{9,1... | collective-permute-start | bytes 1966088 | tf_op jit(solution)/shard_map/ppermute | solution.py:53
  59.8 40.2 %collective-permute-start.5 = (bf16[640,512]{1,0:T(8,128)(2,1)}, bf16[640,512]{1,0:T(8,128)(2,1)}, u32[]{:S(2)}, u32[]{:S(2)}) collective-permute-start(bf16[640,512]{1,0:T(8,128)(2,1)} %shard_map.443), channel_id=1, source_target_pairs={{0,4},{4,0},{1,5},{5,1},{2,6},{6,2},{3,7},{7,3},{8,12},{12,8},{9,1... | collective-permute-start | bytes 1966088 | tf_op jit(solution)/shard_map/ppermute | solution.py:53
  61.3 53.8 %collective-permute-start.6 = (bf16[320,1280]{1,0:T(8,128)(2,1)}, bf16[320,1280]{1,0:T(8,128)(2,1)S(1)}, u32[]{:S(2)}, u32[]{:S(2)}) collective-permute-start(bf16[320,1280]{1,0:T(8,128)(2,1)} %shard_map.444), channel_id=1, source_target_pairs={{0,4},{4,0},{1,5},{5,1},{2,6},{6,2},{3,7},{7,3},{8,12},{12,8},{9,1... | collective-permute-start | bytes 2457608 | tf_op jit(solution)/shard_map/ppermute | solution.py:53
  64.6 67.4 %collective-permute-start.18 = (bf16[320,1280]{1,0:T(8,128)(2,1)}, bf16[320,1280]{1,0:T(8,128)(2,1)}, u32[]{:S(2)}, u32[]{:S(2)}) collective-permute-start(bf16[320,1280]{1,0:T(8,128)(2,1)} %collective-permute-done.4.refs_1_), channel_id=1, source_target_pairs={{0,8},{8,0},{16,24},{24,16},{1,9},{9,1},{17,25},{25,17},{2,10},{10... | collective-permute-start | bytes 2457608 | tf_op jit(solution)/shard_map/ppermute | solution.py:53
  119.9 21.2 %collective-permute-start.12 = (bf16[320,1280]{1,0:T(8,128)(2,1)}, bf16[320,1280]{1,0:T(8,128)(2,1)S(1)}, u32[]{:S(2)}, u32[]{:S(2)}) collective-permute-start(bf16[320,1280]{1,0:T(8,128)(2,1)} %shard_map.449), channel_id=1, source_target_pairs={{0,4},{4,0},{1,5},{5,1},{2,6},{6,2},{3,7},{7,3},{8,12},{12,8},{9,1... | collective-permute-start | bytes 2457608 | tf_op jit(solution)/shard_map/ppermute | solution.py:53
  130.5 21.1 %collective-permute-start.19 = (bf16[320,1280]{1,0:T(8,128)(2,1)S(1)}, bf16[320,1280]{1,0:T(8,128)(2,1)S(1)}, u32[]{:S(2)}, u32[]{:S(2)}) collective-permute-start(bf16[320,1280]{1,0:T(8,128)(2,1)S(1)} %copy-done.55), channel_id=1, source_target_pairs={{0,8},{8,0},{16,24},{24,16},{1,9},{9,1},{17,25},{25,17},{2,10},{10... | collective-permute-start | bytes 2457608 | tf_op jit(solution)/shard_map/ppermute | solution.py:53
  140.5 26.3 %collective-permute-start.16 = (bf16[256,1280]{1,0:T(8,128)(2,1)S(1)}, bf16[256,1280]{1,0:T(8,128)(2,1)S(1)}, u32[]{:S(2)}, u32[]{:S(2)}) collective-permute-start(bf16[256,1280]{1,0:T(8,128)(2,1)S(1)} %add_convert_fusion.18.refs_0_), channel_id=1, source_target_pairs={{0,2},{1,3},{2,0},{3,1},{4,6},{5,7},{6,4},{7,5},{8,10},{9,11},{10,... | collective-permute-start | bytes 1966088 | tf_op jit(solution)/shard_map/ppermute | solution.py:53
  141.1 27.2 %collective-permute-start.20 = (bf16[320,1280]{1,0:T(8,128)(2,1)S(1)}, bf16[320,1280]{1,0:T(8,128)(2,1)S(1)}, u32[]{:S(2)}, u32[]{:S(2)}) collective-permute-start(bf16[320,1280]{1,0:T(8,128)(2,1)S(1)} %collective-permute-done.12.refs_7_), channel_id=1, source_target_pairs={{0,8},{8,0},{16,24},{24,16},{1,9},{9,1},{17,25},{25,17},{2,10},{10... | collective-permute-start | bytes 2457608 | tf_op jit(solution)/shard_map/ppermute | solution.py:53
  161.8 26.3 %collective-permute-start.22 = (bf16[256,1280]{1,0:T(8,128)(2,1)S(1)}, bf16[256,1280]{1,0:T(8,128)(2,1)}, u32[]{:S(2)}, u32[]{:S(2)}) collective-permute-start(bf16[256,1280]{1,0:T(8,128)(2,1)S(1)} %shard_map.448.refs_6_.refs_4_.refs_0_.refs_3_), channel_id=1, source_target_pairs={{0,1},{1,0},{2,3},{3,2},{4,5},{5,4},{6,7},{7,6},{8,9},{9,8},{10,11... | collective-permute-start | bytes 1966088 | tf_op jit(solution)/shard_map/ppermute | solution.py:53
  167.7 34.5 %collective-permute-start.21 = (bf16[256,1280]{1,0:T(8,128)(2,1)S(1)}, bf16[256,1280]{1,0:T(8,128)(2,1)}, u32[]{:S(2)}, u32[]{:S(2)}) collective-permute-start(bf16[256,1280]{1,0:T(8,128)(2,1)S(1)} %shard_map.451.refs_4_.refs_0_.refs_5_), channel_id=1, source_target_pairs={{0,1},{1,0},{2,3},{3,2},{4,5},{5,4},{6,7},{7,6},{8,9},{9,8},{10,11... | collective-permute-start | bytes 1966088 | tf_op jit(solution)/shard_map/ppermute | solution.py:53
  213.5 23.6 %collective-permute-start.25 = (bf16[256,1280]{1,0:T(8,128)(2,1)}, bf16[256,1280]{1,0:T(8,128)(2,1)}, u32[]{:S(2)}, u32[]{:S(2)}) collective-permute-start(bf16[256,1280]{1,0:T(8,128)(2,1)} %get-tuple-element.187.refs_7_), channel_id=1, source_target_pairs={{0,1},{1,0},{2,3},{3,2},{4,5},{5,4},{6,7},{7,6},{8,9},{9,8},{10,11... | collective-permute-start | bytes 1966088 | tf_op jit(solution)/shard_map/ppermute | solution.py:53
  228.9 31.6 %collective-permute-start.23 = (bf16[256,1280]{1,0:T(8,128)(2,1)}, bf16[256,1280]{1,0:T(8,128)(2,1)}, u32[]{:S(2)}, u32[]{:S(2)}) collective-permute-start(bf16[256,1280]{1,0:T(8,128)(2,1)} %get-tuple-element.189.refs_7_.refs_9_), channel_id=1, source_target_pairs={{0,1},{1,0},{2,3},{3,2},{4,5},{5,4},{6,7},{7,6},{8,9},{9,8},{10,11... | collective-permute-start | bytes 1966088 | tf_op jit(solution)/shard_map/ppermute | solution.py:53
  288.0 21.5 %collective-permute-start.40 = (bf16[256,1280]{1,0:T(8,128)(2,1)}, bf16[256,1280]{1,0:T(8,128)(2,1)}, u32[]{:S(2)}, u32[]{:S(2)}) collective-permute-start(bf16[256,1280]{1,0:T(8,128)(2,1)} %get-tuple-element.227), channel_id=1, source_target_pairs={{0,1},{1,0},{2,3},{3,2},{4,5},{5,4},{6,7},{7,6},{8,9},{9,8},{10,11... | collective-permute-start | bytes 1966088 | tf_op jit(solution)/shard_map/ppermute | solution.py:53
  309.0 30.9 %collective-permute-start.37 = (bf16[256,1280]{1,0:T(8,128)(2,1)}, bf16[256,1280]{1,0:T(8,128)(2,1)}, u32[]{:S(2)}, u32[]{:S(2)}) collective-permute-start(bf16[256,1280]{1,0:T(8,128)(2,1)} %get-tuple-element.211), channel_id=1, source_target_pairs={{0,1},{1,0},{2,3},{3,2},{4,5},{5,4},{6,7},{7,6},{8,9},{9,8},{10,11... | collective-permute-start | bytes 1966088 | tf_op jit(solution)/shard_map/ppermute | solution.py:53
  309.0 38.9 %collective-permute-start.38 = (bf16[640,1280]{1,0:T(8,128)(2,1)}, bf16[640,1280]{1,0:T(8,128)(2,1)}, u32[]{:S(2)}, u32[]{:S(2)}) collective-permute-start(bf16[640,1280]{1,0:T(8,128)(2,1)} %get-tuple-element.221), channel_id=1, source_target_pairs={{0,4},{4,0},{1,5},{5,1},{2,6},{6,2},{3,7},{7,3},{8,12},{12,8},{9,1... | collective-permute-start | bytes 4915208 | tf_op jit(solution)/shard_map/ppermute | solution.py:53
  311.5 44.1 %collective-permute-start.41 = (bf16[256,1280]{1,0:T(8,128)(2,1)}, bf16[256,1280]{1,0:T(8,128)(2,1)}, u32[]{:S(2)}, u32[]{:S(2)}) collective-permute-start(bf16[256,1280]{1,0:T(8,128)(2,1)} %add_convert_fusion.13.refs_4_), channel_id=1, source_target_pairs={{0,2},{1,3},{2,0},{3,1},{4,6},{5,7},{6,4},{7,5},{8,10},{9,11},{10,... | collective-permute-start | bytes 1966088 | tf_op jit(solution)/shard_map/ppermute | solution.py:53
  326.6 32.0 %collective-permute-start.44 = (bf16[256,1280]{1,0:T(8,128)(2,1)}, bf16[256,1280]{1,0:T(8,128)(2,1)}, u32[]{:S(2)}, u32[]{:S(2)}) collective-permute-start(bf16[256,1280]{1,0:T(8,128)(2,1)} %get-tuple-element.238), channel_id=1, source_target_pairs={{0,1},{1,0},{2,3},{3,2},{4,5},{5,4},{6,7},{7,6},{8,9},{9,8},{10,11... | collective-permute-start | bytes 1966088 | tf_op jit(solution)/shard_map/ppermute | solution.py:53
  336.3 117.7 %collective-permute-start.48 = (bf16[640,1280]{1,0:T(8,128)(2,1)}, bf16[640,1280]{1,0:T(8,128)(2,1)}, u32[]{:S(2)}, u32[]{:S(2)}) collective-permute-start(bf16[640,1280]{1,0:T(8,128)(2,1)} %get-tuple-element.248), channel_id=1, source_target_pairs={{0,4},{4,0},{1,5},{5,1},{2,6},{6,2},{3,7},{7,3},{8,12},{12,8},{9,1... | collective-permute-start | bytes 4915208 | tf_op jit(solution)/shard_map/ppermute | solution.py:53
  360.2 37.6 %collective-permute-start.45 = (bf16[256,1280]{1,0:T(8,128)(2,1)S(1)}, bf16[256,1280]{1,0:T(8,128)(2,1)S(1)}, u32[]{:S(2)}, u32[]{:S(2)}) collective-permute-start(bf16[256,1280]{1,0:T(8,128)(2,1)S(1)} %add_convert_fusion.12.refs_4_), channel_id=1, source_target_pairs={{0,2},{1,3},{2,0},{3,1},{4,6},{5,7},{6,4},{7,5},{8,10},{9,11},{10,... | collective-permute-start | bytes 1966088 | tf_op jit(solution)/shard_map/ppermute | solution.py:53
  363.7 33.3 %collective-permute-start.39 = (bf16[640,512]{1,0:T(8,128)(2,1)S(1)}, bf16[640,512]{1,0:T(8,128)(2,1)S(1)}, u32[]{:S(2)}, u32[]{:S(2)}) collective-permute-start(bf16[640,512]{1,0:T(8,128)(2,1)S(1)} %bitcast.145), channel_id=1, source_target_pairs={{0,4},{4,0},{1,5},{5,1},{2,6},{6,2},{3,7},{7,3},{8,12},{12,8},{9,1... | collective-permute-start | bytes 1966088 | tf_op jit(solution)/shard_map/ppermute | solution.py:53
  375.2 53.7 %collective-permute-start.43 = (bf16[640,512]{1,0:T(8,128)(2,1)}, bf16[640,512]{1,0:T(8,128)(2,1)}, u32[]{:S(2)}, u32[]{:S(2)}) collective-permute-start(bf16[640,512]{1,0:T(8,128)(2,1)} %bitcast.35), channel_id=1, source_target_pairs={{0,4},{4,0},{1,5},{5,1},{2,6},{6,2},{3,7},{7,3},{8,12},{12,8},{9,1... | collective-permute-start | bytes 1966088 | tf_op jit(solution)/shard_map/ppermute | solution.py:53
  387.5 48.4 %collective-permute-start.49 = (bf16[320,1280]{1,0:T(8,128)(2,1)}, bf16[320,1280]{1,0:T(8,128)(2,1)}, u32[]{:S(2)}, u32[]{:S(2)}) collective-permute-start(bf16[320,1280]{1,0:T(8,128)(2,1)} %get-tuple-element.232.refs_5_), channel_id=1, source_target_pairs={{0,8},{24,16},{1,9},{25,17},{2,10},{26,18},{3,11},{27,19},{4,12},{... | collective-permute-start | bytes 2457608 | tf_op jit(solution)/shard_map/ppermute | solution.py:106
  406.7 33.0 %collective-permute-start.50 = (bf16[320,1280]{1,0:T(8,128)(2,1)}, bf16[320,1280]{1,0:T(8,128)(2,1)}, u32[]{:S(2)}, u32[]{:S(2)}) collective-permute-start(bf16[320,1280]{1,0:T(8,128)(2,1)} %get-tuple-element.257), channel_id=1, source_target_pairs={{0,8},{24,16},{1,9},{25,17},{2,10},{26,18},{3,11},{27,19},{4,12},{... | collective-permute-start | bytes 2457608 | tf_op jit(solution)/shard_map/ppermute | solution.py:106
  410.8 23.2 %collective-permute-start.58 = (bf16[256,1280]{1,0:T(8,128)(2,1)}, bf16[256,1280]{1,0:T(8,128)(2,1)S(1)}, u32[]{:S(2)}, u32[]{:S(2)}) collective-permute-start(bf16[256,1280]{1,0:T(8,128)(2,1)} %convolution_convert_fusion), channel_id=1, source_target_pairs={{0,1},{1,0},{2,3},{3,2},{4,5},{5,4},{6,7},{7,6},{8,9},{9,8},{10,11... | collective-permute-start | bytes 1966088 | tf_op jit(solution)/shard_map/ppermute | solution.py:53
  428.9 40.1 %collective-permute-start.47 = (bf16[640,512]{1,0:T(8,128)(2,1)}, bf16[640,512]{1,0:T(8,128)(2,1)S(1)}, u32[]{:S(2)}, u32[]{:S(2)}) collective-permute-start(bf16[640,512]{1,0:T(8,128)(2,1)} %bitcast.36), channel_id=1, source_target_pairs={{0,4},{4,0},{1,5},{5,1},{2,6},{6,2},{3,7},{7,3},{8,12},{12,8},{9,1... | collective-permute-start | bytes 1966088 | tf_op jit(solution)/shard_map/ppermute | solution.py:53
  434.0 45.5 %collective-permute-start.55 = (bf16[256,1280]{1,0:T(8,128)(2,1)}, bf16[256,1280]{1,0:T(8,128)(2,1)}, u32[]{:S(2)}, u32[]{:S(2)}) collective-permute-start(bf16[256,1280]{1,0:T(8,128)(2,1)} %convolution_convert_fusion.1), channel_id=1, source_target_pairs={{0,1},{1,0},{2,3},{3,2},{4,5},{5,4},{6,7},{7,6},{8,9},{9,8},{10,11... | collective-permute-start | bytes 1966088 | tf_op jit(solution)/shard_map/ppermute | solution.py:53
  435.8 39.0 %collective-permute-start.59 = (bf16[256,1280]{1,0:T(8,128)(2,1)}, bf16[256,1280]{1,0:T(8,128)(2,1)}, u32[]{:S(2)}, u32[]{:S(2)}) collective-permute-start(bf16[256,1280]{1,0:T(8,128)(2,1)} %fusion.2), channel_id=1, source_target_pairs={{0,2},{1,3},{2,0},{3,1},{4,6},{5,7},{6,4},{7,5},{8,10},{9,11},{10,... | collective-permute-start | bytes 1966088 | tf_op jit(solution)/shard_map/ppermute | solution.py:53
  439.7 87.1 %collective-permute-start.64 = (bf16[160,1280]{1,0:T(8,128)(2,1)}, bf16[160,1280]{1,0:T(8,128)(2,1)}, u32[]{:S(2)}, u32[]{:S(2)}) collective-permute-start(bf16[160,1280]{1,0:T(8,128)(2,1)} %fusion.32), channel_id=1, source_target_pairs={{0,4},{4,0},{1,5},{5,1},{2,6},{6,2},{3,7},{7,3},{8,12},{12,8},{9,1... | collective-permute-start | bytes 1228808 | tf_op jit(solution)/shard_map/ppermute | solution.py:53
  454.0 49.1 %collective-permute-start.51 = (bf16[320,1280]{1,0:T(8,128)(2,1)S(1)}, bf16[320,1280]{1,0:T(8,128)(2,1)}, u32[]{:S(2)}, u32[]{:S(2)}) collective-permute-start(bf16[320,1280]{1,0:T(8,128)(2,1)S(1)} %copy-done.28), channel_id=1, source_target_pairs={{8,16},{16,8},{9,17},{17,9},{10,18},{18,10},{11,19},{19,11},{12,20... | collective-permute-start | bytes 2457608 | tf_op jit(solution)/shard_map/ppermute | solution.py:109
  469.0 35.6 %collective-permute-start.65 = (bf16[320,1280]{1,0:T(8,128)(2,1)}, bf16[320,1280]{1,0:T(8,128)(2,1)}, u32[]{:S(2)}, u32[]{:S(2)}) collective-permute-start(bf16[320,1280]{1,0:T(8,128)(2,1)} %get-tuple-element.258.refs_5_), channel_id=1, source_target_pairs={{0,8},{24,16},{1,9},{25,17},{2,10},{26,18},{3,11},{27,19},{4,12},{... | collective-permute-start | bytes 2457608 | tf_op jit(solution)/shard_map/ppermute | solution.py:106
  474.8 47.9 %collective-permute-start.92 = (bf16[320,1280]{1,0:T(8,128)(2,1)}, bf16[320,1280]{1,0:T(8,128)(2,1)}, u32[]{:S(2)}, u32[]{:S(2)}) collective-permute-start(bf16[320,1280]{1,0:T(8,128)(2,1)} %add_convert_fusion.10.rest_5_), channel_id=1, source_target_pairs={{8,16},{16,8},{9,17},{17,9},{10,18},{18,10},{11,19},{19,11},{12,20... | collective-permute-start | bytes 2457608 | tf_op jit(solution)/shard_map/ppermute | solution.py:109
  503.1 28.8 %collective-permute-start.52 = (bf16[256,1280]{1,0:T(8,128)(2,1)}, bf16[256,1280]{1,0:T(8,128)(2,1)}, u32[]{:S(2)}, u32[]{:S(2)}) collective-permute-start(bf16[256,1280]{1,0:T(8,128)(2,1)} %convolution_convert_fusion.2), channel_id=1, source_target_pairs={{0,1},{1,0},{2,3},{3,2},{4,5},{5,4},{6,7},{7,6},{8,9},{9,8},{10,11... | collective-permute-start | bytes 1966088 | tf_op jit(solution)/shard_map/ppermute | solution.py:53
  504.6 30.1 %collective-permute-start.56 = (bf16[256,1280]{1,0:T(8,128)(2,1)}, bf16[256,1280]{1,0:T(8,128)(2,1)S(1)}, u32[]{:S(2)}, u32[]{:S(2)}) collective-permute-start(bf16[256,1280]{1,0:T(8,128)(2,1)} %fusion.1), channel_id=1, source_target_pairs={{0,2},{1,3},{2,0},{3,1},{4,6},{5,7},{6,4},{7,5},{8,10},{9,11},{10,... | collective-permute-start | bytes 1966088 | tf_op jit(solution)/shard_map/ppermute | solution.py:53
  517.0 84.9 %collective-permute-start.69 = (bf16[640,1280]{1,0:T(8,128)(2,1)}, bf16[640,1280]{1,0:T(8,128)(2,1)}, u32[]{:S(2)}, u32[]{:S(2)}) collective-permute-start(bf16[640,1280]{1,0:T(8,128)(2,1)} %shard_map.487), channel_id=1, source_target_pairs={{0,4},{4,0},{1,5},{5,1},{2,6},{6,2},{3,7},{7,3},{8,12},{12,8},{9,1... | collective-permute-start | bytes 4915208 | tf_op jit(solution)/shard_map/ppermute | solution.py:53
  522.8 61.1 %collective-permute-start.61 = (bf16[160,1280]{1,0:T(8,128)(2,1)}, bf16[160,1280]{1,0:T(8,128)(2,1)S(1)}, u32[]{:S(2)}, u32[]{:S(2)}) collective-permute-start(bf16[160,1280]{1,0:T(8,128)(2,1)} %get-tuple-element.264), channel_id=1, source_target_pairs={{0,4},{4,0},{1,5},{5,1},{2,6},{6,2},{3,7},{7,3},{8,12},{12,8},{9,1... | collective-permute-start | bytes 1228808 | tf_op jit(solution)/shard_map/ppermute | solution.py:53
  526.9 54.7 %collective-permute-start.62 = (bf16[160,1280]{1,0:T(8,128)(2,1)}, bf16[160,1280]{1,0:T(8,128)(2,1)S(1)}, u32[]{:S(2)}, u32[]{:S(2)}) collective-permute-start(bf16[160,1280]{1,0:T(8,128)(2,1)} %get-tuple-element.265), channel_id=1, source_target_pairs={{0,4},{4,0},{1,5},{5,1},{2,6},{6,2},{3,7},{7,3},{8,12},{12,8},{9,1... | collective-permute-start | bytes 1228808 | tf_op jit(solution)/shard_map/ppermute | solution.py:53
  548.0 29.5 %collective-permute-start.53 = (bf16[256,1280]{1,0:T(8,128)(2,1)S(1)}, bf16[256,1280]{1,0:T(8,128)(2,1)S(1)}, u32[]{:S(2)}, u32[]{:S(2)}) collective-permute-start(bf16[256,1280]{1,0:T(8,128)(2,1)S(1)} %fusion), channel_id=1, source_target_pairs={{0,2},{1,3},{2,0},{3,1},{4,6},{5,7},{6,4},{7,5},{8,10},{9,11},{10,... | collective-permute-start | bytes 1966088 | tf_op jit(solution)/shard_map/ppermute | solution.py:53
  549.8 27.7 %collective-permute-start.63 = (bf16[160,1280]{1,0:T(8,128)(2,1)}, bf16[160,1280]{1,0:T(8,128)(2,1)S(1)}, u32[]{:S(2)}, u32[]{:S(2)}) collective-permute-start(bf16[160,1280]{1,0:T(8,128)(2,1)} %get-tuple-element.266), channel_id=1, source_target_pairs={{0,4},{4,0},{1,5},{5,1},{2,6},{6,2},{3,7},{7,3},{8,12},{12,8},{9,1... | collective-permute-start | bytes 1228808 | tf_op jit(solution)/shard_map/ppermute | solution.py:53
  577.5 69.9 %collective-permute-start.33 = (f32[256,1280]{1,0:T(8,128)}, f32[256,1280]{1,0:T(8,128)}, u32[]{:S(2)}, u32[]{:S(2)}) collective-permute-start(f32[256,1280]{1,0:T(8,128)} %get-tuple-element.202.own), channel_id=1, source_target_pairs={{0,1},{1,0},{2,3},{3,2},{4,5},{5,4},{6,7},{7,6},{8,9},{9,8},{10,11... | collective-permute-start | bytes 3932168 | tf_op jit(solution)/shard_map/ppermute | solution.py:53
  577.5 70.0 %collective-permute-start.32 = (f32[256,1280]{1,0:T(8,128)}, f32[256,1280]{1,0:T(8,128)}, u32[]{:S(2)}, u32[]{:S(2)}) collective-permute-start(f32[256,1280]{1,0:T(8,128)} %get-tuple-element.201.own), channel_id=1, source_target_pairs={{0,1},{1,0},{2,3},{3,2},{4,5},{5,4},{6,7},{7,6},{8,9},{9,8},{10,11... | collective-permute-start | bytes 3932168 | tf_op jit(solution)/shard_map/ppermute | solution.py:53
  581.6 67.2 %collective-permute-start.31 = (f32[256,1280]{1,0:T(8,128)}, f32[256,1280]{1,0:T(8,128)}, u32[]{:S(2)}, u32[]{:S(2)}) collective-permute-start(f32[256,1280]{1,0:T(8,128)} %get-tuple-element.200.own), channel_id=1, source_target_pairs={{0,1},{1,0},{2,3},{3,2},{4,5},{5,4},{6,7},{7,6},{8,9},{9,8},{10,11... | collective-permute-start | bytes 3932168 | tf_op jit(solution)/shard_map/ppermute | solution.py:53
  587.9 25.9 %collective-permute-start.72 = (bf16[160,1280]{1,0:T(8,128)(2,1)S(1)}, bf16[160,1280]{1,0:T(8,128)(2,1)S(1)}, u32[]{:S(2)}, u32[]{:S(2)}) collective-permute-start(bf16[160,1280]{1,0:T(8,128)(2,1)S(1)} %get-tuple-element.291), channel_id=1, source_target_pairs={{0,8},{24,16},{1,9},{25,17},{2,10},{26,18},{3,11},{27,19},{4,12},{... | collective-permute-start | bytes 1228808 | tf_op jit(solution)/shard_map/ppermute | solution.py:106
  619.1 26.8 %collective-permute-start.84 = (bf16[320,1280]{1,0:T(8,128)(2,1)S(1)}, bf16[320,1280]{1,0:T(8,128)(2,1)S(1)}, u32[]{:S(2)}, u32[]{:S(2)}) collective-permute-start(bf16[320,1280]{1,0:T(8,128)(2,1)S(1)} %get-tuple-element.302), channel_id=1, source_target_pairs={{0,8},{24,16},{1,9},{25,17},{2,10},{26,18},{3,11},{27,19},{4,12},{... | collective-permute-start | bytes 2457608 | tf_op jit(solution)/shard_map/ppermute | solution.py:106
  628.7 33.9 %collective-permute-start.87 = (bf16[320,1280]{1,0:T(8,128)(2,1)S(1)}, bf16[320,1280]{1,0:T(8,128)(2,1)S(1)}, u32[]{:S(2)}, u32[]{:S(2)}) collective-permute-start(bf16[320,1280]{1,0:T(8,128)(2,1)S(1)} %get-tuple-element.303), channel_id=1, source_target_pairs={{0,8},{24,16},{1,9},{25,17},{2,10},{26,18},{3,11},{27,19},{4,12},{... | collective-permute-start | bytes 2457608 | tf_op jit(solution)/shard_map/ppermute | solution.py:106
  645.9 23.1 %collective-permute-start.93 = (bf16[320,1280]{1,0:T(8,128)(2,1)S(1)}, bf16[320,1280]{1,0:T(8,128)(2,1)S(1)}, u32[]{:S(2)}, u32[]{:S(2)}) collective-permute-start(bf16[320,1280]{1,0:T(8,128)(2,1)S(1)} %copy-done.58), channel_id=1, source_target_pairs={{8,0},{16,24},{9,1},{17,25},{10,2},{18,26},{11,3},{19,27},{12,4},{... | collective-permute-start | bytes 2457608 | tf_op jit(solution)/shard_map/ppermute | solution.py:111
  647.4 40.8 %collective-permute-start.60 = (f32[256,1280]{1,0:T(8,128)S(1)}, f32[256,1280]{1,0:T(8,128)S(1)}, u32[]{:S(2)}, u32[]{:S(2)}) collective-permute-start(f32[256,1280]{1,0:T(8,128)S(1)} %copy-done.49), channel_id=1, source_target_pairs={{0,1},{1,0},{2,3},{3,2},{4,5},{5,4},{6,7},{7,6},{8,9},{9,8},{10,11... | collective-permute-start | bytes 3932168 | tf_op jit(solution)/shard_map/ppermute | solution.py:53
  647.5 37.0 %collective-permute-start.94 = (bf16[320,1280]{1,0:T(8,128)(2,1)S(1)}, bf16[320,1280]{1,0:T(8,128)(2,1)S(1)}, u32[]{:S(2)}, u32[]{:S(2)}) collective-permute-start(bf16[320,1280]{1,0:T(8,128)(2,1)S(1)} %copy-done.57), channel_id=1, source_target_pairs={{8,0},{16,24},{9,1},{17,25},{10,2},{18,26},{11,3},{19,27},{12,4},{... | collective-permute-start | bytes 2457608 | tf_op jit(solution)/shard_map/ppermute | solution.py:111
  648.8 21.0 %collective-permute-start.79 = (bf16[160,1280]{1,0:T(8,128)(2,1)S(1)}, bf16[160,1280]{1,0:T(8,128)(2,1)S(1)}, u32[]{:S(2)}, u32[]{:S(2)}) collective-permute-start(bf16[160,1280]{1,0:T(8,128)(2,1)S(1)} %add_convert_fusion.22), channel_id=1, source_target_pairs={{8,16},{16,8},{9,17},{17,9},{10,18},{18,10},{11,19},{19,11},{12,20... | collective-permute-start | bytes 1228808 | tf_op jit(solution)/shard_map/ppermute | solution.py:109
  662.6 23.2 %collective-permute-start.85 = (bf16[320,1280]{1,0:T(8,128)(2,1)S(1)}, bf16[320,1280]{1,0:T(8,128)(2,1)S(1)}, u32[]{:S(2)}, u32[]{:S(2)}) collective-permute-start(bf16[320,1280]{1,0:T(8,128)(2,1)S(1)} %add_convert_fusion.4), channel_id=1, source_target_pairs={{8,16},{16,8},{9,17},{17,9},{10,18},{18,10},{11,19},{19,11},{12,20... | collective-permute-start | bytes 2457608 | tf_op jit(solution)/shard_map/ppermute | solution.py:109
  669.9 48.3 %collective-permute-start.57 = (f32[256,1280]{1,0:T(8,128)S(1)}, f32[256,1280]{1,0:T(8,128)S(1)}, u32[]{:S(2)}, u32[]{:S(2)}) collective-permute-start(f32[256,1280]{1,0:T(8,128)S(1)} %add_add_fusion.1.own), channel_id=1, source_target_pairs={{0,1},{1,0},{2,3},{3,2},{4,5},{5,4},{6,7},{7,6},{8,9},{9,8},{10,11... | collective-permute-start | bytes 3932168 | tf_op jit(solution)/shard_map/ppermute | solution.py:53
  669.9 46.5 %collective-permute-start.88 = (bf16[320,1280]{1,0:T(8,128)(2,1)S(1)}, bf16[320,1280]{1,0:T(8,128)(2,1)S(1)}, u32[]{:S(2)}, u32[]{:S(2)}) collective-permute-start(bf16[320,1280]{1,0:T(8,128)(2,1)S(1)} %add_convert_fusion.2), channel_id=1, source_target_pairs={{8,16},{16,8},{9,17},{17,9},{10,18},{18,10},{11,19},{19,11},{12,20... | collective-permute-start | bytes 2457608 | tf_op jit(solution)/shard_map/ppermute | solution.py:109
  684.5 36.0 %collective-permute-start.90 = (bf16[320,1280]{1,0:T(8,128)(2,1)S(1)}, bf16[320,1280]{1,0:T(8,128)(2,1)S(1)}, u32[]{:S(2)}, u32[]{:S(2)}) collective-permute-start(bf16[320,1280]{1,0:T(8,128)(2,1)S(1)} %add_convert_fusion.5.rest_4_.whole), channel_id=1, source_target_pairs={{8,0},{16,24},{9,1},{17,25},{10,2},{18,26},{11,3},{19,27},{12,4},{... | collective-permute-start | bytes 2457608 | tf_op jit(solution)/shard_map/ppermute | solution.py:111
  685.8 30.5 %collective-permute-start.83 = (bf16[160,1280]{1,0:T(8,128)(2,1)S(1)}, bf16[160,1280]{1,0:T(8,128)(2,1)S(1)}, u32[]{:S(2)}, u32[]{:S(2)}) collective-permute-start(bf16[160,1280]{1,0:T(8,128)(2,1)S(1)} %add_convert_fusion.19.whole), channel_id=1, source_target_pairs={{8,0},{16,24},{9,1},{17,25},{10,2},{18,26},{11,3},{19,27},{12,4},{... | collective-permute-start | bytes 1228808 | tf_op jit(solution)/shard_map/ppermute | solution.py:111
  688.2 45.6 %collective-permute-start.91 = (bf16[320,1280]{1,0:T(8,128)(2,1)S(1)}, bf16[320,1280]{1,0:T(8,128)(2,1)S(1)}, u32[]{:S(2)}, u32[]{:S(2)}) collective-permute-start(bf16[320,1280]{1,0:T(8,128)(2,1)S(1)} %add_convert_fusion.7.rest_3_.whole), channel_id=1, source_target_pairs={{8,0},{16,24},{9,1},{17,25},{10,2},{18,26},{11,3},{19,27},{12,4},{... | collective-permute-start | bytes 2457608 | tf_op jit(solution)/shard_map/ppermute | solution.py:111
  716.3 81.3 %collective-permute-start.54 = (f32[256,1280]{1,0:T(8,128)}, f32[256,1280]{1,0:T(8,128)}, u32[]{:S(2)}, u32[]{:S(2)}) collective-permute-start(f32[256,1280]{1,0:T(8,128)} %add_add_fusion.2.own), channel_id=1, source_target_pairs={{0,1},{1,0},{2,3},{3,2},{4,5},{5,4},{6,7},{7,6},{8,9},{9,8},{10,11... | collective-permute-start | bytes 3932168 | tf_op jit(solution)/shard_map/ppermute | solution.py:53
  719.2 23.4 %collective-permute-start.80 = (bf16[160,1280]{1,0:T(8,128)(2,1)S(1)}, bf16[160,1280]{1,0:T(8,128)(2,1)S(1)}, u32[]{:S(2)}, u32[]{:S(2)}) collective-permute-start(bf16[160,1280]{1,0:T(8,128)(2,1)S(1)} %add_convert_fusion.21.whole), channel_id=1, source_target_pairs={{8,0},{16,24},{9,1},{17,25},{10,2},{18,26},{11,3},{19,27},{12,4},{... | collective-permute-start | bytes 1228808 | tf_op jit(solution)/shard_map/ppermute | solution.py:111
  720.5 83.9 %collective-permute-start.86 = (bf16[320,1280]{1,0:T(8,128)(2,1)}, bf16[320,1280]{1,0:T(8,128)(2,1)}, u32[]{:S(2)}, u32[]{:S(2)}) collective-permute-start(bf16[320,1280]{1,0:T(8,128)(2,1)} %add_convert_fusion.3.whole), channel_id=1, source_target_pairs={{8,0},{16,24},{9,1},{17,25},{10,2},{18,26},{11,3},{19,27},{12,4},{... | collective-permute-start | bytes 2457608 | tf_op jit(solution)/shard_map/ppermute | solution.py:111
  721.8 79.1 %collective-permute-start.89 = (bf16[320,1280]{1,0:T(8,128)(2,1)}, bf16[320,1280]{1,0:T(8,128)(2,1)}, u32[]{:S(2)}, u32[]{:S(2)}) collective-permute-start(bf16[320,1280]{1,0:T(8,128)(2,1)} %add_convert_fusion.1.whole), channel_id=1, source_target_pairs={{8,0},{16,24},{9,1},{17,25},{10,2},{18,26},{11,3},{19,27},{12,4},{... | collective-permute-start | bytes 2457608 | tf_op jit(solution)/shard_map/ppermute | solution.py:111
  734.8 60.2 %collective-permute-start.74 = (bf16[160,1280]{1,0:T(8,128)(2,1)}, bf16[160,1280]{1,0:T(8,128)(2,1)}, u32[]{:S(2)}, u32[]{:S(2)}) collective-permute-start(bf16[160,1280]{1,0:T(8,128)(2,1)} %add_convert_fusion.25.whole), channel_id=1, source_target_pairs={{8,0},{16,24},{9,1},{17,25},{10,2},{18,26},{11,3},{19,27},{12,4},{... | collective-permute-start | bytes 1228808 | tf_op jit(solution)/shard_map/ppermute | solution.py:111
  743.4 49.0 %collective-permute-start.77 = (bf16[160,1280]{1,0:T(8,128)(2,1)S(1)}, bf16[160,1280]{1,0:T(8,128)(2,1)}, u32[]{:S(2)}, u32[]{:S(2)}) collective-permute-start(bf16[160,1280]{1,0:T(8,128)(2,1)S(1)} %add_convert_fusion.23.whole), channel_id=1, source_target_pairs={{8,0},{16,24},{9,1},{17,25},{10,2},{18,26},{11,3},{19,27},{12,4},{... | collective-permute-start | bytes 1228808 | tf_op jit(solution)/shard_map/ppermute | solution.py:111
  (257 other events, 3443.6 us)

commit v4 on v3

--- a/solution.py
+++ b/solution.py
@@ -25,7 +25,9 @@
 MASKED = -1e30
 VMEM_BYTES = 40 * 1024 * 1024
 LARGE_VMEM_BYTES = 56 * 1024 * 1024
+SMALL_VMEM_BYTES = 16 * 1024 * 1024
 F32 = jnp.float32
+SMALL_COST = pl.CostEstimate(flops=1000, bytes_accessed=1000, transcendentals=0)
 LOW = jnp.bfloat16
 
 
@@ -94,22 +96,138 @@
     )(values, *deps)
 
 
+def add_kernel(count, *refs):
+    total = refs[0][...].astype(F32)
+    for ref in refs[1:count]:
+        total = total + ref[...].astype(F32)
+    refs[-1][...] = total.astype(refs[-1].dtype)
+
+
+def added(terms, out):
+    if len(terms[0].shape) == 1:
+        return lax.optimization_barrier(sum(term.astype(F32) for term in terms).astype(out))
+    return pl.pallas_call(
+        partial(add_kernel, len(terms)),
+        in_specs=[IN_VMEM] * len(terms),
+        out_shape=jax.ShapeDtypeStruct(terms[0].shape, out),
+        compiler_params=pltpu.CompilerParams(vmem_limit_bytes=SMALL_VMEM_BYTES),
+        cost_estimate=SMALL_COST,
+    )(*terms)
+
+
+def rows_kernel(features, weights, own_out, other_out):
+    half = own_out.shape[0]
+    other_out[...] = dot(features[:, half:], weights[...], (0, 0), LOW)
+    own_out[...] = dot(features[:, :half], weights[...], (0, 0))
+
+
+def to_rows(features, weights):
+    half = features.shape[1] // 2
+    width = weights.shape[1]
+    return pl.pallas_call(
+        rows_kernel,
+        in_specs=[IN_VMEM] * 2,
+        out_shape=[
+            jax.ShapeDtypeStruct((half, width), F32),
+            jax.ShapeDtypeStruct((half, width), LOW),
+        ],
+        compiler_params=pltpu.CompilerParams(vmem_limit_bytes=VMEM_BYTES),
+        cost_estimate=SMALL_COST,
+    )(features, weights)
+
+
 def tensor_sum(own_part, other_part):
-    from_core = trade(other_part, "tensor", 1)
-    pair = split_low(own_part + from_core.astype(F32))
+    pair = added([own_part, trade(other_part, "tensor", 1)], LOW)
     return (pair, trade(pair, "tensor", 2))
 
 
 def group_sum(values):
     dtype = values.dtype
-    pair = lax.optimization_barrier(
-        add_low(values, lax.ppermute(values, "group", [(0, 1), (3, 2)])).astype(dtype)
-    )
-    whole = lax.optimization_barrier(
-        add_low(pair, lax.ppermute(pair, "group", [(1, 2), (2, 1)])).astype(dtype)
-    )
+    pair = added([values, lax.ppermute(values, "group", [(0, 1), (3, 2)])], dtype)
+    whole = added([pair, lax.ppermute(pair, "group", [(1, 2), (2, 1)])], dtype)
     back = lax.ppermute(whole, "group", [(1, 0), (2, 3)])
     return (pair, whole, back)
+
+
+def chain_kernel(count, *refs):
+    shifts, outs = refs[:count], refs[count : 2 * count]
+    landed = refs[2 * count : 3 * count]
+    crossed = refs[3 * count : 4 * count]
+    pairs = refs[4 * count : 5 * count]
+    sems = refs[5 * count]
+    here = lax.axis_index("group")
+    at_end = (here == 0) | (here == 3)
+    middle = jnp.where(here < 2, 1, 2)
+    end = jnp.where(here < 2, 0, 3)
+    facing = 3 - middle
+    barrier = pltpu.get_barrier_semaphore()
+
+    def remote(source, target, k, step, to):
+        return pltpu.make_async_remote_copy(
+            src_ref=source,
+            dst_ref=target,
+            send_sem=sems.at[k, 2 * step],
+            recv_sem=sems.at[k, 2 * step + 1],
+            device_id={"group": to},
+            device_id_type=pl.DeviceIdType.MESH,
+        )
+
+    inward = [remote(shifts[k], landed[k], k, 0, middle) for k in range(count)]
+    across = [remote(pairs[k], crossed[k], k, 1, facing) for k in range(count)]
+    outward = [remote(outs[k], landed[k], k, 2, end) for k in range(count)]
+
+    @pl.when(at_end)
+    def _():
+        pl.semaphore_signal(
+            barrier, inc=1, device_id={"group": middle}, device_id_type=pl.DeviceIdType.MESH
+        )
+        pl.semaphore_wait(barrier, 1)
+        for copy in inward:
+            copy.start()
+        for k in range(count):
+            outward[k].wait_recv()
+            outs[k][...] = landed[k][...]
+        for copy in inward:
+            copy.wait_send()
+
+    @pl.when(jnp.logical_not(at_end))
+    def _():
+        for to in (end, facing):
+            pl.semaphore_signal(
+                barrier, inc=1, device_id={"group": to}, device_id_type=pl.DeviceIdType.MESH
+            )
+        pl.semaphore_wait(barrier, 2)
+        for k in range(count + 1):
+            if k < count:
+                inward[k].wait_recv()
+                total = shifts[k][...].astype(F32) + landed[k][...].astype(F32)
+                pairs[k][...] = total.astype(pairs[k].dtype)
+                across[k].start()
+            if k > 0:
+                across[k - 1].wait_recv()
+                total = pairs[k - 1][...].astype(F32) + crossed[k - 1][...].astype(F32)
+                outs[k - 1][...] = total.astype(outs[k - 1].dtype)
+                outward[k - 1].start()
+        for k in range(count):
+            across[k].wait_send()
+            outward[k].wait_send()
+
+
+def chain_sum(shifts, deps):
+    count = len(shifts)
+    shapes = [jax.ShapeDtypeStruct(shift.shape, shift.dtype) for shift in shifts]
+    buffers = [pltpu.VMEM(shift.shape, shift.dtype) for shift in shifts]
+    return pl.pallas_call(
+        ordered_after(partial(chain_kernel, count), count, deps),
+        in_specs=[IN_VMEM] * count + [UNREAD] * len(deps),
+        out_specs=[IN_VMEM] * count,
+        out_shape=shapes,
+        scratch_shapes=buffers * 3 + [pltpu.SemaphoreType.DMA((count, 6))],
+        compiler_params=pltpu.CompilerParams(
+            collective_id=0, has_side_effects=True, vmem_limit_bytes=VMEM_BYTES
+        ),
+        cost_estimate=SMALL_COST,
+    )(*shifts, *deps)
 
 
 def mask_bias(seg_q, place_q, seg_k, place_k):
@@ -145,11 +263,7 @@
             jax.ShapeDtypeStruct((2 * width, rows), LOW),
         ],
         compiler_params=pltpu.CompilerParams(vmem_limit_bytes=VMEM_BYTES),
-        cost_estimate=pl.CostEstimate(
-            flops=2 * total * rows * model_width,
-            bytes_accessed=2 * total * model_width + 6 * total * rows,
-            transcendentals=0,
-        ),
+        cost_estimate=SMALL_COST,
     )(weights, own, other, scale, *deps)
 
 
@@ -197,9 +311,7 @@
             jax.ShapeDtypeStruct((width, 1), F32),
         ],
         compiler_params=pltpu.CompilerParams(vmem_limit_bytes=VMEM_BYTES),
-        cost_estimate=pl.CostEstimate(
-            flops=40 * total * rows, bytes_accessed=14 * total * rows, transcendentals=rows
-        ),
+        cost_estimate=SMALL_COST,
     )(own, arrived, query_grad, projected, scale, *deps)
 
 
@@ -244,11 +356,7 @@
         out_shape=[jax.ShapeDtypeStruct((parts * own_part, width), F32)]
         + [jax.ShapeDtypeStruct((own_part, width), LOW)] * parts,
         compiler_params=pltpu.CompilerParams(vmem_limit_bytes=VMEM_BYTES),
-        cost_estimate=pl.CostEstimate(
-            flops=2 * count * rows * total * width,
-            bytes_accessed=2 * count * rows * (total + width) + 3 * total * width,
-            transcendentals=0,
-        ),
+        cost_estimate=SMALL_COST,
     )(me, *lefts, *[side for right in rights for side in right], *deps)
 
 
@@ -279,7 +387,6 @@
 def attend(head_count, places, query, key_value, deps=()):
     blocks, _, rows = key_value.shape
     width, count = query.shape
-    work = head_count * blocks * rows * count * HEAD_DIM * 4
     return pl.pallas_call(
         ordered_after(partial(attend_kernel, head_count), 6, deps),
         in_specs=[IN_VMEM] * 6 + [UNREAD] * len(deps),
@@ -290,9 +397,7 @@
         ),
         scratch_shapes=[pltpu.VMEM((blocks * rows, count), F32)],
         compiler_params=pltpu.CompilerParams(vmem_limit_bytes=VMEM_BYTES),
-        cost_estimate=pl.CostEstimate(
-            flops=4 * work, bytes_accessed=6 * width * count, transcendentals=work // 256
-        ),
+        cost_estimate=SMALL_COST,
     )(*places, query, key_value, *deps)
 
 
@@ -304,15 +409,20 @@
     place_k,
     query,
     key_value,
-    heads_back,
+    rows_own,
+    rows_other,
+    weights,
     summed,
     total,
     query_grad,
     own_grad,
     other_grad,
     bias,
+    heads_back,
 ):
     blocks, _, rows = key_value.shape
+    rows_back = jnp.concatenate([rows_own[...], rows_other[...]], axis=0)
+    heads_back[...] = dot(weights[...], rows_back, (1, 1), LOW)
     width = head_count * HEAD_DIM
     for j in range(blocks):
         part = pl.ds(j * rows, rows)
@@ -346,24 +456,21 @@
         query_grad[cols, :] = acc
 
 
-def attend_back(head_count, places, query, key_value, heads_back, summed, total, deps=()):
+def attend_back(head_count, places, query, key_value, rows_back, weights, summed, total, deps=()):
     blocks, both, rows = key_value.shape
     width, count = query.shape
-    work = head_count * blocks * rows * count * HEAD_DIM * 2
     return pl.pallas_call(
-        ordered_after(partial(attend_back_kernel, head_count), 9, deps),
-        in_specs=[IN_VMEM] * 9 + [UNREAD] * len(deps),
+        ordered_after(partial(attend_back_kernel, head_count), 11, deps),
+        in_specs=[IN_VMEM] * 11 + [UNREAD] * len(deps),
         out_shape=(
             jax.ShapeDtypeStruct((width, count), F32),
             jax.ShapeDtypeStruct((both, rows), F32),
             jax.ShapeDtypeStruct((blocks - 1, both, rows), LOW if blocks == 2 else F32),
         ),
-        scratch_shapes=[pltpu.VMEM((blocks * rows, count), F32)],
+        scratch_shapes=[pltpu.VMEM((blocks * rows, count), F32), pltpu.VMEM((width, count), LOW)],
         compiler_params=pltpu.CompilerParams(vmem_limit_bytes=VMEM_BYTES),
-        cost_estimate=pl.CostEstimate(
-            flops=5 * 4 * work, bytes_accessed=16 * width * count, transcendentals=work // 128
-        ),
-    )(*places, query, key_value, heads_back, summed, total, *deps)
+        cost_estimate=SMALL_COST,
+    )(*places, query, key_value, *rows_back, weights, summed, total, *deps)
 
 
 def sigmoid(values):
@@ -435,11 +542,7 @@
         ],
         scratch_shapes=[pltpu.VMEM((2 * half, width), F32)],
         compiler_params=pltpu.CompilerParams(vmem_limit_bytes=LARGE_VMEM_BYTES),
-        cost_estimate=pl.CostEstimate(
-            flops=12 * half * width * units,
-            bytes_accessed=6 * width * units + 20 * half * units + 10 * half * width,
-            transcendentals=2 * half * units,
-        ),
+        cost_estimate=SMALL_COST,
     )(own, other, *feed_full, scale_up, scale_gate, *deps)
 
 
@@ -525,11 +628,7 @@
         ],
         scratch_shapes=[pltpu.VMEM((2 * half, width), F32)],
         compiler_params=pltpu.CompilerParams(vmem_limit_bytes=LARGE_VMEM_BYTES),
-        cost_estimate=pl.CostEstimate(
-            flops=12 * half * width * units,
-            bytes_accessed=6 * width * units + 24 * half * units + 10 * half * width,
-            transcendentals=2 * half * units,
-        ),
+        cost_estimate=SMALL_COST,
     )(own, other, up, gate, *feed_full, scale_up, scale_gate, *deps)
 
 
@@ -560,11 +659,7 @@
             jax.ShapeDtypeStruct((part, width), LOW),
         ],
         compiler_params=pltpu.CompilerParams(vmem_limit_bytes=LARGE_VMEM_BYTES),
-        cost_estimate=pl.CostEstimate(
-            flops=2 * count * rows * units * width,
-            bytes_accessed=2 * count * rows * (units + width) + 3 * units * width,
-            transcendentals=0,
-        ),
+        cost_estimate=SMALL_COST,
     )(*lefts, *[side for right in rights for side in right], *deps)
 
 
@@ -638,11 +733,7 @@
         out_specs=[flat] * len(outs) + term,
         out_shape=[jax.ShapeDtypeStruct((half, width), kind) for kind in outs] + term_shape,
         compiler_params=pltpu.CompilerParams(vmem_limit_bytes=VMEM_BYTES),
-        cost_estimate=pl.CostEstimate(
-            flops=40 * half * width,
-            bytes_accessed=(2 * len(arrays) + 4 * len(outs)) * half * width,
-            transcendentals=4 * half,
-        ),
+        cost_estimate=SMALL_COST,
     )(*arrays, rates, *deps)
 
 
@@ -724,21 +815,23 @@
         + [jax.ShapeDtypeStruct((rows // chunks, width), LOW)] * chunks,
         input_output_aliases={6 + n: n for n in range(len(earlier))},
         compiler_params=pltpu.CompilerParams(vmem_limit_bytes=VMEM_BYTES),
-        cost_estimate=pl.CostEstimate(
-            flops=30 * rows * width, bytes_accessed=32 * rows * width, transcendentals=rows * width
-        ),
+        cost_estimate=SMALL_COST,
     )(own_block, gradient, partner, master, first, second, *earlier, *deps)
 
 
+TAG = jax.ShapeDtypeStruct((8, 128), F32)
+
+
 def outer_kernel(group_count, at_end, whole, back, master, outer, *rest):
-    momentum_out, result_out = rest[-2:]
+    momentum_out, result_out, tag_out = rest[-3:]
     shift = jnp.where(at_end[0] == 1, back[...].astype(F32), whole[...].astype(F32)) / group_count
     momentum, result = outer_step(master[0], shift, outer[0], True)
     momentum_out[0] = momentum
     result_out[0] = result
-
-
-def outer_slab(which, chunk, group_count, at_end, whole, back, master, outer, earlier, deps=()):
+    tag_out[...] = jnp.zeros_like(tag_out)
+
+
+def outer_slab(which, chunk, group_count, at_end, whole, back, master, outer, earlier, deps):
     slabs, rows, width = master.shape
     part = whole.shape[0]
     tile = row_tile(part)
@@ -753,14 +846,12 @@
             num_scalar_prefetch=1,
             grid=(steps,),
             in_specs=[flat, flat, slab, slab] + [UNREAD] * (len(earlier) + len(deps)),
-            out_specs=[slab, slab],
+            out_specs=[slab, slab, pl.BlockSpec(TAG.shape, lambda i, at: (0, 0))],
         ),
-        out_shape=[result, result],
+        out_shape=[result, result, TAG],
         input_output_aliases={5 + n: n for n in range(len(earlier))},
         compiler_params=pltpu.CompilerParams(vmem_limit_bytes=VMEM_BYTES),
-        cost_estimate=pl.CostEstimate(
-            flops=20 * part * width, bytes_accessed=20 * part * width, transcendentals=part
-        ),
+        cost_estimate=SMALL_COST,
     )(at_end, whole, back, master, outer, *earlier, *deps)
 
 
@@ -771,15 +862,20 @@
         self.arrays = (master, first, second)
         self.outer_state = outer
         self.inner_outs = None
+        self.outer_outs = None
         self.sums = {}
-
-    def inner(self, which, gradient, deps):
+        self.shifts = {}
+
+    def inner(self, which, gradient, deps, chain=True):
         own, partner, block = gradient
         outs = adam_slab(
             which, self.chunks, block, own, partner, *self.arrays, self.inner_outs, deps
         )
         self.inner_outs = outs[:3]
-        self.sums[which] = [group_sum(shift) for shift in outs[3:]]
+        if chain:
+            self.sums[which] = [group_sum(shift) for shift in outs[3:]]
+        else:
+            self.shifts[which] = list(outs[3:])
         return outs[3]
 
     def pairs(self, which):
@@ -788,22 +884,27 @@
     def wholes(self, which):
         return [step[1] for step in self.sums[which]]
 
-    def outer(self):
-        outs = None
-        for which, chunk_sums in self.sums.items():
-            for chunk, (_, whole, back) in enumerate(chunk_sums):
-                outs = outer_slab(
-                    which,
-                    chunk,
-                    lax.axis_size("group"),
-                    self.at_end,
-                    whole,
-                    back,
-                    self.arrays[0],
-                    self.outer_state,
-                    outs,
-                )
-        return (*self.inner_outs, *outs)
+    def outer(self, which, tags, also=()):
+        for chunk, (_, whole, back) in enumerate(self.sums[which]):
+            if chunk < len(also):
+                tags = tags + also[chunk]
+            *self.outer_outs, tag = outer_slab(
+                which,
+                chunk,
+                lax.axis_size("group"),
+                self.at_end,
+                whole,
+                back,
+                self.arrays[0],
+                self.outer_state,
+                self.outer_outs,
+                tags,
+            )
+            tags = [tag]
+        return tags
+
+    def outs(self):
+        return (*self.inner_outs, *self.outer_outs)
 
 
 def place_kernel(core, own, other, *rest):
@@ -835,9 +936,7 @@
         out_shape=jax.ShapeDtypeStruct((1, count, 2 * half, width), F32),
         input_output_aliases={3: 0} if earlier else {},
         compiler_params=pltpu.CompilerParams(vmem_limit_bytes=VMEM_BYTES),
-        cost_estimate=pl.CostEstimate(
-            flops=0, bytes_accessed=16 * half * width, transcendentals=0
-        ),
+        cost_estimate=SMALL_COST,
     )(core, own, other, *earlier, *deps)
 
 
@@ -964,35 +1063,7 @@
         for b in micros
     ]
 
-    if pair:
-        arrivals = []
-        before = triple_across
-        feed_full = []
-        for which in range(3):
-            source = feed_low[which]
-            part = own_units // 2
-            piece = tie(jnp.where(even_group, source[:part], source[part:]), before)
-            across = trade(piece, "ctx", 1)
-            before = across
-            arrivals.append(across)
-            along = trade(across, "group", 1)
-            feed_full.append(
-                jnp.concatenate([source, ordered(even_group, across, along, 0)], axis=0)
-            )
-        part = own_rows // 2
-        piece = tie(
-            jnp.where(even_group, attention_low[3, :part], attention_low[3, part:]), triple_across
-        )
-        across = trade(piece, "ctx", 1)
-        output_other = ordered(even_group, across, trade(across, "group", 1), 0)
-        output_weights = ordered(ctx_first, attention_low[3], output_other, 0)
-    else:
-        output_weights = lax.all_gather(attention_low[3], "ctx", axis=0, tiled=True)
-        feed_full = list(lax.all_gather(feed_low, "ctx", axis=1, tiled=True))
-        arrivals = []
-    up_weights, gate_weights, down_weights = feed_full
-
-    projections, query_low, key_values = [], [], []
+    projections, query_low, local_sides = [], [], []
     for b in micros:
         projected, query, key_value = project(
             head_count,
@@ -1004,12 +1075,34 @@
         )
         projections.append(projected)
         query_low.append(query)
+        local_sides.append(key_value)
+
+    def all_sides(b, deps):
         if pair:
-            sent = tie(key_value, arrivals[0]) if b == 0 else key_value
-            key_values.append(jnp.stack([key_value, trade(sent, "ctx", 1)]))
-        else:
-            gathered = lax.all_gather(key_value, "ctx", axis=0)
-            key_values.append(jnp.take(gathered, block_ids, axis=0))
+            sent = tie(local_sides[b], *deps) if deps else local_sides[b]
+            return jnp.stack([local_sides[b], trade(sent, "ctx", 1)])
+        return jnp.take(lax.all_gather(local_sides[b], "ctx", axis=0), block_ids, axis=0)
+
+    def across_and_along(source, deps):
+        part = source.shape[0] // 2
+        piece = tie(jnp.where(even_group, source[:part], source[part:]), *deps)
+        across = trade(piece, "ctx", 1)
+        return (across, ordered(even_group, across, trade(across, "group", 1), 0))
+
+    arrivals = []
+    feed_full = []
+
+    def gather_feed(which, deps):
+        across, other = across_and_along(feed_low[which], deps)
+        arrivals.append(across)
+        feed_full.append(jnp.concatenate([feed_low[which], other], axis=0))
+
+    if pair:
+        gather_feed(0, [triple_across])
+        _, output_other = across_and_along(attention_low[3], [triple_across])
+        output_weights = ordered(ctx_first, attention_low[3], output_other, 0)
+    else:
+        output_weights = lax.all_gather(attention_low[3], "ctx", axis=0, tiled=True)
 
     rates_both = jnp.stack([rate_attention, rate_feed])
     scale_up = scale_up.reshape(1, units)
@@ -1022,31 +1115,43 @@
         )
         normed_rows.append((normed_low, trade(normed_low, "tensor", 1)))
 
+    last = micro_count - 1
+    key_values = []
     for b in micros:
-        deps = totals[-1:] + arrivals[1:2] * (b == 0)
-        if b == micro_count - 1 and b > 1:
-            normed_part(0, totals[-1:])
-            deps = [normed_rows[0][0]] + arrivals[2:]
+        if b < last:
+            key_values.append(all_sides(b, []))
+        if b == last:
+            if pair:
+                for which in (1, 2):
+                    gather_feed(which, totals[:1])
+            key_values.append(all_sides(b, totals[-1:]))
+        deps = totals[-1:]
+        if b == last:
+            for n in range(last):
+                normed_part(n, deps + arrivals[1:2] * (n == last - 1))
+                deps = [normed_rows[-1][0]]
+            deps = deps + arrivals[2:]
         summed, total, heads_low = attend(
             head_count, places[b], query_low[b], key_values[b], deps
         )
         summeds.append(summed)
         totals.append(total)
         heads_lows.append(heads_low)
-        other_part = dot(heads_low[:, half:], output_weights, (0, 0), LOW)
-        own_part = dot(heads_low[:, :half], output_weights, (0, 0))
-        attention_sums.append((*tensor_sum(own_part, other_part), token_own[b]))
-    for b in micros[len(normed_rows) :]:
-        normed_part(b, [rows_of[0] for rows_of in normed_rows[-1:]] + totals[-1:])
-
+        attention_sums.append((*tensor_sum(*to_rows(heads_low, output_weights)), token_own[b]))
+
+    if not pair:
+        feed_full = list(lax.all_gather(feed_low, "ctx", axis=1, tiled=True))
+    up_weights, gate_weights, down_weights = feed_full
     ups, gates, hidden_rows, feed_parts = [], [], [], []
     for b in micros:
+        if b == last:
+            normed_part(b, [feed_parts[-1][1]] if b > 0 else totals[-1:])
         up, gate, hidden, own_part, other_part = feed_forward(
             *normed_rows[b],
             feed_full,
             scale_up,
             scale_gate,
-            [normed_rows[-1][0] if b == 0 else feed_parts[-1][1]],
+            [totals[-1] if b == 0 else feed_parts[-1][1]],
         )
         ups.append(up)
         gates.append(gate)
@@ -1093,19 +1198,17 @@
         )
         skips.append(skip)
         attention_rate_terms.append(term)
-        attention_back_rows.append(
-            jnp.concatenate([attention_back, trade(attention_back, "tensor", 1)], axis=0)
-        )
+        attention_back_rows.append((attention_back, trade(attention_back, "tensor", 1)))
 
     def attention_part_back(b, deps):
-        heads_back = dot(output_weights, attention_back_rows[b], (1, 1), LOW)
         attention_grads.append(
             attend_back(
                 head_count,
                 places[b],
                 query_low[b],
                 key_values[b],
-                heads_back,
+                attention_back_rows[b],
+                output_weights,
                 summeds[b],
                 totals[b],
                 deps,
@@ -1124,14 +1227,13 @@
             block = me.reshape(1)
         return (gradient, trade(other.astype(LOW), "ctx", 1), block)
 
-    def feed_gradient(lefts, rights, deps, hold=()):
+    def feed_gradient(lefts, rights, deps):
         if not pair:
             right = jnp.concatenate([side for entry in rights for side in entry], axis=0)
             grad = to_owner(dot(jnp.concatenate(lefts, axis=0), right, (0, 0)), False)
             return (grad, grad[0])
         own, other = weight_grad(lefts, rights, deps)
-        sent = tie(other, *hold) if hold else other
-        return ((own, trade(sent, "ctx", 1), jnp.zeros((1,), jnp.int32)), own)
+        return ((own, trade(other, "ctx", 1), jnp.zeros((1,), jnp.int32)), own)
 
     triples, head_terms, input_sums = [], [], []
 
@@ -1149,11 +1251,8 @@
         )
         triples.append(triple)
         head_terms.append(terms)
-        other_part = dot(triple[:, half:], triple_weights, (0, 0), LOW)
-        own_part = dot(triple[:, :half], triple_weights, (0, 0))
-        input_sums.append(tensor_sum(own_part, other_part))
-
-    last = micro_count - 1
+        input_sums.append(tensor_sum(*to_rows(triple, triple_weights)))
+
     tag = feed_parts[-1][1]
     for b in micros:
         output_part(b, [tag])
@@ -1164,6 +1263,7 @@
         feed_part_back(b, [tag])
         tag = hidden_terms[b]
     up_grad, tag = feed_gradient(up_back_rows, normed_rows, [tag])
+    gate_grad, tag = feed_gradient(gate_back_rows, normed_rows, [tag])
     feed_steps = MatrixSteps(
         2 if own_units % 320 == 0 else 1,
         at_end,
@@ -1172,44 +1272,54 @@
         feedforward_second,
         feedforward_outer,
     )
+    attention_steps = MatrixSteps(
+        1,
+        at_end,
+        attention_weights,
+        attention_first,
+        attention_second,
+        attention_outer,
+    )
     side_arrivals = []
-
-    def send_sides(b):
+    arrived_grads = {0: [down_grad[1]], 1: [up_grad[1]]} if pair else {}
+    for b in micros:
+        if b > 0:
+            first_part_back(b, [tag])
+            tag = attention_rate_terms[b]
+        attention_part_back(b, [tag] + arrived_grads.get(b, []))
+        tag = attention_grads[b][0]
         if pair:
             side_arrivals.append(trade(attention_grads[b][2][0], "ctx", 1))
-
-    token_halves_of = [(token_own[b], token_other[b]) for b in micros]
-    arrived_down = [down_grad[1]] if pair else []
-    attention_part_back(0, [tag] + arrived_down)
-    send_sides(0)
-    first_part_back(1, [attention_grads[0][0]])
-    attention_part_back(1, [attention_rate_terms[1]])
-    send_sides(1)
-    tag = feed_steps.inner(2, down_grad, [attention_grads[1][0]])
-    sides_part_back(0, [tag])
-    for b in micros[2:]:
-        first_part_back(b, [head_terms[-1]])
-        attention_part_back(b, [attention_rate_terms[b]])
-        send_sides(b)
-        sides_part_back(b - 1, [attention_grads[b][0]])
-    output_grad = to_owner(
-        dot(
-            jnp.concatenate(heads_lows, axis=1), jnp.concatenate(attention_back_rows, axis=0), (1, 0)
-        ),
-        True,
+        if b == last - 1:
+            tag = feed_steps.inner(2, down_grad, [tag])
+    if pair:
+        own, other = triple_grad(me.reshape(1), 1, heads_lows, attention_back_rows, [tag])
+        output_grad = (own, trade(other, "ctx", 1), jnp.zeros((1,), jnp.int32))
+        output_arrived = [output_grad[1]]
+        gate_arrived = [gate_grad[1]]
+        tag = own
+    else:
+        right = jnp.concatenate([side for rows_of in attention_back_rows for side in rows_of], axis=0)
+        output_grad = to_owner(dot(jnp.concatenate(heads_lows, axis=1), right, (1, 0)), True)
+        output_arrived = []
+        gate_arrived = []
+    token_sides = [(token_own[b], token_other[b]) for b in micros]
+    tag = feed_steps.inner(0, up_grad, [tag])
+    tag = feed_steps.inner(
+        1, gate_grad, [tag] + feed_steps.pairs(2)[:1] + side_arrivals[:1], False
     )
-    gate_grad, gate_tag = feed_gradient(
-        gate_back_rows,
-        normed_rows,
-        [head_terms[-1]] + feed_steps.pairs(2)[:1],
-        side_arrivals[-1:],
-    )
-    tag = feed_steps.inner(0, up_grad, [gate_tag] + feed_steps.pairs(2))
-    sides_part_back(last, [tag])
+    for b in micros:
+        deps = [tag]
+        if b == 0:
+            deps += feed_steps.pairs(2) + side_arrivals[1:2]
+        elif b < last:
+            deps += side_arrivals[-1:]
+        else:
+            deps += feed_steps.pairs(0)[:1] + feed_steps.wholes(2)[:1] + output_arrived
+        sides_part_back(b, deps)
+        tag = head_terms[b]
     if pair:
-        own, *others = triple_grad(
-            me.reshape(1), 3, triples, token_halves_of, feed_steps.wholes(2)[:1]
-        )
+        own, *others = triple_grad(me.reshape(1), 3, triples, token_sides, [tag])
         tag = own
         projection_grads = [
             (own, trade(others[which], "ctx", 1), jnp.full((1,), which, jnp.int32))
@@ -1218,10 +1328,11 @@
     else:
         triple_all = dot(
             jnp.concatenate(triples, axis=1),
-            jnp.concatenate([side for sides in token_halves_of for side in sides], axis=0),
+            jnp.concatenate([side for sides in token_sides for side in sides], axis=0),
             (1, 0),
         ).reshape(3, head_width, model_width)
         projection_grads = [to_owner(triple_all[which], True) for which in range(3)]
+    tag = attention_steps.inner(3, output_grad, [tag] + feed_steps.wholes(2) + feed_steps.pairs(0), False)
 
     block_output = None
     for b in micros:
@@ -1232,9 +1343,32 @@
             outputs[b],
             trade(outputs[b], "tensor", 1),
             block_output,
-            [tag],
-        )
-
+            [head_terms[0]],
+        )
+
+    input_gradient = None
+
+    def place_input(b, deps):
+        input_own = added([skips[b], *input_sums[b]], F32)
+        return place_rows(
+            b,
+            micro_count,
+            core_index,
+            input_own,
+            trade(input_own, "tensor", 1),
+            input_gradient,
+            deps,
+        )
+
+    input_gradient = place_input(0, [tag])
+    tags = feed_steps.outer(2, [tag])
+    tag = attention_steps.inner(0, projection_grads[0], tags, False)
+    input_gradient = place_input(1, [tag])
+    for which in (1, 2):
+        tag = attention_steps.inner(which, projection_grads[which], [tag], False)
+    tags = feed_steps.outer(0, [tag])
+    for b in micros[2:]:
+        input_gradient = place_input(b, [tag])
     rate_terms = jnp.concatenate([sum(attention_rate_terms), sum(feed_rate_terms)], axis=0)
     rate_terms = rate_terms + trade(rate_terms, "tensor", 1)
     head_terms = sum(head_terms).reshape(head_width)
@@ -1257,32 +1391,6 @@
         heads_grad = lax.psum_scatter(head_terms, "ctx", scatter_dimension=0, tiled=True)
         hidden_grad = lax.psum_scatter(hidden_terms, "ctx", scatter_dimension=1, tiled=True)
         rates_grad = lax.psum_scatter(rate_terms, "ctx", scatter_dimension=1, tiled=True)
-
-    attention_steps = MatrixSteps(
-        1,
-        at_end,
-        attention_weights,
-        attention_first,
-        attention_second,
-        attention_outer,
-    )
-    attention_steps.inner(3, output_grad, [tag])
-    input_gradient = None
-    arrived_inputs = [sums[1] for sums in input_sums]
-    feed_steps.inner(1, gate_grad, feed_steps.pairs(0) + arrived_inputs[:2])
-    for which in range(3):
-        attention_steps.inner(
-            which,
-            projection_grads[which],
-            feed_steps.wholes(0) + arrived_inputs[2:] if which == 0 else [],
-        )
-    for b in micros:
-        input_own = skips[b] + add_low(*input_sums[b])
-        input_gradient = place_rows(
-            b, micro_count, core_index, input_own, trade(input_own, "tensor", 1), input_gradient
-        )
-    feed_outs = feed_steps.outer()
-    attention_outs = attention_steps.outer()
 
     masters = (head_scales, hidden_scales, residual_rates)
     firsts = (heads_first[0], hidden_first[0], rates_first[0])
@@ -1302,8 +1410,25 @@
         small_moments.append(moment)
         small_variances.append(variance)
         small_shifts.append((masters[which] - updated).reshape(-1))
-    _, whole, back = group_sum(jnp.concatenate(small_shifts))
-    shift_flat = jnp.where(at_end == 1, back, whole) / group_count
+    shift_flat = jnp.concatenate(small_shifts)
+    flat_size = shift_flat.size
+    flat_rows = -(-flat_size // 1024) * 8
+    shift_flat = jnp.pad(shift_flat, (0, flat_rows * 128 - flat_size)).reshape(flat_rows, 128)
+    feed_shifts = feed_steps.shifts[1]
+    attention_shifts = attention_steps.shifts
+    *chained, shift_flat = chain_sum(
+        [*feed_shifts, *[attention_shifts[which][0] for which in (3, 0, 1, 2)], shift_flat], tags
+    )
+    shift_flat = shift_flat.reshape(-1)[:flat_size] / group_count
+    feed_steps.sums[1] = [(None, total, total) for total in chained[: len(feed_shifts)]]
+    for which, total in zip((3, 0, 1, 2), chained[len(feed_shifts) :]):
+        attention_steps.sums[which] = [(None, total, total)]
+    tags = feed_steps.outer(1, [])
+    for which in (3, 0, 1, 2):
+        tags = attention_steps.outer(which, tags)
+    feed_outs = feed_steps.outs()
+    attention_outs = attention_steps.outs()
+
     small_momenta, small_results = [], []
     start = 0
     for which in range(3):

time: 815 us -> 725 us (0.89)
  Pallas kernels: 266 us -> 443 us
  waiting for transfers between devices: 250 us -> 91.5 us
  starting transfers between devices: 130 us -> 67.5 us
  other arithmetic: 69.3 us -> 36.3 us
  matrix products: 27.4 us -> 0 us
  local copies, waits for them, and re-layouts: 61.5 us -> 78 us
    pallas_call x3 -> x33, Pallas kernels: 24.4 us -> 192 us  [the longest x1 107 us: chain_sum(): pl.pallas_call(ordered_after(partial(chain_kernel, count), count, deps),...]
    ppermute x11 -> x4, waiting for transfers between devices: 82.3 us -> 9.33 us  [group_sum(): back = lax.ppermute(whole, 'group', [(1, 0), (2, 3)])]
    ppermute x65, waiting for transfers between devices: 131 us -> 82.2 us  [trade(): return lax.ppermute(values, axis, [(i, i ^ bit) for i in range(count)])]
    ppermute x11 -> x4, starting transfers between devices: 58.3 us -> 13.2 us  [group_sum(): lax.ppermute(values, 'group', [(0, 1), (3, 2)])]
    ppermute x11 -> x4, waiting for transfers between devices: 36.4 us -> 0.01 us  [group_sum(): lax.ppermute(values, 'group', [(0, 1), (3, 2)])]
    dot_general x16 -> x0, matrix products: 27.4 us -> none  [dot(): lax.dot_general(left, right, (((contract[0],), (contract[1],)), ((), ()))...]
    convert_element_type x27 -> x0, other arithmetic: 26 us -> none  [the longest x6 9.73 us: split_low(): return lax.optimization_barrier(values.astype(LOW))]
    unnamed x461 -> x468, local copies, waits for them, and re-layouts: 49.1 us -> 68.9 us
  transfers between devices with their start and end apart: 98 -> 77, of which waited for: 32 -> 19; matrix products, arithmetic and copies ran while one was open for 15% -> 6% of each run, Pallas kernels for 33% -> 61%
where the time goes in v4:
time: 725 us; the launch traced here: 719 us
  Pallas kernels  443 us (61%)
  waiting for transfers between devices  91.5 us (13%)
  local copies, waits for them, and re-layouts  78 us (11%)
  starting transfers between devices  67.5 us (9%)
  other arithmetic  36.3 us (5%)
    pallas_call x1, Pallas kernels, chain_sum(): pl.pallas_call(ordered_after(partial(chain_kernel, count), count, deps),...  107 us
    ppermute x65, waiting for transfers between devices, trade(): return lax.ppermute(values, axis, [(i, i ^ bit) for i in range(count)])  82.2 us
    unnamed x468, local copies, waits for them, and re-layouts  68.9 us
    pallas_call x23, Pallas kernels, added(): pl.pallas_call(partial(add_kernel, len(terms)), in_specs=[IN_VMEM] * len(...  46.6 us
    pallas_call x7, Pallas kernels, adam_slab(): pl.pallas_call(partial(adam_kernel, has_partner, chunks), grid_spec=pltpu...  44.8 us
    ppermute x65, starting transfers between devices, trade(): return lax.ppermute(values, axis, [(i, i ^ bit) for i in range(count)])  42.3 us
    pallas_call x3, Pallas kernels, feed_backward(): pl.pallas_call(ordered_after(partial(feed_back_kernel, math.sqrt(width)),...  41.1 us
    pallas_call x3, Pallas kernels, feed_forward(): pl.pallas_call(ordered_after(partial(feed_kernel, math.sqrt(width)), 7, d...  34 us
  transfers between devices with their start and end apart: 77, of which 19 were waited for; matrix products, arithmetic and copies ran while one was open for 6% of the time, Pallas kernels for 61%

profile of v4, /device:TPU:0, one launch (start us, length us, event | category | flops | bytes accessed | tf_op | source)
XLA Modules:
  0.0 719.0 jit_solution(1040659048113915622)
XLA Ops:
  3.8 2.9 collective-permute-start
  9.0 4.6 broadcast_select_fusion
  26.5 11.1 %collective-permute-done.1 = bf16[3,80,1280]{2,1,0:T(8,128)(2,1)} collective-permute-done((bf16[3,80,1280]{2,1,0:T(8,128)(2,1)}, bf16[3,80,1280]{2,1,0:T(8,128)(2,1)}, u32[]{:S(2)}, u32[]{:S(2)}) %collective-permute-start.1) | collective-permute-done | bytes 614432 | tf_op jit(solution)/shard_map/ppermute | solution.py:55
  65.5 3.3 shard_map.442
  79.5 3.3 shard_map.443
  104.1 21.4 %collective-permute-done.5 = bf16[640,512]{1,0:T(8,128)(2,1)S(1)} collective-permute-done((bf16[640,512]{1,0:T(8,128)(2,1)}, bf16[640,512]{1,0:T(8,128)(2,1)S(1)}, u32[]{:S(2)}, u32[]{:S(2)}) %collective-permute-start.5) | collective-permute-done | bytes 655392 | tf_op jit(solution)/shard_map/ppermute | solution.py:55
  128.6 3.3 shard_map.454
  137.2 8.6 %collective-permute-done.19 = bf16[320,1280]{1,0:T(8,128)(2,1)S(1)} collective-permute-done((bf16[320,1280]{1,0:T(8,128)(2,1)}, bf16[320,1280]{1,0:T(8,128)(2,1)S(1)}, u32[]{:S(2)}, u32[]{:S(2)}) %collective-permute-start.19) | collective-permute-done | bytes 819232 | tf_op jit(solution)/shard_map/ppermute | solution.py:55
  152.2 11.2 %shard_map.458 = (f32[512,1280]{1,0:T(8,128)}, f32[512,1280]{1,0:T(8,128)}, bf16[512,1280]{1,0:T(8,128)(2,1)}, f32[256,1280]{1,0:T(8,128)}, bf16[256,1280]{1,0:T(8,128)(2,1)}) custom-call(bf16[256,1280]{1,0:T(8,128)(2,1)} %copy-done.28, bf16[256,1280]{1,0:T(8,128)(2,1)} %copy-done.199, bf16[1280,1280]{1,0:T(8,128)(2,1)} %pad_maximum_fusion.refs_2_.refs_4_, ...), custom_call_target="tpu_custom_call" | custom-call | flops 1000 | bytes 1000 | tf_op jit(solution)/shard_map/pallas_call | solution.py:531
  163.5 11.5 %shard_map.459 = (f32[512,1280]{1,0:T(8,128)}, f32[512,1280]{1,0:T(8,128)}, bf16[512,1280]{1,0:T(8,128)(2,1)}, f32[256,1280]{1,0:T(8,128)}, bf16[256,1280]{1,0:T(8,128)(2,1)}) custom-call(bf16[256,1280]{1,0:T(8,128)(2,1)} %copy-done.27, bf16[256,1280]{1,0:T(8,128)(2,1)} %collective-permute-done.16.refs_1_.refs_6_, ...), custom_call_target="tpu_custom_call" | custom-call | flops 1000 | bytes 1000 | tf_op jit(solution)/shard_map/pallas_call | solution.py:531
  181.6 11.3 %shard_map.461 = (f32[512,1280]{1,0:T(8,128)}, f32[512,1280]{1,0:T(8,128)}, bf16[512,1280]{1,0:T(8,128)(2,1)}, f32[256,1280]{1,0:T(8,128)}, bf16[256,1280]{1,0:T(8,128)(2,1)}) custom-call(bf16[256,1280]{1,0:T(8,128)(2,1)} %copy-done.43, bf16[256,1280]{1,0:T(8,128)(2,1)} %collective-permute-done.22.refs_1_.refs_8_, ...), custom_call_target="tpu_custom_call" | custom-call | flops 1000 | bytes 1000 | tf_op jit(solution)/shard_map/pallas_call | solution.py:531
  192.9 3.9 collective-permute-done.28.refs_4_
  197.9 4.0 shard_map.465
  201.9 2.5 shard_map.463.refs_3_
  205.8 13.7 %shard_map.466 = (bf16[512,1280]{1,0:T(8,128)(2,1)}, bf16[512,1280]{1,0:T(8,128)(2,1)}, f32[2,1280]{1,0:T(2,128)}, f32[256,1280]{1,0:T(8,128)}, bf16[256,1280]{1,0:T(8,128)(2,1)}) custom-call(bf16[256,1280]{1,0:T(8,128)(2,1)} %copy-done.94, bf16[256,1280]{1,0:T(8,128)(2,1)} %copy-done.200, f32[512,1280]{1,0:T(8,128)} %get-tuple-element.229.refs_2_, ...), custom_call_target="tpu_custom_call" | custom-call | flops 1000 | bytes 1000 | tf_op jit(solution)/shard_map/pallas_call | solution.py:616
  224.3 4.4 shard_map.467
  233.2 13.7 %shard_map.468 = (bf16[512,1280]{1,0:T(8,128)(2,1)}, bf16[512,1280]{1,0:T(8,128)(2,1)}, f32[2,1280]{1,0:T(2,128)}, f32[256,1280]{1,0:T(8,128)}, bf16[256,1280]{1,0:T(8,128)(2,1)}) custom-call(bf16[256,1280]{1,0:T(8,128)(2,1)} %copy-done.109, bf16[256,1280]{1,0:T(8,128)(2,1)} %copy-done.202, f32[512,1280]{1,0:T(8,128)} %get-tuple-element.233.refs_2_, ...), custom_call_target="tpu_custom_call" | custom-call | flops 1000 | bytes 1000 | tf_op jit(solution)/shard_map/pallas_call | solution.py:616
  250.8 4.1 shard_map.469
  254.9 2.5 shard_map.470.refs_4_
  258.8 9.7 %shard_map.471 = (f32[640,1280]{1,0:T(8,128)}, bf16[640,1280]{1,0:T(8,128)(2,1)}) custom-call(bf16[512,1280]{1,0:T(8,128)(2,1)} %get-tuple-element.242.refs_0_, bf16[512,1280]{1,0:T(8,128)(2,1)} %get-tuple-element.243.refs_1_, bf16[512,1280]{1,0:T(8,128)(2,1)} %get-tuple-element.244.refs_2_, bf16[256,1280]{1,0:T(8,128)(2,1)} %copy-done.94, ...), custom_call_target="tpu_custom_call" | custom-call | flops 1000 | bytes 1000 | tf_op jit(solution)/shard_map/pallas_call | solution.py:654
  270.0 4.4 collective-permute-done.35.refs_5_
  277.6 3.5 shard_map.472
  282.9 13.6 %shard_map.473 = (bf16[512,1280]{1,0:T(8,128)(2,1)}, bf16[512,1280]{1,0:T(8,128)(2,1)}, f32[2,1280]{1,0:T(2,128)}, f32[256,1280]{1,0:T(8,128)}, bf16[256,1280]{1,0:T(8,128)(2,1)}) custom-call(bf16[256,1280]{1,0:T(8,128)(2,1)} %copy-done.95, bf16[256,1280]{1,0:T(8,128)(2,1)} %copy-done.201, f32[512,1280]{1,0:T(8,128)} %get-tuple-element.251.refs_2_, ...), custom_call_target="tpu_custom_call" | custom-call | flops 1000 | bytes 1000 | tf_op jit(solution)/shard_map/pallas_call | solution.py:616
  296.5 9.8 %shard_map.474 = (f32[640,1280]{1,0:T(8,128)}, bf16[640,1280]{1,0:T(8,128)(2,1)}) custom-call(bf16[512,1280]{1,0:T(8,128)(2,1)} %get-tuple-element.255.refs_0_, bf16[512,1280]{1,0:T(8,128)(2,1)} %get-tuple-element.256.refs_1_, bf16[512,1280]{1,0:T(8,128)(2,1)} %get-tuple-element.257.refs_2_, bf16[256,1280]{1,0:T(8,128)(2,1)} %copy-done.28, ...), custom_call_target="tpu_custom_call" | custom-call | flops 1000 | bytes 1000 | tf_op jit(solution)/shard_map/pallas_call | solution.py:654
  308.3 2.7 collective-permute-done.42.refs_1_
  312.5 10.0 %shard_map.475 = (f32[640,1280]{1,0:T(8,128)}, bf16[640,1280]{1,0:T(8,128)(2,1)}) custom-call(bf16[512,1280]{1,0:T(8,128)(2,1)} %get-tuple-element.249.refs_0_, bf16[512,1280]{1,0:T(8,128)(2,1)} %get-tuple-element.250.refs_1_, bf16[512,1280]{1,0:T(8,128)(2,1)} %get-tuple-element.254.refs_2_, bf16[256,1280]{1,0:T(8,128)(2,1)} %copy-done.28, ...), custom_call_target="tpu_custom_call" | custom-call | flops 1000 | bytes 1000 | tf_op jit(solution)/shard_map/pallas_call | solution.py:654
  326.5 10.3 %shard_map.476 = (f32[320,512]{1,0:T(8,128)S(1)}, f32[640,512]{1,0:T(8,128)S(1)}, bf16[1,640,512]{2,1,0:T(8,128)(2,1)}) custom-call(s32[1,512]{1,0:T(1,128)S(1)} %get-tuple-element.423.refs_0_, s32[1,512]{1,0:T(1,128)S(1)} %slice.299.refs_1_, s32[1024,1]{1,0:T(8,128)S(1)} %bitcast.138, s32[1024,1]{1,0:T(8,128)S(1)} %bitcast.130, ...), custom_call_target="tpu_custom_call" | custom-call | flops 1000 | bytes 1000 | tf_op jit(solution)/shard_map/pallas_call | solution.py:462
  337.8 3.3 shard_map.478
  346.5 8.8 %shard_map.479 = (f32[320,512]{1,0:T(8,128)S(1)}, f32[640,512]{1,0:T(8,128)S(1)}, bf16[1,640,512]{2,1,0:T(8,128)(2,1)}) custom-call(s32[1,512]{1,0:T(1,128)S(1)} %get-tuple-element.424.refs_0_, s32[1,512]{1,0:T(1,128)S(1)} %slice.299.refs_1_, s32[1024,1]{1,0:T(8,128)S(1)} %bitcast.136, s32[1024,1]{1,0:T(8,128)S(1)} %bitcast.131, ...), custom_call_target="tpu_custom_call" | custom-call | flops 1000 | bytes 1000 | tf_op jit(solution)/shard_map/pallas_call | solution.py:462
  355.4 11.1 %shard_map.480 = (f32[1,3,640,1280]{3,2,1,0:T(8,128)}, f32[1,3,640,1280]{3,2,1,0:T(8,128)}, f32[1,3,640,1280]{3,2,1,0:T(8,128)}, bf16[320,1280]{1,0:T(8,128)(2,1)S(1)}, bf16[320,1280]{1,0:T(8,128)(2,1)}) custom-call(s32[1]{0:T(128)} %constant.31.clone.1.offset, f32[640,1280]{1,0:T(8,128)S(1)} %copy-done.30, ...), custom_call_target="tpu_custom_call" | custom-call | flops 1000 | bytes 1000 | tf_op jit(solution)/shard_map/pallas_call | solution.py:805
  368.4 2.7 shard_map.482
  372.2 3.1 collective-permute-start.48
  379.1 8.9 %shard_map.483 = (f32[320,512]{1,0:T(8,128)S(1)}, f32[640,512]{1,0:T(8,128)S(1)}, bf16[1,640,512]{2,1,0:T(8,128)(2,1)}) custom-call(s32[1,512]{1,0:T(1,128)S(1)} %get-tuple-element.425.refs_0_, s32[1,512]{1,0:T(1,128)S(1)} %slice.299.refs_1_, s32[1024,1]{1,0:T(8,128)S(1)} %bitcast.134, s32[1024,1]{1,0:T(8,128)S(1)} %bitcast.132, ...), custom_call_target="tpu_custom_call" | custom-call | flops 1000 | bytes 1000 | tf_op jit(solution)/shard_map/pallas_call | solution.py:462
  388.1 4.2 shard_map.484
  392.3 10.9 %shard_map.485 = (f32[1,3,640,1280]{3,2,1,0:T(8,128)}, f32[1,3,640,1280]{3,2,1,0:T(8,128)}, f32[1,3,640,1280]{3,2,1,0:T(8,128)}, bf16[320,1280]{1,0:T(8,128)(2,1)}, bf16[320,1280]{1,0:T(8,128)(2,1)}) custom-call(s32[1]{0:T(128)} %constant.31.clone.1.offset, f32[640,1280]{1,0:T(8,128)S(1)} %copy-done.36, ...), custom_call_target="tpu_custom_call", output_to_operand_aliasing={{0}: (6, {}), {1}: (7, {}), {2}: (8, {})} | custom-call | flops 1000 | bytes 1000 | tf_op jit(solution)/shard_map/pallas_call | solution.py:805
  409.7 3.2 collective-permute-done.50.refs_8_.refs_1_
  422.5 10.1 %shard_map.487 = (f32[1,3,640,1280]{3,2,1,0:T(8,128)}, f32[1,3,640,1280]{3,2,1,0:T(8,128)}, f32[1,3,640,1280]{3,2,1,0:T(8,128)}, bf16[320,1280]{1,0:T(8,128)(2,1)S(1)}, bf16[320,1280]{1,0:T(8,128)(2,1)S(1)}) custom-call(s32[1]{0:T(128)} %constant.31.clone.1.offset, ...), custom_call_target="tpu_custom_call", output_to_operand_aliasing={{0}: (6, {}), {1}: (7, {}), {2}: (8, {})} | custom-call | flops 1000 | bytes 1000 | tf_op jit(solution)/shard_map/pallas_call | solution.py:805
  437.7 6.4 collective-permute-start.65
  450.5 2.7 shard_map.494.refs_6_.rest_3_.refs_0_
  459.2 4.8 shard_map.506
  472.5 5.5 collective-permute-done.72
  487.8 3.3 shard_map.490.rest_0_
  491.1 3.3 shard_map.491.rest_0_
  494.4 3.5 shard_map.492
  500.9 3.6 shard_map.509
  510.8 2.5 shard_map.519.whole
  519.1 10.5 %collective-permute-done.56.refs_2_ = bf16[256,1280]{1,0:T(8,128)(2,1)} collective-permute-done((bf16[256,1280]{1,0:T(8,128)(2,1)}, bf16[256,1280]{1,0:T(8,128)(2,1)}, u32[]{:S(2)}, u32[]{:S(2)}) %collective-permute-start.56) | collective-permute-done | bytes 655392 | tf_op jit(solution)/shard_map/ppermute | solution.py:55
  532.8 2.7 shard_map.505.own
  535.5 2.7 shard_map.502.own
  538.2 2.7 shard_map.499.own
  541.4 7.6 %collective-permute-done.67.back = bf16[320,1280]{1,0:T(8,128)(2,1)} collective-permute-done((bf16[320,1280]{1,0:T(8,128)(2,1)}, bf16[320,1280]{1,0:T(8,128)(2,1)}, u32[]{:S(2)}, u32[]{:S(2)}) %collective-permute-start.67) | collective-permute-done | bytes 819232 | tf_op jit(solution)/shard_map/ppermute | solution.py:148
  549.6 3.8 copy-done
  553.4 3.5 shard_map.511
  556.9 3.6 shard_map.512
  567.5 3.4 shard_map.515
  572.4 3.4 shard_map.516
  575.8 3.5 shard_map.520
  581.1 3.7 shard_map.521
  584.8 107.2 %shard_map.522 = (bf16[320,1280]{1,0:T(8,128)(2,1)S(1)}, bf16[320,1280]{1,0:T(8,128)(2,1)S(1)}, bf16[160,1280]{1,0:T(8,128)(2,1)S(1)}, bf16[160,1280]{1,0:T(8,12...) custom-call(bf16[320,1280]{1,0:T(8,128)(2,1)S(1)} %copy-done.89, ...), custom_call_target="tpu_custom_call" | custom-call | flops 1000 | bytes 1000 | tf_op jit(solution)/shard_map/pallas_call | solution.py:220
  692.1 3.3 shard_map.523
  695.4 3.4 shard_map.524
  708.9 3.3 shard_map.510.rest_0_
  712.2 3.3 shard_map.514.rest_0_
  715.5 3.3 shard_map.517
  (741 shorter events, 233.8 us)
Async XLA Ops:
  3.8 18.1 %collective-permute-start = (bf16[3,80,1280]{2,1,0:T(8,128)(2,1)}, bf16[3,80,1280]{2,1,0:T(8,128)(2,1)}, u32[]{:S(2)}, u32[]{:S(2)}) collective-permute-start(bf16[3,80,1280]{2,1,0:T(8,128)(2,1)} %slice_select_fusion.4), channel_id=1, source_target_pairs={{0,4},{4,0},{1,5},{5,1},{2,6},{6,2},{3,7},{7,3},{8,12},{12,8},{9,1... | collective-permute-start | bytes 1843208 | tf_op jit(solution)/shard_map/ppermute | solution.py:55
  6.9 17.0 %collective-permute-start.2 = (bf16[2720]{0:T(1024)(128)(2,1)S(1)}, bf16[2720]{0:T(1024)(128)(2,1)S(1)}, u32[]{:S(2)}, u32[]{:S(2)}) collective-permute-start(bf16[2720]{0:T(1024)(128)(2,1)S(1)} %concatenate.162), channel_id=1, source_target_pairs={{0,4},{4,0},{1,5},{5,1},{2,6},{6,2},{3,7},{7,3},{8,12},{12,8},{9,1... | collective-permute-start | bytes 16328 | tf_op jit(solution)/shard_map/ppermute | solution.py:55
  21.9 15.7 %collective-permute-start.1 = (bf16[3,80,1280]{2,1,0:T(8,128)(2,1)}, bf16[3,80,1280]{2,1,0:T(8,128)(2,1)}, u32[]{:S(2)}, u32[]{:S(2)}) collective-permute-start(bf16[3,80,1280]{2,1,0:T(8,128)(2,1)} %collective-permute-done.refs_1_), channel_id=1, source_target_pairs={{0,8},{8,0},{16,24},{24,16},{1,9},{9,1},{17,25},{25,17},{2,10},{10... | collective-permute-start | bytes 1843208 | tf_op jit(solution)/shard_map/ppermute | solution.py:55
  24.4 25.8 %collective-permute-start.6 = (bf16[80,1280]{1,0:T(8,128)(2,1)}, bf16[80,1280]{1,0:T(8,128)(2,1)}, u32[]{:S(2)}, u32[]{:S(2)}) collective-permute-start(bf16[80,1280]{1,0:T(8,128)(2,1)} %shard_map.445), channel_id=1, source_target_pairs={{0,4},{4,0},{1,5},{5,1},{2,6},{6,2},{3,7},{7,3},{8,12},{12,8},{9,1... | collective-permute-start | bytes 614408 | tf_op jit(solution)/shard_map/ppermute | solution.py:55
  25.9 35.6 %collective-permute-start.17 = (bf16[320,1280]{1,0:T(8,128)(2,1)}, bf16[320,1280]{1,0:T(8,128)(2,1)}, u32[]{:S(2)}, u32[]{:S(2)}) collective-permute-start(bf16[320,1280]{1,0:T(8,128)(2,1)} %shard_map.457), channel_id=1, source_target_pairs={{0,4},{4,0},{1,5},{5,1},{2,6},{6,2},{3,7},{7,3},{8,12},{12,8},{9,1... | collective-permute-start | bytes 2457608 | tf_op jit(solution)/shard_map/ppermute | solution.py:55
  45.0 19.0 %collective-permute-start.4 = (bf16[640,512]{1,0:T(8,128)(2,1)}, bf16[640,512]{1,0:T(8,128)(2,1)}, u32[]{:S(2)}, u32[]{:S(2)}) collective-permute-start(bf16[640,512]{1,0:T(8,128)(2,1)} %get-tuple-element.209), channel_id=1, source_target_pairs={{0,4},{4,0},{1,5},{5,1},{2,6},{6,2},{3,7},{7,3},{8,12},{12,8},{9,1... | collective-permute-start | bytes 1966088 | tf_op jit(solution)/shard_map/ppermute | solution.py:55
  57.9 20.1 %collective-permute-start.3 = (bf16[640,512]{1,0:T(8,128)(2,1)}, bf16[640,512]{1,0:T(8,128)(2,1)}, u32[]{:S(2)}, u32[]{:S(2)}) collective-permute-start(bf16[640,512]{1,0:T(8,128)(2,1)} %get-tuple-element.207), channel_id=1, source_target_pairs={{0,4},{4,0},{1,5},{5,1},{2,6},{6,2},{3,7},{7,3},{8,12},{12,8},{9,1... | collective-permute-start | bytes 1966088 | tf_op jit(solution)/shard_map/ppermute | solution.py:55
  61.6 30.3 %collective-permute-start.18 = (bf16[320,1280]{1,0:T(8,128)(2,1)}, bf16[320,1280]{1,0:T(8,128)(2,1)}, u32[]{:S(2)}, u32[]{:S(2)}) collective-permute-start(bf16[320,1280]{1,0:T(8,128)(2,1)} %collective-permute-done.17), channel_id=1, source_target_pairs={{0,8},{8,0},{16,24},{24,16},{1,9},{9,1},{17,25},{25,17},{2,10},{10... | collective-permute-start | bytes 2457608 | tf_op jit(solution)/shard_map/ppermute | solution.py:55
  70.9 23.2 %collective-permute-start.13 = (bf16[320,1280]{1,0:T(8,128)(2,1)}, bf16[320,1280]{1,0:T(8,128)(2,1)}, u32[]{:S(2)}, u32[]{:S(2)}) collective-permute-start(bf16[320,1280]{1,0:T(8,128)(2,1)} %shard_map.453), channel_id=1, source_target_pairs={{0,4},{4,0},{1,5},{5,1},{2,6},{6,2},{3,7},{7,3},{8,12},{12,8},{9,1... | collective-permute-start | bytes 2457608 | tf_op jit(solution)/shard_map/ppermute | solution.py:55
  77.8 18.8 %collective-permute-start.10 = (bf16[256,1280]{1,0:T(8,128)(2,1)}, bf16[256,1280]{1,0:T(8,128)(2,1)}, u32[]{:S(2)}, u32[]{:S(2)}) collective-permute-start(bf16[256,1280]{1,0:T(8,128)(2,1)} %get-tuple-element.217), channel_id=1, source_target_pairs={{0,1},{1,0},{2,3},{3,2},{4,5},{5,4},{6,7},{7,6},{8,9},{9,8},{10,11... | collective-permute-start | bytes 1966088 | tf_op jit(solution)/shard_map/ppermute | solution.py:55
  90.5 35.1 %collective-permute-start.12 = (bf16[320,1280]{1,0:T(8,128)(2,1)}, bf16[320,1280]{1,0:T(8,128)(2,1)}, u32[]{:S(2)}, u32[]{:S(2)}) collective-permute-start(bf16[320,1280]{1,0:T(8,128)(2,1)} %shard_map.451), channel_id=1, source_target_pairs={{0,4},{4,0},{1,5},{5,1},{2,6},{6,2},{3,7},{7,3},{8,12},{12,8},{9,1... | collective-permute-start | bytes 2457608 | tf_op jit(solution)/shard_map/ppermute | solution.py:55
  91.9 33.6 %collective-permute-start.5 = (bf16[640,512]{1,0:T(8,128)(2,1)}, bf16[640,512]{1,0:T(8,128)(2,1)S(1)}, u32[]{:S(2)}, u32[]{:S(2)}) collective-permute-start(bf16[640,512]{1,0:T(8,128)(2,1)} %shard_map.444), channel_id=1, source_target_pairs={{0,4},{4,0},{1,5},{5,1},{2,6},{6,2},{3,7},{7,3},{8,12},{12,8},{9,1... | collective-permute-start | bytes 1966088 | tf_op jit(solution)/shard_map/ppermute | solution.py:55
  94.2 39.1 %collective-permute-start.20 = (bf16[320,1280]{1,0:T(8,128)(2,1)}, bf16[320,1280]{1,0:T(8,128)(2,1)S(1)}, u32[]{:S(2)}, u32[]{:S(2)}) collective-permute-start(bf16[320,1280]{1,0:T(8,128)(2,1)} %collective-permute-done.13.refs_7_), channel_id=1, source_target_pairs={{0,8},{8,0},{16,24},{24,16},{1,9},{9,1},{17,25},{25,17},{2,10},{10... | collective-permute-start | bytes 2457608 | tf_op jit(solution)/shard_map/ppermute | solution.py:55
  98.5 27.7 %collective-permute-start.11 = (bf16[256,1280]{1,0:T(8,128)(2,1)S(1)}, bf16[256,1280]{1,0:T(8,128)(2,1)S(1)}, u32[]{:S(2)}, u32[]{:S(2)}) collective-permute-start(bf16[256,1280]{1,0:T(8,128)(2,1)S(1)} %shard_map.449.refs_0_), channel_id=1, source_target_pairs={{0,2},{1,3},{2,0},{3,1},{4,6},{5,7},{6,4},{7,5},{8,10},{9,11},{10,... | collective-permute-start | bytes 1966088 | tf_op jit(solution)/shard_map/ppermute | solution.py:55
  101.4 26.3 %collective-permute-start.9 = (bf16[256,1280]{1,0:T(8,128)(2,1)S(1)}, bf16[256,1280]{1,0:T(8,128)(2,1)S(1)}, u32[]{:S(2)}, u32[]{:S(2)}) collective-permute-start(bf16[256,1280]{1,0:T(8,128)(2,1)S(1)} %shard_map.447.refs_0_), channel_id=1, source_target_pairs={{0,2},{1,3},{2,0},{3,1},{4,6},{5,7},{6,4},{7,5},{8,10},{9,11},{10,... | collective-permute-start | bytes 1966088 | tf_op jit(solution)/shard_map/ppermute | solution.py:55
  125.6 20.2 %collective-permute-start.19 = (bf16[320,1280]{1,0:T(8,128)(2,1)}, bf16[320,1280]{1,0:T(8,128)(2,1)S(1)}, u32[]{:S(2)}, u32[]{:S(2)}) collective-permute-start(bf16[320,1280]{1,0:T(8,128)(2,1)} %collective-permute-done.12.refs_5_), channel_id=1, source_target_pairs={{0,8},{8,0},{16,24},{24,16},{1,9},{9,1},{17,25},{25,17},{2,10},{10... | collective-permute-start | bytes 2457608 | tf_op jit(solution)/shard_map/ppermute | solution.py:55
  126.9 24.4 %collective-permute-start.21 = (bf16[256,1280]{1,0:T(8,128)(2,1)S(1)}, bf16[256,1280]{1,0:T(8,128)(2,1)S(1)}, u32[]{:S(2)}, u32[]{:S(2)}) collective-permute-start(bf16[256,1280]{1,0:T(8,128)(2,1)S(1)} %shard_map.450.refs_4_.refs_0_.refs_3_), channel_id=1, source_target_pairs={{0,1},{1,0},{2,3},{3,2},{4,5},{5,4},{6,7},{7,6},{8,9},{9,8},{10,11... | collective-permute-start | bytes 1966088 | tf_op jit(solution)/shard_map/ppermute | solution.py:55
  128.5 35.0 %collective-permute-start.16 = (bf16[256,1280]{1,0:T(8,128)(2,1)S(1)}, bf16[256,1280]{1,0:T(8,128)(2,1)}, u32[]{:S(2)}, u32[]{:S(2)}) collective-permute-start(bf16[256,1280]{1,0:T(8,128)(2,1)S(1)} %shard_map.452.refs_6_.refs_0_.refs_5_), channel_id=1, source_target_pairs={{0,1},{1,0},{2,3},{3,2},{4,5},{5,4},{6,7},{7,6},{8,9},{9,8},{10,11... | collective-permute-start | bytes 1966088 | tf_op jit(solution)/shard_map/ppermute | solution.py:55
  132.8 16.9 %collective-permute-start.14 = (bf16[256,1280]{1,0:T(8,128)(2,1)S(1)}, bf16[256,1280]{1,0:T(8,128)(2,1)S(1)}, u32[]{:S(2)}, u32[]{:S(2)}) collective-permute-start(bf16[256,1280]{1,0:T(8,128)(2,1)S(1)} %get-tuple-element.220), channel_id=1, source_target_pairs={{0,1},{1,0},{2,3},{3,2},{4,5},{5,4},{6,7},{7,6},{8,9},{9,8},{10,11... | collective-permute-start | bytes 1966088 | tf_op jit(solution)/shard_map/ppermute | solution.py:55
  149.8 25.2 %collective-permute-start.15 = (bf16[256,1280]{1,0:T(8,128)(2,1)S(1)}, bf16[256,1280]{1,0:T(8,128)(2,1)}, u32[]{:S(2)}, u32[]{:S(2)}) collective-permute-start(bf16[256,1280]{1,0:T(8,128)(2,1)S(1)} %shard_map.456.refs_0_), channel_id=1, source_target_pairs={{0,2},{1,3},{2,0},{3,1},{4,6},{5,7},{6,4},{7,5},{8,10},{9,11},{10,... | collective-permute-start | bytes 1966088 | tf_op jit(solution)/shard_map/ppermute | solution.py:55
  179.8 17.0 %collective-permute-start.28 = (bf16[256,1280]{1,0:T(8,128)(2,1)}, bf16[256,1280]{1,0:T(8,128)(2,1)}, u32[]{:S(2)}, u32[]{:S(2)}) collective-permute-start(bf16[256,1280]{1,0:T(8,128)(2,1)} %shard_map.464.refs_3_), channel_id=1, source_target_pairs={{0,2},{1,3},{2,0},{3,1},{4,6},{5,7},{6,4},{7,5},{8,10},{9,11},{10,... | collective-permute-start | bytes 1966088 | tf_op jit(solution)/shard_map/ppermute | solution.py:55
  180.3 21.6 %collective-permute-start.25 = (bf16[256,1280]{1,0:T(8,128)(2,1)}, bf16[256,1280]{1,0:T(8,128)(2,1)}, u32[]{:S(2)}, u32[]{:S(2)}) collective-permute-start(bf16[256,1280]{1,0:T(8,128)(2,1)} %get-tuple-element.223.refs_4_.refs_7_), channel_id=1, source_target_pairs={{0,1},{1,0},{2,3},{3,2},{4,5},{5,4},{6,7},{7,6},{8,9},{9,8},{10,11... | collective-permute-start | bytes 1966088 | tf_op jit(solution)/shard_map/ppermute | solution.py:55
  204.4 17.0 %collective-permute-start.26 = (bf16[256,1280]{1,0:T(8,128)(2,1)}, bf16[256,1280]{1,0:T(8,128)(2,1)}, u32[]{:S(2)}, u32[]{:S(2)}) collective-permute-start(bf16[256,1280]{1,0:T(8,128)(2,1)} %shard_map.463.refs_3_), channel_id=1, source_target_pairs={{0,2},{1,3},{2,0},{3,1},{4,6},{5,7},{6,4},{7,5},{8,10},{9,11},{10,... | collective-permute-start | bytes 1966088 | tf_op jit(solution)/shard_map/ppermute | solution.py:55
  204.9 24.6 %collective-permute-start.23 = (bf16[256,1280]{1,0:T(8,128)(2,1)}, bf16[256,1280]{1,0:T(8,128)(2,1)}, u32[]{:S(2)}, u32[]{:S(2)}) collective-permute-start(bf16[256,1280]{1,0:T(8,128)(2,1)} %get-tuple-element.225.refs_7_.refs_9_), channel_id=1, source_target_pairs={{0,1},{1,0},{2,3},{3,2},{4,5},{5,4},{6,7},{7,6},{8,9},{9,8},{10,11... | collective-permute-start | bytes 1966088 | tf_op jit(solution)/shard_map/ppermute | solution.py:55
  231.6 17.5 %collective-permute-start.24 = (bf16[256,1280]{1,0:T(8,128)(2,1)}, bf16[256,1280]{1,0:T(8,128)(2,1)}, u32[]{:S(2)}, u32[]{:S(2)}) collective-permute-start(bf16[256,1280]{1,0:T(8,128)(2,1)} %shard_map.462.refs_3_), channel_id=1, source_target_pairs={{0,2},{1,3},{2,0},{3,1},{4,6},{5,7},{6,4},{7,5},{8,10},{9,11},{10,... | collective-permute-start | bytes 1966088 | tf_op jit(solution)/shard_map/ppermute | solution.py:55
  232.1 22.8 %collective-permute-start.34 = (bf16[256,1280]{1,0:T(8,128)(2,1)}, bf16[256,1280]{1,0:T(8,128)(2,1)}, u32[]{:S(2)}, u32[]{:S(2)}) collective-permute-start(bf16[256,1280]{1,0:T(8,128)(2,1)} %get-tuple-element.241), channel_id=1, source_target_pairs={{0,1},{1,0},{2,3},{3,2},{4,5},{5,4},{6,7},{7,6},{8,9},{9,8},{10,11... | collective-permute-start | bytes 1966088 | tf_op jit(solution)/shard_map/ppermute | solution.py:55
  257.4 17.0 %collective-permute-start.35 = (bf16[256,1280]{1,0:T(8,128)(2,1)}, bf16[256,1280]{1,0:T(8,128)(2,1)}, u32[]{:S(2)}, u32[]{:S(2)}) collective-permute-start(bf16[256,1280]{1,0:T(8,128)(2,1)} %shard_map.470.refs_4_), channel_id=1, source_target_pairs={{0,2},{1,3},{2,0},{3,1},{4,6},{5,7},{6,4},{7,5},{8,10},{9,11},{10,... | collective-permute-start | bytes 1966088 | tf_op jit(solution)/shard_map/ppermute | solution.py:55
  268.5 54.0 %collective-permute-start.38 = (bf16[640,1280]{1,0:T(8,128)(2,1)}, bf16[640,1280]{1,0:T(8,128)(2,1)}, u32[]{:S(2)}, u32[]{:S(2)}) collective-permute-start(bf16[640,1280]{1,0:T(8,128)(2,1)} %get-tuple-element.261), channel_id=1, source_target_pairs={{0,4},{4,0},{1,5},{5,1},{2,6},{6,2},{3,7},{7,3},{8,12},{12,8},{9,1... | collective-permute-start | bytes 4915208 | tf_op jit(solution)/shard_map/ppermute | solution.py:55
  306.3 39.7 %collective-permute-start.41 = (bf16[640,1280]{1,0:T(8,128)(2,1)}, bf16[640,1280]{1,0:T(8,128)(2,1)}, u32[]{:S(2)}, u32[]{:S(2)}) collective-permute-start(bf16[640,1280]{1,0:T(8,128)(2,1)} %get-tuple-element.266), channel_id=1, source_target_pairs={{0,4},{4,0},{1,5},{5,1},{2,6},{6,2},{3,7},{7,3},{8,12},{12,8},{9,1... | collective-permute-start | bytes 4915208 | tf_op jit(solution)/shard_map/ppermute | solution.py:55
  307.8 14.7 %collective-permute-start.37 = (bf16[256,1280]{1,0:T(8,128)(2,1)}, bf16[256,1280]{1,0:T(8,128)(2,1)}, u32[]{:S(2)}, u32[]{:S(2)}) collective-permute-start(bf16[256,1280]{1,0:T(8,128)(2,1)} %get-tuple-element.247.refs_6_.refs_4_), channel_id=1, source_target_pairs={{0,1},{1,0},{2,3},{3,2},{4,5},{5,4},{6,7},{7,6},{8,9},{9,8},{10,11... | collective-permute-start | bytes 1966088 | tf_op jit(solution)/shard_map/ppermute | solution.py:55
  312.0 25.8 %collective-permute-start.43 = (bf16[256,1280]{1,0:T(8,128)(2,1)}, bf16[256,1280]{1,0:T(8,128)(2,1)}, u32[]{:S(2)}, u32[]{:S(2)}) collective-permute-start(bf16[256,1280]{1,0:T(8,128)(2,1)} %shard_map.477.refs_4_), channel_id=1, source_target_pairs={{0,2},{1,3},{2,0},{3,1},{4,6},{5,7},{6,4},{7,5},{8,10},{9,11},{10,... | collective-permute-start | bytes 1966088 | tf_op jit(solution)/shard_map/ppermute | solution.py:55
  312.4 30.4 %collective-permute-start.45 = (bf16[256,1280]{1,0:T(8,128)(2,1)}, bf16[256,1280]{1,0:T(8,128)(2,1)}, u32[]{:S(2)}, u32[]{:S(2)}) collective-permute-start(bf16[256,1280]{1,0:T(8,128)(2,1)} %get-tuple-element.279), channel_id=1, source_target_pairs={{0,1},{1,0},{2,3},{3,2},{4,5},{5,4},{6,7},{7,6},{8,9},{9,8},{10,11... | collective-permute-start | bytes 1966088 | tf_op jit(solution)/shard_map/ppermute | solution.py:55
  342.8 32.6 %collective-permute-start.33 = (f32[256,1280]{1,0:T(8,128)}, f32[256,1280]{1,0:T(8,128)}, u32[]{:S(2)}, u32[]{:S(2)}) collective-permute-start(f32[256,1280]{1,0:T(8,128)} %get-tuple-element.238.own), channel_id=1, source_target_pairs={{0,1},{1,0},{2,3},{3,2},{4,5},{5,4},{6,7},{7,6},{8,9},{9,8},{10,11... | collective-permute-start | bytes 3932168 | tf_op jit(solution)/shard_map/ppermute | solution.py:55
  344.1 22.3 %collective-permute-start.46 = (bf16[256,1280]{1,0:T(8,128)(2,1)S(1)}, bf16[256,1280]{1,0:T(8,128)(2,1)S(1)}, u32[]{:S(2)}, u32[]{:S(2)}) collective-permute-start(bf16[256,1280]{1,0:T(8,128)(2,1)S(1)} %shard_map.481.refs_4_), channel_id=1, source_target_pairs={{0,2},{1,3},{2,0},{3,1},{4,6},{5,7},{6,4},{7,5},{8,10},{9,11},{10,... | collective-permute-start | bytes 1966088 | tf_op jit(solution)/shard_map/ppermute | solution.py:55
  345.7 31.3 %collective-permute-start.32 = (f32[256,1280]{1,0:T(8,128)}, f32[256,1280]{1,0:T(8,128)}, u32[]{:S(2)}, u32[]{:S(2)}) collective-permute-start(f32[256,1280]{1,0:T(8,128)} %get-tuple-element.237.own), channel_id=1, source_target_pairs={{0,1},{1,0},{2,3},{3,2},{4,5},{5,4},{6,7},{7,6},{8,9},{9,8},{10,11... | collective-permute-start | bytes 3932168 | tf_op jit(solution)/shard_map/ppermute | solution.py:55
  345.9 57.3 %collective-permute-start.40 = (bf16[640,1280]{1,0:T(8,128)(2,1)}, bf16[640,1280]{1,0:T(8,128)(2,1)S(1)}, u32[]{:S(2)}, u32[]{:S(2)}) collective-permute-start(bf16[640,1280]{1,0:T(8,128)(2,1)} %get-tuple-element.265), channel_id=1, source_target_pairs={{0,4},{4,0},{1,5},{5,1},{2,6},{6,2},{3,7},{7,3},{8,12},{12,8},{9,1... | collective-permute-start | bytes 4915208 | tf_op jit(solution)/shard_map/ppermute | solution.py:55
  372.2 36.1 %collective-permute-start.48 = (bf16[320,1280]{1,0:T(8,128)(2,1)S(1)}, bf16[320,1280]{1,0:T(8,128)(2,1)}, u32[]{:S(2)}, u32[]{:S(2)}) collective-permute-start(bf16[320,1280]{1,0:T(8,128)(2,1)S(1)} %get-tuple-element.280.refs_7_.refs_0_), channel_id=1, source_target_pairs={{0,8},{24,16},{1,9},{25,17},{2,10},{26,18},{3,11},{27,19},{4,12},{... | collective-permute-start | bytes 2457608 | tf_op jit(solution)/shard_map/ppermute | solution.py:146
  375.4 30.1 %collective-permute-start.39 = (bf16[640,512]{1,0:T(8,128)(2,1)}, bf16[640,512]{1,0:T(8,128)(2,1)S(1)}, u32[]{:S(2)}, u32[]{:S(2)}) collective-permute-start(bf16[640,512]{1,0:T(8,128)(2,1)} %bitcast.34), channel_id=1, source_target_pairs={{0,4},{4,0},{1,5},{5,1},{2,6},{6,2},{3,7},{7,3},{8,12},{12,8},{9,1... | collective-permute-start | bytes 1966088 | tf_op jit(solution)/shard_map/ppermute | solution.py:55
  377.0 37.2 %collective-permute-start.49 = (bf16[320,1280]{1,0:T(8,128)(2,1)}, bf16[320,1280]{1,0:T(8,128)(2,1)S(1)}, u32[]{:S(2)}, u32[]{:S(2)}) collective-permute-start(bf16[320,1280]{1,0:T(8,128)(2,1)} %get-tuple-element.291.refs_0_), channel_id=1, source_target_pairs={{0,8},{24,16},{1,9},{25,17},{2,10},{26,18},{3,11},{27,19},{4,12},{... | collective-permute-start | bytes 2457608 | tf_op jit(solution)/shard_map/ppermute | solution.py:146
  378.5 34.3 %collective-permute-start.50 = (bf16[640,512]{1,0:T(8,128)(2,1)}, bf16[640,512]{1,0:T(8,128)(2,1)S(1)}, u32[]{:S(2)}, u32[]{:S(2)}) collective-permute-start(bf16[640,512]{1,0:T(8,128)(2,1)} %bitcast.35), channel_id=1, source_target_pairs={{0,4},{4,0},{1,5},{5,1},{2,6},{6,2},{3,7},{7,3},{8,12},{12,8},{9,1... | collective-permute-start | bytes 1966088 | tf_op jit(solution)/shard_map/ppermute | solution.py:55
  403.3 42.5 %collective-permute-start.52 = (bf16[320,1280]{1,0:T(8,128)(2,1)}, bf16[320,1280]{1,0:T(8,128)(2,1)}, u32[]{:S(2)}, u32[]{:S(2)}) collective-permute-start(bf16[320,1280]{1,0:T(8,128)(2,1)} %get-tuple-element.289.rest_3_.refs_0_), channel_id=1, source_target_pairs={{0,8},{24,16},{1,9},{25,17},{2,10},{26,18},{3,11},{27,19},{4,12},{... | collective-permute-start | bytes 2457608 | tf_op jit(solution)/shard_map/ppermute | solution.py:146
  406.8 37.3 %collective-permute-start.51 = (bf16[640,512]{1,0:T(8,128)(2,1)}, bf16[640,512]{1,0:T(8,128)(2,1)}, u32[]{:S(2)}, u32[]{:S(2)}) collective-permute-start(bf16[640,512]{1,0:T(8,128)(2,1)} %bitcast.36), channel_id=1, source_target_pairs={{0,4},{4,0},{1,5},{5,1},{2,6},{6,2},{3,7},{7,3},{8,12},{12,8},{9,1... | collective-permute-start | bytes 1966088 | tf_op jit(solution)/shard_map/ppermute | solution.py:55
  408.3 57.1 %collective-permute-start.31 = (f32[256,1280]{1,0:T(8,128)}, f32[256,1280]{1,0:T(8,128)}, u32[]{:S(2)}, u32[]{:S(2)}) collective-permute-start(f32[256,1280]{1,0:T(8,128)} %get-tuple-element.236.own), channel_id=1, source_target_pairs={{0,1},{1,0},{2,3},{3,2},{4,5},{5,4},{6,7},{7,6},{8,9},{9,8},{10,11... | collective-permute-start | bytes 3932168 | tf_op jit(solution)/shard_map/ppermute | solution.py:55
  413.7 24.0 %collective-permute-start.54 = (bf16[160,1280]{1,0:T(8,128)(2,1)}, bf16[160,1280]{1,0:T(8,128)(2,1)}, u32[]{:S(2)}, u32[]{:S(2)}) collective-permute-start(bf16[160,1280]{1,0:T(8,128)(2,1)} %get-tuple-element.300), channel_id=1, source_target_pairs={{0,4},{4,0},{1,5},{5,1},{2,6},{6,2},{3,7},{7,3},{8,12},{12,8},{9,1... | collective-permute-start | bytes 1228808 | tf_op jit(solution)/shard_map/ppermute | solution.py:55
  415.1 34.8 %collective-permute-start.53 = (bf16[320,1280]{1,0:T(8,128)(2,1)S(1)}, bf16[320,1280]{1,0:T(8,128)(2,1)}, u32[]{:S(2)}, u32[]{:S(2)}) collective-permute-start(bf16[320,1280]{1,0:T(8,128)(2,1)S(1)} %shard_map.486.rest_4_.refs_6_.refs_0_), channel_id=1, source_target_pairs={{8,16},{16,8},{9,17},{17,9},{10,18},{18,10},{11,19},{19,11},{12,20... | collective-permute-start | bytes 2457608 | tf_op jit(solution)/shard_map/ppermute | solution.py:147
  437.7 27.9 %collective-permute-start.65 = (bf16[320,1280]{1,0:T(8,128)(2,1)}, bf16[320,1280]{1,0:T(8,128)(2,1)}, u32[]{:S(2)}, u32[]{:S(2)}) collective-permute-start(bf16[320,1280]{1,0:T(8,128)(2,1)} %get-tuple-element.314.refs_0_), channel_id=1, source_target_pairs={{0,8},{24,16},{1,9},{25,17},{2,10},{26,18},{3,11},{27,19},{4,12},{... | collective-permute-start | bytes 2457608 | tf_op jit(solution)/shard_map/ppermute | solution.py:146
  444.1 26.8 %collective-permute-start.64 = (bf16[320,1280]{1,0:T(8,128)(2,1)}, bf16[320,1280]{1,0:T(8,128)(2,1)}, u32[]{:S(2)}, u32[]{:S(2)}) collective-permute-start(bf16[320,1280]{1,0:T(8,128)(2,1)} %shard_map.488.refs_7_.refs_0_), channel_id=1, source_target_pairs={{8,16},{16,8},{9,17},{17,9},{10,18},{18,10},{11,19},{19,11},{12,20... | collective-permute-start | bytes 2457608 | tf_op jit(solution)/shard_map/ppermute | solution.py:147
  445.8 22.1 %collective-permute-start.61 = (bf16[256,1280]{1,0:T(8,128)(2,1)}, bf16[256,1280]{1,0:T(8,128)(2,1)}, u32[]{:S(2)}, u32[]{:S(2)}) collective-permute-start(bf16[256,1280]{1,0:T(8,128)(2,1)} %get-tuple-element.311), channel_id=1, source_target_pairs={{0,1},{1,0},{2,3},{3,2},{4,5},{5,4},{6,7},{7,6},{8,9},{9,8},{10,11... | collective-permute-start | bytes 1966088 | tf_op jit(solution)/shard_map/ppermute | solution.py:55
  449.9 30.1 %collective-permute-start.58 = (bf16[256,1280]{1,0:T(8,128)(2,1)}, bf16[256,1280]{1,0:T(8,128)(2,1)}, u32[]{:S(2)}, u32[]{:S(2)}) collective-permute-start(bf16[256,1280]{1,0:T(8,128)(2,1)} %get-tuple-element.307), channel_id=1, source_target_pairs={{0,1},{1,0},{2,3},{3,2},{4,5},{5,4},{6,7},{7,6},{8,9},{9,8},{10,11... | collective-permute-start | bytes 1966088 | tf_op jit(solution)/shard_map/ppermute | solution.py:55
  465.4 20.8 %collective-permute-start.55 = (bf16[256,1280]{1,0:T(8,128)(2,1)}, bf16[256,1280]{1,0:T(8,128)(2,1)}, u32[]{:S(2)}, u32[]{:S(2)}) collective-permute-start(bf16[256,1280]{1,0:T(8,128)(2,1)} %get-tuple-element.303), channel_id=1, source_target_pairs={{0,1},{1,0},{2,3},{3,2},{4,5},{5,4},{6,7},{7,6},{8,9},{9,8},{10,11... | collective-permute-start | bytes 1966088 | tf_op jit(solution)/shard_map/ppermute | solution.py:55
  466.1 19.6 %collective-permute-start.66 = (bf16[160,1280]{1,0:T(8,128)(2,1)}, bf16[160,1280]{1,0:T(8,128)(2,1)S(1)}, u32[]{:S(2)}, u32[]{:S(2)}) collective-permute-start(bf16[160,1280]{1,0:T(8,128)(2,1)} %get-tuple-element.316), channel_id=1, source_target_pairs={{0,4},{4,0},{1,5},{5,1},{2,6},{6,2},{3,7},{7,3},{8,12},{12,8},{9,1... | collective-permute-start | bytes 1228808 | tf_op jit(solution)/shard_map/ppermute | solution.py:55
  470.9 37.1 %collective-permute-start.75 = (bf16[320,1280]{1,0:T(8,128)(2,1)}, bf16[320,1280]{1,0:T(8,128)(2,1)}, u32[]{:S(2)}, u32[]{:S(2)}) collective-permute-start(bf16[320,1280]{1,0:T(8,128)(2,1)} %shard_map.494.refs_6_.rest_3_.refs_0_), channel_id=1, source_target_pairs={{8,16},{16,8},{9,17},{17,9},{10,18},{18,10},{11,19},{19,11},{12,20... | collective-permute-start | bytes 2457608 | tf_op jit(solution)/shard_map/ppermute | solution.py:147
  478.0 31.3 %collective-permute-start.73 = (bf16[320,1280]{1,0:T(8,128)(2,1)}, bf16[320,1280]{1,0:T(8,128)(2,1)}, u32[]{:S(2)}, u32[]{:S(2)}) collective-permute-start(bf16[320,1280]{1,0:T(8,128)(2,1)} %shard_map.508.rest_4_.refs_0_), channel_id=1, source_target_pairs={{8,16},{16,8},{9,17},{17,9},{10,18},{18,10},{11,19},{19,11},{12,20... | collective-permute-start | bytes 2457608 | tf_op jit(solution)/shard_map/ppermute | solution.py:147
  480.0 27.5 %collective-permute-start.70 = (bf16[160,1280]{1,0:T(8,128)(2,1)}, bf16[160,1280]{1,0:T(8,128)(2,1)}, u32[]{:S(2)}, u32[]{:S(2)}) collective-permute-start(bf16[160,1280]{1,0:T(8,128)(2,1)} %copy-done.193), channel_id=1, source_target_pairs={{0,4},{4,0},{1,5},{5,1},{2,6},{6,2},{3,7},{7,3},{8,12},{12,8},{9,1... | collective-permute-start | bytes 1228808 | tf_op jit(solution)/shard_map/ppermute | solution.py:55
  485.7 30.0 %collective-permute-start.62 = (bf16[256,1280]{1,0:T(8,128)(2,1)}, bf16[256,1280]{1,0:T(8,128)(2,1)}, u32[]{:S(2)}, u32[]{:S(2)}) collective-permute-start(bf16[256,1280]{1,0:T(8,128)(2,1)} %shard_map.504.refs_1_), channel_id=1, source_target_pairs={{0,2},{1,3},{2,0},{3,1},{4,6},{5,7},{6,4},{7,5},{8,10},{9,11},{10,... | collective-permute-start | bytes 1966088 | tf_op jit(solution)/shard_map/ppermute | solution.py:55
  486.2 31.5 %collective-permute-start.59 = (bf16[256,1280]{1,0:T(8,128)(2,1)}, bf16[256,1280]{1,0:T(8,128)(2,1)}, u32[]{:S(2)}, u32[]{:S(2)}) collective-permute-start(bf16[256,1280]{1,0:T(8,128)(2,1)} %shard_map.501.refs_1_), channel_id=1, source_target_pairs={{0,2},{1,3},{2,0},{3,1},{4,6},{5,7},{6,4},{7,5},{8,10},{9,11},{10,... | collective-permute-start | bytes 1966088 | tf_op jit(solution)/shard_map/ppermute | solution.py:55
  507.4 22.2 %collective-permute-start.56 = (bf16[256,1280]{1,0:T(8,128)(2,1)}, bf16[256,1280]{1,0:T(8,128)(2,1)}, u32[]{:S(2)}, u32[]{:S(2)}) collective-permute-start(bf16[256,1280]{1,0:T(8,128)(2,1)} %shard_map.498.refs_1_), channel_id=1, source_target_pairs={{0,2},{1,3},{2,0},{3,1},{4,6},{5,7},{6,4},{7,5},{8,10},{9,11},{10,... | collective-permute-start | bytes 1966088 | tf_op jit(solution)/shard_map/ppermute | solution.py:55
  508.0 32.8 %collective-permute-start.68 = (bf16[320,1280]{1,0:T(8,128)(2,1)}, bf16[320,1280]{1,0:T(8,128)(2,1)}, u32[]{:S(2)}, u32[]{:S(2)}) collective-permute-start(bf16[320,1280]{1,0:T(8,128)(2,1)} %copy-done.33), channel_id=1, source_target_pairs={{8,0},{16,24},{9,1},{17,25},{10,2},{18,26},{11,3},{19,27},{12,4},{... | collective-permute-start | bytes 2457608 | tf_op jit(solution)/shard_map/ppermute | solution.py:148
  509.3 39.6 %collective-permute-start.67 = (bf16[320,1280]{1,0:T(8,128)(2,1)}, bf16[320,1280]{1,0:T(8,128)(2,1)}, u32[]{:S(2)}, u32[]{:S(2)}) collective-permute-start(bf16[320,1280]{1,0:T(8,128)(2,1)} %copy-done.57), channel_id=1, source_target_pairs={{8,0},{16,24},{9,1},{17,25},{10,2},{18,26},{11,3},{19,27},{12,4},{... | collective-permute-start | bytes 2457608 | tf_op jit(solution)/shard_map/ppermute | solution.py:148
  515.7 60.1 %collective-permute-start.76 = (bf16[320,1280]{1,0:T(8,128)(2,1)}, bf16[320,1280]{1,0:T(8,128)(2,1)}, u32[]{:S(2)}, u32[]{:S(2)}) collective-permute-start(bf16[320,1280]{1,0:T(8,128)(2,1)} %shard_map.519.whole), channel_id=1, source_target_pairs={{8,0},{16,24},{9,1},{17,25},{10,2},{18,26},{11,3},{19,27},{12,4},{... | collective-permute-start | bytes 2457608 | tf_op jit(solution)/shard_map/ppermute | solution.py:148
  517.8 63.3 %collective-permute-start.74 = (bf16[320,1280]{1,0:T(8,128)(2,1)}, bf16[320,1280]{1,0:T(8,128)(2,1)}, u32[]{:S(2)}, u32[]{:S(2)}) collective-permute-start(bf16[320,1280]{1,0:T(8,128)(2,1)} %shard_map.518.whole), channel_id=1, source_target_pairs={{8,0},{16,24},{9,1},{17,25},{10,2},{18,26},{11,3},{19,27},{12,4},{... | collective-permute-start | bytes 2457608 | tf_op jit(solution)/shard_map/ppermute | solution.py:148
  540.9 168.0 %collective-permute-start.63 = (f32[256,1280]{1,0:T(8,128)}, f32[256,1280]{1,0:T(8,128)}, u32[]{:S(2)}, u32[]{:S(2)}) collective-permute-start(f32[256,1280]{1,0:T(8,128)} %shard_map.505.own), channel_id=1, source_target_pairs={{0,1},{1,0},{2,3},{3,2},{4,5},{5,4},{6,7},{7,6},{8,9},{9,8},{10,11... | collective-permute-start | bytes 3932168 | tf_op jit(solution)/shard_map/ppermute | solution.py:55
  540.9 171.3 %collective-permute-start.60 = (f32[256,1280]{1,0:T(8,128)}, f32[256,1280]{1,0:T(8,128)}, u32[]{:S(2)}, u32[]{:S(2)}) collective-permute-start(f32[256,1280]{1,0:T(8,128)} %shard_map.502.own), channel_id=1, source_target_pairs={{0,1},{1,0},{2,3},{3,2},{4,5},{5,4},{6,7},{7,6},{8,9},{9,8},{10,11... | collective-permute-start | bytes 3932168 | tf_op jit(solution)/shard_map/ppermute | solution.py:55
  549.0 166.5 %collective-permute-start.57 = (f32[256,1280]{1,0:T(8,128)}, f32[256,1280]{1,0:T(8,128)}, u32[]{:S(2)}, u32[]{:S(2)}) collective-permute-start(f32[256,1280]{1,0:T(8,128)} %shard_map.499.own), channel_id=1, source_target_pairs={{0,1},{1,0},{2,3},{3,2},{4,5},{5,4},{6,7},{7,6},{8,9},{9,8},{10,11... | collective-permute-start | bytes 3932168 | tf_op jit(solution)/shard_map/ppermute | solution.py:55
  (243 other events, 1482.3 us)

commit v5 on v4

--- a/solution.py
+++ b/solution.py
@@ -27,6 +27,7 @@
 LARGE_VMEM_BYTES = 56 * 1024 * 1024
 SMALL_VMEM_BYTES = 16 * 1024 * 1024
 F32 = jnp.float32
+LONG_COST = pl.CostEstimate(flops=10**11, bytes_accessed=10**8, transcendentals=0)
 SMALL_COST = pl.CostEstimate(flops=1000, bytes_accessed=1000, transcendentals=0)
 LOW = jnp.bfloat16
 
@@ -103,16 +104,16 @@
     refs[-1][...] = total.astype(refs[-1].dtype)
 
 
-def added(terms, out):
+def added(terms, out, deps=()):
     if len(terms[0].shape) == 1:
         return lax.optimization_barrier(sum(term.astype(F32) for term in terms).astype(out))
     return pl.pallas_call(
-        partial(add_kernel, len(terms)),
-        in_specs=[IN_VMEM] * len(terms),
+        ordered_after(partial(add_kernel, len(terms)), len(terms), deps),
+        in_specs=[IN_VMEM] * len(terms) + [UNREAD] * len(deps),
         out_shape=jax.ShapeDtypeStruct(terms[0].shape, out),
         compiler_params=pltpu.CompilerParams(vmem_limit_bytes=SMALL_VMEM_BYTES),
         cost_estimate=SMALL_COST,
-    )(*terms)
+    )(*terms, *deps)
 
 
 def rows_kernel(features, weights, own_out, other_out):
@@ -226,7 +227,7 @@
         compiler_params=pltpu.CompilerParams(
             collective_id=0, has_side_effects=True, vmem_limit_bytes=VMEM_BYTES
         ),
-        cost_estimate=SMALL_COST,
+        cost_estimate=LONG_COST,
     )(*shifts, *deps)
 
 
@@ -317,7 +318,7 @@
 
 def triple_grad_kernel(count, parts, own_part, me, *refs):
     lefts, rights = refs[:count], refs[count : 3 * count]
-    own_out, other_outs = refs[3 * count], refs[3 * count + 1 :]
+    own_out, other_out = refs[3 * count :]
     right = jnp.concatenate([ref[...] for ref in rights], axis=0)
     rows = lefts[0].shape[0] // parts
     for side in range(2):
@@ -339,8 +340,7 @@
         if side == 0:
             own_out[...] = total
         else:
-            for n in range(parts):
-                other_outs[n][...] = total[n * own_part : (n + 1) * own_part, :].astype(LOW)
+            other_out[...] = total.astype(LOW)
 
 
 def triple_grad(me, parts, lefts, rights, deps=()):
@@ -353,8 +353,10 @@
         in_specs=[pl.BlockSpec(memory_space=pltpu.SMEM)]
         + [IN_VMEM] * (3 * count)
         + [UNREAD] * len(deps),
-        out_shape=[jax.ShapeDtypeStruct((parts * own_part, width), F32)]
-        + [jax.ShapeDtypeStruct((own_part, width), LOW)] * parts,
+        out_shape=[
+            jax.ShapeDtypeStruct((parts * own_part, width), F32),
+            jax.ShapeDtypeStruct((parts * own_part, width), LOW),
+        ],
         compiler_params=pltpu.CompilerParams(vmem_limit_bytes=VMEM_BYTES),
         cost_estimate=SMALL_COST,
     )(me, *lefts, *[side for right in rights for side in right], *deps)
@@ -793,6 +795,7 @@
         partner = jnp.zeros((tile, width), LOW)
     flat = pl.BlockSpec((tile, width), lambda i, at: (i, 0))
     held = pl.BlockSpec((tile, width), lambda i, at: (at[0] * steps + i, 0))
+    partner_spec = flat if not has_partner or partner.shape[0] == rows else held
     once = pl.BlockSpec((tile, width), lambda i, at: (0, 0))
     slab = pl.BlockSpec((1, tile, width), lambda i, at: (which, i, 0))
     grouped = pl.BlockSpec((1, 1, tile, width), lambda i, at: (0, which, i, 0))
@@ -807,7 +810,7 @@
         grid_spec=pltpu.PrefetchScalarGridSpec(
             num_scalar_prefetch=1,
             grid=(steps,),
-            in_specs=[held, flat if has_partner else once, slab, grouped, grouped]
+            in_specs=[held, partner_spec if has_partner else once, slab, grouped, grouped]
             + [UNREAD] * (len(earlier) + len(deps)),
             out_specs=[grouped, grouped, grouped] + pieces,
         ),
@@ -856,8 +859,9 @@
 
 
 class MatrixSteps:
-    def __init__(self, chunks, at_end, master, first, second, outer):
+    def __init__(self, chunks, late_chunks, at_end, master, first, second, outer):
         self.chunks = chunks
+        self.late_chunks = late_chunks
         self.at_end = at_end.reshape(1)
         self.arrays = (master, first, second)
         self.outer_state = outer
@@ -868,9 +872,8 @@
 
     def inner(self, which, gradient, deps, chain=True):
         own, partner, block = gradient
-        outs = adam_slab(
-            which, self.chunks, block, own, partner, *self.arrays, self.inner_outs, deps
-        )
+        chunks = self.chunks if chain else self.late_chunks
+        outs = adam_slab(which, chunks, block, own, partner, *self.arrays, self.inner_outs, deps)
         self.inner_outs = outs[:3]
         if chain:
             self.sums[which] = [group_sum(shift) for shift in outs[3:]]
@@ -1266,6 +1269,7 @@
     gate_grad, tag = feed_gradient(gate_back_rows, normed_rows, [tag])
     feed_steps = MatrixSteps(
         2 if own_units % 320 == 0 else 1,
+        4 if own_units % 640 == 0 else 1,
         at_end,
         feedforward_weights,
         feedforward_first,
@@ -1273,6 +1277,7 @@
         feedforward_outer,
     )
     attention_steps = MatrixSteps(
+        1,
         1,
         at_end,
         attention_weights,
@@ -1304,7 +1309,7 @@
         output_arrived = []
         gate_arrived = []
     token_sides = [(token_own[b], token_other[b]) for b in micros]
-    tag = feed_steps.inner(0, up_grad, [tag])
+    tag = feed_steps.inner(0, up_grad, [tag], False)
     tag = feed_steps.inner(
         1, gate_grad, [tag] + feed_steps.pairs(2)[:1] + side_arrivals[:1], False
     )
@@ -1315,15 +1320,15 @@
         elif b < last:
             deps += side_arrivals[-1:]
         else:
-            deps += feed_steps.pairs(0)[:1] + feed_steps.wholes(2)[:1] + output_arrived
+            deps += feed_steps.wholes(2)[:1] + output_arrived
         sides_part_back(b, deps)
         tag = head_terms[b]
     if pair:
-        own, *others = triple_grad(me.reshape(1), 3, triples, token_sides, [tag])
+        own, other = triple_grad(me.reshape(1), 3, triples, token_sides, [tag])
         tag = own
+        arrived = trade(other, "ctx", 1)
         projection_grads = [
-            (own, trade(others[which], "ctx", 1), jnp.full((1,), which, jnp.int32))
-            for which in range(3)
+            (own, arrived, jnp.full((1,), which, jnp.int32)) for which in range(3)
         ]
     else:
         triple_all = dot(
@@ -1332,7 +1337,7 @@
             (1, 0),
         ).reshape(3, head_width, model_width)
         projection_grads = [to_owner(triple_all[which], True) for which in range(3)]
-    tag = attention_steps.inner(3, output_grad, [tag] + feed_steps.wholes(2) + feed_steps.pairs(0), False)
+    tag = attention_steps.inner(3, output_grad, [tag] + feed_steps.wholes(2), False)
 
     block_output = None
     for b in micros:
@@ -1349,7 +1354,7 @@
     input_gradient = None
 
     def place_input(b, deps):
-        input_own = added([skips[b], *input_sums[b]], F32)
+        input_own = added([skips[b], *input_sums[b]], F32, deps)
         return place_rows(
             b,
             micro_count,
@@ -1360,15 +1365,9 @@
             deps,
         )
 
-    input_gradient = place_input(0, [tag])
-    tags = feed_steps.outer(2, [tag])
-    tag = attention_steps.inner(0, projection_grads[0], tags, False)
-    input_gradient = place_input(1, [tag])
-    for which in (1, 2):
+    for which in range(3):
         tag = attention_steps.inner(which, projection_grads[which], [tag], False)
-    tags = feed_steps.outer(0, [tag])
-    for b in micros[2:]:
-        input_gradient = place_input(b, [tag])
+    tags = [tag]
     rate_terms = jnp.concatenate([sum(attention_rate_terms), sum(feed_rate_terms)], axis=0)
     rate_terms = rate_terms + trade(rate_terms, "tensor", 1)
     head_terms = sum(head_terms).reshape(head_width)
@@ -1414,18 +1413,26 @@
     flat_size = shift_flat.size
     flat_rows = -(-flat_size // 1024) * 8
     shift_flat = jnp.pad(shift_flat, (0, flat_rows * 128 - flat_size)).reshape(flat_rows, 128)
-    feed_shifts = feed_steps.shifts[1]
+    feed_shifts = feed_steps.shifts[0] + feed_steps.shifts[1]
     attention_shifts = attention_steps.shifts
     *chained, shift_flat = chain_sum(
         [*feed_shifts, *[attention_shifts[which][0] for which in (3, 0, 1, 2)], shift_flat], tags
     )
     shift_flat = shift_flat.reshape(-1)[:flat_size] / group_count
-    feed_steps.sums[1] = [(None, total, total) for total in chained[: len(feed_shifts)]]
+    for which in (0, 1):
+        start = which * (len(feed_shifts) // 2)
+        feed_steps.sums[which] = [
+            (None, total, total) for total in chained[start : start + len(feed_shifts) // 2]
+        ]
     for which, total in zip((3, 0, 1, 2), chained[len(feed_shifts) :]):
         attention_steps.sums[which] = [(None, total, total)]
-    tags = feed_steps.outer(1, [])
+    tags = [chained[0]]
+    for which in (2, 0, 1):
+        tags = feed_steps.outer(which, tags)
     for which in (3, 0, 1, 2):
         tags = attention_steps.outer(which, tags)
+    for b in micros:
+        input_gradient = place_input(b, [chained[0]])
     feed_outs = feed_steps.outs()
     attention_outs = attention_steps.outs()
 

time: 725 us -> 768 us (1.059)
  Pallas kernels: 443 us -> 476 us
  local copies, waits for them, and re-layouts: 78 us -> 98.3 us
  starting transfers between devices: 67.5 us -> 52.7 us
    pallas_call x1, Pallas kernels: 107 us -> 146 us  [chain_sum(): pl.pallas_call(ordered_after(partial(chain_kernel, count), count, deps),...]
    ppermute x4 -> x2, waiting for transfers between devices: 0.01 us -> 22.9 us  [group_sum(): lax.ppermute(values, 'group', [(0, 1), (3, 2)])]
    unnamed x468 -> x544, local copies, waits for them, and re-layouts: 68.9 us -> 88.2 us
    ppermute x65 -> x63, waiting for transfers between devices: 82.2 us -> 68.5 us  [trade(): return lax.ppermute(values, axis, [(i, i ^ bit) for i in range(count)])]
    pallas_call x23 -> x19, Pallas kernels: 46.6 us -> 37.2 us  [added(): pl.pallas_call(ordered_after(partial(add_kernel, len(terms)), len(terms),...]
    ppermute x4 -> x2, waiting for transfers between devices: 9.33 us -> 0.01 us  [group_sum(): back = lax.ppermute(whole, 'group', [(1, 0), (2, 3)])]
    ppermute x4 -> x2, starting transfers between devices: 13.2 us -> 4.43 us  [group_sum(): lax.ppermute(values, 'group', [(0, 1), (3, 2)])]
    pallas_call x10 -> x14, Pallas kernels: 27 us -> 34.8 us  [outer_slab(): pl.pallas_call(partial(outer_kernel, group_count), grid_spec=pltpu.Prefet...]
  transfers between devices with their start and end apart: 77 -> 69, of which waited for: 19 -> 15; matrix products, arithmetic and copies ran while one was open for 6% -> 7% of each run, Pallas kernels for 61% -> 62%
where the time goes in v5:
time: 768 us; the launch traced here: 761 us
  Pallas kernels  476 us (62%)
  local copies, waits for them, and re-layouts  98.3 us (13%)
  waiting for transfers between devices  91.4 us (12%)
  starting transfers between devices  52.7 us (7%)
  other arithmetic  39.1 us (5%)
    pallas_call x1, Pallas kernels, chain_sum(): pl.pallas_call(ordered_after(partial(chain_kernel, count), count, deps),...  146 us
    unnamed x544, local copies, waits for them, and re-layouts  88.2 us
    ppermute x63, waiting for transfers between devices, trade(): return lax.ppermute(values, axis, [(i, i ^ bit) for i in range(count)])  68.5 us
    pallas_call x7, Pallas kernels, adam_slab(): pl.pallas_call(partial(adam_kernel, has_partner, chunks), grid_spec=pltpu...  45.3 us
    ppermute x63, starting transfers between devices, trade(): return lax.ppermute(values, axis, [(i, i ^ bit) for i in range(count)])  42.4 us
    pallas_call x3, Pallas kernels, feed_backward(): pl.pallas_call(ordered_after(partial(feed_back_kernel, math.sqrt(width)),...  41.1 us
    pallas_call x19, Pallas kernels, added(): pl.pallas_call(ordered_after(partial(add_kernel, len(terms)), len(terms),...  37.2 us
    pallas_call x14, Pallas kernels, outer_slab(): pl.pallas_call(partial(outer_kernel, group_count), grid_spec=pltpu.Prefet...  34.8 us
  transfers between devices with their start and end apart: 69, of which 15 were waited for; matrix products, arithmetic and copies ran while one was open for 7% of the time, Pallas kernels for 62%

profile of v5, /device:TPU:0, one launch (start us, length us, event | category | flops | bytes accessed | tf_op | source)
XLA Modules:
  0.0 761.2 jit_solution(5828518907434095206)
XLA Ops:
  3.7 2.9 collective-permute-start
  9.0 4.6 broadcast_select_fusion
  27.5 10.0 %collective-permute-done.1 = bf16[3,80,1280]{2,1,0:T(8,128)(2,1)} collective-permute-done((bf16[3,80,1280]{2,1,0:T(8,128)(2,1)}, bf16[3,80,1280]{2,1,0:T(8,128)(2,1)}, u32[]{:S(2)}, u32[]{:S(2)}) %collective-permute-start.1) | collective-permute-done | bytes 614432 | tf_op jit(solution)/shard_map/ppermute | solution.py:56
  39.5 2.6 maximum_select_fusion
  66.0 3.3 shard_map.442
  80.1 3.3 shard_map.443
  104.8 21.7 %collective-permute-done.5 = bf16[640,512]{1,0:T(8,128)(2,1)S(1)} collective-permute-done((bf16[640,512]{1,0:T(8,128)(2,1)}, bf16[640,512]{1,0:T(8,128)(2,1)S(1)}, u32[]{:S(2)}, u32[]{:S(2)}) %collective-permute-start.5) | collective-permute-done | bytes 655392 | tf_op jit(solution)/shard_map/ppermute | solution.py:56
  130.3 3.3 shard_map.454
  138.4 8.1 %collective-permute-done.19 = bf16[320,1280]{1,0:T(8,128)(2,1)S(1)} collective-permute-done((bf16[320,1280]{1,0:T(8,128)(2,1)}, bf16[320,1280]{1,0:T(8,128)(2,1)S(1)}, u32[]{:S(2)}, u32[]{:S(2)}) %collective-permute-start.19) | collective-permute-done | bytes 819232 | tf_op jit(solution)/shard_map/ppermute | solution.py:56
  153.0 11.2 %shard_map.458 = (f32[512,1280]{1,0:T(8,128)}, f32[512,1280]{1,0:T(8,128)}, bf16[512,1280]{1,0:T(8,128)(2,1)}, f32[256,1280]{1,0:T(8,128)}, bf16[256,1280]{1,0:T(8,128)(2,1)}) custom-call(bf16[256,1280]{1,0:T(8,128)(2,1)} %copy-done.25, bf16[256,1280]{1,0:T(8,128)(2,1)} %copy-done.234, bf16[1280,1280]{1,0:T(8,128)(2,1)} %pad_maximum_fusion.refs_2_.refs_4_, ...), custom_call_target="tpu_custom_call" | custom-call | flops 1000 | bytes 1000 | tf_op jit(solution)/shard_map/pallas_call | solution.py:533
  164.3 11.7 %shard_map.459 = (f32[512,1280]{1,0:T(8,128)}, f32[512,1280]{1,0:T(8,128)}, bf16[512,1280]{1,0:T(8,128)(2,1)}, f32[256,1280]{1,0:T(8,128)}, bf16[256,1280]{1,0:T(8,128)(2,1)}) custom-call(bf16[256,1280]{1,0:T(8,128)(2,1)} %copy-done.24, bf16[256,1280]{1,0:T(8,128)(2,1)} %collective-permute-done.16.refs_1_.refs_6_, ...), custom_call_target="tpu_custom_call" | custom-call | flops 1000 | bytes 1000 | tf_op jit(solution)/shard_map/pallas_call | solution.py:533
  182.3 11.4 %shard_map.461 = (f32[512,1280]{1,0:T(8,128)}, f32[512,1280]{1,0:T(8,128)}, bf16[512,1280]{1,0:T(8,128)(2,1)}, f32[256,1280]{1,0:T(8,128)}, bf16[256,1280]{1,0:T(8,128)(2,1)}) custom-call(bf16[256,1280]{1,0:T(8,128)(2,1)} %copy-done.37, bf16[256,1280]{1,0:T(8,128)(2,1)} %collective-permute-done.22.refs_1_.refs_8_, ...), custom_call_target="tpu_custom_call" | custom-call | flops 1000 | bytes 1000 | tf_op jit(solution)/shard_map/pallas_call | solution.py:533
  193.6 4.0 collective-permute-done.28.refs_4_
  198.7 3.2 shard_map.465
  202.0 2.5 shard_map.463.refs_3_
  205.8 13.7 %shard_map.466 = (bf16[512,1280]{1,0:T(8,128)(2,1)}, bf16[512,1280]{1,0:T(8,128)(2,1)}, f32[2,1280]{1,0:T(2,128)}, f32[256,1280]{1,0:T(8,128)}, bf16[256,1280]{1,0:T(8,128)(2,1)}) custom-call(bf16[256,1280]{1,0:T(8,128)(2,1)} %copy-done.81, bf16[256,1280]{1,0:T(8,128)(2,1)} %copy-done.235, f32[512,1280]{1,0:T(8,128)} %get-tuple-element.249.refs_2_, ...), custom_call_target="tpu_custom_call" | custom-call | flops 1000 | bytes 1000 | tf_op jit(solution)/shard_map/pallas_call | solution.py:618
  224.4 3.3 shard_map.467
  232.1 13.7 %shard_map.468 = (bf16[512,1280]{1,0:T(8,128)(2,1)}, bf16[512,1280]{1,0:T(8,128)(2,1)}, f32[2,1280]{1,0:T(2,128)}, f32[256,1280]{1,0:T(8,128)}, bf16[256,1280]{1,0:T(8,128)(2,1)}) custom-call(bf16[256,1280]{1,0:T(8,128)(2,1)} %copy-done.102, bf16[256,1280]{1,0:T(8,128)(2,1)} %copy-done.237, f32[512,1280]{1,0:T(8,128)} %get-tuple-element.253.refs_2_, ...), custom_call_target="tpu_custom_call" | custom-call | flops 1000 | bytes 1000 | tf_op jit(solution)/shard_map/pallas_call | solution.py:618
  249.9 3.3 shard_map.469
  254.2 2.5 shard_map.470.refs_4_
  258.0 9.7 %shard_map.471 = (f32[640,1280]{1,0:T(8,128)}, bf16[640,1280]{1,0:T(8,128)(2,1)}) custom-call(bf16[512,1280]{1,0:T(8,128)(2,1)} %get-tuple-element.262.refs_0_, bf16[512,1280]{1,0:T(8,128)(2,1)} %get-tuple-element.263.refs_1_, bf16[512,1280]{1,0:T(8,128)(2,1)} %get-tuple-element.264.refs_2_, bf16[256,1280]{1,0:T(8,128)(2,1)} %copy-done.81, ...), custom_call_target="tpu_custom_call" | custom-call | flops 1000 | bytes 1000 | tf_op jit(solution)/shard_map/pallas_call | solution.py:656
  269.3 4.4 collective-permute-done.35.refs_5_
  277.0 3.6 shard_map.472
  282.2 13.6 %shard_map.473 = (bf16[512,1280]{1,0:T(8,128)(2,1)}, bf16[512,1280]{1,0:T(8,128)(2,1)}, f32[2,1280]{1,0:T(2,128)}, f32[256,1280]{1,0:T(8,128)}, bf16[256,1280]{1,0:T(8,128)(2,1)}) custom-call(bf16[256,1280]{1,0:T(8,128)(2,1)} %copy-done.82, bf16[256,1280]{1,0:T(8,128)(2,1)} %copy-done.236, f32[512,1280]{1,0:T(8,128)} %get-tuple-element.271.refs_2_, ...), custom_call_target="tpu_custom_call" | custom-call | flops 1000 | bytes 1000 | tf_op jit(solution)/shard_map/pallas_call | solution.py:618
  295.9 9.8 %shard_map.474 = (f32[640,1280]{1,0:T(8,128)}, bf16[640,1280]{1,0:T(8,128)(2,1)}) custom-call(bf16[512,1280]{1,0:T(8,128)(2,1)} %get-tuple-element.275.refs_0_, bf16[512,1280]{1,0:T(8,128)(2,1)} %get-tuple-element.276.refs_1_, bf16[512,1280]{1,0:T(8,128)(2,1)} %get-tuple-element.277.refs_2_, bf16[256,1280]{1,0:T(8,128)(2,1)} %copy-done.25, ...), custom_call_target="tpu_custom_call" | custom-call | flops 1000 | bytes 1000 | tf_op jit(solution)/shard_map/pallas_call | solution.py:656
  309.9 9.8 %shard_map.475 = (f32[640,1280]{1,0:T(8,128)}, bf16[640,1280]{1,0:T(8,128)(2,1)}) custom-call(bf16[512,1280]{1,0:T(8,128)(2,1)} %get-tuple-element.269.refs_0_, bf16[512,1280]{1,0:T(8,128)(2,1)} %get-tuple-element.270.refs_1_, bf16[512,1280]{1,0:T(8,128)(2,1)} %get-tuple-element.274.refs_2_, bf16[256,1280]{1,0:T(8,128)(2,1)} %copy-done.25, ...), custom_call_target="tpu_custom_call" | custom-call | flops 1000 | bytes 1000 | tf_op jit(solution)/shard_map/pallas_call | solution.py:656
  323.7 10.3 %shard_map.476 = (f32[320,512]{1,0:T(8,128)S(1)}, f32[640,512]{1,0:T(8,128)S(1)}, bf16[1,640,512]{2,1,0:T(8,128)(2,1)}) custom-call(s32[1,512]{1,0:T(1,128)S(1)} %get-tuple-element.463.refs_0_, s32[1,512]{1,0:T(1,128)S(1)} %slice.299.refs_1_, s32[1024,1]{1,0:T(8,128)S(1)} %bitcast.138, s32[1024,1]{1,0:T(8,128)S(1)} %bitcast.130, ...), custom_call_target="tpu_custom_call" | custom-call | flops 1000 | bytes 1000 | tf_op jit(solution)/shard_map/pallas_call | solution.py:464
  334.0 3.5 shard_map.478
  343.6 8.8 %shard_map.479 = (f32[320,512]{1,0:T(8,128)S(1)}, f32[640,512]{1,0:T(8,128)S(1)}, bf16[1,640,512]{2,1,0:T(8,128)(2,1)}) custom-call(s32[1,512]{1,0:T(1,128)S(1)} %get-tuple-element.464.refs_0_, s32[1,512]{1,0:T(1,128)S(1)} %slice.299.refs_1_, s32[1024,1]{1,0:T(8,128)S(1)} %bitcast.136, s32[1024,1]{1,0:T(8,128)S(1)} %bitcast.131, ...), custom_call_target="tpu_custom_call" | custom-call | flops 1000 | bytes 1000 | tf_op jit(solution)/shard_map/pallas_call | solution.py:464
  353.5 10.5 %shard_map.480 = (f32[1,3,640,1280]{3,2,1,0:T(8,128)}, f32[1,3,640,1280]{3,2,1,0:T(8,128)}, f32[1,3,640,1280]{3,2,1,0:T(8,128)}, bf16[320,1280]{1,0:T(8,128)(2,1)S(1)}, bf16[320,1280]{1,0:T(8,128)(2,1)S(1)}) custom-call(s32[1]{0:T(128)} %constant.31.clone.1.offset, f32[640,1280]{1,0:T(8,128)S(1)} %copy-done.27, ...), custom_call_target="tpu_custom_call" | custom-call | flops 1000 | bytes 1000 | tf_op jit(solution)/shard_map/pallas_call | solution.py:808
  363.9 3.1 collective-permute-start.48
  368.4 2.6 collective-permute-start.39
  371.0 2.6 shard_map.482
  373.8 11.9 %collective-permute-done.48.refs_1_ = bf16[320,1280]{1,0:T(8,128)(2,1)S(1)} collective-permute-done((bf16[320,1280]{1,0:T(8,128)(2,1)S(1)}, bf16[320,1280]{1,0:T(8,128)(2,1)S(1)}, u32[]{:S(2)}, u32[]{:S(2)}) %collective-permute-start.48) | collective-permute-done | bytes 819232 | tf_op jit(solution)/shard_map/ppermute | solution.py:147
  390.1 11.0 %collective-permute-done.49.refs_1_ = bf16[320,1280]{1,0:T(8,128)(2,1)S(1)} collective-permute-done((bf16[320,1280]{1,0:T(8,128)(2,1)S(1)}, bf16[320,1280]{1,0:T(8,128)(2,1)S(1)}, u32[]{:S(2)}, u32[]{:S(2)}) %collective-permute-start.49) | collective-permute-done | bytes 819232 | tf_op jit(solution)/shard_map/ppermute | solution.py:147
  411.5 8.9 %shard_map.483 = (f32[320,512]{1,0:T(8,128)S(1)}, f32[640,512]{1,0:T(8,128)S(1)}, bf16[1,640,512]{2,1,0:T(8,128)(2,1)}) custom-call(s32[1,512]{1,0:T(1,128)S(1)} %get-tuple-element.465.refs_0_, s32[1,512]{1,0:T(1,128)S(1)} %slice.299.refs_1_, s32[1024,1]{1,0:T(8,128)S(1)} %bitcast.134, s32[1024,1]{1,0:T(8,128)S(1)} %bitcast.132, ...), custom_call_target="tpu_custom_call" | custom-call | flops 1000 | bytes 1000 | tf_op jit(solution)/shard_map/pallas_call | solution.py:464
  421.5 3.7 shard_map.484
  430.2 10.4 %shard_map.485 = (f32[1,3,640,1280]{3,2,1,0:T(8,128)}, f32[1,3,640,1280]{3,2,1,0:T(8,128)}, f32[1,3,640,1280]{3,2,1,0:T(8,128)}, bf16[160,1280]{1,0:T(8,128)(2,1...) custom-call(s32[1]{0:T(128)} %constant.31.clone.1.offset, ...), custom_call_target="tpu_custom_call", output_to_operand_aliasing={{0}: (6, {}), {1}: (7, {}), {2}: (8, {})} | custom-call | flops 1000 | bytes 1000 | tf_op jit(solution)/shard_map/pallas_call | solution.py:808
  442.9 10.8 %shard_map.487 = (f32[1,3,640,1280]{3,2,1,0:T(8,128)}, f32[1,3,640,1280]{3,2,1,0:T(8,128)}, f32[1,3,640,1280]{3,2,1,0:T(8,128)}, bf16[160,1280]{1,0:T(8,128)(2,1...) custom-call(s32[1]{0:T(128)} %constant.31.clone.1.offset, ...), custom_call_target="tpu_custom_call", output_to_operand_aliasing={{0}: (6, {}), {1}: (7, {}), {2}: (8, {})} | custom-call | flops 1000 | bytes 1000 | tf_op jit(solution)/shard_map/pallas_call | solution.py:808
  468.3 2.6 shard_map.494.refs_6_.rest_1_.whole
  483.4 5.0 shard_map.498
  492.5 2.5 shard_map.499.rest_2_.whole
  495.1 3.5 shard_map.500
  510.2 10.7 %collective-permute-done.57.partner = bf16[480,1280]{1,0:T(8,128)(2,1)} collective-permute-done((bf16[480,1280]{1,0:T(8,128)(2,1)}, bf16[480,1280]{1,0:T(8,128)(2,1)}, u32[]{:S(2)}, u32[]{:S(2)}) %collective-permute-start.57) | collective-permute-done | bytes 1228832 | tf_op jit(solution)/shard_map/ppermute | solution.py:56
  527.4 3.4 shard_map.501
  530.9 3.3 shard_map.502
  534.2 3.4 shard_map.503
  540.9 146.3 %shard_map.504 = (bf16[160,1280]{1,0:T(8,128)(2,1)S(1)}, bf16[160,1280]{1,0:T(8,128)(2,1)S(1)}, bf16[160,1280]{1,0:T(8,128)(2,1)S(1)}, bf16[160,1280]{1,0:T(8,12...) custom-call(bf16[160,1280]{1,0:T(8,128)(2,1)S(1)} %copy-done.199, ...), custom_call_target="tpu_custom_call" | custom-call | flops 99999997952 | bytes 100000000 | tf_op jit(solution)/shard_map/pallas_call | solution.py:221
  687.3 3.7 shard_map.511.own
  691.0 2.6 shard_map.508.own
  698.1 3.1 shard_map.490.rest_0_
  712.6 3.5 shard_map.515
  716.1 3.5 shard_map.516
  719.6 2.7 shard_map.517
  722.3 2.7 shard_map.518
  725.1 2.7 shard_map.519
  727.8 2.7 shard_map.520
  730.5 2.7 shard_map.521
  733.2 2.7 shard_map.522
  735.9 2.7 shard_map.523
  738.6 2.8 shard_map.524
  751.5 3.3 shard_map.512.rest_0_
  754.8 3.3 shard_map.513.rest_0_
  758.1 2.9 shard_map.514
  (800 shorter events, 239.7 us)
Async XLA Ops:
  3.7 18.1 %collective-permute-start = (bf16[3,80,1280]{2,1,0:T(8,128)(2,1)}, bf16[3,80,1280]{2,1,0:T(8,128)(2,1)}, u32[]{:S(2)}, u32[]{:S(2)}) collective-permute-start(bf16[3,80,1280]{2,1,0:T(8,128)(2,1)} %slice_select_fusion.4), channel_id=1, source_target_pairs={{0,4},{4,0},{1,5},{5,1},{2,6},{6,2},{3,7},{7,3},{8,12},{12,8},{9,1... | collective-permute-start | bytes 1843208 | tf_op jit(solution)/shard_map/ppermute | solution.py:56
  6.9 18.1 %collective-permute-start.2 = (bf16[2720]{0:T(1024)(128)(2,1)S(1)}, bf16[2720]{0:T(1024)(128)(2,1)S(1)}, u32[]{:S(2)}, u32[]{:S(2)}) collective-permute-start(bf16[2720]{0:T(1024)(128)(2,1)S(1)} %concatenate.162), channel_id=1, source_target_pairs={{0,4},{4,0},{1,5},{5,1},{2,6},{6,2},{3,7},{7,3},{8,12},{12,8},{9,1... | collective-permute-start | bytes 16328 | tf_op jit(solution)/shard_map/ppermute | solution.py:56
  21.8 15.7 %collective-permute-start.1 = (bf16[3,80,1280]{2,1,0:T(8,128)(2,1)}, bf16[3,80,1280]{2,1,0:T(8,128)(2,1)}, u32[]{:S(2)}, u32[]{:S(2)}) collective-permute-start(bf16[3,80,1280]{2,1,0:T(8,128)(2,1)} %collective-permute-done.refs_1_), channel_id=1, source_target_pairs={{0,8},{8,0},{16,24},{24,16},{1,9},{9,1},{17,25},{25,17},{2,10},{10... | collective-permute-start | bytes 1843208 | tf_op jit(solution)/shard_map/ppermute | solution.py:56
  25.4 26.3 %collective-permute-start.6 = (bf16[80,1280]{1,0:T(8,128)(2,1)}, bf16[80,1280]{1,0:T(8,128)(2,1)}, u32[]{:S(2)}, u32[]{:S(2)}) collective-permute-start(bf16[80,1280]{1,0:T(8,128)(2,1)} %shard_map.445), channel_id=1, source_target_pairs={{0,4},{4,0},{1,5},{5,1},{2,6},{6,2},{3,7},{7,3},{8,12},{12,8},{9,1... | collective-permute-start | bytes 614408 | tf_op jit(solution)/shard_map/ppermute | solution.py:56
  27.0 36.2 %collective-permute-start.17 = (bf16[320,1280]{1,0:T(8,128)(2,1)}, bf16[320,1280]{1,0:T(8,128)(2,1)}, u32[]{:S(2)}, u32[]{:S(2)}) collective-permute-start(bf16[320,1280]{1,0:T(8,128)(2,1)} %shard_map.457), channel_id=1, source_target_pairs={{0,4},{4,0},{1,5},{5,1},{2,6},{6,2},{3,7},{7,3},{8,12},{12,8},{9,1... | collective-permute-start | bytes 2457608 | tf_op jit(solution)/shard_map/ppermute | solution.py:56
  46.5 18.0 %collective-permute-start.4 = (bf16[640,512]{1,0:T(8,128)(2,1)}, bf16[640,512]{1,0:T(8,128)(2,1)}, u32[]{:S(2)}, u32[]{:S(2)}) collective-permute-start(bf16[640,512]{1,0:T(8,128)(2,1)} %get-tuple-element.229), channel_id=1, source_target_pairs={{0,4},{4,0},{1,5},{5,1},{2,6},{6,2},{3,7},{7,3},{8,12},{12,8},{9,1... | collective-permute-start | bytes 1966088 | tf_op jit(solution)/shard_map/ppermute | solution.py:56
  51.7 9.6 %collective-permute-start.7 = (bf16[80,1280]{1,0:T(8,128)(2,1)}, bf16[80,1280]{1,0:T(8,128)(2,1)S(1)}, u32[]{:S(2)}, u32[]{:S(2)}) collective-permute-start(bf16[80,1280]{1,0:T(8,128)(2,1)} %collective-permute-done.6), channel_id=1, source_target_pairs={{0,8},{8,0},{16,24},{24,16},{1,9},{9,1},{17,25},{25,17},{2,10},{10... | collective-permute-start | bytes 614408 | tf_op jit(solution)/shard_map/ppermute | solution.py:56
  59.4 19.1 %collective-permute-start.3 = (bf16[640,512]{1,0:T(8,128)(2,1)}, bf16[640,512]{1,0:T(8,128)(2,1)}, u32[]{:S(2)}, u32[]{:S(2)}) collective-permute-start(bf16[640,512]{1,0:T(8,128)(2,1)} %get-tuple-element.227), channel_id=1, source_target_pairs={{0,4},{4,0},{1,5},{5,1},{2,6},{6,2},{3,7},{7,3},{8,12},{12,8},{9,1... | collective-permute-start | bytes 1966088 | tf_op jit(solution)/shard_map/ppermute | solution.py:56
  63.1 29.3 %collective-permute-start.18 = (bf16[320,1280]{1,0:T(8,128)(2,1)}, bf16[320,1280]{1,0:T(8,128)(2,1)}, u32[]{:S(2)}, u32[]{:S(2)}) collective-permute-start(bf16[320,1280]{1,0:T(8,128)(2,1)} %collective-permute-done.17), channel_id=1, source_target_pairs={{0,8},{8,0},{16,24},{24,16},{1,9},{9,1},{17,25},{25,17},{2,10},{10... | collective-permute-start | bytes 2457608 | tf_op jit(solution)/shard_map/ppermute | solution.py:56
  71.5 24.1 %collective-permute-start.13 = (bf16[320,1280]{1,0:T(8,128)(2,1)}, bf16[320,1280]{1,0:T(8,128)(2,1)}, u32[]{:S(2)}, u32[]{:S(2)}) collective-permute-start(bf16[320,1280]{1,0:T(8,128)(2,1)} %shard_map.453), channel_id=1, source_target_pairs={{0,4},{4,0},{1,5},{5,1},{2,6},{6,2},{3,7},{7,3},{8,12},{12,8},{9,1... | collective-permute-start | bytes 2457608 | tf_op jit(solution)/shard_map/ppermute | solution.py:56
  78.3 19.7 %collective-permute-start.10 = (bf16[256,1280]{1,0:T(8,128)(2,1)}, bf16[256,1280]{1,0:T(8,128)(2,1)}, u32[]{:S(2)}, u32[]{:S(2)}) collective-permute-start(bf16[256,1280]{1,0:T(8,128)(2,1)} %get-tuple-element.237), channel_id=1, source_target_pairs={{0,1},{1,0},{2,3},{3,2},{4,5},{5,4},{6,7},{7,6},{8,9},{9,8},{10,11... | collective-permute-start | bytes 1966088 | tf_op jit(solution)/shard_map/ppermute | solution.py:56
  86.3 14.7 %collective-permute-start.8 = (bf16[256,1280]{1,0:T(8,128)(2,1)}, bf16[256,1280]{1,0:T(8,128)(2,1)}, u32[]{:S(2)}, u32[]{:S(2)}) collective-permute-start(bf16[256,1280]{1,0:T(8,128)(2,1)} %get-tuple-element.234), channel_id=1, source_target_pairs={{0,1},{1,0},{2,3},{3,2},{4,5},{5,4},{6,7},{7,6},{8,9},{9,8},{10,11... | collective-permute-start | bytes 1966088 | tf_op jit(solution)/shard_map/ppermute | solution.py:56
  91.0 35.6 %collective-permute-start.12 = (bf16[320,1280]{1,0:T(8,128)(2,1)}, bf16[320,1280]{1,0:T(8,128)(2,1)}, u32[]{:S(2)}, u32[]{:S(2)}) collective-permute-start(bf16[320,1280]{1,0:T(8,128)(2,1)} %shard_map.451), channel_id=1, source_target_pairs={{0,4},{4,0},{1,5},{5,1},{2,6},{6,2},{3,7},{7,3},{8,12},{12,8},{9,1... | collective-permute-start | bytes 2457608 | tf_op jit(solution)/shard_map/ppermute | solution.py:56
  92.5 34.0 %collective-permute-start.5 = (bf16[640,512]{1,0:T(8,128)(2,1)}, bf16[640,512]{1,0:T(8,128)(2,1)S(1)}, u32[]{:S(2)}, u32[]{:S(2)}) collective-permute-start(bf16[640,512]{1,0:T(8,128)(2,1)} %shard_map.444), channel_id=1, source_target_pairs={{0,4},{4,0},{1,5},{5,1},{2,6},{6,2},{3,7},{7,3},{8,12},{12,8},{9,1... | collective-permute-start | bytes 1966088 | tf_op jit(solution)/shard_map/ppermute | solution.py:56
  95.6 39.0 %collective-permute-start.20 = (bf16[320,1280]{1,0:T(8,128)(2,1)}, bf16[320,1280]{1,0:T(8,128)(2,1)S(1)}, u32[]{:S(2)}, u32[]{:S(2)}) collective-permute-start(bf16[320,1280]{1,0:T(8,128)(2,1)} %collective-permute-done.13.refs_7_), channel_id=1, source_target_pairs={{0,8},{8,0},{16,24},{24,16},{1,9},{9,1},{17,25},{25,17},{2,10},{10... | collective-permute-start | bytes 2457608 | tf_op jit(solution)/shard_map/ppermute | solution.py:56
  99.5 28.3 %collective-permute-start.11 = (bf16[256,1280]{1,0:T(8,128)(2,1)S(1)}, bf16[256,1280]{1,0:T(8,128)(2,1)S(1)}, u32[]{:S(2)}, u32[]{:S(2)}) collective-permute-start(bf16[256,1280]{1,0:T(8,128)(2,1)S(1)} %shard_map.449.refs_0_), channel_id=1, source_target_pairs={{0,2},{1,3},{2,0},{3,1},{4,6},{5,7},{6,4},{7,5},{8,10},{9,11},{10,... | collective-permute-start | bytes 1966088 | tf_op jit(solution)/shard_map/ppermute | solution.py:56
  102.2 26.8 %collective-permute-start.9 = (bf16[256,1280]{1,0:T(8,128)(2,1)S(1)}, bf16[256,1280]{1,0:T(8,128)(2,1)S(1)}, u32[]{:S(2)}, u32[]{:S(2)}) collective-permute-start(bf16[256,1280]{1,0:T(8,128)(2,1)S(1)} %shard_map.447.refs_0_), channel_id=1, source_target_pairs={{0,2},{1,3},{2,0},{3,1},{4,6},{5,7},{6,4},{7,5},{8,10},{9,11},{10,... | collective-permute-start | bytes 1966088 | tf_op jit(solution)/shard_map/ppermute | solution.py:56
  126.6 19.9 %collective-permute-start.19 = (bf16[320,1280]{1,0:T(8,128)(2,1)}, bf16[320,1280]{1,0:T(8,128)(2,1)S(1)}, u32[]{:S(2)}, u32[]{:S(2)}) collective-permute-start(bf16[320,1280]{1,0:T(8,128)(2,1)} %collective-permute-done.12.refs_5_), channel_id=1, source_target_pairs={{0,8},{8,0},{16,24},{24,16},{1,9},{9,1},{17,25},{25,17},{2,10},{10... | collective-permute-start | bytes 2457608 | tf_op jit(solution)/shard_map/ppermute | solution.py:56
  128.5 23.7 %collective-permute-start.21 = (bf16[256,1280]{1,0:T(8,128)(2,1)S(1)}, bf16[256,1280]{1,0:T(8,128)(2,1)S(1)}, u32[]{:S(2)}, u32[]{:S(2)}) collective-permute-start(bf16[256,1280]{1,0:T(8,128)(2,1)S(1)} %shard_map.450.refs_4_.refs_0_.refs_3_), channel_id=1, source_target_pairs={{0,1},{1,0},{2,3},{3,2},{4,5},{5,4},{6,7},{7,6},{8,9},{9,8},{10,11... | collective-permute-start | bytes 1966088 | tf_op jit(solution)/shard_map/ppermute | solution.py:56
  129.7 34.6 %collective-permute-start.16 = (bf16[256,1280]{1,0:T(8,128)(2,1)S(1)}, bf16[256,1280]{1,0:T(8,128)(2,1)}, u32[]{:S(2)}, u32[]{:S(2)}) collective-permute-start(bf16[256,1280]{1,0:T(8,128)(2,1)S(1)} %shard_map.452.refs_6_.refs_0_.refs_5_), channel_id=1, source_target_pairs={{0,1},{1,0},{2,3},{3,2},{4,5},{5,4},{6,7},{7,6},{8,9},{9,8},{10,11... | collective-permute-start | bytes 1966088 | tf_op jit(solution)/shard_map/ppermute | solution.py:56
  134.5 15.9 %collective-permute-start.14 = (bf16[256,1280]{1,0:T(8,128)(2,1)S(1)}, bf16[256,1280]{1,0:T(8,128)(2,1)S(1)}, u32[]{:S(2)}, u32[]{:S(2)}) collective-permute-start(bf16[256,1280]{1,0:T(8,128)(2,1)S(1)} %get-tuple-element.240), channel_id=1, source_target_pairs={{0,1},{1,0},{2,3},{3,2},{4,5},{5,4},{6,7},{7,6},{8,9},{9,8},{10,11... | collective-permute-start | bytes 1966088 | tf_op jit(solution)/shard_map/ppermute | solution.py:56
  150.5 25.6 %collective-permute-start.15 = (bf16[256,1280]{1,0:T(8,128)(2,1)S(1)}, bf16[256,1280]{1,0:T(8,128)(2,1)}, u32[]{:S(2)}, u32[]{:S(2)}) collective-permute-start(bf16[256,1280]{1,0:T(8,128)(2,1)S(1)} %shard_map.456.refs_0_), channel_id=1, source_target_pairs={{0,2},{1,3},{2,0},{3,1},{4,6},{5,7},{6,4},{7,5},{8,10},{9,11},{10,... | collective-permute-start | bytes 1966088 | tf_op jit(solution)/shard_map/ppermute | solution.py:56
  164.3 14.2 %collective-permute-start.27 = (bf16[256,1280]{1,0:T(8,128)(2,1)}, bf16[256,1280]{1,0:T(8,128)(2,1)}, u32[]{:S(2)}, u32[]{:S(2)}) collective-permute-start(bf16[256,1280]{1,0:T(8,128)(2,1)} %get-tuple-element.242.refs_7_), channel_id=1, source_target_pairs={{0,1},{1,0},{2,3},{3,2},{4,5},{5,4},{6,7},{7,6},{8,9},{9,8},{10,11... | collective-permute-start | bytes 1966088 | tf_op jit(solution)/shard_map/ppermute | solution.py:56
  180.5 17.1 %collective-permute-start.28 = (bf16[256,1280]{1,0:T(8,128)(2,1)}, bf16[256,1280]{1,0:T(8,128)(2,1)}, u32[]{:S(2)}, u32[]{:S(2)}) collective-permute-start(bf16[256,1280]{1,0:T(8,128)(2,1)} %shard_map.464.refs_3_), channel_id=1, source_target_pairs={{0,2},{1,3},{2,0},{3,1},{4,6},{5,7},{6,4},{7,5},{8,10},{9,11},{10,... | collective-permute-start | bytes 1966088 | tf_op jit(solution)/shard_map/ppermute | solution.py:56
  180.9 21.1 %collective-permute-start.25 = (bf16[256,1280]{1,0:T(8,128)(2,1)}, bf16[256,1280]{1,0:T(8,128)(2,1)}, u32[]{:S(2)}, u32[]{:S(2)}) collective-permute-start(bf16[256,1280]{1,0:T(8,128)(2,1)} %get-tuple-element.243.refs_4_.refs_7_), channel_id=1, source_target_pairs={{0,1},{1,0},{2,3},{3,2},{4,5},{5,4},{6,7},{7,6},{8,9},{9,8},{10,11... | collective-permute-start | bytes 1966088 | tf_op jit(solution)/shard_map/ppermute | solution.py:56
  204.6 16.9 %collective-permute-start.26 = (bf16[256,1280]{1,0:T(8,128)(2,1)}, bf16[256,1280]{1,0:T(8,128)(2,1)}, u32[]{:S(2)}, u32[]{:S(2)}) collective-permute-start(bf16[256,1280]{1,0:T(8,128)(2,1)} %shard_map.463.refs_3_), channel_id=1, source_target_pairs={{0,2},{1,3},{2,0},{3,1},{4,6},{5,7},{6,4},{7,5},{8,10},{9,11},{10,... | collective-permute-start | bytes 1966088 | tf_op jit(solution)/shard_map/ppermute | solution.py:56
  205.0 23.6 %collective-permute-start.23 = (bf16[256,1280]{1,0:T(8,128)(2,1)}, bf16[256,1280]{1,0:T(8,128)(2,1)}, u32[]{:S(2)}, u32[]{:S(2)}) collective-permute-start(bf16[256,1280]{1,0:T(8,128)(2,1)} %get-tuple-element.245.refs_7_.refs_9_), channel_id=1, source_target_pairs={{0,1},{1,0},{2,3},{3,2},{4,5},{5,4},{6,7},{7,6},{8,9},{9,8},{10,11... | collective-permute-start | bytes 1966088 | tf_op jit(solution)/shard_map/ppermute | solution.py:56
  230.9 17.2 %collective-permute-start.24 = (bf16[256,1280]{1,0:T(8,128)(2,1)}, bf16[256,1280]{1,0:T(8,128)(2,1)}, u32[]{:S(2)}, u32[]{:S(2)}) collective-permute-start(bf16[256,1280]{1,0:T(8,128)(2,1)} %shard_map.462.refs_3_), channel_id=1, source_target_pairs={{0,2},{1,3},{2,0},{3,1},{4,6},{5,7},{6,4},{7,5},{8,10},{9,11},{10,... | collective-permute-start | bytes 1966088 | tf_op jit(solution)/shard_map/ppermute | solution.py:56
  231.3 22.9 %collective-permute-start.34 = (bf16[256,1280]{1,0:T(8,128)(2,1)}, bf16[256,1280]{1,0:T(8,128)(2,1)}, u32[]{:S(2)}, u32[]{:S(2)}) collective-permute-start(bf16[256,1280]{1,0:T(8,128)(2,1)} %get-tuple-element.261), channel_id=1, source_target_pairs={{0,1},{1,0},{2,3},{3,2},{4,5},{5,4},{6,7},{7,6},{8,9},{9,8},{10,11... | collective-permute-start | bytes 1966088 | tf_op jit(solution)/shard_map/ppermute | solution.py:56
  256.8 17.0 %collective-permute-start.35 = (bf16[256,1280]{1,0:T(8,128)(2,1)}, bf16[256,1280]{1,0:T(8,128)(2,1)}, u32[]{:S(2)}, u32[]{:S(2)}) collective-permute-start(bf16[256,1280]{1,0:T(8,128)(2,1)} %shard_map.470.refs_4_), channel_id=1, source_target_pairs={{0,2},{1,3},{2,0},{3,1},{4,6},{5,7},{6,4},{7,5},{8,10},{9,11},{10,... | collective-permute-start | bytes 1966088 | tf_op jit(solution)/shard_map/ppermute | solution.py:56
  267.7 52.0 %collective-permute-start.38 = (bf16[640,1280]{1,0:T(8,128)(2,1)}, bf16[640,1280]{1,0:T(8,128)(2,1)}, u32[]{:S(2)}, u32[]{:S(2)}) collective-permute-start(bf16[640,1280]{1,0:T(8,128)(2,1)} %get-tuple-element.281), channel_id=1, source_target_pairs={{0,4},{4,0},{1,5},{5,1},{2,6},{6,2},{3,7},{7,3},{8,12},{12,8},{9,1... | collective-permute-start | bytes 4915208 | tf_op jit(solution)/shard_map/ppermute | solution.py:56
  269.3 37.8 %collective-permute-start.42 = (bf16[256,1280]{1,0:T(8,128)(2,1)}, bf16[256,1280]{1,0:T(8,128)(2,1)}, u32[]{:S(2)}, u32[]{:S(2)}) collective-permute-start(bf16[256,1280]{1,0:T(8,128)(2,1)} %get-tuple-element.289), channel_id=1, source_target_pairs={{0,1},{1,0},{2,3},{3,2},{4,5},{5,4},{6,7},{7,6},{8,9},{9,8},{10,11... | collective-permute-start | bytes 1966088 | tf_op jit(solution)/shard_map/ppermute | solution.py:56
  305.6 37.9 %collective-permute-start.41 = (bf16[640,1280]{1,0:T(8,128)(2,1)}, bf16[640,1280]{1,0:T(8,128)(2,1)}, u32[]{:S(2)}, u32[]{:S(2)}) collective-permute-start(bf16[640,1280]{1,0:T(8,128)(2,1)} %get-tuple-element.286), channel_id=1, source_target_pairs={{0,4},{4,0},{1,5},{5,1},{2,6},{6,2},{3,7},{7,3},{8,12},{12,8},{9,1... | collective-permute-start | bytes 4915208 | tf_op jit(solution)/shard_map/ppermute | solution.py:56
  307.1 12.6 %collective-permute-start.37 = (bf16[256,1280]{1,0:T(8,128)(2,1)}, bf16[256,1280]{1,0:T(8,128)(2,1)}, u32[]{:S(2)}, u32[]{:S(2)}) collective-permute-start(bf16[256,1280]{1,0:T(8,128)(2,1)} %get-tuple-element.267.refs_6_.refs_4_), channel_id=1, source_target_pairs={{0,1},{1,0},{2,3},{3,2},{4,5},{5,4},{6,7},{7,6},{8,9},{9,8},{10,11... | collective-permute-start | bytes 1966088 | tf_op jit(solution)/shard_map/ppermute | solution.py:56
  309.2 24.8 %collective-permute-start.43 = (bf16[256,1280]{1,0:T(8,128)(2,1)}, bf16[256,1280]{1,0:T(8,128)(2,1)}, u32[]{:S(2)}, u32[]{:S(2)}) collective-permute-start(bf16[256,1280]{1,0:T(8,128)(2,1)} %shard_map.477.refs_4_), channel_id=1, source_target_pairs={{0,2},{1,3},{2,0},{3,1},{4,6},{5,7},{6,4},{7,5},{8,10},{9,11},{10,... | collective-permute-start | bytes 1966088 | tf_op jit(solution)/shard_map/ppermute | solution.py:56
  309.7 29.8 %collective-permute-start.45 = (bf16[256,1280]{1,0:T(8,128)(2,1)}, bf16[256,1280]{1,0:T(8,128)(2,1)}, u32[]{:S(2)}, u32[]{:S(2)}) collective-permute-start(bf16[256,1280]{1,0:T(8,128)(2,1)} %get-tuple-element.299), channel_id=1, source_target_pairs={{0,1},{1,0},{2,3},{3,2},{4,5},{5,4},{6,7},{7,6},{8,9},{9,8},{10,11... | collective-permute-start | bytes 1966088 | tf_op jit(solution)/shard_map/ppermute | solution.py:56
  339.0 87.5 %collective-permute-start.40 = (bf16[640,1280]{1,0:T(8,128)(2,1)}, bf16[640,1280]{1,0:T(8,128)(2,1)}, u32[]{:S(2)}, u32[]{:S(2)}) collective-permute-start(bf16[640,1280]{1,0:T(8,128)(2,1)} %get-tuple-element.285), channel_id=1, source_target_pairs={{0,4},{4,0},{1,5},{5,1},{2,6},{6,2},{3,7},{7,3},{8,12},{12,8},{9,1... | collective-permute-start | bytes 4915208 | tf_op jit(solution)/shard_map/ppermute | solution.py:56
  340.8 30.2 %collective-permute-start.46 = (bf16[256,1280]{1,0:T(8,128)(2,1)S(1)}, bf16[256,1280]{1,0:T(8,128)(2,1)S(1)}, u32[]{:S(2)}, u32[]{:S(2)}) collective-permute-start(bf16[256,1280]{1,0:T(8,128)(2,1)S(1)} %shard_map.481.refs_4_), channel_id=1, source_target_pairs={{0,2},{1,3},{2,0},{3,1},{4,6},{5,7},{6,4},{7,5},{8,10},{9,11},{10,... | collective-permute-start | bytes 1966088 | tf_op jit(solution)/shard_map/ppermute | solution.py:56
  363.9 21.7 %collective-permute-start.48 = (bf16[320,1280]{1,0:T(8,128)(2,1)S(1)}, bf16[320,1280]{1,0:T(8,128)(2,1)S(1)}, u32[]{:S(2)}, u32[]{:S(2)}) collective-permute-start(bf16[320,1280]{1,0:T(8,128)(2,1)S(1)} %get-tuple-element.300.refs_7_.refs_0_), channel_id=1, source_target_pairs={{0,8},{24,16},{1,9},{25,17},{2,10},{26,18},{3,11},{27,19},{4,12},{... | collective-permute-start | bytes 2457608 | tf_op jit(solution)/shard_map/ppermute | solution.py:147
  367.0 34.1 %collective-permute-start.49 = (bf16[320,1280]{1,0:T(8,128)(2,1)S(1)}, bf16[320,1280]{1,0:T(8,128)(2,1)S(1)}, u32[]{:S(2)}, u32[]{:S(2)}) collective-permute-start(bf16[320,1280]{1,0:T(8,128)(2,1)S(1)} %get-tuple-element.311.refs_0_), channel_id=1, source_target_pairs={{0,8},{24,16},{1,9},{25,17},{2,10},{26,18},{3,11},{27,19},{4,12},{... | collective-permute-start | bytes 2457608 | tf_op jit(solution)/shard_map/ppermute | solution.py:147
  368.4 59.3 %collective-permute-start.39 = (bf16[640,512]{1,0:T(8,128)(2,1)}, bf16[640,512]{1,0:T(8,128)(2,1)}, u32[]{:S(2)}, u32[]{:S(2)}) collective-permute-start(bf16[640,512]{1,0:T(8,128)(2,1)} %bitcast.34), channel_id=1, source_target_pairs={{0,4},{4,0},{1,5},{5,1},{2,6},{6,2},{3,7},{7,3},{8,12},{12,8},{9,1... | collective-permute-start | bytes 1966088 | tf_op jit(solution)/shard_map/ppermute | solution.py:56
  373.6 13.1 %collective-permute-start.47 = (bf16[256,1280]{1,0:T(8,128)(2,1)S(1)}, bf16[256,1280]{1,0:T(8,128)(2,1)S(1)}, u32[]{:S(2)}, u32[]{:S(2)}) collective-permute-start(bf16[256,1280]{1,0:T(8,128)(2,1)S(1)} %get-tuple-element.301.refs_6_.refs_8_), channel_id=1, source_target_pairs={{0,1},{1,0},{2,3},{3,2},{4,5},{5,4},{6,7},{7,6},{8,9},{9,8},{10,11... | collective-permute-start | bytes 1966088 | tf_op jit(solution)/shard_map/ppermute | solution.py:56
  385.7 42.9 %collective-permute-start.58 = (f32[2,1280]{1,0:T(2,128)S(1)}, f32[2,1280]{1,0:T(2,128)S(1)}, u32[]{:S(2)}, u32[]{:S(2)}) collective-permute-start(f32[2,1280]{1,0:T(2,128)S(1)} %pad_maximum_fusion.7), channel_id=1, source_target_pairs={{0,1},{1,0},{2,3},{3,2},{4,5},{5,4},{6,7},{7,6},{8,9},{9,8},{10,11... | collective-permute-start | bytes 30728 | tf_op jit(solution)/shard_map/ppermute | solution.py:56
  387.6 68.4 %collective-permute-start.50 = (bf16[640,512]{1,0:T(8,128)(2,1)}, bf16[640,512]{1,0:T(8,128)(2,1)}, u32[]{:S(2)}, u32[]{:S(2)}) collective-permute-start(bf16[640,512]{1,0:T(8,128)(2,1)} %bitcast.35), channel_id=1, source_target_pairs={{0,4},{4,0},{1,5},{5,1},{2,6},{6,2},{3,7},{7,3},{8,12},{12,8},{9,1... | collective-permute-start | bytes 1966088 | tf_op jit(solution)/shard_map/ppermute | solution.py:56
  402.0 66.3 %collective-permute-start.52 = (bf16[320,1280]{1,0:T(8,128)(2,1)}, bf16[320,1280]{1,0:T(8,128)(2,1)}, u32[]{:S(2)}, u32[]{:S(2)}) collective-permute-start(bf16[320,1280]{1,0:T(8,128)(2,1)} %shard_map.486.rest_4_.refs_6_.refs_0_), channel_id=1, source_target_pairs={{8,16},{16,8},{9,17},{17,9},{10,18},{18,10},{11,19},{19,11},{12,20... | collective-permute-start | bytes 2457608 | tf_op jit(solution)/shard_map/ppermute | solution.py:148
  426.6 35.9 %collective-permute-start.51 = (bf16[640,512]{1,0:T(8,128)(2,1)}, bf16[640,512]{1,0:T(8,128)(2,1)}, u32[]{:S(2)}, u32[]{:S(2)}) collective-permute-start(bf16[640,512]{1,0:T(8,128)(2,1)} %bitcast.36), channel_id=1, source_target_pairs={{0,4},{4,0},{1,5},{5,1},{2,6},{6,2},{3,7},{7,3},{8,12},{12,8},{9,1... | collective-permute-start | bytes 1966088 | tf_op jit(solution)/shard_map/ppermute | solution.py:56
  427.7 43.2 %collective-permute-start.53 = (bf16[160,1280]{1,0:T(8,128)(2,1)}, bf16[160,1280]{1,0:T(8,128)(2,1)}, u32[]{:S(2)}, u32[]{:S(2)}) collective-permute-start(bf16[160,1280]{1,0:T(8,128)(2,1)} %get-tuple-element.320), channel_id=1, source_target_pairs={{0,4},{4,0},{1,5},{5,1},{2,6},{6,2},{3,7},{7,3},{8,12},{12,8},{9,1... | collective-permute-start | bytes 1228808 | tf_op jit(solution)/shard_map/ppermute | solution.py:56
  428.6 63.0 %collective-permute-start.56 = (bf16[320,1280]{1,0:T(8,128)(2,1)}, bf16[320,1280]{1,0:T(8,128)(2,1)}, u32[]{:S(2)}, u32[]{:S(2)}) collective-permute-start(bf16[320,1280]{1,0:T(8,128)(2,1)} %shard_map.488.refs_7_.refs_0_), channel_id=1, source_target_pairs={{8,16},{16,8},{9,17},{17,9},{10,18},{18,10},{11,19},{19,11},{12,20... | collective-permute-start | bytes 2457608 | tf_op jit(solution)/shard_map/ppermute | solution.py:148
  462.4 16.8 %collective-permute-start.64 = (bf16[256,1280]{1,0:T(8,128)(2,1)}, bf16[256,1280]{1,0:T(8,128)(2,1)}, u32[]{:S(2)}, u32[]{:S(2)}) collective-permute-start(bf16[256,1280]{1,0:T(8,128)(2,1)} %get-tuple-element.357), channel_id=1, source_target_pairs={{0,1},{1,0},{2,3},{3,2},{4,5},{5,4},{6,7},{7,6},{8,9},{9,8},{10,11... | collective-permute-start | bytes 1966088 | tf_op jit(solution)/shard_map/ppermute | solution.py:56
  474.1 25.3 %collective-permute-start.59 = (f32[2720]{0:T(1024)S(1)}, f32[2720]{0:T(1024)S(1)}, u32[]{:S(2)}, u32[]{:S(2)}) collective-permute-start(f32[2720]{0:T(1024)S(1)} %concatenate.193), channel_id=1, source_target_pairs={{0,4},{4,0},{1,5},{5,1},{2,6},{6,2},{3,7},{7,3},{8,12},{12,8},{9,1... | collective-permute-start | bytes 32648 | tf_op jit(solution)/shard_map/ppermute | solution.py:56
  475.3 220.1 %collective-permute-start.33 = (f32[256,1280]{1,0:T(8,128)}, f32[256,1280]{1,0:T(8,128)}, u32[]{:S(2)}, u32[]{:S(2)}) collective-permute-start(f32[256,1280]{1,0:T(8,128)} %copy-done.177), channel_id=1, source_target_pairs={{0,1},{1,0},{2,3},{3,2},{4,5},{5,4},{6,7},{7,6},{8,9},{9,8},{10,11... | collective-permute-start | bytes 3932168 | tf_op jit(solution)/shard_map/ppermute | solution.py:56
  478.9 21.8 %collective-permute-start.61 = (bf16[256,1280]{1,0:T(8,128)(2,1)}, bf16[256,1280]{1,0:T(8,128)(2,1)}, u32[]{:S(2)}, u32[]{:S(2)}) collective-permute-start(bf16[256,1280]{1,0:T(8,128)(2,1)} %get-tuple-element.354), channel_id=1, source_target_pairs={{0,1},{1,0},{2,3},{3,2},{4,5},{5,4},{6,7},{7,6},{8,9},{9,8},{10,11... | collective-permute-start | bytes 1966088 | tf_op jit(solution)/shard_map/ppermute | solution.py:56
  482.8 54.9 %collective-permute-start.65 = (bf16[256,1280]{1,0:T(8,128)(2,1)}, bf16[256,1280]{1,0:T(8,128)(2,1)}, u32[]{:S(2)}, u32[]{:S(2)}) collective-permute-start(bf16[256,1280]{1,0:T(8,128)(2,1)} %shard_map.510.refs_1_), channel_id=1, source_target_pairs={{0,2},{1,3},{2,0},{3,1},{4,6},{5,7},{6,4},{7,5},{8,10},{9,11},{10,... | collective-permute-start | bytes 1966088 | tf_op jit(solution)/shard_map/ppermute | solution.py:56
  491.6 29.3 %collective-permute-start.57 = (bf16[480,1280]{1,0:T(8,128)(2,1)}, bf16[480,1280]{1,0:T(8,128)(2,1)}, u32[]{:S(2)}, u32[]{:S(2)}) collective-permute-start(bf16[480,1280]{1,0:T(8,128)(2,1)} %get-tuple-element.335), channel_id=1, source_target_pairs={{0,4},{4,0},{1,5},{5,1},{2,6},{6,2},{3,7},{7,3},{8,12},{12,8},{9,1... | collective-permute-start | bytes 3686408 | tf_op jit(solution)/shard_map/ppermute | solution.py:56
  499.4 6.3 collective-permute-start.54
  504.2 34.0 %collective-permute-start.62 = (bf16[256,1280]{1,0:T(8,128)(2,1)}, bf16[256,1280]{1,0:T(8,128)(2,1)}, u32[]{:S(2)}, u32[]{:S(2)}) collective-permute-start(bf16[256,1280]{1,0:T(8,128)(2,1)} %shard_map.507.refs_1_), channel_id=1, source_target_pairs={{0,2},{1,3},{2,0},{3,1},{4,6},{5,7},{6,4},{7,5},{8,10},{9,11},{10,... | collective-permute-start | bytes 1966088 | tf_op jit(solution)/shard_map/ppermute | solution.py:56
  507.7 31.7 %collective-permute-start.55 = (bf16[256,1280]{1,0:T(8,128)(2,1)}, bf16[256,1280]{1,0:T(8,128)(2,1)}, u32[]{:S(2)}, u32[]{:S(2)}) collective-permute-start(bf16[256,1280]{1,0:T(8,128)(2,1)} %shard_map.497.refs_1_), channel_id=1, source_target_pairs={{0,2},{1,3},{2,0},{3,1},{4,6},{5,7},{6,4},{7,5},{8,10},{9,11},{10,... | collective-permute-start | bytes 1966088 | tf_op jit(solution)/shard_map/ppermute | solution.py:56
  520.9 174.6 %collective-permute-start.32 = (f32[256,1280]{1,0:T(8,128)}, f32[256,1280]{1,0:T(8,128)S(1)}, u32[]{:S(2)}, u32[]{:S(2)}) collective-permute-start(f32[256,1280]{1,0:T(8,128)} %copy-done.179), channel_id=1, source_target_pairs={{0,1},{1,0},{2,3},{3,2},{4,5},{5,4},{6,7},{7,6},{8,9},{9,8},{10,11... | collective-permute-start | bytes 3932168 | tf_op jit(solution)/shard_map/ppermute | solution.py:56
  537.6 159.3 %collective-permute-start.31 = (f32[256,1280]{1,0:T(8,128)S(1)}, f32[256,1280]{1,0:T(8,128)S(1)}, u32[]{:S(2)}, u32[]{:S(2)}) collective-permute-start(f32[256,1280]{1,0:T(8,128)S(1)} %copy-done.182), channel_id=1, source_target_pairs={{0,1},{1,0},{2,3},{3,2},{4,5},{5,4},{6,7},{7,6},{8,9},{9,8},{10,11... | collective-permute-start | bytes 3932168 | tf_op jit(solution)/shard_map/ppermute | solution.py:56
  538.2 171.6 %collective-permute-start.68 = (bf16[320,1280]{1,0:T(8,128)(2,1)}, bf16[320,1280]{1,0:T(8,128)(2,1)}, u32[]{:S(2)}, u32[]{:S(2)}) collective-permute-start(bf16[320,1280]{1,0:T(8,128)(2,1)} %shard_map.494.refs_6_.rest_1_.whole), channel_id=1, source_target_pairs={{8,0},{16,24},{9,1},{17,25},{10,2},{18,26},{11,3},{19,27},{12,4},{... | collective-permute-start | bytes 2457608 | tf_op jit(solution)/shard_map/ppermute | solution.py:149
  539.5 176.7 %collective-permute-start.67 = (bf16[320,1280]{1,0:T(8,128)(2,1)}, bf16[320,1280]{1,0:T(8,128)(2,1)}, u32[]{:S(2)}, u32[]{:S(2)}) collective-permute-start(bf16[320,1280]{1,0:T(8,128)(2,1)} %shard_map.499.rest_2_.whole), channel_id=1, source_target_pairs={{8,0},{16,24},{9,1},{17,25},{10,2},{18,26},{11,3},{19,27},{12,4},{... | collective-permute-start | bytes 2457608 | tf_op jit(solution)/shard_map/ppermute | solution.py:149
  695.4 56.1 %collective-permute-start.66 = (f32[256,1280]{1,0:T(8,128)}, f32[256,1280]{1,0:T(8,128)}, u32[]{:S(2)}, u32[]{:S(2)}) collective-permute-start(f32[256,1280]{1,0:T(8,128)} %shard_map.511.own), channel_id=1, source_target_pairs={{0,1},{1,0},{2,3},{3,2},{4,5},{5,4},{6,7},{7,6},{8,9},{9,8},{10,11... | collective-permute-start | bytes 3932168 | tf_op jit(solution)/shard_map/ppermute | solution.py:56
  696.5 58.3 %collective-permute-start.63 = (f32[256,1280]{1,0:T(8,128)}, f32[256,1280]{1,0:T(8,128)}, u32[]{:S(2)}, u32[]{:S(2)}) collective-permute-start(f32[256,1280]{1,0:T(8,128)} %shard_map.508.own), channel_id=1, source_target_pairs={{0,1},{1,0},{2,3},{3,2},{4,5},{5,4},{6,7},{7,6},{8,9},{9,8},{10,11... | collective-permute-start | bytes 3932168 | tf_op jit(solution)/shard_map/ppermute | solution.py:56
  698.1 60.0 %collective-permute-start.60 = (f32[256,1280]{1,0:T(8,128)S(1)}, f32[256,1280]{1,0:T(8,128)}, u32[]{:S(2)}, u32[]{:S(2)}) collective-permute-start(f32[256,1280]{1,0:T(8,128)S(1)} %shard_map.505.own), channel_id=1, source_target_pairs={{0,1},{1,0},{2,3},{3,2},{4,5},{5,4},{6,7},{7,6},{8,9},{9,8},{10,11... | collective-permute-start | bytes 3932168 | tf_op jit(solution)/shard_map/ppermute | solution.py:56
  (272 other events, 2138.2 us)
